TPU v7x, 32 devices: a whole 2x2x4 slice. The times are simulated.
32 devices in a mesh: freq: 4 (over x, core), span: 4 (over z), wall: 2 (over y).
Axes of the slice: x: 2, y: 2, z: 4, core: 2. Of those that a mesh axis runs over, the one named last changes fastest.
Arguments:
- amplitudes: float32 [2, 5, 128, 32768], P(None, None, 'wall', ('freq', 'span')), may hold values from -20 to 20
- upstream: float32 [2, 5, 128, 32768], P(None, None, 'wall', ('freq', 'span')), may hold values from -6 to 6
- harmonic_mask: int32 [32768], P(('freq', 'span')), may hold values 0 or 1
- quadratic_coefficients: float32 [5, 5, 5], replicated, may hold values from -1.25 to 1.25
- slab_inverse: float32 [2, 320, 320], P('wall'), may hold values from -1 to 2
- lower_coupling: float32 [2, 5, 5], P('wall'), may hold values from -2.5 to 2.5
- upper_coupling: float32 [2, 5, 5], P('wall'), may hold values from -2.5 to 2.5
- reduced_lower: float32 [2, 10, 10], P('wall'), may hold values from -1 to 1
- reduced_upper: float32 [2, 10, 10], P('wall'), may hold values from -1 to 1
- reduced_pivot: float32 [2, 10, 10], P('wall'), may hold values from -2 to 3
Outputs:
- new_amplitudes: float32 [2, 5, 128, 32768], P(None, None, 'wall', ('freq', 'span'))
- wavenumber_shift: float32 [2, 32768], P(None, ('freq', 'span'))
Inputs may be any that keep to these rules, and one draw needn't show every extreme that they name: `harmonic_mask`: 1 marks a retained mode.
All inputs are finite; a program needn't handle non-finite values. No bound on the sum of `harmonic_mask` on one device may be relied on, other than what follows from the above.
Results may differ from a plain program's by a relative error of at most 0.0001.
Values sent between devices are 32-bit elements; how exact they have to be, the bound alone decides.
No kernel may reach another device: no remote copies, remote signals or barrier semaphores. Data moves between devices by JAX's collectives and lax.ppermute only.
A program may use at most 64 MiB of HBM per device.

v0:
```python
import functools
import math

import jax
import jax.numpy as jnp
import numpy as np
from jax import lax
from jax.experimental import pallas as pl
from jax.experimental.pallas import tpu as pltpu
from jax.sharding import PartitionSpec as P

NF = 128
NB = 256

epsilon = 1e-06

SPLIT = lax.Precision.HIGH
FULL = lax.Precision.HIGHEST
GATHERED_ROWS = 24


def tables():
    def turns(length):
        counter = np.arange(length)
        angles = (counter[:, None] * counter[None, :] % length) * (2.0 * math.pi / length)
        return np.cos(angles), np.sin(angles)

    cos_time, sin_time = turns(NF)
    cos_span, sin_span = turns(NB)
    scale = 1.0 / math.sqrt(NF * NB)
    out = (
        np.block([[cos_time, -sin_time], [sin_time, cos_time]]),
        np.concatenate([cos_span, -sin_span], 0) * scale,
        np.concatenate([cos_span, -sin_span], 1) * scale,
        np.block([[cos_time, sin_time], [-sin_time, cos_time]]),
    )
    return [jnp.asarray(table.astype(np.float32)) for table in out]


def params(megabytes=40):
    return pltpu.CompilerParams(vmem_limit_bytes=megabytes * 1024 * 1024)


def whole(array):
    zeros = (0,) * array.ndim
    return pl.BlockSpec(array.shape, lambda *_: zeros)


def prepare_body(x_ref, mask_ref, out_ref):
    keep = mask_ref[...]
    rows, _, freqs, _ = out_ref.shape
    for part in range(2):
        kept = x_ref[part, 0] * keep
        out_ref[:, 0, :, part * NB : (part + 1) * NB] = kept.reshape(rows, freqs, NB)


def prepare(amplitudes, keep, start, rows):
    _, variables, _, modes = amplitudes.shape
    freqs = modes // NB
    at = start // rows
    return pl.pallas_call(
        prepare_body,
        grid=(variables,),
        in_specs=[
            pl.BlockSpec((2, 1, rows, modes), lambda v: (0, v, at, 0)),
            pl.BlockSpec((1, modes), lambda v: (0, 0)),
        ],
        out_specs=pl.BlockSpec((rows, 1, freqs, 2 * NB), lambda v: (0, v, 0, 0)),
        out_shape=jax.ShapeDtypeStruct((rows, variables, freqs, 2 * NB), jnp.float32),
        compiler_params=params(),
        name="prepare",
    )(amplitudes, keep)


def nonlinear_body(q_ref, in_ref, wi_ref, ei_ref, ef_ref, wf_ref, out_ref, field_ref, force_ref):
    devices, _, variables, freqs, _ = in_ref.shape
    for v in range(variables):
        modes = in_ref[:, 0, v].reshape(NF, 2 * NB)
        stacked = jnp.concatenate([modes[:, :NB], modes[:, NB:]], axis=0)
        turned = jnp.dot(
            wi_ref[...], stacked, precision=SPLIT, preferred_element_type=jnp.float32
        )
        beside = jnp.concatenate([turned[:NF], turned[NF:]], axis=1)
        field_ref[v] = jnp.dot(
            beside, ei_ref[...], precision=SPLIT, preferred_element_type=jnp.float32
        )
    pairs = [(a, b) for a in range(variables) for b in range(a + 1, variables)]
    weights = [
        [q_ref[w * variables + a, b] + q_ref[w * variables + b, a] for a, b in pairs]
        for w in range(variables)
    ]
    step = 8
    for row in range(0, NF, step):
        at = slice(row, row + step)
        values = [field_ref[v, at] for v in range(variables)]
        total = [None] * variables
        for i, (a, b) in enumerate(pairs):
            product = values[a] * values[b]
            for w in range(variables):
                term = weights[w][i] * product
                total[w] = term if total[w] is None else total[w] + term
        for w in range(variables):
            force_ref[w, at] = total[w]
    for w in range(variables):
        spread = jnp.dot(
            force_ref[w], ef_ref[...], precision=SPLIT, preferred_element_type=jnp.float32
        )
        stacked = jnp.concatenate([spread[:, :NB], spread[:, NB:]], axis=0)
        turned = jnp.dot(
            wf_ref[...], stacked, precision=SPLIT, preferred_element_type=jnp.float32
        )
        for part in range(2):
            piece = turned[part * NF : (part + 1) * NF]
            out_ref[:, 0, w, :, part * NB : (part + 1) * NB] = piece.reshape(devices, freqs, NB)


def nonlinear(block, coefficients, transforms):
    devices, points, variables, freqs, lanes = block.shape
    spec = pl.BlockSpec((devices, 1, variables, freqs, lanes), lambda j: (0, j, 0, 0, 0))
    flops = points * variables * 12 * NF * NB * (NF + NB) * 2
    return pl.pallas_call(
        nonlinear_body,
        grid=(points,),
        in_specs=[pl.BlockSpec(memory_space=pltpu.SMEM), spec] + [whole(t) for t in transforms],
        out_specs=spec,
        out_shape=jax.ShapeDtypeStruct(block.shape, jnp.float32),
        scratch_shapes=[pltpu.VMEM((variables, NF, NB), jnp.float32)] * 2,
        compiler_params=params(),
        cost_estimate=pl.CostEstimate(
            flops=flops, bytes_accessed=2 * block.size * 4, transcendentals=0
        ),
        name="nonlinear",
    )(coefficients, block, *transforms)


def adjoint_body(x_ref, mask_ref, inverse_ref, out_ref, edge_ref):
    _, variables, heights, lanes = x_ref.shape
    extent = variables * heights
    keep = mask_ref[...]
    weight = jnp.zeros((1, lanes), jnp.float32)
    for part in range(2):
        kept = x_ref[part].reshape(extent, lanes) * keep
        weight = weight + jnp.sum(kept * kept, axis=0, keepdims=True)
        moved = jnp.dot(
            inverse_ref[...], kept, precision=SPLIT, preferred_element_type=jnp.float32
        )
        out_ref[part] = moved.reshape(variables, heights, lanes)
        for end, point in enumerate((0, heights - 1)):
            for v in range(variables):
                row = part * 2 * variables + end * variables + v
                at = v * heights + point
                edge_ref[row : row + 1] = moved[at : at + 1]
    last = 4 * variables
    edge_ref[last : last + 1] = weight
    edge_ref[last + 1 :] = jnp.zeros((GATHERED_ROWS - last - 1, lanes), jnp.float32)


def adjoint(amplitudes, keep, inverse_t):
    _, variables, heights, modes = amplitudes.shape
    spec = pl.BlockSpec((2, variables, heights, NB), lambda i: (0, 0, 0, i))
    return pl.pallas_call(
        adjoint_body,
        grid=(modes // NB,),
        in_specs=[spec, pl.BlockSpec((1, NB), lambda i: (0, i)), whole(inverse_t)],
        out_specs=[spec, pl.BlockSpec((GATHERED_ROWS, NB), lambda i: (0, i))],
        out_shape=[
            jax.ShapeDtypeStruct(amplitudes.shape, jnp.float32),
            jax.ShapeDtypeStruct((GATHERED_ROWS, modes), jnp.float32),
        ],
        compiler_params=params(),
        name="adjoint",
    )(amplitudes, keep, inverse_t)


def absorb_body(first, *refs):
    if first:
        in_ref, up_ref, mask_ref, edge_ref, adj_ref, out_ref, sum_ref = refs
    else:
        in_ref, up_ref, mask_ref, edge_ref, adj_ref, before_ref, out_ref, sum_ref = refs
    rows, _, freqs, _ = in_ref.shape
    ends = edge_ref.shape[1]
    keep = mask_ref[...]

    @pl.when(pl.program_id(0) == 0)
    def _():
        if first:
            sum_ref[...] = jnp.zeros(sum_ref.shape, jnp.float32)
        else:
            sum_ref[...] = before_ref[...]

    sides = []
    for part in range(2):
        forced = in_ref[:, 0, :, part * NB : (part + 1) * NB].reshape(rows, freqs * NB)
        side = (forced + up_ref[part, 0]) * keep
        out_ref[part, 0] = side
        at = slice(part * ends, (part + 1) * ends)
        sum_ref[at] += jnp.dot(
            edge_ref[0], side, precision=SPLIT, preferred_element_type=jnp.float32
        )
        sides.append(side)
    real, imag = adj_ref[0, 0], adj_ref[1, 0]
    at = 2 * ends
    sum_ref[at : at + 1] += jnp.sum(real * sides[0] + imag * sides[1], axis=0, keepdims=True)
    sum_ref[at + 1 : at + 2] += jnp.sum(real * sides[1] - imag * sides[0], axis=0, keepdims=True)


def absorb(block, upstream, keep, edges, adjoint_modes, before, start):
    rows, variables, freqs, lanes = block.shape
    modes = keep.shape[1]
    at = start // rows
    ends = edges.shape[1]
    grid_spec = pl.BlockSpec((2, 1, rows, modes), lambda v: (0, v, at, 0))
    sums = pl.BlockSpec((GATHERED_ROWS, modes), lambda v: (0, 0))
    operands = [block, upstream, keep, edges, adjoint_modes]
    in_specs = [
        pl.BlockSpec((rows, 1, freqs, lanes), lambda v: (0, v, 0, 0)),
        grid_spec,
        pl.BlockSpec((1, modes), lambda v: (0, 0)),
        pl.BlockSpec((1, ends, rows), lambda v: (v, 0, 0)),
        grid_spec,
    ]
    if before is not None:
        operands.append(before)
        in_specs.append(sums)
    return pl.pallas_call(
        functools.partial(absorb_body, before is None),
        grid=(variables,),
        in_specs=in_specs,
        out_specs=[pl.BlockSpec((2, 1, rows, modes), lambda v: (0, v, 0, 0)), sums],
        out_shape=[
            jax.ShapeDtypeStruct((2, variables, rows, modes), jnp.float32),
            jax.ShapeDtypeStruct((GATHERED_ROWS, modes), jnp.float32),
        ],
        compiler_params=params(),
        name="absorb",
    )(*operands)


def finish_body(chunks, walls, *refs):
    sides, refs = refs[:chunks], refs[chunks:]
    bounds, refs = refs[:walls], refs[walls:]
    edges, refs = refs[:walls], refs[walls:]
    solve_ref, chain_ref, out_ref, shift_ref = refs
    _, variables, heights, lanes = out_ref.shape
    ends = 2 * variables
    pushed = []
    for part in range(2):
        at = slice(part * ends, (part + 1) * ends)
        everywhere = jnp.concatenate([ref[at] for ref in bounds], axis=0)
        pushed.append(
            jnp.dot(
                chain_ref[...], everywhere, precision=FULL, preferred_element_type=jnp.float32
            )
        )
        stacked = [ref[part].reshape(-1, lanes) for ref in sides]
        stacked = jnp.concatenate(stacked + [pushed[part][:ends]], axis=0)
        moved = jnp.dot(
            solve_ref[...], stacked, precision=SPLIT, preferred_element_type=jnp.float32
        )
        out_ref[part] = moved.reshape(variables, heights, lanes)
    real = imag = weight = 0.0
    for wall in range(walls):
        at = slice(wall * ends, (wall + 1) * ends)
        push = [pushed[part][at] for part in range(2)]
        edge = [edges[wall][part * ends : (part + 1) * ends] for part in range(2)]
        row = 2 * ends
        squares = edges[wall][row : row + 1]
        taken = jnp.sum(edge[0] * push[0] + edge[1] * push[1], axis=0, keepdims=True)
        real = real + (bounds[wall][row : row + 1] - taken - squares)
        taken = jnp.sum(edge[0] * push[1] - edge[1] * push[0], axis=0, keepdims=True)
        imag = imag + (bounds[wall][row + 1 : row + 2] - taken)
        weight = weight + squares
    weight = weight + epsilon
    shift_ref[0:1] = imag / weight
    shift_ref[1:2] = -real / weight


def finish(sides, bounds, edges, solve, chain, heights):
    _, variables, _, modes = sides[0].shape
    walls = len(bounds)
    small = pl.BlockSpec((GATHERED_ROWS, NB), lambda i: (0, i))
    return pl.pallas_call(
        functools.partial(finish_body, len(sides), walls),
        grid=(modes // NB,),
        in_specs=[
            pl.BlockSpec((2, variables, side.shape[2], NB), lambda i: (0, 0, 0, i))
            for side in sides
        ]
        + [small] * (2 * walls)
        + [whole(solve), whole(chain)],
        out_specs=[
            pl.BlockSpec((2, variables, heights, NB), lambda i: (0, 0, 0, i)),
            pl.BlockSpec((2, NB), lambda i: (0, i)),
        ],
        out_shape=[
            jax.ShapeDtypeStruct((2, variables, heights, modes), jnp.float32),
            jax.ShapeDtypeStruct((2, modes), jnp.float32),
        ],
        compiler_params=params(),
        name="finish",
    )(*sides, *bounds, *edges, solve, chain)


def around(block, axis):
    count = lax.axis_size(axis)
    return [block] + [
        lax.ppermute(block, axis, [(i, (i + d) % count) for i in range(count)])
        for d in range(1, count)
    ]


def interface_chain(lower_coupling, upper_coupling, reduced_lower, reduced_upper, reduced_pivot):
    gathered = [
        lax.all_gather(part[0], "wall")
        for part in (lower_coupling, upper_coupling, reduced_lower, reduced_upper, reduced_pivot)
    ]
    low, up, red_low, red_up, pivot = gathered
    walls = low.shape[0]
    ends = red_low.shape[1]
    half = ends // 2
    dot = functools.partial(jnp.dot, precision=FULL)
    units = jnp.eye(walls * ends, dtype=jnp.float32).reshape(walls, ends, walls * ends)
    ahead = [units[0]]
    for j in range(1, walls):
        ahead.append(units[j] - dot(red_low[j], ahead[j - 1]))
    interface = [None] * walls
    interface[-1] = dot(pivot[-1], ahead[-1])
    for j in range(walls - 2, -1, -1):
        interface[j] = dot(pivot[j], ahead[j] - dot(red_up[j], interface[j + 1]))
    none = jnp.zeros((half, walls * ends), jnp.float32)
    rows = []
    for j in range(walls):
        rows.append(dot(low[j], interface[j - 1][half:]) if j > 0 else none)
        rows.append(dot(up[j], interface[j + 1][:half]) if j < walls - 1 else none)
    chain = jnp.concatenate(rows, axis=0).reshape(walls, ends, walls, ends)
    order = (lax.axis_index("wall") - jnp.arange(walls)) % walls
    chain = jnp.take(jnp.take(chain, order, axis=0), order, axis=2)
    return chain.reshape(walls * ends, walls * ends)


def local(
    amplitudes,
    upstream,
    harmonic_mask,
    quadratic_coefficients,
    slab_inverse,
    lower_coupling,
    upper_coupling,
    reduced_lower,
    reduced_upper,
    reduced_pivot,
):
    _, variables, heights, modes = amplitudes.shape
    freqs = modes // NB
    extent = variables * heights
    axes = ("freq", "span")
    devices = lax.axis_size("freq") * lax.axis_size("span")
    points = heights // devices
    sizes = [points // 2, points // 2] if points % 2 == 0 else [points]
    starts = [devices * sum(sizes[:i]) for i in range(len(sizes))]
    transforms = tables()
    keep = harmonic_mask.astype(jnp.float32).reshape(1, modes)
    coefficients = quadratic_coefficients.reshape(variables * variables, variables)

    def exchange(block):
        return lax.all_to_all(block, axes, split_axis=0, concat_axis=0, tiled=True)

    arrived = []
    for start, size in zip(starts, sizes):
        arrived.append(exchange(prepare(amplitudes, keep, start, devices * size)))

    inverse = slab_inverse[0]
    columns = inverse.reshape(extent, variables, heights)
    end_rows = inverse.reshape(variables, heights, variables, heights)
    end_rows = jnp.concatenate([end_rows[:, 0], end_rows[:, heights - 1]], axis=0)
    end_rows = jnp.swapaxes(end_rows, 0, 1)
    end_columns = jnp.concatenate([columns[:, :, 0], columns[:, :, heights - 1]], axis=1)
    cuts = [slice(start, start + devices * size) for start, size in zip(starts, sizes)]
    solve = jnp.concatenate(
        [columns[:, :, cut].reshape(extent, -1) for cut in cuts] + [-end_columns], axis=1
    )
    adjoint_modes, edge = adjoint(amplitudes, keep, inverse.T)
    edges = around(edge, "wall")
    chain = interface_chain(
        lower_coupling, upper_coupling, reduced_lower, reduced_upper, reduced_pivot
    )

    returned = []
    for block, size in zip(arrived, sizes):
        shape = block.shape
        forced = nonlinear(block.reshape((devices, size) + shape[1:]), coefficients, transforms)
        returned.append(exchange(forced.reshape(shape)))

    sides = []
    sums = None
    for block, start, cut in zip(returned, starts, cuts):
        side, sums = absorb(
            block, upstream, keep, end_rows[:, :, cut], adjoint_modes, sums, start
        )
        sides.append(side)
    bounds = around(sums, "wall")
    new_amplitudes, wavenumber_shift = finish(sides, bounds, edges, solve, chain, heights)
    return (new_amplitudes, wavenumber_shift)


def solution(mesh):
    placed = (
        P(None, None, "wall", ("freq", "span")),
        P(None, None, "wall", ("freq", "span")),
        P(("freq", "span")),
        P(),
        P("wall", None, None),
        P("wall", None, None),
        P("wall", None, None),
        P("wall", None, None),
        P("wall", None, None),
        P("wall", None, None),
    )
    return jax.shard_map(
        local,
        mesh=mesh,
        in_specs=placed,
        out_specs=(P(None, None, "wall", ("freq", "span")), P(None, ("freq", "span"))),
        check_vma=False,
    )
```

profile of v0, /device:TPU:10, one launch (start us, length us, event | category | flops | bytes accessed | tf_op | source)
XLA Modules:
  0.0 293.2 jit_solution(7343663189800574967)
XLA Ops:
  0.6 0.7 convert_element_type.8
  1.3 2.5 copy-done
  3.8 2.8 prepare.2
  6.7 6.2 %all-to-all-start = ((f32[32,5,8,512]{3,2,1,0:T(8,128)}), f32[32,5,8,512]{3,2,1,0:T(8,128)}, u32[]{:S(2)}, u32[]{:S(2)}) async-start(f32[32,5,8,512]{3,2,1,0:T(8,128)} %prepare.2), calls=%async_computation | async-start | bytes 5242880 | tf_op jit(solution)/shard_map/all_to_all | solution.py:366
  12.9 2.5 copy-done.1
  15.4 3.0 %prepare.3 = f32[32,5,8,512]{3,2,1,0:T(8,128)} custom-call(f32[2,5,64,2048]{3,2,1,0:T(8,128)S(1)} %copy-done.1, f32[1,2048]{1,0:T(1,128)S(1)} %bitcast.66), custom_call_target="tpu_custom_call" | custom-call | tf_op jit(solution)/shard_map/prepare/pallas_call | solution.py:61
  18.4 51.6 %all-to-all-done = f32[32,5,8,512]{3,2,1,0:T(8,128)} async-done(((f32[32,5,8,512]{3,2,1,0:T(8,128)}), f32[32,5,8,512]{3,2,1,0:T(8,128)}, u32[]{:S(2)}, u32[]{:S(2)}) %all-to-all-start) | async-done | bytes 2621472 | tf_op jit(solution)/shard_map/all_to_all | solution.py:366
  70.0 8.0 %all-to-all-start.2 = ((f32[32,5,8,512]{3,2,1,0:T(8,128)}), f32[32,5,8,512]{3,2,1,0:T(8,128)}, u32[]{:S(2)}, u32[]{:S(2)}) async-start(f32[32,5,8,512]{3,2,1,0:T(8,128)} %prepare.3), calls=%async_computation.2 | async-start | bytes 5242880 | tf_op jit(solution)/shard_map/all_to_all | solution.py:366
  78.1 1.0 copy-done.14
  79.1 1.0 copy-done.16
  80.1 8.0 %nonlinear.2 = f32[16,2,5,8,512]{4,3,2,1,0:T(8,128)S(1)} custom-call(f32[25,5]{1,0:T(8,128)S(1)} %reshape.120.q_ref, f32[16,2,5,8,512]{4,3,2,1,0:T(8,128)} %bitcast.1.in_ref, f32[256,256]{1,0:T(8,128)S(1)} %copy-done.18, f32[512,256]{1,0:T(8,128)S(1)} %copy-done.14, f32[256,512]{1,0:T(8,128)S(1)} %copy-done.16, f32[256,256]{1,0:T(8,128)S(1)} %copy-done.19), custom_call_target="tpu_custom_call" | custom-call | flops 3019898880 | bytes 5242880 | tf_op jit(solution)/shard_map/nonlinear/pallas_call | solution.py:121
  88.1 1.5 copy-done.11
  89.6 45.5 %all-to-all-done.2 = f32[32,5,8,512]{3,2,1,0:T(8,128)} async-done(((f32[32,5,8,512]{3,2,1,0:T(8,128)}), f32[32,5,8,512]{3,2,1,0:T(8,128)}, u32[]{:S(2)}, u32[]{:S(2)}) %all-to-all-start.2) | async-done | bytes 2621472 | tf_op jit(solution)/shard_map/all_to_all | solution.py:366
  135.1 7.4 %all-to-all-start.1 = ((f32[32,5,8,512]{3,2,1,0:T(8,128)}), f32[32,5,8,512]{3,2,1,0:T(8,128)S(1)}, u32[]{:S(2)}, u32[]{:S(2)}) async-start(f32[32,5,8,512]{3,2,1,0:T(8,128)} %bitcast.64), calls=%async_computation.1 | async-start | bytes 5242880 | tf_op jit(solution)/shard_map/all_to_all | solution.py:366
  142.5 1.0 copy-done.15
  143.5 1.0 copy-done.17
  144.6 8.0 %nonlinear.3 = f32[16,2,5,8,512]{4,3,2,1,0:T(8,128)S(1)} custom-call(f32[25,5]{1,0:T(8,128)S(1)} %reshape.120.q_ref, f32[16,2,5,8,512]{4,3,2,1,0:T(8,128)} %bitcast.8.in_ref, f32[256,256]{1,0:T(8,128)S(1)} %copy-done.18, f32[512,256]{1,0:T(8,128)S(1)} %copy-done.15, f32[256,512]{1,0:T(8,128)S(1)} %copy-done.17, f32[256,256]{1,0:T(8,128)S(1)} %copy-done.19), custom_call_target="tpu_custom_call" | custom-call | flops 3019898880 | bytes 5242880 | tf_op jit(solution)/shard_map/nonlinear/pallas_call | solution.py:121
  152.6 1.5 copy-done.8
  154.0 45.5 %all-to-all-done.1.refs_0_ = f32[32,5,8,512]{3,2,1,0:T(8,128)S(1)} async-done(((f32[32,5,8,512]{3,2,1,0:T(8,128)}), f32[32,5,8,512]{3,2,1,0:T(8,128)S(1)}, u32[]{:S(2)}, u32[]{:S(2)}) %all-to-all-start.1) | async-done | bytes 2621472 | tf_op jit(solution)/shard_map/all_to_all | solution.py:366
  199.6 1.5 copy-done.6
  201.1 7.3 %all-to-all-start.3 = ((f32[32,5,8,512]{3,2,1,0:T(8,128)}), f32[32,5,8,512]{3,2,1,0:T(8,128)S(1)}, u32[]{:S(2)}, u32[]{:S(2)}) async-start(f32[32,5,8,512]{3,2,1,0:T(8,128)} %bitcast.63), calls=%async_computation.3 | async-start | bytes 5242880 | tf_op jit(solution)/shard_map/all_to_all | solution.py:366
  208.4 1.2 copy.81
  209.6 2.5 copy-done.2
  212.1 6.7 %adjoint.1 = (f32[2,5,64,2048]{3,2,1,0:T(8,128)S(1)}, f32[24,2048]{1,0:T(8,128)S(1)}) custom-call(f32[2,5,64,2048]{3,2,1,0:T(8,128)S(1)} %copy-done.2, f32[1,2048]{1,0:T(1,128)S(1)} %bitcast.67, f32[320,320]{1,0:T(8,128)S(1)} %bitcast.60), custom_call_target="tpu_custom_call" | custom-call | tf_op jit(solution)/shard_map/adjoint/pallas_call | solution.py:161
  218.8 2.3 copy-done.5
  221.1 1.5 collective-permute-start.1
  222.7 2.3 reshape_squeeze.6
  225.0 0.8 copy.86
  225.8 0.8 fusion.11
  226.6 1.8 copy.85
  228.5 1.8 copy.84
  230.3 0.7 copy.91
  231.0 0.7 copy.90
  231.7 0.7 copy.89
  232.4 4.3 %all_gather.19 = f32[2,5,5]{2,1,0:T(8,128)S(1)} all-gather(f32[1,5,5]{2,1,0:T(8,128)S(1)} %copy.91), channel_id=1, replica_groups=mesh['freq'=4,'span'=4,'wall'=2] {'wall'}, dimensions={0}, use_global_device_ids=true | all-gather | bytes 300 | tf_op jit(solution)/shard_map/all_gather | solution.py:314
  236.7 4.3 %all_gather.17 = f32[2,5,5]{2,1,0:T(8,128)S(1)} all-gather(f32[1,5,5]{2,1,0:T(8,128)S(1)} %copy.89), channel_id=1, replica_groups=mesh['freq'=4,'span'=4,'wall'=2] {'wall'}, dimensions={0}, use_global_device_ids=true | all-gather | bytes 300 | tf_op jit(solution)/shard_map/all_gather | solution.py:314
  241.0 4.4 %all_gather.15 = f32[2,10,10]{2,1,0:T(8,128)S(1)} all-gather(f32[1,10,10]{2,1,0:T(8,128)S(1)} %copy.87), channel_id=1, replica_groups=mesh['freq'=4,'span'=4,'wall'=2] {'wall'}, dimensions={0}, use_global_device_ids=true | all-gather | bytes 1200 | tf_op jit(solution)/shard_map/all_gather | solution.py:314
  245.4 4.4 %all_gather.16 = f32[2,10,10]{2,1,0:T(8,128)S(1)} all-gather(f32[1,10,10]{2,1,0:T(8,128)S(1)} %copy.88), channel_id=1, replica_groups=mesh['freq'=4,'span'=4,'wall'=2] {'wall'}, dimensions={0}, use_global_device_ids=true | all-gather | bytes 1200 | tf_op jit(solution)/shard_map/all_gather | solution.py:314
  249.7 4.5 %all_gather.18 = f32[2,10,10]{2,1,0:T(8,128)S(1)} all-gather(f32[1,10,10]{2,1,0:T(8,128)S(1)} %copy.90), channel_id=1, replica_groups=mesh['freq'=4,'span'=4,'wall'=2] {'wall'}, dimensions={0}, use_global_device_ids=true | all-gather | bytes 1200 | tf_op jit(solution)/shard_map/all_gather | solution.py:314
  254.3 0.1 fusion.1
  254.4 0.1 fusion.2
  254.5 0.1 fusion
  254.7 0.1 convolution_bitcast_fusion
  254.8 0.1 convolution_bitcast_fusion.3
  255.0 0.1 convolution_bitcast_fusion.4
  255.1 0.1 reshape.103
  255.2 0.6 gather_fusion
  255.8 0.1 broadcast_select_fusion
  255.9 0.6 gather_fusion.1
  256.5 0.7 gather.12
  257.3 0.7 broadcast_in_dim.28
  258.0 0.8 fusion.10
  258.8 1.4 pad_maximum_fusion.refs_6_
  260.2 2.5 copy-done.3
  262.7 1.7 copy-done.7
  264.4 5.0 %absorb.2 = (f32[2,5,32,2048]{3,2,1,0:T(8,128)S(1)}, f32[24,2048]{1,0:T(8,128)S(1)}) custom-call(f32[32,5,8,512]{3,2,1,0:T(8,128)S(1)} %copy-done.7, f32[2,5,64,2048]{3,2,1,0:T(8,128)S(1)} %copy-done.3, f32[1,2048]{1,0:T(1,128)S(1)} %bitcast.68, f32[5,10,32]{2,1,0:T(8,128)S(1)} %get-tuple-element.21.refs_3_, f32[2,5,64,2048]{3,2,1,0:T(8,128)} %copy-done.5), custom_call_target="tpu_custom_call" | custom-call | tf_op jit(solution)/shard_map/absorb/pallas_call | solution.py:225
  269.4 1.5 copy-done.9
  270.9 0.7 copy-done.12
  271.6 2.5 copy-done.4
  274.1 0.9 copy-done.13
  275.0 5.1 %absorb.3 = (f32[2,5,32,2048]{3,2,1,0:T(8,128)S(1)}, f32[24,2048]{1,0:T(8,128)S(1)}) custom-call(f32[32,5,8,512]{3,2,1,0:T(8,128)S(1)} %all-to-all-done.3.refs_0_, f32[2,5,64,2048]{3,2,1,0:T(8,128)S(1)} %copy-done.4, f32[1,2048]{1,0:T(1,128)S(1)} %bitcast.69, f32[5,10,32]{2,1,0:T(8,128)S(1)} %get-tuple-element.20.refs_3_, f32[2,5,64,2048]{3,2,1,0:T(8,128)} %copy-done.5, ...), custom_call_target="tpu_custom_call" | custom-call | tf_op jit(solution)/shard_map/absorb/pallas_call | solution.py:225
  280.1 0.6 collective-permute-start
  280.8 5.1 %collective-permute-done.refs_3_ = f32[24,2048]{1,0:T(8,128)S(1)} collective-permute-done((f32[24,2048]{1,0:T(8,128)S(1)}, f32[24,2048]{1,0:T(8,128)S(1)}, u32[]{:S(2)}, u32[]{:S(2)}) %collective-permute-start) | collective-permute-done | bytes 196640 | tf_op jit(solution)/shard_map/ppermute | solution.py:307
  285.9 7.4 %finish.1 = (f32[2,5,64,2048]{3,2,1,0:T(8,128)}, f32[2,2048]{1,0:T(2,128)}) custom-call(f32[2,5,32,2048]{3,2,1,0:T(8,128)S(1)} %copy-done.10, f32[2,5,32,2048]{3,2,1,0:T(8,128)S(1)} %get-tuple-element.11.refs_1_, f32[24,2048]{1,0:T(8,128)S(1)} %get-tuple-element.12.refs_2_, f32[24,2048]{1,0:T(8,128)S(1)} %collective-permute-done.refs_3_, ...), custom_call_target="tpu_custom_call" | custom-call | tf_op jit(solution)/shard_map/finish/pallas_call | solution.py:282
  (55 shorter events, 0.4 us)
Async XLA Ops:
  1.3 2.5 copy-start
  6.7 63.3 %all-to-all-start = ((f32[32,5,8,512]{3,2,1,0:T(8,128)}), f32[32,5,8,512]{3,2,1,0:T(8,128)}, u32[]{:S(2)}, u32[]{:S(2)}) async-start(f32[32,5,8,512]{3,2,1,0:T(8,128)} %prepare.2), calls=%async_computation | async-start | bytes 5242880 | tf_op jit(solution)/shard_map/all_to_all | solution.py:366
  12.9 2.5 copy-start.1
  18.4 59.6 %copy-start.21 = (f32[5,5,5]{2,1,0:T(8,128)S(1)}, f32[5,5,5]{2,1,0:T(8,128)}, u32[]{:S(2)}) copy-start(f32[5,5,5]{2,1,0:T(8,128)} %param.17) | copy-start | bytes 1504
  18.4 59.7 %copy-start.18 = (f32[256,256]{1,0:T(8,128)S(1)}, f32[256,256]{1,0:T(8,128)}, u32[]{:S(2)}) copy-start(f32[256,256]{1,0:T(8,128)} %constant.56.clone.wi_ref) | copy-start | bytes 786436
  18.4 59.7 %copy-start.19 = (f32[256,256]{1,0:T(8,128)S(1)}, f32[256,256]{1,0:T(8,128)}, u32[]{:S(2)}) copy-start(f32[256,256]{1,0:T(8,128)} %constant.59.clone.wf_ref) | copy-start | bytes 786436
  70.0 65.1 %all-to-all-start.2 = ((f32[32,5,8,512]{3,2,1,0:T(8,128)}), f32[32,5,8,512]{3,2,1,0:T(8,128)}, u32[]{:S(2)}, u32[]{:S(2)}) async-start(f32[32,5,8,512]{3,2,1,0:T(8,128)} %prepare.3), calls=%async_computation.2 | async-start | bytes 5242880 | tf_op jit(solution)/shard_map/all_to_all | solution.py:366
  78.1 1.0 copy-start.14
  79.1 1.0 copy-start.16
  88.1 1.5 copy-start.11
  135.1 64.5 %all-to-all-start.1 = ((f32[32,5,8,512]{3,2,1,0:T(8,128)}), f32[32,5,8,512]{3,2,1,0:T(8,128)S(1)}, u32[]{:S(2)}, u32[]{:S(2)}) async-start(f32[32,5,8,512]{3,2,1,0:T(8,128)} %bitcast.64), calls=%async_computation.1 | async-start | bytes 5242880 | tf_op jit(solution)/shard_map/all_to_all | solution.py:366
  142.5 1.0 copy-start.15
  143.5 1.0 copy-start.17
  152.6 1.5 copy-start.8
  199.6 1.5 copy-start.6
  201.1 70.5 %all-to-all-start.3 = ((f32[32,5,8,512]{3,2,1,0:T(8,128)}), f32[32,5,8,512]{3,2,1,0:T(8,128)S(1)}, u32[]{:S(2)}, u32[]{:S(2)}) async-start(f32[32,5,8,512]{3,2,1,0:T(8,128)} %bitcast.63), calls=%async_computation.3 | async-start | bytes 5242880 | tf_op jit(solution)/shard_map/all_to_all | solution.py:366
  209.6 2.5 copy-start.2
  218.8 2.4 copy-start.5
  221.1 9.8 %copy-start.22 = (f32[1,10,10]{2,0,1:T(1,128)S(1)}, f32[1,10,10]{2,0,1:T(1,128)}, u32[]{:S(2)}) copy-start(f32[1,10,10]{2,0,1:T(1,128)} %param.21) | copy-start | bytes 1204
  221.1 9.8 %copy-start.23 = (f32[1,10,10]{2,0,1:T(1,128)S(1)}, f32[1,10,10]{2,0,1:T(1,128)}, u32[]{:S(2)}) copy-start(f32[1,10,10]{2,0,1:T(1,128)} %param.23) | copy-start | bytes 1204
  221.1 59.6 %collective-permute-start.1 = (f32[24,2048]{1,0:T(8,128)S(1)}, f32[24,2048]{1,0:T(8,128)S(1)}, u32[]{:S(2)}, u32[]{:S(2)}) collective-permute-start(f32[24,2048]{1,0:T(8,128)S(1)} %get-tuple-element.13.refs_4_), channel_id=1, source_target_pairs={{0,1},{1,0},{2,3},{3,2},{4,5},{5,4},{6,7},{7,6},{8,9},{9,8},{10,11... | collective-permute-start | bytes 589832 | tf_op jit(solution)/shard_map/ppermute | solution.py:307
  260.2 2.5 copy-start.3
  262.7 1.7 copy-start.7
  269.4 1.5 copy-start.9
  270.9 0.7 copy-start.12
  271.6 2.5 copy-start.4
  274.1 0.9 copy-start.13
  275.0 5.8 %copy-start.20 = (f32[20,20]{1,0:T(8,128)S(1)}, f32[20,20]{1,0:T(8,128)}, u32[]{:S(2)}) copy-start(f32[20,20]{1,0:T(8,128)} %gather.12) | copy-start | bytes 4804
  275.0 5.8 %copy-start.24 = (pred[20]{0:T(512)(128)(4,1)S(1)}, pred[20]{0:T(512)(128)(4,1)}, u32[]{:S(2)}) copy-start(pred[20]{0:T(512)(128)(4,1)} %broadcast_in_dim.28) | copy-start | bytes 64
  275.0 10.9 %copy-start.10 = (f32[2,5,32,2048]{3,2,1,0:T(8,128)S(1)}, f32[2,5,32,2048]{3,2,1,0:T(8,128)}, u32[]{:S(2)}) copy-start(f32[2,5,32,2048]{3,2,1,0:T(8,128)} %copy-done.9) | copy-start | bytes 7864324
  280.1 5.7 %collective-permute-start = (f32[24,2048]{1,0:T(8,128)S(1)}, f32[24,2048]{1,0:T(8,128)S(1)}, u32[]{:S(2)}, u32[]{:S(2)}) collective-permute-start(f32[24,2048]{1,0:T(8,128)S(1)} %get-tuple-element.12.refs_2_), channel_id=1, source_target_pairs={{0,1},{1,0},{2,3},{3,2},{4,5},{5,4},{6,7},{7,6},{8,9},{9,8},{10,11... | collective-permute-start | bytes 589832 | tf_op jit(solution)/shard_map/ppermute | solution.py:307
where the time goes:
time: 296 us; the launch traced here: 293 us
  waiting for transfers between devices  148 us (50%)
  Pallas kernels  45.9 us (16%)
  local copies, waits for them, and re-layouts  42.7 us (14%)
  starting transfers between devices  31.1 us (11%)
  blocking collectives  21.9 us (7%)
    all_to_all x4, waiting for transfers between devices, exchange(): return lax.all_to_all(block, axes, split_axis=0, concat_axis=0, tiled=True)  143 us
    unnamed x57, local copies, waits for them, and re-layouts  31.6 us
    all_to_all x4, starting transfers between devices, exchange(): return lax.all_to_all(block, axes, split_axis=0, concat_axis=0, tiled=True)  29 us
    all_gather x5, blocking collectives, interface_chain(): lax.all_gather(part[0], 'wall')  21.9 us
    pallas_call x2, Pallas kernels, nonlinear(): pl.pallas_call(nonlinear_body, grid=(points,), in_specs=[pl.BlockSpec(mem...  15.9 us
    pallas_call x2, Pallas kernels, absorb(): pl.pallas_call(functools.partial(absorb_body, before is None), grid=(vari...  10.1 us
    pallas_call x1, Pallas kernels, finish(): pl.pallas_call(functools.partial(finish_body, len(sides), walls), grid=(m...  7.35 us
    pallas_call x1, Pallas kernels, adjoint(): pl.pallas_call(adjoint_body, grid=(modes // NB,), in_specs=[spec, pl.Bloc...  6.66 us
  transfers between devices with their start and end apart: 6, of which 4 were waited for; matrix products, arithmetic and copies ran while one was open for 6% of the time, Pallas kernels for 12%

commit v1 on v0

v1 whole, which is shorter than its diff:
```python
import functools
import math

import jax
import jax.numpy as jnp
import numpy as np
from jax import lax
from jax.experimental import pallas as pl
from jax.experimental.pallas import tpu as pltpu
from jax.sharding import PartitionSpec as P

NF = 128
NB = 256

epsilon = 1e-06

SPLIT = lax.Precision.HIGH
FULL = lax.Precision.HIGHEST
GATHERED_ROWS = 24


def tables():
    def turns(length):
        counter = np.arange(length)
        angles = (counter[:, None] * counter[None, :] % length) * (2.0 * math.pi / length)
        return np.cos(angles), np.sin(angles)

    cos_time, sin_time = turns(NF)
    cos_span, sin_span = turns(NB)
    scale = 1.0 / math.sqrt(NF * NB)
    out = (
        np.block([[cos_time, -sin_time], [sin_time, cos_time]]),
        np.concatenate([cos_span, -sin_span], 0) * scale,
        np.concatenate([cos_span, -sin_span], 1) * scale,
        np.block([[cos_time, sin_time], [-sin_time, cos_time]]),
    )
    return [jnp.asarray(table.astype(np.float32)) for table in out]


def params(megabytes=16):
    return pltpu.CompilerParams(vmem_limit_bytes=megabytes * 1024 * 1024)


def whole(array):
    zeros = (0,) * array.ndim
    return pl.BlockSpec(array.shape, lambda *_: zeros)


def in_hbm(array):
    return pltpu.with_memory_space_constraint(array, pltpu.HBM)


def kept_modes(mask_ref):
    return mask_ref[...].astype(jnp.float32).reshape(1, -1)


def prepare_body(x_ref, mask_ref, out_ref):
    keep = kept_modes(mask_ref)
    rows, _, freqs, _ = out_ref.shape
    for part in range(2):
        kept = x_ref[part, 0] * keep
        out_ref[:, 0, :, part * NB : (part + 1) * NB] = kept.reshape(rows, freqs, NB)


def prepare(amplitudes, keep, cut):
    _, variables, _, modes = amplitudes.shape
    freqs = modes // NB
    rows = cut.stop - cut.start
    at = cut.start // rows
    return pl.pallas_call(
        prepare_body,
        grid=(variables,),
        in_specs=[
            pl.BlockSpec((2, 1, rows, modes), lambda v: (0, v, at, 0)),
            pl.BlockSpec((modes,), lambda v: (0,)),
        ],
        out_specs=pl.BlockSpec((rows, 1, freqs, 2 * NB), lambda v: (0, v, 0, 0)),
        out_shape=pltpu.HBM((rows, variables, freqs, 2 * NB), jnp.float32),
        compiler_params=params(),
        name="prepare",
    )(in_hbm(amplitudes), keep)


def partner(place_ref, j, i, spans):
    return (place_ref[0] ^ j) * spans + (place_ref[1] ^ i)


def prepare_apart_body(place_ref, x_ref, mask_ref, *refs):
    out_refs, rows_ref = refs[:-1], refs[-1]
    keep = kept_modes(mask_ref)
    rows, freqs, _ = rows_ref.shape
    spans = len(out_refs)
    for part in range(2):
        kept = x_ref[part, 0] * keep
        rows_ref[:, :, part * NB : (part + 1) * NB] = kept.reshape(rows, freqs, NB)
    for i, out_ref in enumerate(out_refs):
        for j in range(out_ref.shape[0]):
            out_ref[j, 0] = rows_ref[partner(place_ref, j, i, spans)]


def prepare_apart(place, amplitudes, keep, cut, groups, spans):
    _, variables, _, modes = amplitudes.shape
    freqs = modes // NB
    rows = cut.stop - cut.start
    at = cut.start // rows
    return pl.pallas_call(
        prepare_apart_body,
        grid=(variables,),
        in_specs=[
            pl.BlockSpec(memory_space=pltpu.SMEM),
            pl.BlockSpec((2, 1, rows, modes), lambda v: (0, v, at, 0)),
            pl.BlockSpec((modes,), lambda v: (0,)),
        ],
        out_specs=[pl.BlockSpec((groups, 1, freqs, 2 * NB), lambda v: (0, v, 0, 0))] * spans,
        out_shape=[jax.ShapeDtypeStruct((groups, variables, freqs, 2 * NB), jnp.float32)] * spans,
        scratch_shapes=[pltpu.VMEM((rows, freqs, 2 * NB), jnp.float32)],
        compiler_params=params(),
        name="prepare_apart",
    )(place, in_hbm(amplitudes), keep)


def transform(read, write, q_ref, table_refs, field_ref, force_ref):
    wi_ref, ei_ref, ef_ref, wf_ref = table_refs
    variables = field_ref.shape[0]
    for v in range(variables):
        modes = read(v)
        stacked = jnp.concatenate([modes[:, :NB], modes[:, NB:]], axis=0)
        turned = jnp.dot(
            wi_ref[...], stacked, precision=SPLIT, preferred_element_type=jnp.float32
        )
        beside = jnp.concatenate([turned[:NF], turned[NF:]], axis=1)
        field_ref[v] = jnp.dot(
            beside, ei_ref[...], precision=SPLIT, preferred_element_type=jnp.float32
        )
    pairs = [(a, b) for a in range(variables) for b in range(a + 1, variables)]
    weights = [
        [q_ref[w * variables + a, b] + q_ref[w * variables + b, a] for a, b in pairs]
        for w in range(variables)
    ]
    step = 8
    for row in range(0, NF, step):
        at = slice(row, row + step)
        values = [field_ref[v, at] for v in range(variables)]
        total = [None] * variables
        for i, (a, b) in enumerate(pairs):
            product = values[a] * values[b]
            for w in range(variables):
                term = weights[w][i] * product
                total[w] = term if total[w] is None else total[w] + term
        for w in range(variables):
            force_ref[w, at] = total[w]
    for w in range(variables):
        spread = jnp.dot(
            force_ref[w], ef_ref[...], precision=SPLIT, preferred_element_type=jnp.float32
        )
        stacked = jnp.concatenate([spread[:, :NB], spread[:, NB:]], axis=0)
        turned = jnp.dot(
            wf_ref[...], stacked, precision=SPLIT, preferred_element_type=jnp.float32
        )
        for part in range(2):
            write(w, part, turned[part * NF : (part + 1) * NF])


def nonlinear_body(q_ref, in_ref, *refs):
    table_refs, out_ref, work_refs = refs[:4], refs[4], refs[5:]
    devices, _, _, freqs, _ = in_ref.shape

    def read(v):
        return in_ref[:, 0, v].reshape(NF, 2 * NB)

    def write(w, part, piece):
        at = slice(part * NB, (part + 1) * NB)
        out_ref[:, 0, w, :, at] = piece.reshape(devices, freqs, NB)

    transform(read, write, q_ref, table_refs, *work_refs)


def work_shapes(variables):
    return [pltpu.VMEM((variables, NF, NB), jnp.float32)] * 2


def nonlinear_cost(points, variables):
    return pl.CostEstimate(
        flops=points * variables * 12 * NF * NB * (NF + NB) * 2,
        bytes_accessed=points * variables * NF * NB * 16,
        transcendentals=0,
    )


def nonlinear(block, coefficients, transforms):
    devices, points, variables, freqs, lanes = block.shape
    spec = pl.BlockSpec((devices, 1, variables, freqs, lanes), lambda j: (0, j, 0, 0, 0))
    return pl.pallas_call(
        nonlinear_body,
        grid=(points,),
        in_specs=[pl.BlockSpec(memory_space=pltpu.SMEM), spec] + [whole(t) for t in transforms],
        out_specs=spec,
        out_shape=pltpu.HBM(block.shape, jnp.float32),
        scratch_shapes=work_shapes(variables),
        compiler_params=params(24),
        cost_estimate=nonlinear_cost(points, variables),
        name="nonlinear",
    )(coefficients, block, *transforms)


def nonlinear_apart_body(groups, place_ref, q_ref, *refs):
    in_refs, refs = refs[:groups], refs[groups:]
    table_refs, refs = refs[:4], refs[4:]
    out_refs, refs = refs[:groups], refs[groups:]
    rows_ref, work_refs = refs[0], refs[1:]
    devices, _, freqs, _ = rows_ref.shape
    spans = devices // groups
    for j in range(groups):
        for i in range(spans):
            rows_ref[partner(place_ref, j, i, spans)] = in_refs[j][i]

    def read(v):
        return rows_ref[:, v].reshape(NF, 2 * NB)

    def write(w, part, piece):
        at = slice(part * NB, (part + 1) * NB)
        rows_ref[:, w, :, at] = piece.reshape(devices, freqs, NB)

    transform(read, write, q_ref, table_refs, *work_refs)
    for j in range(groups):
        for i in range(spans):
            out_refs[j][i] = rows_ref[partner(place_ref, j, i, spans)]


def nonlinear_apart(place, blocks, coefficients, transforms):
    groups = len(blocks)
    spans, variables, freqs, lanes = blocks[0].shape
    smem = pl.BlockSpec(memory_space=pltpu.SMEM)
    return pl.pallas_call(
        functools.partial(nonlinear_apart_body, groups),
        grid=(1,),
        in_specs=[smem, smem]
        + [whole(block) for block in blocks]
        + [whole(table) for table in transforms],
        out_specs=[whole(block) for block in blocks],
        out_shape=[jax.ShapeDtypeStruct(block.shape, jnp.float32) for block in blocks],
        scratch_shapes=[pltpu.VMEM((groups * spans, variables, freqs, lanes), jnp.float32)]
        + work_shapes(variables),
        compiler_params=params(24),
        cost_estimate=nonlinear_cost(1, variables),
        name="nonlinear_apart",
    )(place, coefficients, *blocks, *transforms)


def base_body(cuts, x_ref, up_ref, mask_ref, inverse_ref, turned_ref, *refs):
    out_refs, (edge_ref, solved_ref, sum_ref) = refs[: len(cuts)], refs[len(cuts) :]
    _, variables, heights, lanes = x_ref.shape
    extent = variables * heights
    ends = 2 * variables
    keep = kept_modes(mask_ref)
    kept, solved = [], []
    for part in range(2):
        kept.append(x_ref[part].reshape(extent, lanes) * keep)
        moved = jnp.dot(
            turned_ref[...], kept[part], precision=SPLIT, preferred_element_type=jnp.float32
        )
        grid = moved.reshape(variables, heights, lanes)
        for cut, out_ref in zip(cuts, out_refs):
            out_ref[part] = grid[:, cut]
        side = up_ref[part].reshape(extent, lanes) * keep
        solved.append(
            jnp.dot(inverse_ref[...], side, precision=SPLIT, preferred_element_type=jnp.float32)
        )
        solved_ref[part] = solved[part].reshape(variables, heights, lanes)
        for end, point in enumerate((0, heights - 1)):
            for v in range(variables):
                row = part * ends + end * variables + v
                at = v * heights + point
                edge_ref[row : row + 1] = moved[at : at + 1]
                sum_ref[row : row + 1] = solved[part][at : at + 1]

    def total(value):
        return jnp.sum(value, axis=0, keepdims=True)

    row = 2 * ends
    none = jnp.zeros((GATHERED_ROWS - row - 1, lanes), jnp.float32)
    edge_ref[row : row + 1] = total(kept[0] * kept[0] + kept[1] * kept[1])
    edge_ref[row + 1 :] = none
    sum_ref[row : row + 1] = total(kept[0] * solved[0] + kept[1] * solved[1])
    sum_ref[row + 1 : row + 2] = total(kept[0] * solved[1] - kept[1] * solved[0])
    sum_ref[row + 2 :] = none[1:]


def base(amplitudes, upstream, keep, inverse, turned, cuts):
    _, variables, heights, modes = amplitudes.shape

    def rows_spec(rows):
        return pl.BlockSpec((2, variables, rows, NB), lambda i: (0, 0, 0, i))

    def rows_shape(rows):
        return jax.ShapeDtypeStruct((2, variables, rows, modes), jnp.float32)

    lengths = [cut.stop - cut.start for cut in cuts]
    small = pl.BlockSpec((GATHERED_ROWS, NB), lambda i: (0, i))
    small_shape = jax.ShapeDtypeStruct((GATHERED_ROWS, modes), jnp.float32)
    return pl.pallas_call(
        functools.partial(base_body, cuts),
        grid=(modes // NB,),
        in_specs=[rows_spec(heights)] * 2
        + [pl.BlockSpec((NB,), lambda i: (i,)), whole(inverse), whole(turned)],
        out_specs=[rows_spec(rows) for rows in lengths] + [small, rows_spec(heights), small],
        out_shape=[rows_shape(rows) for rows in lengths]
        + [small_shape, rows_shape(heights), small_shape],
        compiler_params=params(24),
        name="base",
    )(in_hbm(amplitudes), in_hbm(upstream), keep, inverse, turned)


def absorb_rows(read, mask_ref, edge_ref, adj_ref, before_ref, out_ref, sum_ref):
    ends = edge_ref.shape[1]
    rows = out_ref.shape[2]
    keep = kept_modes(mask_ref)

    @pl.when(pl.program_id(0) == 0)
    def _():
        sum_ref[...] = before_ref[...]

    sides = []
    for part in range(2):
        side = read(part).reshape(rows, -1) * keep
        out_ref[part, 0] = side
        at = slice(part * ends, (part + 1) * ends)
        sum_ref[at] += jnp.dot(
            edge_ref[0], side, precision=SPLIT, preferred_element_type=jnp.float32
        )
        sides.append(side)
    real, imag = adj_ref[0, 0], adj_ref[1, 0]
    at = 2 * ends
    sum_ref[at : at + 1] += jnp.sum(real * sides[0] + imag * sides[1], axis=0, keepdims=True)
    sum_ref[at + 1 : at + 2] += jnp.sum(real * sides[1] - imag * sides[0], axis=0, keepdims=True)


def absorb_body(in_ref, *refs):
    def read(part):
        return in_ref[:, 0, :, part * NB : (part + 1) * NB]

    absorb_rows(read, *refs)


def absorb_apart_body(spans, place_ref, *refs):
    in_refs, refs, rows_ref = refs[:spans], refs[spans:-1], refs[-1]
    for i, in_ref in enumerate(in_refs):
        for j in range(in_ref.shape[0]):
            rows_ref[partner(place_ref, j, i, spans)] = in_ref[j, 0]

    def read(part):
        return rows_ref[:, :, part * NB : (part + 1) * NB]

    absorb_rows(read, *refs)


def absorb(place, blocks, keep, edges, adjoint_modes, before):
    blocks = list(blocks)
    apart = place is not None
    _, variables, rows, modes = adjoint_modes.shape
    ends = edges.shape[1]
    grid_spec = pl.BlockSpec((2, 1, rows, modes), lambda v: (0, v, 0, 0))
    sums = pl.BlockSpec((GATHERED_ROWS, modes), lambda v: (0, 0))
    length, _, freqs, lanes = blocks[0].shape
    in_specs = [pl.BlockSpec((length, 1, freqs, lanes), lambda v: (0, v, 0, 0))] * len(blocks)
    in_specs += [
        pl.BlockSpec((modes,), lambda v: (0,)),
        pl.BlockSpec((1, ends, rows), lambda v: (v, 0, 0)),
        grid_spec,
        sums,
    ]
    operands = blocks + [keep, edges, adjoint_modes, before]
    body, scratch = absorb_body, []
    if apart:
        operands = [place] + operands
        in_specs = [pl.BlockSpec(memory_space=pltpu.SMEM)] + in_specs
        body = functools.partial(absorb_apart_body, len(blocks))
        scratch = [pltpu.VMEM((rows, freqs, lanes), jnp.float32)]
    return pl.pallas_call(
        body,
        grid=(variables,),
        in_specs=in_specs,
        out_specs=[grid_spec, sums],
        out_shape=[
            jax.ShapeDtypeStruct((2, variables, rows, modes), jnp.float32),
            jax.ShapeDtypeStruct((GATHERED_ROWS, modes), jnp.float32),
        ],
        scratch_shapes=scratch,
        compiler_params=params(),
        name="absorb_apart" if apart else "absorb",
    )(*operands)


def solve_body(side_ref, before_ref, inverse_ref, out_ref):
    _, variables, heights, lanes = out_ref.shape
    for part in range(2):
        moved = jnp.dot(
            inverse_ref[...],
            side_ref[part].reshape(-1, lanes),
            precision=SPLIT,
            preferred_element_type=jnp.float32,
        )
        out_ref[part] = before_ref[part] + moved.reshape(variables, heights, lanes)


def solve(side, before, inverse):
    _, variables, rows, modes = side.shape
    heights = before.shape[2]
    spec = pl.BlockSpec((2, variables, heights, NB), lambda i: (0, 0, 0, i))
    side_spec = pl.BlockSpec((2, variables, rows, NB), lambda i: (0, 0, 0, i))
    return pl.pallas_call(
        solve_body,
        grid=(modes // NB,),
        in_specs=[side_spec, spec, whole(inverse)],
        out_specs=spec,
        out_shape=jax.ShapeDtypeStruct(before.shape, jnp.float32),
        compiler_params=params(),
        name="solve",
    )(side, before, inverse)


def finish_body(walls, extent, solved_ref, *refs):
    bounds, refs = refs[:walls], refs[walls:]
    edges, refs = refs[:walls], refs[walls:]
    chain_ref, out_ref, shift_ref = refs
    _, variables, heights, lanes = out_ref.shape
    ends = 2 * variables
    pushed = []
    for part in range(2):
        at = slice(part * ends, (part + 1) * ends)
        everywhere = [ref[at] for ref in bounds]
        spare = chain_ref.shape[1] // 3 - walls * ends
        if spare:
            everywhere.append(jnp.zeros((spare, lanes), jnp.float32))
        everywhere = jnp.concatenate(everywhere, axis=0)
        high = everywhere.astype(jnp.bfloat16)
        low = (everywhere - high.astype(jnp.float32)).astype(jnp.bfloat16)
        moved = jnp.dot(
            chain_ref[...],
            jnp.concatenate([high, low, high], axis=0),
            preferred_element_type=jnp.float32,
        )
        pushed.append(moved[extent:])
        out_ref[part] = solved_ref[part] - moved[:extent].reshape(variables, heights, lanes)
    real = imag = weight = 0.0
    for wall in range(walls):
        at = slice(wall * ends, (wall + 1) * ends)
        push = [pushed[part][at] for part in range(2)]
        edge = [edges[wall][part * ends : (part + 1) * ends] for part in range(2)]
        row = 2 * ends
        squares = edges[wall][row : row + 1]
        taken = jnp.sum(edge[0] * push[0] + edge[1] * push[1], axis=0, keepdims=True)
        real = real + (bounds[wall][row : row + 1] - taken - squares)
        taken = jnp.sum(edge[0] * push[1] - edge[1] * push[0], axis=0, keepdims=True)
        imag = imag + (bounds[wall][row + 1 : row + 2] - taken)
        weight = weight + squares
    weight = weight + epsilon
    shift_ref[0:1] = imag / weight
    shift_ref[1:2] = -real / weight


def finish(solved, bounds, edges, chain):
    _, variables, heights, modes = solved.shape
    walls = len(bounds)
    lanes = min(2 * NB, modes)
    small = pl.BlockSpec((GATHERED_ROWS, lanes), lambda i: (0, i))
    spec = pl.BlockSpec((2, variables, heights, lanes), lambda i: (0, 0, 0, i))
    return pl.pallas_call(
        functools.partial(finish_body, walls, variables * heights),
        grid=(modes // lanes,),
        in_specs=[spec] + [small] * (2 * walls) + [whole(chain)],
        out_specs=[spec, pl.BlockSpec((2, lanes), lambda i: (0, i))],
        out_shape=[
            jax.ShapeDtypeStruct(solved.shape, jnp.float32),
            jax.ShapeDtypeStruct((2, modes), jnp.float32),
        ],
        compiler_params=params(),
        name="finish",
    )(solved, *bounds, *edges, chain)


def around(block, axis):
    count = lax.axis_size(axis)
    return [block] + [
        lax.ppermute(block, axis, [(i, (i + d) % count) for i in range(count)])
        for d in range(1, count)
    ]


PACKED_ROWS = 16


def pack_body(*refs):
    in_refs, out_ref = refs[:-1], refs[-1]
    out_ref[...] = jnp.zeros(out_ref.shape, jnp.float32)
    for i, ref in enumerate(in_refs):
        rows, columns = ref.shape[1:]
        out_ref[i, :rows, :columns] = ref[0]


def pack(parts):
    return pl.pallas_call(
        pack_body,
        out_shape=jax.ShapeDtypeStruct((len(parts), PACKED_ROWS, 128), jnp.float32),
        name="pack",
    )(*parts)


def upper_bits(value):
    return value.astype(jnp.bfloat16).astype(jnp.float32)


def constants_body(cuts, variables, walls, place_ref, inverse_ref, *refs):
    packed, refs = refs[:walls], refs[walls:]
    turned_ref, refs = refs[0], refs[1:]
    column_refs, refs = refs[: len(cuts)], refs[len(cuts) :]
    row_refs, refs = refs[: len(cuts)], refs[len(cuts) :]
    chain_ref, all_ref, step_ref = refs
    extent = inverse_ref.shape[0]
    heights = extent // variables
    ends = 2 * variables
    matrix = inverse_ref[...]
    turned = matrix.T
    turned_ref[...] = turned
    for cut, column_ref, row_ref in zip(cuts, column_refs, row_refs):
        pieces = []
        for v in range(variables):
            part = matrix[:, v * heights : (v + 1) * heights][:, cut]
            pieces.append(part)
            for end, point in enumerate((0, heights - 1)):
                for w in range(variables):
                    at = w * heights + point
                    row = end * variables + w
                    row_ref[v, row : row + 1] = part[at : at + 1]
        column_ref[...] = jnp.concatenate(pieces, axis=1)

    def dot(a, b):
        return jnp.dot(a, b, precision=FULL, preferred_element_type=jnp.float32)

    size = walls * PACKED_ROWS
    for d in range(walls):
        all_ref[(place_ref[0] - d + walls) % walls] = packed[d][...]

    def small(j, kind):
        return all_ref[j, kind][:, :PACKED_ROWS]

    row = lax.broadcasted_iota(jnp.int32, (PACKED_ROWS, size), 0)
    column = lax.broadcasted_iota(jnp.int32, (PACKED_ROWS, size), 1)
    units = []
    for j in range(walls):
        d = (place_ref[0] - j + walls) % walls
        hit = (column == d * ends + row) & (row < ends)
        units.append(jnp.where(hit, 1.0, 0.0))
    ahead = [units[0]]
    for j in range(1, walls):
        ahead.append(units[j] - dot(small(j, 2), ahead[j - 1]))
    interface = [None] * walls
    interface[-1] = dot(small(walls - 1, 4), ahead[-1])
    for j in range(walls - 2, -1, -1):
        interface[j] = dot(small(j, 4), ahead[j] - dot(small(j, 3), interface[j + 1]))
    for j in range(walls):
        none = jnp.zeros((variables, size), jnp.float32)
        under, over = none, none
        if j > 0:
            last = jnp.concatenate([interface[j - 1][variables:], none], axis=0)[:PACKED_ROWS]
            under = dot(small(j, 0), last)[:variables]
        if j < walls - 1:
            over = dot(small(j, 1), interface[j + 1])[:variables]
        step_ref[(place_ref[0] - j + walls) % walls] = jnp.concatenate(
            [under, over, jnp.zeros((PACKED_ROWS - ends, size), jnp.float32)], axis=0
        )
    pushes = [step_ref[d][:ends] for d in range(walls)]
    edge = [turned[v * heights : v * heights + 1] for v in range(variables)]
    edge += [turned[(v + 1) * heights - 1 : (v + 1) * heights] for v in range(variables)]
    edge.append(jnp.zeros((PACKED_ROWS - ends, extent), jnp.float32))
    edge = jnp.concatenate(edge, axis=0).T
    own = dot(edge, step_ref[0])
    spare = chain_ref.shape[0] - extent - walls * ends
    full = [own] + pushes
    if spare:
        full.append(jnp.zeros((spare, size), jnp.float32))
    full = jnp.concatenate(full, axis=0)
    high = upper_bits(full)
    chain_ref[...] = jnp.concatenate([high, high, full - high], axis=1).astype(jnp.bfloat16)


def constants(place, inverse, packed, cuts, variables):
    walls = len(packed)
    extent = inverse.shape[0]
    heights = extent // variables
    ends = 2 * variables
    lengths = [cut.stop - cut.start for cut in cuts]
    size = walls * PACKED_ROWS
    rows = extent + walls * ends + (-walls * ends) % 16
    f32 = jnp.float32
    return pl.pallas_call(
        functools.partial(constants_body, cuts, variables, walls),
        in_specs=[pl.BlockSpec(memory_space=pltpu.SMEM)]
        + [pl.BlockSpec(memory_space=pltpu.VMEM)] * (1 + walls),
        out_shape=[jax.ShapeDtypeStruct((extent, extent), f32)]
        + [jax.ShapeDtypeStruct((extent, variables * n), f32) for n in lengths]
        + [jax.ShapeDtypeStruct((variables, ends, n), f32) for n in lengths]
        + [jax.ShapeDtypeStruct((rows, 3 * size), jnp.bfloat16)],
        scratch_shapes=[
            pltpu.VMEM((walls,) + packed[0].shape, f32),
            pltpu.VMEM((walls, PACKED_ROWS, size), f32),
        ],
        compiler_params=params(),
        name="constants",
    )(place, inverse, *packed)


def local(
    amplitudes,
    upstream,
    harmonic_mask,
    quadratic_coefficients,
    slab_inverse,
    lower_coupling,
    upper_coupling,
    reduced_lower,
    reduced_upper,
    reduced_pivot,
):
    _, variables, heights, modes = amplitudes.shape
    axes = ("freq", "span")
    groups, spans = lax.axis_size("freq"), lax.axis_size("span")
    devices = groups * spans
    points = heights // devices
    apart = points > 1 and groups & (groups - 1) == 0 and spans & (spans - 1) == 0
    edge_at = heights - devices if apart else heights
    cuts = [slice(0, edge_at)] + ([slice(edge_at, heights)] if apart else [])
    keep = harmonic_mask
    place = jnp.stack([lax.axis_index("freq"), lax.axis_index("span")]).astype(jnp.int32)
    wall = lax.axis_index("wall").reshape(1).astype(jnp.int32)
    transforms = tables()
    coefficients = quadratic_coefficients.reshape(variables * variables, variables)

    def exchange(block):
        return lax.all_to_all(block, axes, split_axis=0, concat_axis=0, tiled=True)

    def swap(blocks, axis, only=None):
        count = len(blocks)
        return [
            lax.ppermute(block, axis, [(at, at ^ i) for at in range(count)])
            if i and (only is None or i in only)
            else block
            for i, block in enumerate(blocks)
        ]

    def regroup(blocks):
        return [jnp.stack([block[j] for block in blocks]) for j in range(blocks[0].shape[0])]

    far = {spans // 2}
    main = prepare(amplitudes, keep, cuts[0])
    if apart:
        main, amplitudes = lax.optimization_barrier((main, amplitudes))
        sent = prepare_apart(place, amplitudes, keep, cuts[1], groups, spans)
        arrived = swap(sent, "span", set(range(spans)) - far)
    main = exchange(main)

    inverse = slab_inverse[0]
    parts = (lower_coupling, upper_coupling, reduced_lower, reduced_upper, reduced_pivot)
    packed = around(pack(parts), "wall")
    turned, *rest, chain = constants(wall, inverse, packed, cuts, variables)
    columns, end_rows = rest[: len(cuts)], rest[len(cuts) :]
    *adjoint_modes, edge, solved, sums = base(
        amplitudes, upstream, keep, inverse, turned, cuts
    )
    edges = around(edge, "wall")
    held = (main, columns, end_rows, chain, adjoint_modes, edges, solved, sums)
    held = lax.optimization_barrier(held)
    main, columns, end_rows, chain, adjoint_modes, edges, solved, sums = held

    if apart:
        main, arrived = lax.optimization_barrier((main, arrived))
        arrived = swap(arrived, "span", far)
    size = edge_at // devices
    shape = main.shape
    main = nonlinear(main.reshape((devices, size) + shape[1:]), coefficients, transforms)
    main = main.reshape(shape)
    if apart:
        main, arrived = lax.optimization_barrier((main, arrived))
    main = exchange(main)
    if apart:
        arrived = swap(regroup(arrived), "freq")
        forced = nonlinear_apart(place, arrived, coefficients, transforms)
        returned = swap(regroup(swap(forced, "freq")), "span")

    side, sums = absorb(None, [main], keep, end_rows[0], adjoint_modes[0], sums)
    if apart:
        solved = solve(side, solved, columns[0])
        solved, sums, adjoint_modes[1], edges, chain, columns[1] = lax.optimization_barrier(
            (solved, sums, adjoint_modes[1], edges, chain, columns[1])
        )
        side, sums = absorb(place, returned, keep, end_rows[1], adjoint_modes[1], sums)
    bounds = around(sums, "wall")
    solved = solve(side, solved, columns[-1])
    new_amplitudes, wavenumber_shift = finish(solved, bounds, edges, chain)
    return (new_amplitudes, wavenumber_shift)


def solution(mesh):
    placed = (
        P(None, None, "wall", ("freq", "span")),
        P(None, None, "wall", ("freq", "span")),
        P(("freq", "span")),
        P(),
        P("wall", None, None),
        P("wall", None, None),
        P("wall", None, None),
        P("wall", None, None),
        P("wall", None, None),
        P("wall", None, None),
    )
    return jax.shard_map(
        local,
        mesh=mesh,
        in_specs=placed,
        out_specs=(P(None, None, "wall", ("freq", "span")), P(None, ("freq", "span"))),
        check_vma=False,
    )
```

time: 296 us -> 270 us (0.912)
  blocking collectives: 21.9 us -> 0 us
  local copies, waits for them, and re-layouts: 42.7 us -> 23.3 us
  Pallas kernels: 45.9 us -> 63 us
  waiting for transfers between devices: 148 us -> 140 us
  starting transfers between devices: 31.1 us -> 37 us
    all_to_all x4 -> x2, waiting for transfers between devices: 143 us -> 67.5 us  [exchange(): return lax.all_to_all(block, axes, split_axis=0, concat_axis=0, tiled=True)]
    ppermute x0 -> x12, waiting for transfers between devices: none -> 65 us  [swap(): lax.ppermute(block, axis, [(at, at ^ i) for at in range(count)])]
    all_gather x5 -> x0, blocking collectives: 21.9 us -> none  [interface_chain(): lax.all_gather(part[0], 'wall')]
    pallas_call x4 -> x10, Pallas kernels: 24.1 us -> 44 us  [the longest x1 12.6 us: base(): pl.pallas_call(functools.partial(base_body, cuts), grid=(modes // NB,), i...]
    ppermute x0 -> x12, starting transfers between devices: none -> 19.4 us  [swap(): lax.ppermute(block, axis, [(at, at ^ i) for at in range(count)])]
    all_to_all x4 -> x2, starting transfers between devices: 29 us -> 13 us  [exchange(): return lax.all_to_all(block, axes, split_axis=0, concat_axis=0, tiled=True)]
    unnamed x57 -> x63, local copies, waits for them, and re-layouts: 31.6 us -> 21 us
    reshape x3 -> x0, local copies, waits for them, and re-layouts: 3.72 us -> none  [the longest x2 3.64 us: local(): columns[:, :, cut].reshape(extent, -1)]
  transfers between devices with their start and end apart: 6 -> 17, of which waited for: 4 -> 10; matrix products, arithmetic and copies ran while one was open for 6% -> 3% of each run, Pallas kernels for 12% -> 19%
where the time goes in v1:
time: 270 us; the launch traced here: 267 us
  waiting for transfers between devices  140 us (52%)
  Pallas kernels  63 us (23%)
  starting transfers between devices  37 us (14%)
  local copies, waits for them, and re-layouts  23.3 us (9%)
    all_to_all x2, waiting for transfers between devices, exchange(): return lax.all_to_all(block, axes, split_axis=0, concat_axis=0, tiled=True)  67.5 us
    ppermute x12, waiting for transfers between devices, swap(): lax.ppermute(block, axis, [(at, at ^ i) for at in range(count)])  65 us
    unnamed x63, local copies, waits for them, and re-layouts  21 us
    ppermute x12, starting transfers between devices, swap(): lax.ppermute(block, axis, [(at, at ^ i) for at in range(count)])  19.4 us
    all_to_all x2, starting transfers between devices, exchange(): return lax.all_to_all(block, axes, split_axis=0, concat_axis=0, tiled=True)  13 us
    pallas_call x1, Pallas kernels, nonlinear(): pl.pallas_call(nonlinear_body, grid=(points,), in_specs=[pl.BlockSpec(mem...  12.9 us
    pallas_call x1, Pallas kernels, base(): pl.pallas_call(functools.partial(base_body, cuts), grid=(modes // NB,), i...  12.6 us
    pallas_call x2, Pallas kernels, solve(): pl.pallas_call(solve_body, grid=(modes // NB,), in_specs=[side_spec, spec...  8.8 us
  transfers between devices with their start and end apart: 17, of which 10 were waited for; matrix products, arithmetic and copies ran while one was open for 3% of the time, Pallas kernels for 19%

profile of v1, /device:TPU:10, one launch (start us, length us, event | category | flops | bytes accessed | tf_op | source)
XLA Modules:
  0.0 267.1 jit_solution(6222767402757642017)
XLA Ops:
  0.6 0.7 copy-done.5
  1.3 6.1 %prepare.1 = f32[48,5,8,512]{3,2,1,0:T(8,128)} custom-call(f32[2,5,64,2048]{3,2,1,0:T(8,128)} %x_ref.3, s32[2048]{0:T(1024)S(1)} %copy-done.5), custom_call_target="tpu_custom_call" | custom-call | tf_op jit(solution)/shard_map/prepare/pallas_call | solution.py:70
  7.4 6.4 %all-to-all-start = ((f32[48,5,8,512]{3,2,1,0:T(8,128)}), f32[48,5,8,512]{3,2,1,0:T(8,128)}, u32[]{:S(2)}, u32[]{:S(2)}) async-start(f32[48,5,8,512]{3,2,1,0:T(8,128)} %prepare.1), calls=%async_computation | async-start | bytes 7864320 | tf_op jit(solution)/shard_map/all_to_all | solution.py:640
  13.9 0.1 pad_add_fusion.place_ref
  14.0 4.0 %prepare_apart.1 = (f32[4,5,8,512]{3,2,1,0:T(8,128)S(1)}, f32[4,5,8,512]{3,2,1,0:T(8,128)}, f32[4,5,8,512]{3,2,1,0:T(8,128)S(1)}, f32[4,5,8,512]{3,2,1,0:T(8,128)}) custom-call(s32[2]{0:T(128)S(1)} %pad_add_fusion.place_ref, f32[2,5,64,2048]{3,2,1,0:T(8,128)} %x_ref.3, s32[2048]{0:T(1024)S(1)} %copy-done.6), custom_call_target="tpu_custom_call" | custom-call | tf_op jit(solution)/shard_map/prepare_apart/pallas_call | solution.py:106
  18.0 0.6 collective-permute-start.2
  18.6 2.4 collective-permute-start.3
  21.0 0.6 copy.17.refs_0_
  21.6 0.6 copy.18.refs_1_
  22.1 0.6 copy.19.refs_2_
  22.7 0.6 copy.20.refs_3_
  23.3 0.6 copy.21.refs_4_
  23.9 1.4 pack.1.refs_0_
  25.3 1.5 collective-permute-start
  26.8 2.7 %collective-permute-done.refs_1_ = f32[5,16,128]{2,1,0:T(8,128)S(1)} collective-permute-done((f32[5,16,128]{2,1,0:T(8,128)}, f32[5,16,128]{2,1,0:T(8,128)S(1)}, u32[]{:S(2)}, u32[]{:S(2)}) %collective-permute-start) | collective-permute-done | bytes 40992 | tf_op jit(solution)/shard_map/ppermute | solution.py:485
  29.5 0.8 copy-done.9
  30.3 1.1 constants.1
  31.4 0.6 copy-done.10
  32.1 0.6 copy-done.12
  32.7 12.6 %base.1 = (f32[2,5,48,2048]{3,2,1,0:T(8,128)S(1)}, f32[2,5,16,2048]{3,2,1,0:T(8,128)S(1)}, f32[24,2048]{1,0:T(8,128)S(1)}, f32[2,5,64,2048]{3,2,1,0:T(8,128)S(1)}, f32[24,2048]{1,0:T(8,128)S(1)}) custom-call(f32[2,5,64,2048]{3,2,1,0:T(8,128)} %x_ref.3, f32[2,5,64,2048]{3,2,1,0:T(8,128)} %up_ref.1, s32[2048]{0:T(1024)S(1)} %copy-done.6, ...), custom_call_target="tpu_custom_call" | custom-call | tf_op jit(solution)/shard_map/base/pallas_call | solution.py:301
  45.3 2.3 copy-done
  47.7 1.9 copy-done.2
  49.6 0.7 copy-done.7
  50.2 1.5 collective-permute-start.1
  51.8 4.1 %collective-permute-done.1.refs_3_ = f32[24,2048]{1,0:T(8,128)S(1)} collective-permute-done((f32[24,2048]{1,0:T(8,128)S(1)}, f32[24,2048]{1,0:T(8,128)S(1)}, u32[]{:S(2)}, u32[]{:S(2)}) %collective-permute-start.1) | collective-permute-done | bytes 196640 | tf_op jit(solution)/shard_map/ppermute | solution.py:485
  55.9 50.1 %all-to-all-done = f32[48,5,8,512]{3,2,1,0:T(8,128)} async-done(((f32[48,5,8,512]{3,2,1,0:T(8,128)}), f32[48,5,8,512]{3,2,1,0:T(8,128)}, u32[]{:S(2)}, u32[]{:S(2)}) %all-to-all-start) | async-done | bytes 3932192 | tf_op jit(solution)/shard_map/all_to_all | solution.py:640
  106.0 8.9 %collective-permute-done.3 = f32[4,5,8,512]{3,2,1,0:T(8,128)} collective-permute-done((f32[4,5,8,512]{3,2,1,0:T(8,128)}, f32[4,5,8,512]{3,2,1,0:T(8,128)}, u32[]{:S(2)}, u32[]{:S(2)}) %collective-permute-start.3) | collective-permute-done | bytes 327712 | tf_op jit(solution)/shard_map/ppermute | solution.py:645
  114.9 1.0 copy-done.16
  116.0 1.0 copy-done.18
  117.0 0.9 copy-done.20
  118.0 0.9 copy-done.22
  118.9 12.9 %nonlinear.1 = f32[16,3,5,8,512]{4,3,2,1,0:T(8,128)} custom-call(f32[25,5]{1,0:T(8,128)S(1)} %reshape.20.q_ref, f32[16,3,5,8,512]{4,3,2,1,0:T(8,128)} %bitcast.4.in_ref, f32[256,256]{1,0:T(8,128)S(1)} %copy-done.20, f32[512,256]{1,0:T(8,128)S(1)} %copy-done.16, f32[256,512]{1,0:T(8,128)S(1)} %copy-done.18, f32[256,256]{1,0:T(8,128)S(1)} %copy-done.22), custom_call_target="tpu_custom_call" | custom-call | flops 4529848320 | bytes 7864320 | tf_op jit(solution)/shard_map/nonlinear/pallas_call | solution.py:193
  131.8 6.6 %all-to-all-start.1 = ((f32[48,5,8,512]{3,2,1,0:T(8,128)}), f32[48,5,8,512]{3,2,1,0:T(8,128)}, u32[]{:S(2)}, u32[]{:S(2)}) async-start(f32[48,5,8,512]{3,2,1,0:T(8,128)} %bitcast.8), calls=%async_computation.1 | async-start | bytes 7864320 | tf_op jit(solution)/shard_map/all_to_all | solution.py:640
  138.4 0.0 copy-start.19
  138.4 1.2 fusion.6
  139.6 1.1 fusion.4
  140.7 0.2 collective-permute-start.5
  140.9 0.6 collective-permute-start.6
  141.6 1.2 collective-permute-start.7
  142.8 23.2 %collective-permute-done.6.refs_2_ = f32[4,5,8,512]{3,2,1,0:T(8,128)S(1)} collective-permute-done((f32[4,5,8,512]{3,2,1,0:T(8,128)S(1)}, f32[4,5,8,512]{3,2,1,0:T(8,128)S(1)}, u32[]{:S(2)}, u32[]{:S(2)}) %collective-permute-start.6) | collective-permute-done | bytes 327712 | tf_op jit(solution)/shard_map/ppermute | solution.py:645
  166.1 8.7 %collective-permute-done.7.refs_3_ = f32[4,5,8,512]{3,2,1,0:T(8,128)S(1)} collective-permute-done((f32[4,5,8,512]{3,2,1,0:T(8,128)S(1)}, f32[4,5,8,512]{3,2,1,0:T(8,128)S(1)}, u32[]{:S(2)}, u32[]{:S(2)}) %collective-permute-start.7) | collective-permute-done | bytes 327712 | tf_op jit(solution)/shard_map/ppermute | solution.py:645
  174.8 4.4 %nonlinear_apart.1 = (f32[4,5,8,512]{3,2,1,0:T(8,128)S(1)}, f32[4,5,8,512]{3,2,1,0:T(8,128)S(1)}, f32[4,5,8,512]{3,2,1,0:T(8,128)S(1)}, f32[4,5,8,512]{3,2,1,0:T(8,128)S(1)}) custom-call(s32[2]{0:T(128)S(1)} %pad_add_fusion.place_ref, f32[25,5]{1,0:T(8,128)S(1)} %reshape.20.q_ref, f32[4,5,8,512]{3,2,1,0:T(8,128)S(1)} %pad_maximum_fusion.refs_0_, ...), custom_call_target="tpu_custom_call" | custom-call | flops 1509949440 | bytes 2621440 | tf_op jit(solution)/shard_map/nonlinear_apart/pallas_call | solution.py:234
  179.2 1.4 collective-permute-start.10
  180.7 0.6 collective-permute-start.9
  181.2 10.8 %collective-permute-done.10 = f32[4,5,8,512]{3,2,1,0:T(8,128)S(1)} collective-permute-done((f32[4,5,8,512]{3,2,1,0:T(8,128)S(1)}, f32[4,5,8,512]{3,2,1,0:T(8,128)S(1)}, u32[]{:S(2)}, u32[]{:S(2)}) %collective-permute-start.10) | collective-permute-done | bytes 327712 | tf_op jit(solution)/shard_map/ppermute | solution.py:645
  192.0 13.4 %collective-permute-done.9 = f32[4,5,8,512]{3,2,1,0:T(8,128)S(1)} collective-permute-done((f32[4,5,8,512]{3,2,1,0:T(8,128)S(1)}, f32[4,5,8,512]{3,2,1,0:T(8,128)S(1)}, u32[]{:S(2)}, u32[]{:S(2)}) %collective-permute-start.9) | collective-permute-done | bytes 327712 | tf_op jit(solution)/shard_map/ppermute | solution.py:645
  205.5 0.8 pad_maximum_fusion.5
  206.3 10.0 %collective-permute-start.11 = (f32[4,5,8,512]{3,2,1,0:T(8,128)}, f32[4,5,8,512]{3,2,1,0:T(8,128)S(1)}, u32[]{:S(2)}, u32[]{:S(2)}) collective-permute-start(f32[4,5,8,512]{3,2,1,0:T(8,128)} %pad_maximum_fusion.5), channel_id=1, source_target_pairs={{0,2},{2,0},{4,6},{6,4},{1,3},{3,1},{5,7},{7,5},{8,10},{10,8},{12,... | collective-permute-start | bytes 983048 | tf_op jit(solution)/shard_map/ppermute | solution.py:645
  216.2 0.8 pad_maximum_fusion.6
  217.0 1.9 collective-permute-start.12
  218.9 0.8 pad_maximum_fusion.7
  219.7 0.6 collective-permute-start.13
  220.3 17.4 %all-to-all-done.1.in_ref = f32[48,5,8,512]{3,2,1,0:T(8,128)} async-done(((f32[48,5,8,512]{3,2,1,0:T(8,128)}), f32[48,5,8,512]{3,2,1,0:T(8,128)}, u32[]{:S(2)}, u32[]{:S(2)}) %all-to-all-start.1) | async-done | bytes 3932192 | tf_op jit(solution)/shard_map/all_to_all | solution.py:640
  237.7 2.1 copy-done.3
  239.8 0.9 copy-done.8
  240.7 0.8 copy-done.13
  241.5 5.4 %absorb.1 = (f32[2,5,48,2048]{3,2,1,0:T(8,128)S(1)}, f32[24,2048]{1,0:T(8,128)S(1)}) custom-call(f32[48,5,8,512]{3,2,1,0:T(8,128)} %all-to-all-done.1.in_ref, s32[2048]{0:T(1024)S(1)} %copy-done.6, f32[5,10,48]{2,1,0:T(8,128)S(1)} %copy-done.13, f32[2,5,48,2048]{3,2,1,0:T(8,128)S(1)} %copy-done.3, f32[24,2048]{1,0:T(8,128)S(1)} %copy-done.8), custom_call_target="tpu_custom_call" | custom-call | tf_op jit(solution)/shard_map/absorb/pallas_call | solution.py:379
  246.9 2.5 copy-done.1
  249.4 4.6 %solve.2.before_ref = f32[2,5,64,2048]{3,2,1,0:T(8,128)S(1)} custom-call(f32[2,5,48,2048]{3,2,1,0:T(8,128)S(1)} %get-tuple-element.92.side_ref, f32[2,5,64,2048]{3,2,1,0:T(8,128)S(1)} %copy-done.1, f32[320,240]{1,0:T(8,128)S(1)} %get-tuple-element.94.inverse_ref), custom_call_target="tpu_custom_call" | custom-call | tf_op jit(solution)/shard_map/solve/pallas_call | solution.py:411
  254.0 2.7 %absorb_apart.1 = (f32[2,5,16,2048]{3,2,1,0:T(8,128)S(1)}, f32[24,2048]{1,0:T(8,128)S(1)}) custom-call(s32[2]{0:T(128)S(1)} %copy-done.15, f32[4,5,8,512]{3,2,1,0:T(8,128)S(1)} %pad_maximum_fusion.4.refs_0_, f32[4,5,8,512]{3,2,1,0:T(8,128)S(1)} %collective-permute-done.11.refs_1_, f32[4,5,8,512]{3,2,1,0:T(8,128)S(1)} %collective-permute-done.12.refs_2_, ...), custom_call_target="tpu_custom_call" | custom-call | tf_op jit(solution)/shard_map/absorb_apart/pallas_call | solution.py:379
  256.8 1.6 collective-permute-start.14
  258.4 4.2 %solve.3.solved_ref = f32[2,5,64,2048]{3,2,1,0:T(8,128)S(1)} custom-call(f32[2,5,16,2048]{3,2,1,0:T(8,128)S(1)} %get-tuple-element.103.side_ref, f32[2,5,64,2048]{3,2,1,0:T(8,128)S(1)} %solve.2.before_ref, f32[320,80]{1,0:T(8,128)S(1)} %get-tuple-element.105.inverse_ref), custom_call_target="tpu_custom_call" | custom-call | tf_op jit(solution)/shard_map/solve/pallas_call | solution.py:411
  262.6 1.0 collective-permute-done.14.refs_1_
  263.5 3.6 %finish.1 = (f32[2,5,64,2048]{3,2,1,0:T(8,128)}, f32[2,2048]{1,0:T(2,128)}) custom-call(f32[2,5,64,2048]{3,2,1,0:T(8,128)S(1)} %solve.3.solved_ref, f32[24,2048]{1,0:T(8,128)S(1)} %get-tuple-element.106.refs_0_, f32[24,2048]{1,0:T(8,128)S(1)} %collective-permute-done.14.refs_1_, f32[24,2048]{1,0:T(8,128)S(1)} %get-tuple-element.107.refs_2_, ...), custom_call_target="tpu_custom_call" | custom-call | tf_op jit(solution)/shard_map/finish/pallas_call | solution.py:468
  (61 shorter events, 0.3 us)
Async XLA Ops:
  0.6 0.7 copy-start.5
  7.4 6.5 %copy-start.6 = (s32[2048]{0:T(1024)S(1)}, s32[2048]{0:T(1024)}, u32[]{:S(2)}) copy-start(s32[2048]{0:T(1024)} %refs_4_.3) | copy-start | bytes 24580
  7.4 98.6 %all-to-all-start = ((f32[48,5,8,512]{3,2,1,0:T(8,128)}), f32[48,5,8,512]{3,2,1,0:T(8,128)}, u32[]{:S(2)}, u32[]{:S(2)}) async-start(f32[48,5,8,512]{3,2,1,0:T(8,128)} %prepare.1), calls=%async_computation | async-start | bytes 7864320 | tf_op jit(solution)/shard_map/all_to_all | solution.py:640
  13.8 7.1 %copy-start.27 = (f32[1,5,5]{2,0,1:T(1,128)S(1)}, f32[1,5,5]{2,0,1:T(1,128)}, u32[]{:S(2)}) copy-start(f32[1,5,5]{2,0,1:T(1,128)} %param.19) | copy-start | bytes 304
  13.8 7.7 %copy-start.28 = (f32[1,5,5]{2,0,1:T(1,128)S(1)}, f32[1,5,5]{2,0,1:T(1,128)}, u32[]{:S(2)}) copy-start(f32[1,5,5]{2,0,1:T(1,128)} %param.20) | copy-start | bytes 304
  13.8 8.3 %copy-start.24 = (f32[1,10,10]{2,0,1:T(1,128)S(1)}, f32[1,10,10]{2,0,1:T(1,128)}, u32[]{:S(2)}) copy-start(f32[1,10,10]{2,0,1:T(1,128)} %param.21) | copy-start | bytes 1204
  13.8 8.9 %copy-start.25 = (f32[1,10,10]{2,0,1:T(1,128)S(1)}, f32[1,10,10]{2,0,1:T(1,128)}, u32[]{:S(2)}) copy-start(f32[1,10,10]{2,0,1:T(1,128)} %param.22) | copy-start | bytes 1204
  13.9 9.5 %copy-start.26 = (f32[1,10,10]{2,0,1:T(1,128)S(1)}, f32[1,10,10]{2,0,1:T(1,128)}, u32[]{:S(2)}) copy-start(f32[1,10,10]{2,0,1:T(1,128)} %param.23) | copy-start | bytes 1204
  13.9 15.6 %copy-start.4 = (f32[1,320,320]{2,1,0:T(8,128)S(1)}, f32[1,320,320]{2,1,0:T(8,128)}, u32[]{:S(2)}) copy-start(f32[1,320,320]{2,1,0:T(8,128)} %param.18) | copy-start | bytes 1228804
  14.0 160.8 %copy-start.14 = (s32[2]{0:T(128)}, s32[2]{0:T(128)S(1)}, u32[]{:S(2)}) copy-start(s32[2]{0:T(128)S(1)} %pad_add_fusion.place_ref) | copy-start | bytes 28
  18.0 88.0 %collective-permute-start.2 = (f32[4,5,8,512]{3,2,1,0:T(8,128)}, f32[4,5,8,512]{3,2,1,0:T(8,128)}, u32[]{:S(2)}, u32[]{:S(2)}) collective-permute-start(f32[4,5,8,512]{3,2,1,0:T(8,128)} %get-tuple-element.71), channel_id=1, source_target_pairs={{0,2},{2,0},{4,6},{6,4},{1,3},{3,1},{5,7},{7,5},{8,10},{10,8},{12,... | collective-permute-start | bytes 983048 | tf_op jit(solution)/shard_map/ppermute | solution.py:645
  18.6 96.4 %collective-permute-start.3 = (f32[4,5,8,512]{3,2,1,0:T(8,128)}, f32[4,5,8,512]{3,2,1,0:T(8,128)}, u32[]{:S(2)}, u32[]{:S(2)}) collective-permute-start(f32[4,5,8,512]{3,2,1,0:T(8,128)} %get-tuple-element.73), channel_id=1, source_target_pairs={{0,6},{2,4},{4,2},{6,0},{1,7},{3,5},{5,3},{7,1},{8,14},{10,12},{12... | collective-permute-start | bytes 983048 | tf_op jit(solution)/shard_map/ppermute | solution.py:645
  25.3 4.2 %collective-permute-start = (f32[5,16,128]{2,1,0:T(8,128)}, f32[5,16,128]{2,1,0:T(8,128)S(1)}, u32[]{:S(2)}, u32[]{:S(2)}) collective-permute-start(f32[5,16,128]{2,1,0:T(8,128)} %pack.1.refs_0_), channel_id=1, source_target_pairs={{0,1},{1,0},{2,3},{3,2},{4,5},{5,4},{6,7},{7,6},{8,9},{9,8},{10,11... | collective-permute-start | bytes 122888 | tf_op jit(solution)/shard_map/ppermute | solution.py:485
  29.5 0.8 copy-start.9
  31.4 0.6 copy-start.10
  32.1 0.6 copy-start.12
  32.7 19.1 %copy-start.23 = (f32[5,5,5]{2,1,0:T(8,128)S(1)}, f32[5,5,5]{2,1,0:T(8,128)}, u32[]{:S(2)}) copy-start(f32[5,5,5]{2,1,0:T(8,128)} %param.17) | copy-start | bytes 1504
  45.3 2.4 copy-start
  47.7 1.9 copy-start.2
  49.6 0.7 copy-start.7
  50.2 5.7 %collective-permute-start.1 = (f32[24,2048]{1,0:T(8,128)S(1)}, f32[24,2048]{1,0:T(8,128)S(1)}, u32[]{:S(2)}, u32[]{:S(2)}) collective-permute-start(f32[24,2048]{1,0:T(8,128)S(1)} %get-tuple-element.107.refs_2_), channel_id=1, source_target_pairs={{0,1},{1,0},{2,3},{3,2},{4,5},{5,4},{6,7},{7,6},{8,9},{9,8},{10,11... | collective-permute-start | bytes 589832 | tf_op jit(solution)/shard_map/ppermute | solution.py:485
  114.9 16.8 %collective-permute-start.4 = (f32[4,5,8,512]{3,2,1,0:T(8,128)S(1)}, f32[4,5,8,512]{3,2,1,0:T(8,128)S(1)}, u32[]{:S(2)}, u32[]{:S(2)}) collective-permute-start(f32[4,5,8,512]{3,2,1,0:T(8,128)S(1)} %get-tuple-element.77), channel_id=1, source_target_pairs={{0,4},{2,6},{4,0},{6,2},{1,5},{3,7},{5,1},{7,3},{8,12},{10,14},{12... | collective-permute-start | bytes 983048 | tf_op jit(solution)/shard_map/ppermute | solution.py:645
  114.9 1.0 copy-start.16
  116.0 1.0 copy-start.18
  117.0 0.9 copy-start.20
  118.0 0.9 copy-start.22
  131.8 105.9 %all-to-all-start.1 = ((f32[48,5,8,512]{3,2,1,0:T(8,128)}), f32[48,5,8,512]{3,2,1,0:T(8,128)}, u32[]{:S(2)}, u32[]{:S(2)}) async-start(f32[48,5,8,512]{3,2,1,0:T(8,128)} %bitcast.8), calls=%async_computation.1 | async-start | bytes 7864320 | tf_op jit(solution)/shard_map/all_to_all | solution.py:640
  138.4 36.4 %copy-start.17 = (f32[512,256]{1,0:T(8,128)S(1)}, f32[512,256]{1,0:T(8,128)}, u32[]{:S(2)}) copy-start(f32[512,256]{1,0:T(8,128)} %constant.20.clone.refs_1_.refs_5_) | copy-start | bytes 1572868
  138.4 36.4 %copy-start.19 = (f32[256,512]{1,0:T(8,128)S(1)}, f32[256,512]{1,0:T(8,128)}, u32[]{:S(2)}) copy-start(f32[256,512]{1,0:T(8,128)} %constant.21.clone.refs_2_.refs_6_) | copy-start | bytes 1572868
  138.4 36.4 %copy-start.21 = (f32[256,256]{1,0:T(8,128)S(1)}, f32[256,256]{1,0:T(8,128)}, u32[]{:S(2)}) copy-start(f32[256,256]{1,0:T(8,128)} %constant.19.clone.refs_0_.refs_4_) | copy-start | bytes 786436
  140.7 2.1 collective-permute-start.5
  140.9 25.1 %collective-permute-start.6 = (f32[4,5,8,512]{3,2,1,0:T(8,128)S(1)}, f32[4,5,8,512]{3,2,1,0:T(8,128)S(1)}, u32[]{:S(2)}, u32[]{:S(2)}) collective-permute-start(f32[4,5,8,512]{3,2,1,0:T(8,128)S(1)} %pad_maximum_fusion.2), channel_id=1, source_target_pairs={{0,16},{8,24},{16,0},{24,8},{1,17},{9,25},{17,1},{25,9},{2,18},{10... | collective-permute-start | bytes 983048 | tf_op jit(solution)/shard_map/ppermute | solution.py:645
  141.6 33.2 %collective-permute-start.7 = (f32[4,5,8,512]{3,2,1,0:T(8,128)S(1)}, f32[4,5,8,512]{3,2,1,0:T(8,128)S(1)}, u32[]{:S(2)}, u32[]{:S(2)}) collective-permute-start(f32[4,5,8,512]{3,2,1,0:T(8,128)S(1)} %pad_maximum_fusion.3), channel_id=1, source_target_pairs={{0,24},{8,16},{16,8},{24,0},{1,25},{9,17},{17,9},{25,1},{2,26},{10... | collective-permute-start | bytes 983048 | tf_op jit(solution)/shard_map/ppermute | solution.py:645
  179.2 12.8 %collective-permute-start.10 = (f32[4,5,8,512]{3,2,1,0:T(8,128)S(1)}, f32[4,5,8,512]{3,2,1,0:T(8,128)S(1)}, u32[]{:S(2)}, u32[]{:S(2)}) collective-permute-start(f32[4,5,8,512]{3,2,1,0:T(8,128)S(1)} %get-tuple-element.86), channel_id=1, source_target_pairs={{0,24},{8,16},{16,8},{24,0},{1,25},{9,17},{17,9},{25,1},{2,26},{10... | collective-permute-start | bytes 983048 | tf_op jit(solution)/shard_map/ppermute | solution.py:645
  180.7 24.8 %collective-permute-start.9 = (f32[4,5,8,512]{3,2,1,0:T(8,128)S(1)}, f32[4,5,8,512]{3,2,1,0:T(8,128)S(1)}, u32[]{:S(2)}, u32[]{:S(2)}) collective-permute-start(f32[4,5,8,512]{3,2,1,0:T(8,128)S(1)} %get-tuple-element.85), channel_id=1, source_target_pairs={{0,16},{8,24},{16,0},{24,8},{1,17},{9,25},{17,1},{25,9},{2,18},{10... | collective-permute-start | bytes 983048 | tf_op jit(solution)/shard_map/ppermute | solution.py:645
  181.2 24.3 %collective-permute-start.8 = (f32[4,5,8,512]{3,2,1,0:T(8,128)S(1)}, f32[4,5,8,512]{3,2,1,0:T(8,128)S(1)}, u32[]{:S(2)}, u32[]{:S(2)}) collective-permute-start(f32[4,5,8,512]{3,2,1,0:T(8,128)S(1)} %get-tuple-element.84), channel_id=1, source_target_pairs={{0,8},{8,0},{16,24},{24,16},{1,9},{9,1},{17,25},{25,17},{2,10},{10... | collective-permute-start | bytes 983048 | tf_op jit(solution)/shard_map/ppermute | solution.py:645
  206.3 47.7 %collective-permute-start.11 = (f32[4,5,8,512]{3,2,1,0:T(8,128)}, f32[4,5,8,512]{3,2,1,0:T(8,128)S(1)}, u32[]{:S(2)}, u32[]{:S(2)}) collective-permute-start(f32[4,5,8,512]{3,2,1,0:T(8,128)} %pad_maximum_fusion.5), channel_id=1, source_target_pairs={{0,2},{2,0},{4,6},{6,4},{1,3},{3,1},{5,7},{7,5},{8,10},{10,8},{12,... | collective-permute-start | bytes 983048 | tf_op jit(solution)/shard_map/ppermute | solution.py:645
  217.0 37.0 %collective-permute-start.12 = (f32[4,5,8,512]{3,2,1,0:T(8,128)}, f32[4,5,8,512]{3,2,1,0:T(8,128)S(1)}, u32[]{:S(2)}, u32[]{:S(2)}) collective-permute-start(f32[4,5,8,512]{3,2,1,0:T(8,128)} %pad_maximum_fusion.6), channel_id=1, source_target_pairs={{0,4},{2,6},{4,0},{6,2},{1,5},{3,7},{5,1},{7,3},{8,12},{10,14},{12... | collective-permute-start | bytes 983048 | tf_op jit(solution)/shard_map/ppermute | solution.py:645
  219.7 34.3 %collective-permute-start.13 = (f32[4,5,8,512]{3,2,1,0:T(8,128)}, f32[4,5,8,512]{3,2,1,0:T(8,128)S(1)}, u32[]{:S(2)}, u32[]{:S(2)}) collective-permute-start(f32[4,5,8,512]{3,2,1,0:T(8,128)} %pad_maximum_fusion.7), channel_id=1, source_target_pairs={{0,6},{2,4},{4,2},{6,0},{1,7},{3,5},{5,3},{7,1},{8,14},{10,12},{12... | collective-permute-start | bytes 983048 | tf_op jit(solution)/shard_map/ppermute | solution.py:645
  237.7 2.1 copy-start.3
  239.8 0.9 copy-start.8
  240.7 0.8 copy-start.13
  246.9 2.5 copy-start.1
  249.4 4.7 %copy-start.15 = (s32[2]{0:T(128)S(1)}, s32[2]{0:T(128)}, u32[]{:S(2)}) copy-start(s32[2]{0:T(128)} %copy-done.14) | copy-start | bytes 28
  256.8 6.8 %collective-permute-start.14 = (f32[24,2048]{1,0:T(8,128)S(1)}, f32[24,2048]{1,0:T(8,128)S(1)}, u32[]{:S(2)}, u32[]{:S(2)}) collective-permute-start(f32[24,2048]{1,0:T(8,128)S(1)} %get-tuple-element.106.refs_0_), channel_id=1, source_target_pairs={{0,1},{1,0},{2,3},{3,2},{4,5},{5,4},{6,7},{7,6},{8,9},{9,8},{10,11... | collective-permute-start | bytes 589832 | tf_op jit(solution)/shard_map/ppermute | solution.py:485
  258.4 5.2 %copy-start.11 = (bf16[352,96]{1,0:T(8,128)(2,1)S(1)}, bf16[352,96]{1,0:T(8,128)(2,1)}, u32[]{:S(2)}) copy-start(bf16[352,96]{1,0:T(8,128)(2,1)} %copy-done.10) | copy-start | bytes 202756

commit v2 on v1

--- a/solution.py
+++ b/solution.py
@@ -42,7 +42,7 @@
 
 
 def whole(array):
-    zeros = (0,) * array.ndim
+    zeros = (0,) * len(array.shape)
     return pl.BlockSpec(array.shape, lambda *_: zeros)
 
 
@@ -78,7 +78,7 @@
         out_shape=pltpu.HBM((rows, variables, freqs, 2 * NB), jnp.float32),
         compiler_params=params(),
         name="prepare",
-    )(in_hbm(amplitudes), keep)
+    )(in_hbm(amplitudes), in_hbm(keep))
 
 
 def partner(place_ref, j, i, spans):
@@ -89,13 +89,13 @@
     out_refs, rows_ref = refs[:-1], refs[-1]
     keep = kept_modes(mask_ref)
     rows, freqs, _ = rows_ref.shape
-    spans = len(out_refs)
+    spans = out_refs[0].shape[0]
     for part in range(2):
         kept = x_ref[part, 0] * keep
         rows_ref[:, :, part * NB : (part + 1) * NB] = kept.reshape(rows, freqs, NB)
-    for i, out_ref in enumerate(out_refs):
-        for j in range(out_ref.shape[0]):
-            out_ref[j, 0] = rows_ref[partner(place_ref, j, i, spans)]
+    for j, out_ref in enumerate(out_refs):
+        for i in range(spans):
+            out_ref[i, 0] = rows_ref[partner(place_ref, j, i, spans)]
 
 
 def prepare_apart(place, amplitudes, keep, cut, groups, spans):
@@ -111,8 +111,8 @@
             pl.BlockSpec((2, 1, rows, modes), lambda v: (0, v, at, 0)),
             pl.BlockSpec((modes,), lambda v: (0,)),
         ],
-        out_specs=[pl.BlockSpec((groups, 1, freqs, 2 * NB), lambda v: (0, v, 0, 0))] * spans,
-        out_shape=[jax.ShapeDtypeStruct((groups, variables, freqs, 2 * NB), jnp.float32)] * spans,
+        out_specs=[pl.BlockSpec((spans, 1, freqs, 2 * NB), lambda v: (0, v, 0, 0))] * groups,
+        out_shape=[jax.ShapeDtypeStruct((spans, variables, freqs, 2 * NB), jnp.float32)] * groups,
         scratch_shapes=[pltpu.VMEM((rows, freqs, 2 * NB), jnp.float32)],
         compiler_params=params(),
         name="prepare_apart",
@@ -200,19 +200,18 @@
         compiler_params=params(24),
         cost_estimate=nonlinear_cost(points, variables),
         name="nonlinear",
-    )(coefficients, block, *transforms)
-
-
-def nonlinear_apart_body(groups, place_ref, q_ref, *refs):
-    in_refs, refs = refs[:groups], refs[groups:]
+    )(coefficients, block, *[in_hbm(table) for table in transforms])
+
+
+def nonlinear_apart_body(groups, spans, place_ref, q_ref, *refs):
+    in_refs, refs = refs[:spans], refs[spans:]
     table_refs, refs = refs[:4], refs[4:]
     out_refs, refs = refs[:groups], refs[groups:]
     rows_ref, work_refs = refs[0], refs[1:]
     devices, _, freqs, _ = rows_ref.shape
-    spans = devices // groups
     for j in range(groups):
         for i in range(spans):
-            rows_ref[partner(place_ref, j, i, spans)] = in_refs[j][i]
+            rows_ref[partner(place_ref, j, i, spans)] = in_refs[i][j]
 
     def read(v):
         return rows_ref[:, v].reshape(NF, 2 * NB)
@@ -228,87 +227,86 @@
 
 
 def nonlinear_apart(place, blocks, coefficients, transforms):
-    groups = len(blocks)
-    spans, variables, freqs, lanes = blocks[0].shape
+    spans = len(blocks)
+    groups, variables, freqs, lanes = blocks[0].shape
+    result = jax.ShapeDtypeStruct((spans, variables, freqs, lanes), jnp.float32)
     smem = pl.BlockSpec(memory_space=pltpu.SMEM)
     return pl.pallas_call(
-        functools.partial(nonlinear_apart_body, groups),
+        functools.partial(nonlinear_apart_body, groups, spans),
         grid=(1,),
         in_specs=[smem, smem]
         + [whole(block) for block in blocks]
         + [whole(table) for table in transforms],
-        out_specs=[whole(block) for block in blocks],
-        out_shape=[jax.ShapeDtypeStruct(block.shape, jnp.float32) for block in blocks],
+        out_specs=[whole(result)] * groups,
+        out_shape=[result] * groups,
         scratch_shapes=[pltpu.VMEM((groups * spans, variables, freqs, lanes), jnp.float32)]
         + work_shapes(variables),
         compiler_params=params(24),
         cost_estimate=nonlinear_cost(1, variables),
         name="nonlinear_apart",
-    )(place, coefficients, *blocks, *transforms)
-
-
-def base_body(cuts, x_ref, up_ref, mask_ref, inverse_ref, turned_ref, *refs):
-    out_refs, (edge_ref, solved_ref, sum_ref) = refs[: len(cuts)], refs[len(cuts) :]
+    )(place, coefficients, *blocks, *[in_hbm(table) for table in transforms])
+
+
+def base_body(cuts, x_ref, up_ref, mask_ref, edge_rows_ref, turned_ref, *refs):
+    out_refs, (edge_ref, sum_ref) = refs[: len(cuts)], refs[len(cuts) :]
     _, variables, heights, lanes = x_ref.shape
     extent = variables * heights
     ends = 2 * variables
     keep = kept_modes(mask_ref)
-    kept, solved = [], []
+    squares, moved, sides = 0.0, [], []
     for part in range(2):
-        kept.append(x_ref[part].reshape(extent, lanes) * keep)
-        moved = jnp.dot(
-            turned_ref[...], kept[part], precision=SPLIT, preferred_element_type=jnp.float32
-        )
-        grid = moved.reshape(variables, heights, lanes)
+        kept = x_ref[part].reshape(extent, lanes) * keep
+        squares = squares + total(kept * kept)
+        moved.append(
+            jnp.dot(turned_ref[...], kept, precision=SPLIT, preferred_element_type=jnp.float32)
+        )
+        grid = moved[part].reshape(variables, heights, lanes)
         for cut, out_ref in zip(cuts, out_refs):
             out_ref[part] = grid[:, cut]
-        side = up_ref[part].reshape(extent, lanes) * keep
-        solved.append(
-            jnp.dot(inverse_ref[...], side, precision=SPLIT, preferred_element_type=jnp.float32)
-        )
-        solved_ref[part] = solved[part].reshape(variables, heights, lanes)
+        sides.append(up_ref[part].reshape(extent, lanes) * keep)
+        sum_ref[part * ends : (part + 1) * ends] = jnp.dot(
+            edge_rows_ref[...], sides[part], precision=SPLIT, preferred_element_type=jnp.float32
+        )
         for end, point in enumerate((0, heights - 1)):
             for v in range(variables):
                 row = part * ends + end * variables + v
                 at = v * heights + point
-                edge_ref[row : row + 1] = moved[at : at + 1]
-                sum_ref[row : row + 1] = solved[part][at : at + 1]
-
-    def total(value):
-        return jnp.sum(value, axis=0, keepdims=True)
-
+                edge_ref[row : row + 1] = moved[part][at : at + 1]
     row = 2 * ends
     none = jnp.zeros((GATHERED_ROWS - row - 1, lanes), jnp.float32)
-    edge_ref[row : row + 1] = total(kept[0] * kept[0] + kept[1] * kept[1])
+    edge_ref[row : row + 1] = squares
     edge_ref[row + 1 :] = none
-    sum_ref[row : row + 1] = total(kept[0] * solved[0] + kept[1] * solved[1])
-    sum_ref[row + 1 : row + 2] = total(kept[0] * solved[1] - kept[1] * solved[0])
+    sum_ref[row : row + 1] = total(moved[0] * sides[0] + moved[1] * sides[1])
+    sum_ref[row + 1 : row + 2] = total(moved[0] * sides[1] - moved[1] * sides[0])
     sum_ref[row + 2 :] = none[1:]
 
 
-def base(amplitudes, upstream, keep, inverse, turned, cuts):
+def total(value):
+    return jnp.sum(value, axis=0, keepdims=True)
+
+
+def base(amplitudes, upstream, keep, edge_rows, turned, cuts):
     _, variables, heights, modes = amplitudes.shape
-
-    def rows_spec(rows):
-        return pl.BlockSpec((2, variables, rows, NB), lambda i: (0, 0, 0, i))
-
-    def rows_shape(rows):
-        return jax.ShapeDtypeStruct((2, variables, rows, modes), jnp.float32)
-
     lengths = [cut.stop - cut.start for cut in cuts]
+    shapes = [(2, variables, rows, modes) for rows in lengths]
+    spec = pl.BlockSpec((2, variables, heights, NB), lambda i: (0, 0, 0, i))
     small = pl.BlockSpec((GATHERED_ROWS, NB), lambda i: (0, i))
     small_shape = jax.ShapeDtypeStruct((GATHERED_ROWS, modes), jnp.float32)
     return pl.pallas_call(
         functools.partial(base_body, cuts),
         grid=(modes // NB,),
-        in_specs=[rows_spec(heights)] * 2
-        + [pl.BlockSpec((NB,), lambda i: (i,)), whole(inverse), whole(turned)],
-        out_specs=[rows_spec(rows) for rows in lengths] + [small, rows_spec(heights), small],
-        out_shape=[rows_shape(rows) for rows in lengths]
-        + [small_shape, rows_shape(heights), small_shape],
+        in_specs=[spec] * 2
+        + [pl.BlockSpec((NB,), lambda i: (i,)), whole(edge_rows), whole(turned)],
+        out_specs=[
+            pl.BlockSpec((2, variables, rows, NB), lambda i: (0, 0, 0, i)) for rows in lengths
+        ]
+        + [small] * 2,
+        out_shape=[pltpu.HBM(shapes[0], jnp.float32)]
+        + [jax.ShapeDtypeStruct(shape, jnp.float32) for shape in shapes[1:]]
+        + [small_shape] * 2,
         compiler_params=params(24),
         name="base",
-    )(in_hbm(amplitudes), in_hbm(upstream), keep, inverse, turned)
+    )(in_hbm(amplitudes), in_hbm(upstream), keep, edge_rows, turned)
 
 
 def absorb_rows(read, mask_ref, edge_ref, adj_ref, before_ref, out_ref, sum_ref):
@@ -369,7 +367,7 @@
         grid_spec,
         sums,
     ]
-    operands = blocks + [keep, edges, adjoint_modes, before]
+    operands = blocks + [keep, edges, adjoint_modes if apart else in_hbm(adjoint_modes), before]
     body, scratch = absorb_body, []
     if apart:
         operands = [place] + operands
@@ -391,32 +389,41 @@
     )(*operands)
 
 
-def solve_body(side_ref, before_ref, inverse_ref, out_ref):
+def solve_body(groups, *refs):
+    side_refs, (up_ref, mask_ref, inverse_ref, out_ref) = refs[:groups], refs[groups:]
     _, variables, heights, lanes = out_ref.shape
+    keep = kept_modes(mask_ref)
     for part in range(2):
+        forced = [ref[part] for ref in side_refs]
+        forced = forced[0] if groups == 1 else jnp.concatenate(forced, axis=1)
+        side = forced + up_ref[part] * keep
+        side = side.reshape(variables * heights, lanes)
+        high = side.astype(jnp.bfloat16)
+        low = (side - high.astype(jnp.float32)).astype(jnp.bfloat16)
         moved = jnp.dot(
             inverse_ref[...],
-            side_ref[part].reshape(-1, lanes),
-            precision=SPLIT,
+            jnp.concatenate([high, low, high], axis=0),
             preferred_element_type=jnp.float32,
         )
-        out_ref[part] = before_ref[part] + moved.reshape(variables, heights, lanes)
-
-
-def solve(side, before, inverse):
-    _, variables, rows, modes = side.shape
-    heights = before.shape[2]
+        out_ref[part] = moved.reshape(variables, heights, lanes)
+
+
+def solve(sides, upstream, keep, inverse):
+    _, variables, heights, modes = upstream.shape
     spec = pl.BlockSpec((2, variables, heights, NB), lambda i: (0, 0, 0, i))
-    side_spec = pl.BlockSpec((2, variables, rows, NB), lambda i: (0, 0, 0, i))
-    return pl.pallas_call(
-        solve_body,
+    return pl.pallas_call(
+        functools.partial(solve_body, len(sides)),
         grid=(modes // NB,),
-        in_specs=[side_spec, spec, whole(inverse)],
+        in_specs=[
+            pl.BlockSpec((2, variables, side.shape[2], NB), lambda i: (0, 0, 0, i))
+            for side in sides
+        ]
+        + [spec, pl.BlockSpec((NB,), lambda i: (i,)), whole(inverse)],
         out_specs=spec,
-        out_shape=jax.ShapeDtypeStruct(before.shape, jnp.float32),
+        out_shape=jax.ShapeDtypeStruct(upstream.shape, jnp.float32),
         compiler_params=params(),
         name="solve",
-    )(side, before, inverse)
+    )(*sides, in_hbm(upstream), keep, inverse)
 
 
 def finish_body(walls, extent, solved_ref, *refs):
@@ -510,29 +517,31 @@
     return value.astype(jnp.bfloat16).astype(jnp.float32)
 
 
+def split_columns(matrix):
+    high = upper_bits(matrix)
+    return jnp.concatenate([high, high, matrix - high], axis=1).astype(jnp.bfloat16)
+
+
 def constants_body(cuts, variables, walls, place_ref, inverse_ref, *refs):
     packed, refs = refs[:walls], refs[walls:]
-    turned_ref, refs = refs[0], refs[1:]
-    column_refs, refs = refs[: len(cuts)], refs[len(cuts) :]
-    row_refs, refs = refs[: len(cuts)], refs[len(cuts) :]
-    chain_ref, all_ref, step_ref = refs
+    turned_ref, split_ref, rows_ref = refs[:3]
+    row_refs, (chain_ref, all_ref, step_ref) = refs[3 : 3 + len(cuts)], refs[3 + len(cuts) :]
     extent = inverse_ref.shape[0]
     heights = extent // variables
     ends = 2 * variables
     matrix = inverse_ref[...]
     turned = matrix.T
     turned_ref[...] = turned
-    for cut, column_ref, row_ref in zip(cuts, column_refs, row_refs):
-        pieces = []
-        for v in range(variables):
-            part = matrix[:, v * heights : (v + 1) * heights][:, cut]
-            pieces.append(part)
-            for end, point in enumerate((0, heights - 1)):
-                for w in range(variables):
-                    at = w * heights + point
-                    row = end * variables + w
-                    row_ref[v, row : row + 1] = part[at : at + 1]
-        column_ref[...] = jnp.concatenate(pieces, axis=1)
+    split_ref[...] = split_columns(matrix)
+    for end, point in enumerate((0, heights - 1)):
+        for w in range(variables):
+            at = w * heights + point
+            row = end * variables + w
+            rows_ref[row : row + 1] = matrix[at : at + 1]
+            for v in range(variables):
+                part = matrix[at : at + 1, v * heights : (v + 1) * heights]
+                for cut, row_ref in zip(cuts, row_refs):
+                    row_ref[v, row : row + 1] = part[:, cut]
 
     def dot(a, b):
         return jnp.dot(a, b, precision=FULL, preferred_element_type=jnp.float32)
@@ -580,8 +589,7 @@
     if spare:
         full.append(jnp.zeros((spare, size), jnp.float32))
     full = jnp.concatenate(full, axis=0)
-    high = upper_bits(full)
-    chain_ref[...] = jnp.concatenate([high, high, full - high], axis=1).astype(jnp.bfloat16)
+    chain_ref[...] = split_columns(full)
 
 
 def constants(place, inverse, packed, cuts, variables):
@@ -597,8 +605,11 @@
         functools.partial(constants_body, cuts, variables, walls),
         in_specs=[pl.BlockSpec(memory_space=pltpu.SMEM)]
         + [pl.BlockSpec(memory_space=pltpu.VMEM)] * (1 + walls),
-        out_shape=[jax.ShapeDtypeStruct((extent, extent), f32)]
-        + [jax.ShapeDtypeStruct((extent, variables * n), f32) for n in lengths]
+        out_shape=[
+            jax.ShapeDtypeStruct((extent, extent), f32),
+            jax.ShapeDtypeStruct((extent, 3 * extent), jnp.bfloat16),
+            jax.ShapeDtypeStruct((ends, extent), f32),
+        ]
         + [jax.ShapeDtypeStruct((variables, ends, n), f32) for n in lengths]
         + [jax.ShapeDtypeStruct((rows, 3 * size), jnp.bfloat16)],
         scratch_shapes=[
@@ -656,21 +667,8 @@
     if apart:
         main, amplitudes = lax.optimization_barrier((main, amplitudes))
         sent = prepare_apart(place, amplitudes, keep, cuts[1], groups, spans)
-        arrived = swap(sent, "span", set(range(spans)) - far)
+        arrived = swap(regroup(swap(sent, "freq")), "span", set(range(spans)) - far)
     main = exchange(main)
-
-    inverse = slab_inverse[0]
-    parts = (lower_coupling, upper_coupling, reduced_lower, reduced_upper, reduced_pivot)
-    packed = around(pack(parts), "wall")
-    turned, *rest, chain = constants(wall, inverse, packed, cuts, variables)
-    columns, end_rows = rest[: len(cuts)], rest[len(cuts) :]
-    *adjoint_modes, edge, solved, sums = base(
-        amplitudes, upstream, keep, inverse, turned, cuts
-    )
-    edges = around(edge, "wall")
-    held = (main, columns, end_rows, chain, adjoint_modes, edges, solved, sums)
-    held = lax.optimization_barrier(held)
-    main, columns, end_rows, chain, adjoint_modes, edges, solved, sums = held
 
     if apart:
         main, arrived = lax.optimization_barrier((main, arrived))
@@ -680,22 +678,28 @@
     main = nonlinear(main.reshape((devices, size) + shape[1:]), coefficients, transforms)
     main = main.reshape(shape)
     if apart:
-        main, arrived = lax.optimization_barrier((main, arrived))
+        main, arrived[spans // 2] = lax.optimization_barrier((main, arrived[spans // 2]))
     main = exchange(main)
+    inverse = slab_inverse[0]
+    parts = (lower_coupling, upper_coupling, reduced_lower, reduced_upper, reduced_pivot)
+    packed = around(pack(parts), "wall")
+    turned, split, edge_rows, *end_rows, chain = constants(wall, inverse, packed, cuts, variables)
+    *adjoint_modes, edge, sums = base(amplitudes, upstream, keep, edge_rows, turned, cuts)
+    edges = around(edge, "wall")
     if apart:
-        arrived = swap(regroup(arrived), "freq")
         forced = nonlinear_apart(place, arrived, coefficients, transforms)
-        returned = swap(regroup(swap(forced, "freq")), "span")
-
-    side, sums = absorb(None, [main], keep, end_rows[0], adjoint_modes[0], sums)
+        returned = regroup(swap(forced, "freq"))
+        held = (returned, split, end_rows, chain, adjoint_modes, edges, sums)
+        held = lax.optimization_barrier(held)
+        returned, split, end_rows, chain, adjoint_modes, edges, sums = held
+        returned = swap(returned, "span")
+
+    sides = [None] * len(cuts)
+    sides[0], sums = absorb(None, [main], keep, end_rows[0], adjoint_modes[0], sums)
     if apart:
-        solved = solve(side, solved, columns[0])
-        solved, sums, adjoint_modes[1], edges, chain, columns[1] = lax.optimization_barrier(
-            (solved, sums, adjoint_modes[1], edges, chain, columns[1])
-        )
-        side, sums = absorb(place, returned, keep, end_rows[1], adjoint_modes[1], sums)
+        sides[1], sums = absorb(place, returned, keep, end_rows[1], adjoint_modes[1], sums)
     bounds = around(sums, "wall")
-    solved = solve(side, solved, columns[-1])
+    solved = solve(sides, upstream, keep, split)
     new_amplitudes, wavenumber_shift = finish(solved, bounds, edges, chain)
     return (new_amplitudes, wavenumber_shift)
 

time: 270 us -> 267 us (0.989)
  starting transfers between devices: 37 us -> 54.5 us
  local copies, waits for them, and re-layouts: 23.3 us -> 8.28 us
    ppermute x12, waiting for transfers between devices: 65 us -> 106 us  [swap(): lax.ppermute(block, axis, [(at, at ^ i) for at in range(count)])]
    all_to_all x2, waiting for transfers between devices: 67.5 us -> 30.4 us  [exchange(): return lax.all_to_all(block, axes, split_axis=0, concat_axis=0, tiled=True)]
    ppermute x12, starting transfers between devices: 19.4 us -> 36.5 us  [swap(): lax.ppermute(block, axis, [(at, at ^ i) for at in range(count)])]
    unnamed x63 -> x39, local copies, waits for them, and re-layouts: 21 us -> 8.1 us
    ppermute x3, waiting for transfers between devices: 7.82 us -> 2.7 us  [around(): lax.ppermute(block, axis, [(i, (i + d) % count) for i in range(count)])]
    pallas_call x3 -> x2, Pallas kernels: 13.2 us -> 13.3 us  [the longest x1 7.78 us: solve(): pl.pallas_call(functools.partial(solve_body, len(sides)), grid=(modes //...]
  transfers between devices with their start and end apart: 17 -> 17, of which waited for: 10 -> 10; matrix products, arithmetic and copies ran while one was open for 3% -> 2% of each run, Pallas kernels for 19% -> 18%
where the time goes in v2:
time: 267 us; the launch traced here: 266 us
  waiting for transfers between devices  139 us (52%)
  Pallas kernels  60.9 us (23%)
  starting transfers between devices  54.5 us (20%)
  local copies, waits for them, and re-layouts  8.28 us (3%)
    ppermute x12, waiting for transfers between devices, swap(): lax.ppermute(block, axis, [(at, at ^ i) for at in range(count)])  106 us
    ppermute x12, starting transfers between devices, swap(): lax.ppermute(block, axis, [(at, at ^ i) for at in range(count)])  36.5 us
    all_to_all x2, waiting for transfers between devices, exchange(): return lax.all_to_all(block, axes, split_axis=0, concat_axis=0, tiled=True)  30.4 us
    all_to_all x2, starting transfers between devices, exchange(): return lax.all_to_all(block, axes, split_axis=0, concat_axis=0, tiled=True)  13.4 us
    pallas_call x1, Pallas kernels, nonlinear(): pl.pallas_call(nonlinear_body, grid=(points,), in_specs=[pl.BlockSpec(mem...  12.4 us
    pallas_call x1, Pallas kernels, base(): pl.pallas_call(functools.partial(base_body, cuts), grid=(modes // NB,), i...  11.1 us
    pallas_call x2, Pallas kernels, absorb(): pl.pallas_call(body, grid=(variables,), in_specs=in_specs, out_specs=[gri...  8.78 us
    unnamed x39, local copies, waits for them, and re-layouts  8.1 us
  transfers between devices with their start and end apart: 17, of which 10 were waited for; matrix products, arithmetic and copies ran while one was open for 2% of the time, Pallas kernels for 18%

profile of v2, /device:TPU:10, one launch (start us, length us, event | category | flops | bytes accessed | tf_op | source)
XLA Modules:
  0.0 266.0 jit_solution(2385956546716239328)
XLA Ops:
  0.6 6.0 %prepare.1 = f32[48,5,8,512]{3,2,1,0:T(8,128)} custom-call(f32[2,5,64,2048]{3,2,1,0:T(8,128)} %x_ref.3, s32[2048]{0:T(1024)} %refs_3_.3), custom_call_target="tpu_custom_call" | custom-call | tf_op jit(solution)/shard_map/prepare/pallas_call | solution.py:70
  6.7 6.4 %all-to-all-start = ((f32[48,5,8,512]{3,2,1,0:T(8,128)}), f32[48,5,8,512]{3,2,1,0:T(8,128)}, u32[]{:S(2)}, u32[]{:S(2)}) async-start(f32[48,5,8,512]{3,2,1,0:T(8,128)} %prepare.1), calls=%async_computation | async-start | bytes 7864320 | tf_op jit(solution)/shard_map/all_to_all | solution.py:651
  13.0 0.1 pad_add_fusion.place_ref
  13.1 3.3 %prepare_apart.1 = (f32[4,5,8,512]{3,2,1,0:T(8,128)S(1)}, f32[4,5,8,512]{3,2,1,0:T(8,128)S(1)}, f32[4,5,8,512]{3,2,1,0:T(8,128)S(1)}, f32[4,5,8,512]{3,2,1,0:T(8,128)S(1)}) custom-call(s32[2]{0:T(128)S(1)} %pad_add_fusion.place_ref, f32[2,5,64,2048]{3,2,1,0:T(8,128)} %x_ref.3, s32[2048]{0:T(1024)S(1)} %copy-done.1), custom_call_target="tpu_custom_call" | custom-call | tf_op jit(solution)/shard_map/prepare_apart/pallas_call | solution.py:106
  16.4 0.2 collective-permute-start
  16.6 0.6 collective-permute-start.1
  17.2 1.1 collective-permute-start.2
  18.4 0.0 collective-permute-done
  18.4 22.3 %collective-permute-done.1 = f32[4,5,8,512]{3,2,1,0:T(8,128)S(1)} collective-permute-done((f32[4,5,8,512]{3,2,1,0:T(8,128)S(1)}, f32[4,5,8,512]{3,2,1,0:T(8,128)S(1)}, u32[]{:S(2)}, u32[]{:S(2)}) %collective-permute-start.1) | collective-permute-done | bytes 327712 | tf_op jit(solution)/shard_map/ppermute | solution.py:656
  40.8 8.7 %collective-permute-done.2 = f32[4,5,8,512]{3,2,1,0:T(8,128)S(1)} collective-permute-done((f32[4,5,8,512]{3,2,1,0:T(8,128)S(1)}, f32[4,5,8,512]{3,2,1,0:T(8,128)S(1)}, u32[]{:S(2)}, u32[]{:S(2)}) %collective-permute-start.2) | collective-permute-done | bytes 327712 | tf_op jit(solution)/shard_map/ppermute | solution.py:656
  49.5 19.1 %collective-permute-start.3 = (f32[4,5,8,512]{3,2,1,0:T(8,128)S(1)}, f32[4,5,8,512]{3,2,1,0:T(8,128)S(1)}, u32[]{:S(2)}, u32[]{:S(2)}) collective-permute-start(f32[4,5,8,512]{3,2,1,0:T(8,128)S(1)} %pad_maximum_fusion.1), channel_id=1, source_target_pairs={{0,2},{2,0},{4,6},{6,4},{1,3},{3,1},{5,7},{7,5},{8,10},{10,8},{12,... | collective-permute-start | bytes 983048 | tf_op jit(solution)/shard_map/ppermute | solution.py:656
  68.7 2.5 collective-permute-start.4
  71.2 14.5 %collective-permute-done.3.refs_1_ = f32[4,5,8,512]{3,2,1,0:T(8,128)S(1)} collective-permute-done((f32[4,5,8,512]{3,2,1,0:T(8,128)S(1)}, f32[4,5,8,512]{3,2,1,0:T(8,128)S(1)}, u32[]{:S(2)}, u32[]{:S(2)}) %collective-permute-start.3) | collective-permute-done | bytes 327712 | tf_op jit(solution)/shard_map/ppermute | solution.py:656
  85.7 28.3 %collective-permute-done.4.refs_3_ = f32[4,5,8,512]{3,2,1,0:T(8,128)S(1)} collective-permute-done((f32[4,5,8,512]{3,2,1,0:T(8,128)S(1)}, f32[4,5,8,512]{3,2,1,0:T(8,128)S(1)}, u32[]{:S(2)}, u32[]{:S(2)}) %collective-permute-start.4) | collective-permute-done | bytes 327712 | tf_op jit(solution)/shard_map/ppermute | solution.py:656
  114.1 0.0 all-to-all-done
  114.1 0.0 collective-permute-start.5
  114.1 12.4 %nonlinear.1 = f32[16,3,5,8,512]{4,3,2,1,0:T(8,128)} custom-call(f32[25,5]{1,0:T(8,128)S(1)} %reshape.20.q_ref, f32[16,3,5,8,512]{4,3,2,1,0:T(8,128)} %bitcast.2.in_ref, f32[256,256]{1,0:T(8,128)} %constant.19.clone.refs_0_.refs_4_, f32[512,256]{1,0:T(8,128)} %constant.20.clone.refs_1_.refs_5_, f32[256,512]{1,0:T(8,128)} %constant.21.clone.refs_2_.refs_6_, ...), custom_call_target="tpu_custom_call" | custom-call | flops 4529848320 | bytes 7864320 | tf_op jit(solution)/shard_map/nonlinear/pallas_call | solution.py:193
  126.5 1.6 collective-permute-done.5.refs_2_
  128.1 7.1 %all-to-all-start.1 = ((f32[48,5,8,512]{3,2,1,0:T(8,128)}), f32[48,5,8,512]{3,2,1,0:T(8,128)}, u32[]{:S(2)}, u32[]{:S(2)}) async-start(f32[48,5,8,512]{3,2,1,0:T(8,128)} %bitcast.7), calls=%async_computation.1 | async-start | bytes 7864320 | tf_op jit(solution)/shard_map/all_to_all | solution.py:651
  135.2 0.0 copy-start.16
  135.2 0.0 copy-start.12
  135.2 0.0 copy-start.13
  135.3 0.0 copy-start.14
  135.3 0.0 copy-start
  135.3 5.5 %nonlinear_apart.1 = (f32[4,5,8,512]{3,2,1,0:T(8,128)S(1)}, f32[4,5,8,512]{3,2,1,0:T(8,128)}, f32[4,5,8,512]{3,2,1,0:T(8,128)S(1)}, f32[4,5,8,512]{3,2,1,0:T(8,128)S(1)}) custom-call(s32[2]{0:T(128)S(1)} %pad_add_fusion.place_ref, f32[25,5]{1,0:T(8,128)S(1)} %reshape.20.q_ref, f32[4,5,8,512]{3,2,1,0:T(8,128)S(1)} %get-tuple-element.55.refs_0_, ...), custom_call_target="tpu_custom_call" | custom-call | flops 1509949440 | bytes 2621440 | tf_op jit(solution)/shard_map/nonlinear_apart/pallas_call | solution.py:234
  140.8 0.2 collective-permute-start.6
  140.9 0.6 copy.19.refs_0_
  141.5 0.6 copy.20.refs_1_
  142.1 0.6 copy.21.refs_2_
  142.7 0.6 copy.22.refs_3_
  143.3 0.6 copy.23.refs_4_
  143.9 1.4 pack.1.refs_0_
  145.3 1.5 collective-permute-start.9
  146.8 2.7 %collective-permute-done.9.refs_1_ = f32[5,16,128]{2,1,0:T(8,128)S(1)} collective-permute-done((f32[5,16,128]{2,1,0:T(8,128)}, f32[5,16,128]{2,1,0:T(8,128)S(1)}, u32[]{:S(2)}, u32[]{:S(2)}) %collective-permute-start.9) | collective-permute-done | bytes 40992 | tf_op jit(solution)/shard_map/ppermute | solution.py:492
  149.5 0.8 copy-done.6
  150.3 1.1 constants.1
  151.4 0.6 copy-done.7
  152.0 0.6 copy-done.9
  152.6 11.1 %base.1 = (f32[2,5,48,2048]{3,2,1,0:T(8,128)}, f32[2,5,16,2048]{3,2,1,0:T(8,128)S(1)}, f32[24,2048]{1,0:T(8,128)S(1)}, f32[24,2048]{1,0:T(8,128)S(1)}) custom-call(f32[2,5,64,2048]{3,2,1,0:T(8,128)} %x_ref.3, f32[2,5,64,2048]{3,2,1,0:T(8,128)} %refs_2_.3, s32[2048]{0:T(1024)S(1)} %copy-done.1, f32[10,320]{1,0:T(8,128)S(1)} %get-tuple-element.67.edge_rows_ref, ...), custom_call_target="tpu_custom_call" | custom-call | tf_op jit(solution)/shard_map/base/pallas_call | solution.py:295
  163.7 0.7 copy-done.4
  164.4 1.5 collective-permute-start.10
  165.9 0.5 collective-permute-start.7
  166.5 0.2 collective-permute-start.8
  166.7 0.0 collective-permute-done.6
  166.7 15.1 %collective-permute-done.7 = f32[4,5,8,512]{3,2,1,0:T(8,128)S(1)} collective-permute-done((f32[4,5,8,512]{3,2,1,0:T(8,128)S(1)}, f32[4,5,8,512]{3,2,1,0:T(8,128)S(1)}, u32[]{:S(2)}, u32[]{:S(2)}) %collective-permute-start.7) | collective-permute-done | bytes 327712 | tf_op jit(solution)/shard_map/ppermute | solution.py:656
  181.9 7.2 %collective-permute-done.8 = f32[4,5,8,512]{3,2,1,0:T(8,128)S(1)} collective-permute-done((f32[4,5,8,512]{3,2,1,0:T(8,128)S(1)}, f32[4,5,8,512]{3,2,1,0:T(8,128)S(1)}, u32[]{:S(2)}, u32[]{:S(2)}) %collective-permute-start.8) | collective-permute-done | bytes 327712 | tf_op jit(solution)/shard_map/ppermute | solution.py:656
  189.1 0.8 pad_maximum_fusion.7
  189.9 0.8 pad_maximum_fusion.6
  190.7 0.8 pad_maximum_fusion.5
  191.5 0.0 collective-permute-done.10.refs_3_
  191.5 0.7 copy-done.2
  192.2 1.9 collective-permute-start.11
  194.1 9.5 %collective-permute-start.12 = (f32[4,5,8,512]{3,2,1,0:T(8,128)}, f32[4,5,8,512]{3,2,1,0:T(8,128)S(1)}, u32[]{:S(2)}, u32[]{:S(2)}) collective-permute-start(f32[4,5,8,512]{3,2,1,0:T(8,128)} %pad_maximum_fusion.6), channel_id=1, source_target_pairs={{0,4},{2,6},{4,0},{6,2},{1,5},{3,7},{5,1},{7,3},{8,12},{10,14},{12... | collective-permute-start | bytes 983048 | tf_op jit(solution)/shard_map/ppermute | solution.py:656
  203.6 0.6 collective-permute-start.13
  204.1 30.4 %all-to-all-done.1.in_ref = f32[48,5,8,512]{3,2,1,0:T(8,128)} async-done(((f32[48,5,8,512]{3,2,1,0:T(8,128)}), f32[48,5,8,512]{3,2,1,0:T(8,128)}, u32[]{:S(2)}, u32[]{:S(2)}) %all-to-all-start.1) | async-done | bytes 3932192 | tf_op jit(solution)/shard_map/all_to_all | solution.py:651
  234.5 0.9 copy-done.5
  235.4 0.8 copy-done.10
  236.2 6.1 %absorb.1 = (f32[2,5,48,2048]{3,2,1,0:T(8,128)S(1)}, f32[24,2048]{1,0:T(8,128)S(1)}) custom-call(f32[48,5,8,512]{3,2,1,0:T(8,128)} %all-to-all-done.1.in_ref, s32[2048]{0:T(1024)S(1)} %copy-done.1, f32[5,10,48]{2,1,0:T(8,128)S(1)} %copy-done.10, f32[2,5,48,2048]{3,2,1,0:T(8,128)} %get-tuple-element.74.refs_2_, f32[24,2048]{1,0:T(8,128)S(1)} %copy-done.5), custom_call_target="tpu_custom_call" | custom-call | tf_op jit(solution)/shard_map/absorb/pallas_call | solution.py:377
  242.3 0.0 collective-permute-done.11.refs_1_
  242.3 8.0 %collective-permute-done.13.refs_3_ = f32[4,5,8,512]{3,2,1,0:T(8,128)S(1)} collective-permute-done((f32[4,5,8,512]{3,2,1,0:T(8,128)}, f32[4,5,8,512]{3,2,1,0:T(8,128)S(1)}, u32[]{:S(2)}, u32[]{:S(2)}) %collective-permute-start.13) | collective-permute-done | bytes 327712 | tf_op jit(solution)/shard_map/ppermute | solution.py:656
  250.3 2.7 %absorb_apart.1 = (f32[2,5,16,2048]{3,2,1,0:T(8,128)S(1)}, f32[24,2048]{1,0:T(8,128)S(1)}) custom-call(s32[2]{0:T(128)S(1)} %pad_add_fusion.place_ref, f32[4,5,8,512]{3,2,1,0:T(8,128)S(1)} %pad_maximum_fusion.4.refs_0_, f32[4,5,8,512]{3,2,1,0:T(8,128)S(1)} %collective-permute-done.11.refs_1_, f32[4,5,8,512]{3,2,1,0:T(8,128)S(1)} %collective-permute-done.12.refs_2_, ...), custom_call_target="tpu_custom_call" | custom-call | tf_op jit(solution)/shard_map/absorb_apart/pallas_call | solution.py:377
  253.0 1.6 collective-permute-start.14
  254.6 7.8 %solve.1.solved_ref = f32[2,5,64,2048]{3,2,1,0:T(8,128)S(1)} custom-call(f32[2,5,48,2048]{3,2,1,0:T(8,128)S(1)} %get-tuple-element.76.refs_0_, f32[2,5,16,2048]{3,2,1,0:T(8,128)S(1)} %get-tuple-element.84.refs_1_, f32[2,5,64,2048]{3,2,1,0:T(8,128)} %refs_2_.3, s32[2048]{0:T(1024)S(1)} %copy-done.1, bf16[320,960]{1,0:T(8,128)(2,1)S(1)} %get-tuple-element.85.refs_4_), custom_call_target="tpu_custom_call" | custom-call | tf_op jit(solution)/shard_map/solve/pallas_call | solution.py:414
  262.4 3.6 %finish.1 = (f32[2,5,64,2048]{3,2,1,0:T(8,128)}, f32[2,2048]{1,0:T(2,128)}) custom-call(f32[2,5,64,2048]{3,2,1,0:T(8,128)S(1)} %solve.1.solved_ref, f32[24,2048]{1,0:T(8,128)S(1)} %get-tuple-element.86.refs_0_, f32[24,2048]{1,0:T(8,128)S(1)} %collective-permute-done.14.refs_1_, f32[24,2048]{1,0:T(8,128)S(1)} %get-tuple-element.87.refs_2_, ...), custom_call_target="tpu_custom_call" | custom-call | tf_op jit(solution)/shard_map/finish/pallas_call | solution.py:475
  (37 shorter events, 0.3 us)
Async XLA Ops:
  6.7 6.5 %copy-start.1 = (s32[2048]{0:T(1024)S(1)}, s32[2048]{0:T(1024)}, u32[]{:S(2)}) copy-start(s32[2048]{0:T(1024)} %refs_3_.3) | copy-start | bytes 24580
  6.7 107.4 %all-to-all-start = ((f32[48,5,8,512]{3,2,1,0:T(8,128)}), f32[48,5,8,512]{3,2,1,0:T(8,128)}, u32[]{:S(2)}, u32[]{:S(2)}) async-start(f32[48,5,8,512]{3,2,1,0:T(8,128)} %prepare.1), calls=%async_computation | async-start | bytes 7864320 | tf_op jit(solution)/shard_map/all_to_all | solution.py:651
  13.1 58.1 %copy-start.11 = (f32[5,5,5]{2,1,0:T(8,128)S(1)}, f32[5,5,5]{2,1,0:T(8,128)}, u32[]{:S(2)}) copy-start(f32[5,5,5]{2,1,0:T(8,128)} %param.17) | copy-start | bytes 1504
  16.4 2.0 collective-permute-start
  16.6 24.1 %collective-permute-start.1 = (f32[4,5,8,512]{3,2,1,0:T(8,128)S(1)}, f32[4,5,8,512]{3,2,1,0:T(8,128)S(1)}, u32[]{:S(2)}, u32[]{:S(2)}) collective-permute-start(f32[4,5,8,512]{3,2,1,0:T(8,128)S(1)} %get-tuple-element.50), channel_id=1, source_target_pairs={{0,16},{8,24},{16,0},{24,8},{1,17},{9,25},{17,1},{25,9},{2,18},{10... | collective-permute-start | bytes 983048 | tf_op jit(solution)/shard_map/ppermute | solution.py:656
  17.2 32.3 %collective-permute-start.2 = (f32[4,5,8,512]{3,2,1,0:T(8,128)S(1)}, f32[4,5,8,512]{3,2,1,0:T(8,128)S(1)}, u32[]{:S(2)}, u32[]{:S(2)}) collective-permute-start(f32[4,5,8,512]{3,2,1,0:T(8,128)S(1)} %get-tuple-element.51), channel_id=1, source_target_pairs={{0,24},{8,16},{16,8},{24,0},{1,25},{9,17},{17,9},{25,1},{2,26},{10... | collective-permute-start | bytes 983048 | tf_op jit(solution)/shard_map/ppermute | solution.py:656
  49.5 36.2 %collective-permute-start.3 = (f32[4,5,8,512]{3,2,1,0:T(8,128)S(1)}, f32[4,5,8,512]{3,2,1,0:T(8,128)S(1)}, u32[]{:S(2)}, u32[]{:S(2)}) collective-permute-start(f32[4,5,8,512]{3,2,1,0:T(8,128)S(1)} %pad_maximum_fusion.1), channel_id=1, source_target_pairs={{0,2},{2,0},{4,6},{6,4},{1,3},{3,1},{5,7},{7,5},{8,10},{10,8},{12,... | collective-permute-start | bytes 983048 | tf_op jit(solution)/shard_map/ppermute | solution.py:656
  68.7 45.4 %collective-permute-start.4 = (f32[4,5,8,512]{3,2,1,0:T(8,128)S(1)}, f32[4,5,8,512]{3,2,1,0:T(8,128)S(1)}, u32[]{:S(2)}, u32[]{:S(2)}) collective-permute-start(f32[4,5,8,512]{3,2,1,0:T(8,128)S(1)} %pad_maximum_fusion.3), channel_id=1, source_target_pairs={{0,6},{2,4},{4,2},{6,0},{1,7},{3,5},{5,3},{7,1},{8,14},{10,12},{12... | collective-permute-start | bytes 983048 | tf_op jit(solution)/shard_map/ppermute | solution.py:656
  114.1 14.1 %collective-permute-start.5 = (f32[4,5,8,512]{3,2,1,0:T(8,128)S(1)}, f32[4,5,8,512]{3,2,1,0:T(8,128)S(1)}, u32[]{:S(2)}, u32[]{:S(2)}) collective-permute-start(f32[4,5,8,512]{3,2,1,0:T(8,128)S(1)} %get-tuple-element.53), channel_id=1, source_target_pairs={{0,4},{2,6},{4,0},{6,2},{1,5},{3,7},{5,1},{7,3},{8,12},{10,14},{12... | collective-permute-start | bytes 983048 | tf_op jit(solution)/shard_map/ppermute | solution.py:656
  128.1 106.4 %all-to-all-start.1 = ((f32[48,5,8,512]{3,2,1,0:T(8,128)}), f32[48,5,8,512]{3,2,1,0:T(8,128)}, u32[]{:S(2)}, u32[]{:S(2)}) async-start(f32[48,5,8,512]{3,2,1,0:T(8,128)} %bitcast.7), calls=%async_computation.1 | async-start | bytes 7864320 | tf_op jit(solution)/shard_map/all_to_all | solution.py:651
  135.2 5.7 %copy-start.15 = (f32[1,5,5]{2,0,1:T(1,128)S(1)}, f32[1,5,5]{2,0,1:T(1,128)}, u32[]{:S(2)}) copy-start(f32[1,5,5]{2,0,1:T(1,128)} %param.19) | copy-start | bytes 304
  135.2 6.3 %copy-start.16 = (f32[1,5,5]{2,0,1:T(1,128)S(1)}, f32[1,5,5]{2,0,1:T(1,128)}, u32[]{:S(2)}) copy-start(f32[1,5,5]{2,0,1:T(1,128)} %param.20) | copy-start | bytes 304
  135.2 6.9 %copy-start.12 = (f32[1,10,10]{2,0,1:T(1,128)S(1)}, f32[1,10,10]{2,0,1:T(1,128)}, u32[]{:S(2)}) copy-start(f32[1,10,10]{2,0,1:T(1,128)} %param.21) | copy-start | bytes 1204
  135.2 7.5 %copy-start.13 = (f32[1,10,10]{2,0,1:T(1,128)S(1)}, f32[1,10,10]{2,0,1:T(1,128)}, u32[]{:S(2)}) copy-start(f32[1,10,10]{2,0,1:T(1,128)} %param.22) | copy-start | bytes 1204
  135.3 8.1 %copy-start.14 = (f32[1,10,10]{2,0,1:T(1,128)S(1)}, f32[1,10,10]{2,0,1:T(1,128)}, u32[]{:S(2)}) copy-start(f32[1,10,10]{2,0,1:T(1,128)} %param.23) | copy-start | bytes 1204
  135.3 14.2 %copy-start = (f32[1,320,320]{2,1,0:T(8,128)S(1)}, f32[1,320,320]{2,1,0:T(8,128)}, u32[]{:S(2)}) copy-start(f32[1,320,320]{2,1,0:T(8,128)} %param.18) | copy-start | bytes 1228804
  140.8 25.9 %collective-permute-start.6 = (f32[4,5,8,512]{3,2,1,0:T(8,128)}, f32[4,5,8,512]{3,2,1,0:T(8,128)S(1)}, u32[]{:S(2)}, u32[]{:S(2)}) collective-permute-start(f32[4,5,8,512]{3,2,1,0:T(8,128)} %get-tuple-element.60), channel_id=1, source_target_pairs={{0,8},{8,0},{16,24},{24,16},{1,9},{9,1},{17,25},{25,17},{2,10},{10... | collective-permute-start | bytes 983048 | tf_op jit(solution)/shard_map/ppermute | solution.py:656
  145.3 4.2 %collective-permute-start.9 = (f32[5,16,128]{2,1,0:T(8,128)}, f32[5,16,128]{2,1,0:T(8,128)S(1)}, u32[]{:S(2)}, u32[]{:S(2)}) collective-permute-start(f32[5,16,128]{2,1,0:T(8,128)} %pack.1.refs_0_), channel_id=1, source_target_pairs={{0,1},{1,0},{2,3},{3,2},{4,5},{5,4},{6,7},{7,6},{8,9},{9,8},{10,11... | collective-permute-start | bytes 122888 | tf_op jit(solution)/shard_map/ppermute | solution.py:492
  149.5 0.8 copy-start.6
  151.4 0.6 copy-start.7
  152.0 0.6 copy-start.9
  163.7 0.7 copy-start.4
  164.4 27.1 %collective-permute-start.10 = (f32[24,2048]{1,0:T(8,128)S(1)}, f32[24,2048]{1,0:T(8,128)S(1)}, u32[]{:S(2)}, u32[]{:S(2)}) collective-permute-start(f32[24,2048]{1,0:T(8,128)S(1)} %get-tuple-element.87.refs_2_), channel_id=1, source_target_pairs={{0,1},{1,0},{2,3},{3,2},{4,5},{5,4},{6,7},{7,6},{8,9},{9,8},{10,11... | collective-permute-start | bytes 589832 | tf_op jit(solution)/shard_map/ppermute | solution.py:492
  165.9 15.9 %collective-permute-start.7 = (f32[4,5,8,512]{3,2,1,0:T(8,128)S(1)}, f32[4,5,8,512]{3,2,1,0:T(8,128)S(1)}, u32[]{:S(2)}, u32[]{:S(2)}) collective-permute-start(f32[4,5,8,512]{3,2,1,0:T(8,128)S(1)} %get-tuple-element.61), channel_id=1, source_target_pairs={{0,16},{8,24},{16,0},{24,8},{1,17},{9,25},{17,1},{25,9},{2,18},{10... | collective-permute-start | bytes 983048 | tf_op jit(solution)/shard_map/ppermute | solution.py:656
  166.5 22.6 %collective-permute-start.8 = (f32[4,5,8,512]{3,2,1,0:T(8,128)S(1)}, f32[4,5,8,512]{3,2,1,0:T(8,128)S(1)}, u32[]{:S(2)}, u32[]{:S(2)}) collective-permute-start(f32[4,5,8,512]{3,2,1,0:T(8,128)S(1)} %get-tuple-element.62), channel_id=1, source_target_pairs={{0,24},{8,16},{16,8},{24,0},{1,25},{9,17},{17,9},{25,1},{2,26},{10... | collective-permute-start | bytes 983048 | tf_op jit(solution)/shard_map/ppermute | solution.py:656
  191.5 0.7 copy-start.2
  192.2 50.1 %collective-permute-start.11 = (f32[4,5,8,512]{3,2,1,0:T(8,128)}, f32[4,5,8,512]{3,2,1,0:T(8,128)S(1)}, u32[]{:S(2)}, u32[]{:S(2)}) collective-permute-start(f32[4,5,8,512]{3,2,1,0:T(8,128)} %pad_maximum_fusion.5), channel_id=1, source_target_pairs={{0,2},{2,0},{4,6},{6,4},{1,3},{3,1},{5,7},{7,5},{8,10},{10,8},{12,... | collective-permute-start | bytes 983048 | tf_op jit(solution)/shard_map/ppermute | solution.py:656
  194.1 48.2 %collective-permute-start.12 = (f32[4,5,8,512]{3,2,1,0:T(8,128)}, f32[4,5,8,512]{3,2,1,0:T(8,128)S(1)}, u32[]{:S(2)}, u32[]{:S(2)}) collective-permute-start(f32[4,5,8,512]{3,2,1,0:T(8,128)} %pad_maximum_fusion.6), channel_id=1, source_target_pairs={{0,4},{2,6},{4,0},{6,2},{1,5},{3,7},{5,1},{7,3},{8,12},{10,14},{12... | collective-permute-start | bytes 983048 | tf_op jit(solution)/shard_map/ppermute | solution.py:656
  203.6 46.7 %collective-permute-start.13 = (f32[4,5,8,512]{3,2,1,0:T(8,128)}, f32[4,5,8,512]{3,2,1,0:T(8,128)S(1)}, u32[]{:S(2)}, u32[]{:S(2)}) collective-permute-start(f32[4,5,8,512]{3,2,1,0:T(8,128)} %pad_maximum_fusion.7), channel_id=1, source_target_pairs={{0,6},{2,4},{4,2},{6,0},{1,7},{3,5},{5,3},{7,1},{8,14},{10,12},{12... | collective-permute-start | bytes 983048 | tf_op jit(solution)/shard_map/ppermute | solution.py:656
  234.5 0.9 copy-start.5
  235.4 0.8 copy-start.10
  253.0 9.4 %collective-permute-start.14 = (f32[24,2048]{1,0:T(8,128)S(1)}, f32[24,2048]{1,0:T(8,128)S(1)}, u32[]{:S(2)}, u32[]{:S(2)}) collective-permute-start(f32[24,2048]{1,0:T(8,128)S(1)} %get-tuple-element.86.refs_0_), channel_id=1, source_target_pairs={{0,1},{1,0},{2,3},{3,2},{4,5},{5,4},{6,7},{7,6},{8,9},{9,8},{10,11... | collective-permute-start | bytes 589832 | tf_op jit(solution)/shard_map/ppermute | solution.py:492
  254.6 7.8 %copy-start.3 = (f32[24,2048]{1,0:T(8,128)S(1)}, f32[24,2048]{1,0:T(8,128)}, u32[]{:S(2)}) copy-start(f32[24,2048]{1,0:T(8,128)} %copy-done.2) | copy-start | bytes 589828
  254.6 7.8 %copy-start.8 = (bf16[352,96]{1,0:T(8,128)(2,1)S(1)}, bf16[352,96]{1,0:T(8,128)(2,1)}, u32[]{:S(2)}) copy-start(bf16[352,96]{1,0:T(8,128)(2,1)} %copy-done.7) | copy-start | bytes 202756

commit v3 on v2

--- a/solution.py
+++ b/solution.py
@@ -3,6 +3,7 @@
 
 import jax
 import jax.numpy as jnp
+import ml_dtypes
 import numpy as np
 from jax import lax
 from jax.experimental import pallas as pl
@@ -29,12 +30,18 @@
     cos_span, sin_span = turns(NB)
     scale = 1.0 / math.sqrt(NF * NB)
     out = (
-        np.block([[cos_time, -sin_time], [sin_time, cos_time]]),
-        np.concatenate([cos_span, -sin_span], 0) * scale,
-        np.concatenate([cos_span, -sin_span], 1) * scale,
-        np.block([[cos_time, sin_time], [-sin_time, cos_time]]),
+        (np.block([[cos_time, -sin_time], [sin_time, cos_time]]), 1),
+        (np.concatenate([cos_span, -sin_span], 0) * scale, 0),
+        (np.concatenate([cos_span, -sin_span], 1) * scale, 0),
+        (np.block([[cos_time, sin_time], [-sin_time, cos_time]]), 1),
     )
-    return [jnp.asarray(table.astype(np.float32)) for table in out]
+
+    def split(table, axis):
+        high = table.astype(ml_dtypes.bfloat16)
+        low = (table - high.astype(np.float64)).astype(ml_dtypes.bfloat16)
+        return jnp.asarray(np.concatenate([high, high, low], axis))
+
+    return [split(table, axis) for table, axis in out]
 
 
 def params(megabytes=16):
@@ -54,29 +61,35 @@
     return mask_ref[...].astype(jnp.float32).reshape(1, -1)
 
 
+def row_step(rows):
+    return rows // 2 if rows % 16 == 0 and rows > 16 else rows
+
+
 def prepare_body(x_ref, mask_ref, out_ref):
     keep = kept_modes(mask_ref)
-    rows, _, freqs, _ = out_ref.shape
-    for part in range(2):
-        kept = x_ref[part, 0] * keep
-        out_ref[:, 0, :, part * NB : (part + 1) * NB] = kept.reshape(rows, freqs, NB)
+    rows, variables, freqs, _ = out_ref.shape
+    for v in range(variables):
+        for part in range(2):
+            kept = x_ref[part, v] * keep
+            out_ref[:, v, :, part * NB : (part + 1) * NB] = kept.reshape(rows, freqs, NB)
 
 
 def prepare(amplitudes, keep, cut):
     _, variables, _, modes = amplitudes.shape
     freqs = modes // NB
     rows = cut.stop - cut.start
-    at = cut.start // rows
+    step = row_step(rows)
+    at = cut.start // step
     return pl.pallas_call(
         prepare_body,
-        grid=(variables,),
+        grid=(rows // step,),
         in_specs=[
-            pl.BlockSpec((2, 1, rows, modes), lambda v: (0, v, at, 0)),
-            pl.BlockSpec((modes,), lambda v: (0,)),
+            pl.BlockSpec((2, variables, step, modes), lambda r: (0, 0, at + r, 0)),
+            pl.BlockSpec((modes,), lambda r: (0,)),
         ],
-        out_specs=pl.BlockSpec((rows, 1, freqs, 2 * NB), lambda v: (0, v, 0, 0)),
+        out_specs=pl.BlockSpec((step, variables, freqs, 2 * NB), lambda r: (r, 0, 0, 0)),
         out_shape=pltpu.HBM((rows, variables, freqs, 2 * NB), jnp.float32),
-        compiler_params=params(),
+        compiler_params=params(24),
         name="prepare",
     )(in_hbm(amplitudes), in_hbm(keep))
 
@@ -119,19 +132,32 @@
     )(place, in_hbm(amplitudes), keep)
 
 
+def halves(value):
+    high = value.astype(jnp.bfloat16)
+    return high, (value - high.astype(jnp.float32)).astype(jnp.bfloat16)
+
+
+def table_times(table, value):
+    high, low = halves(value)
+    value = jnp.concatenate([high, low, high], axis=0)
+    return jnp.dot(table, value, preferred_element_type=jnp.float32)
+
+
+def times_table(value, table):
+    high, low = halves(value)
+    value = jnp.concatenate([high, low, high], axis=1)
+    return jnp.dot(value, table, preferred_element_type=jnp.float32)
+
+
 def transform(read, write, q_ref, table_refs, field_ref, force_ref):
     wi_ref, ei_ref, ef_ref, wf_ref = table_refs
     variables = field_ref.shape[0]
     for v in range(variables):
         modes = read(v)
         stacked = jnp.concatenate([modes[:, :NB], modes[:, NB:]], axis=0)
-        turned = jnp.dot(
-            wi_ref[...], stacked, precision=SPLIT, preferred_element_type=jnp.float32
-        )
+        turned = table_times(wi_ref[...], stacked)
         beside = jnp.concatenate([turned[:NF], turned[NF:]], axis=1)
-        field_ref[v] = jnp.dot(
-            beside, ei_ref[...], precision=SPLIT, preferred_element_type=jnp.float32
-        )
+        field_ref[v] = times_table(beside, ei_ref[...])
     pairs = [(a, b) for a in range(variables) for b in range(a + 1, variables)]
     weights = [
         [q_ref[w * variables + a, b] + q_ref[w * variables + b, a] for a, b in pairs]
@@ -150,13 +176,9 @@
         for w in range(variables):
             force_ref[w, at] = total[w]
     for w in range(variables):
-        spread = jnp.dot(
-            force_ref[w], ef_ref[...], precision=SPLIT, preferred_element_type=jnp.float32
-        )
+        spread = times_table(force_ref[w], ef_ref[...])
         stacked = jnp.concatenate([spread[:, :NB], spread[:, NB:]], axis=0)
-        turned = jnp.dot(
-            wf_ref[...], stacked, precision=SPLIT, preferred_element_type=jnp.float32
-        )
+        turned = table_times(wf_ref[...], stacked)
         for part in range(2):
             write(w, part, turned[part * NF : (part + 1) * NF])
 
@@ -310,32 +332,32 @@
 
 
 def absorb_rows(read, mask_ref, edge_ref, adj_ref, before_ref, out_ref, sum_ref):
+    _, variables, rows, lanes = out_ref.shape
     ends = edge_ref.shape[1]
-    rows = out_ref.shape[2]
     keep = kept_modes(mask_ref)
 
     @pl.when(pl.program_id(0) == 0)
     def _():
         sum_ref[...] = before_ref[...]
 
-    sides = []
+    for v in range(variables):
+        for part in range(2):
+            out_ref[part, v] = read(v, part).reshape(rows, lanes) * keep
+    sides = [out_ref[part].reshape(variables * rows, lanes) for part in range(2)]
     for part in range(2):
-        side = read(part).reshape(rows, -1) * keep
-        out_ref[part, 0] = side
         at = slice(part * ends, (part + 1) * ends)
         sum_ref[at] += jnp.dot(
-            edge_ref[0], side, precision=SPLIT, preferred_element_type=jnp.float32
+            edge_ref[0], sides[part], precision=SPLIT, preferred_element_type=jnp.float32
         )
-        sides.append(side)
-    real, imag = adj_ref[0, 0], adj_ref[1, 0]
+    real, imag = (adj_ref[part].reshape(variables * rows, lanes) for part in range(2))
     at = 2 * ends
-    sum_ref[at : at + 1] += jnp.sum(real * sides[0] + imag * sides[1], axis=0, keepdims=True)
-    sum_ref[at + 1 : at + 2] += jnp.sum(real * sides[1] - imag * sides[0], axis=0, keepdims=True)
+    sum_ref[at : at + 1] += total(real * sides[0] + imag * sides[1])
+    sum_ref[at + 1 : at + 2] += total(real * sides[1] - imag * sides[0])
 
 
 def absorb_body(in_ref, *refs):
-    def read(part):
-        return in_ref[:, 0, :, part * NB : (part + 1) * NB]
+    def read(v, part):
+        return in_ref[:, v, :, part * NB : (part + 1) * NB]
 
     absorb_rows(read, *refs)
 
@@ -344,10 +366,10 @@
     in_refs, refs, rows_ref = refs[:spans], refs[spans:-1], refs[-1]
     for i, in_ref in enumerate(in_refs):
         for j in range(in_ref.shape[0]):
-            rows_ref[partner(place_ref, j, i, spans)] = in_ref[j, 0]
-
-    def read(part):
-        return rows_ref[:, :, part * NB : (part + 1) * NB]
+            rows_ref[partner(place_ref, j, i, spans)] = in_ref[j]
+
+    def read(v, part):
+        return rows_ref[:, v, :, part * NB : (part + 1) * NB]
 
     absorb_rows(read, *refs)
 
@@ -356,27 +378,32 @@
     blocks = list(blocks)
     apart = place is not None
     _, variables, rows, modes = adjoint_modes.shape
-    ends = edges.shape[1]
-    grid_spec = pl.BlockSpec((2, 1, rows, modes), lambda v: (0, v, 0, 0))
-    sums = pl.BlockSpec((GATHERED_ROWS, modes), lambda v: (0, 0))
-    length, _, freqs, lanes = blocks[0].shape
-    in_specs = [pl.BlockSpec((length, 1, freqs, lanes), lambda v: (0, v, 0, 0))] * len(blocks)
-    in_specs += [
-        pl.BlockSpec((modes,), lambda v: (0,)),
-        pl.BlockSpec((1, ends, rows), lambda v: (v, 0, 0)),
+    steps, ends, width = edges.shape
+    step = rows // steps
+    grid_spec = pl.BlockSpec((2, variables, step, modes), lambda r: (0, 0, r, 0))
+    sums = pl.BlockSpec((GATHERED_ROWS, modes), lambda r: (0, 0))
+    _, _, freqs, lanes = blocks[0].shape
+    operands = blocks + [keep, edges, adjoint_modes if apart else in_hbm(adjoint_modes), before]
+    in_specs = [
+        whole(block)
+        if apart
+        else pl.BlockSpec((step, variables, freqs, lanes), lambda r: (r, 0, 0, 0))
+        for block in blocks
+    ] + [
+        pl.BlockSpec((modes,), lambda r: (0,)),
+        pl.BlockSpec((1, ends, width), lambda r: (r, 0, 0)),
         grid_spec,
         sums,
     ]
-    operands = blocks + [keep, edges, adjoint_modes if apart else in_hbm(adjoint_modes), before]
     body, scratch = absorb_body, []
     if apart:
         operands = [place] + operands
         in_specs = [pl.BlockSpec(memory_space=pltpu.SMEM)] + in_specs
         body = functools.partial(absorb_apart_body, len(blocks))
-        scratch = [pltpu.VMEM((rows, freqs, lanes), jnp.float32)]
+        scratch = [pltpu.VMEM((rows, variables, freqs, lanes), jnp.float32)]
     return pl.pallas_call(
         body,
-        grid=(variables,),
+        grid=(steps,),
         in_specs=in_specs,
         out_specs=[grid_spec, sums],
         out_shape=[
@@ -384,7 +411,7 @@
             jax.ShapeDtypeStruct((GATHERED_ROWS, modes), jnp.float32),
         ],
         scratch_shapes=scratch,
-        compiler_params=params(),
+        compiler_params=params(24),
         name="absorb_apart" if apart else "absorb",
     )(*operands)
 
@@ -398,30 +425,25 @@
         forced = forced[0] if groups == 1 else jnp.concatenate(forced, axis=1)
         side = forced + up_ref[part] * keep
         side = side.reshape(variables * heights, lanes)
-        high = side.astype(jnp.bfloat16)
-        low = (side - high.astype(jnp.float32)).astype(jnp.bfloat16)
-        moved = jnp.dot(
-            inverse_ref[...],
-            jnp.concatenate([high, low, high], axis=0),
-            preferred_element_type=jnp.float32,
-        )
+        moved = table_times(inverse_ref[...], side)
         out_ref[part] = moved.reshape(variables, heights, lanes)
 
 
 def solve(sides, upstream, keep, inverse):
     _, variables, heights, modes = upstream.shape
-    spec = pl.BlockSpec((2, variables, heights, NB), lambda i: (0, 0, 0, i))
+    lanes = min(2 * NB, modes)
+    spec = pl.BlockSpec((2, variables, heights, lanes), lambda i: (0, 0, 0, i))
     return pl.pallas_call(
         functools.partial(solve_body, len(sides)),
-        grid=(modes // NB,),
+        grid=(modes // lanes,),
         in_specs=[
-            pl.BlockSpec((2, variables, side.shape[2], NB), lambda i: (0, 0, 0, i))
+            pl.BlockSpec((2, variables, side.shape[2], lanes), lambda i: (0, 0, 0, i))
             for side in sides
         ]
-        + [spec, pl.BlockSpec((NB,), lambda i: (i,)), whole(inverse)],
+        + [spec, pl.BlockSpec((lanes,), lambda i: (i,)), whole(inverse)],
         out_specs=spec,
         out_shape=jax.ShapeDtypeStruct(upstream.shape, jnp.float32),
-        compiler_params=params(),
+        compiler_params=params(24),
         name="solve",
     )(*sides, in_hbm(upstream), keep, inverse)
 
@@ -440,13 +462,7 @@
         if spare:
             everywhere.append(jnp.zeros((spare, lanes), jnp.float32))
         everywhere = jnp.concatenate(everywhere, axis=0)
-        high = everywhere.astype(jnp.bfloat16)
-        low = (everywhere - high.astype(jnp.float32)).astype(jnp.bfloat16)
-        moved = jnp.dot(
-            chain_ref[...],
-            jnp.concatenate([high, low, high], axis=0),
-            preferred_element_type=jnp.float32,
-        )
+        moved = table_times(chain_ref[...], everywhere)
         pushed.append(moved[extent:])
         out_ref[part] = solved_ref[part] - moved[:extent].reshape(variables, heights, lanes)
     real = imag = weight = 0.0
@@ -538,10 +554,15 @@
             at = w * heights + point
             row = end * variables + w
             rows_ref[row : row + 1] = matrix[at : at + 1]
-            for v in range(variables):
-                part = matrix[at : at + 1, v * heights : (v + 1) * heights]
-                for cut, row_ref in zip(cuts, row_refs):
-                    row_ref[v, row : row + 1] = part[:, cut]
+    ends_rows = rows_ref[...]
+    for cut, row_ref in zip(cuts, row_refs):
+        step = row_step(cut.stop - cut.start)
+        for r in range(row_ref.shape[0]):
+            at = cut.start + r * step
+            pieces = [
+                ends_rows[:, v * heights + at : v * heights + at + step] for v in range(variables)
+            ]
+            row_ref[r] = jnp.concatenate(pieces, axis=1)
 
     def dot(a, b):
         return jnp.dot(a, b, precision=FULL, preferred_element_type=jnp.float32)
@@ -610,7 +631,10 @@
             jax.ShapeDtypeStruct((extent, 3 * extent), jnp.bfloat16),
             jax.ShapeDtypeStruct((ends, extent), f32),
         ]
-        + [jax.ShapeDtypeStruct((variables, ends, n), f32) for n in lengths]
+        + [
+            jax.ShapeDtypeStruct((n // row_step(n), ends, variables * row_step(n)), f32)
+            for n in lengths
+        ]
         + [jax.ShapeDtypeStruct((rows, 3 * size), jnp.bfloat16)],
         scratch_shapes=[
             pltpu.VMEM((walls,) + packed[0].shape, f32),

time: 267 us -> 262 us (0.981)
  Pallas kernels: 60.9 us -> 54.2 us
    pallas_call x3, Pallas kernels: 14.8 us -> 10.3 us  [the longest x2 6.34 us: absorb(): pl.pallas_call(body, grid=(steps,), in_specs=in_specs, out_specs=[grid_sp...]
    unnamed x39 -> x35, local copies, waits for them, and re-layouts: 8.1 us -> 6.7 us
  transfers between devices with their start and end apart: 17 -> 17, of which waited for: 10 -> 11; matrix products, arithmetic and copies ran while one was open for 2% -> 2% of each run, Pallas kernels for 18% -> 17%
where the time goes in v3:
time: 262 us; the launch traced here: 261 us
  waiting for transfers between devices  141 us (54%)
  starting transfers between devices  55.2 us (21%)
  Pallas kernels  54.2 us (21%)
  local copies, waits for them, and re-layouts  6.88 us (3%)
    ppermute x12, waiting for transfers between devices, swap(): lax.ppermute(block, axis, [(at, at ^ i) for at in range(count)])  108 us
    ppermute x12, starting transfers between devices, swap(): lax.ppermute(block, axis, [(at, at ^ i) for at in range(count)])  37.2 us
    all_to_all x2, waiting for transfers between devices, exchange(): return lax.all_to_all(block, axes, split_axis=0, concat_axis=0, tiled=True)  30.1 us
    all_to_all x2, starting transfers between devices, exchange(): return lax.all_to_all(block, axes, split_axis=0, concat_axis=0, tiled=True)  13.4 us
    pallas_call x1, Pallas kernels, nonlinear(): pl.pallas_call(nonlinear_body, grid=(points,), in_specs=[pl.BlockSpec(mem...  12 us
    pallas_call x1, Pallas kernels, base(): pl.pallas_call(functools.partial(base_body, cuts), grid=(modes // NB,), i...  11.2 us
    unnamed x35, local copies, waits for them, and re-layouts  6.7 us
    pallas_call x2, Pallas kernels, absorb(): pl.pallas_call(body, grid=(steps,), in_specs=in_specs, out_specs=[grid_sp...  6.34 us
  transfers between devices with their start and end apart: 17, of which 11 were waited for; matrix products, arithmetic and copies ran while one was open for 2% of the time, Pallas kernels for 17%

profile of v3, /device:TPU:10, one launch (start us, length us, event | category | flops | bytes accessed | tf_op | source)
XLA Modules:
  0.0 260.9 jit_solution(7020840784899303186)
XLA Ops:
  0.6 3.9 %prepare.1 = f32[48,5,8,512]{3,2,1,0:T(8,128)} custom-call(f32[2,5,64,2048]{3,2,1,0:T(8,128)} %x_ref.3, s32[2048]{0:T(1024)} %refs_3_.3), custom_call_target="tpu_custom_call" | custom-call | tf_op jit(solution)/shard_map/prepare/pallas_call | solution.py:83
  4.5 6.4 %all-to-all-start = ((f32[48,5,8,512]{3,2,1,0:T(8,128)}), f32[48,5,8,512]{3,2,1,0:T(8,128)}, u32[]{:S(2)}, u32[]{:S(2)}) async-start(f32[48,5,8,512]{3,2,1,0:T(8,128)} %prepare.1), calls=%async_computation | async-start | bytes 7864320 | tf_op jit(solution)/shard_map/all_to_all | solution.py:675
  10.9 0.1 pad_add_fusion.place_ref
  11.0 3.3 %prepare_apart.1 = (f32[4,5,8,512]{3,2,1,0:T(8,128)S(1)}, f32[4,5,8,512]{3,2,1,0:T(8,128)S(1)}, f32[4,5,8,512]{3,2,1,0:T(8,128)S(1)}, f32[4,5,8,512]{3,2,1,0:T(8,128)S(1)}) custom-call(s32[2]{0:T(128)S(1)} %pad_add_fusion.place_ref, f32[2,5,64,2048]{3,2,1,0:T(8,128)} %x_ref.3, s32[2048]{0:T(1024)S(1)} %copy-done.1), custom_call_target="tpu_custom_call" | custom-call | tf_op jit(solution)/shard_map/prepare_apart/pallas_call | solution.py:119
  14.3 0.2 collective-permute-start
  14.5 0.6 collective-permute-start.1
  15.1 1.1 collective-permute-start.2
  16.2 0.0 collective-permute-done
  16.3 22.3 %collective-permute-done.1 = f32[4,5,8,512]{3,2,1,0:T(8,128)S(1)} collective-permute-done((f32[4,5,8,512]{3,2,1,0:T(8,128)S(1)}, f32[4,5,8,512]{3,2,1,0:T(8,128)S(1)}, u32[]{:S(2)}, u32[]{:S(2)}) %collective-permute-start.1) | collective-permute-done | bytes 327712 | tf_op jit(solution)/shard_map/ppermute | solution.py:680
  38.6 8.7 %collective-permute-done.2 = f32[4,5,8,512]{3,2,1,0:T(8,128)S(1)} collective-permute-done((f32[4,5,8,512]{3,2,1,0:T(8,128)S(1)}, f32[4,5,8,512]{3,2,1,0:T(8,128)S(1)}, u32[]{:S(2)}, u32[]{:S(2)}) %collective-permute-start.2) | collective-permute-done | bytes 327712 | tf_op jit(solution)/shard_map/ppermute | solution.py:680
  47.4 19.1 %collective-permute-start.3 = (f32[4,5,8,512]{3,2,1,0:T(8,128)S(1)}, f32[4,5,8,512]{3,2,1,0:T(8,128)S(1)}, u32[]{:S(2)}, u32[]{:S(2)}) collective-permute-start(f32[4,5,8,512]{3,2,1,0:T(8,128)S(1)} %pad_maximum_fusion.1), channel_id=1, source_target_pairs={{0,2},{2,0},{4,6},{6,4},{1,3},{3,1},{5,7},{7,5},{8,10},{10,8},{12,... | collective-permute-start | bytes 983048 | tf_op jit(solution)/shard_map/ppermute | solution.py:680
  66.5 2.5 collective-permute-start.4
  69.1 14.5 %collective-permute-done.3.refs_1_ = f32[4,5,8,512]{3,2,1,0:T(8,128)S(1)} collective-permute-done((f32[4,5,8,512]{3,2,1,0:T(8,128)S(1)}, f32[4,5,8,512]{3,2,1,0:T(8,128)S(1)}, u32[]{:S(2)}, u32[]{:S(2)}) %collective-permute-start.3) | collective-permute-done | bytes 327712 | tf_op jit(solution)/shard_map/ppermute | solution.py:680
  83.6 28.3 %collective-permute-done.4.refs_3_ = f32[4,5,8,512]{3,2,1,0:T(8,128)S(1)} collective-permute-done((f32[4,5,8,512]{3,2,1,0:T(8,128)S(1)}, f32[4,5,8,512]{3,2,1,0:T(8,128)S(1)}, u32[]{:S(2)}, u32[]{:S(2)}) %collective-permute-start.4) | collective-permute-done | bytes 327712 | tf_op jit(solution)/shard_map/ppermute | solution.py:680
  111.9 0.0 all-to-all-done
  111.9 0.0 collective-permute-start.5
  111.9 12.0 %nonlinear.1 = f32[16,3,5,8,512]{4,3,2,1,0:T(8,128)} custom-call(f32[25,5]{1,0:T(8,128)S(1)} %reshape.20.q_ref, f32[16,3,5,8,512]{4,3,2,1,0:T(8,128)} %bitcast.2.in_ref, bf16[256,768]{1,0:T(8,128)(2,1)} %constant.19.clone.refs_0_.refs_4_, bf16[1536,256]{1,0:T(8,128)(2,1)} %constant.20.clone.refs_1_.refs_5_, bf16[768,512]{1,0:T(8,128)(2,1)} %constant.21.clone.refs_2_.refs_6_, ...), custom_call_target="tpu_custom_call" | custom-call | flops 4529848320 | bytes 7864320 | tf_op jit(solution)/shard_map/nonlinear/pallas_call | solution.py:215
  123.9 2.1 collective-permute-done.5.refs_2_
  126.0 7.1 %all-to-all-start.1 = ((f32[48,5,8,512]{3,2,1,0:T(8,128)}), f32[48,5,8,512]{3,2,1,0:T(8,128)}, u32[]{:S(2)}, u32[]{:S(2)}) async-start(f32[48,5,8,512]{3,2,1,0:T(8,128)} %bitcast.7), calls=%async_computation.1 | async-start | bytes 7864320 | tf_op jit(solution)/shard_map/all_to_all | solution.py:675
  133.1 0.0 copy-start.14
  133.1 0.0 copy-start.10
  133.1 0.0 copy-start.11
  133.1 0.0 copy-start.12
  133.1 0.0 copy-start
  133.2 5.5 %nonlinear_apart.1 = (f32[4,5,8,512]{3,2,1,0:T(8,128)S(1)}, f32[4,5,8,512]{3,2,1,0:T(8,128)}, f32[4,5,8,512]{3,2,1,0:T(8,128)S(1)}, f32[4,5,8,512]{3,2,1,0:T(8,128)S(1)}) custom-call(s32[2]{0:T(128)S(1)} %pad_add_fusion.place_ref, f32[25,5]{1,0:T(8,128)S(1)} %reshape.20.q_ref, f32[4,5,8,512]{3,2,1,0:T(8,128)S(1)} %get-tuple-element.55.refs_0_, ...), custom_call_target="tpu_custom_call" | custom-call | flops 1509949440 | bytes 2621440 | tf_op jit(solution)/shard_map/nonlinear_apart/pallas_call | solution.py:256
  138.7 0.2 collective-permute-start.6
  138.8 0.6 copy.19.refs_0_
  139.4 0.6 copy.20.refs_1_
  140.0 0.6 copy.21.refs_2_
  140.6 0.6 copy.22.refs_3_
  141.2 0.6 copy.23.refs_4_
  141.8 1.4 pack.1.refs_0_
  143.2 1.5 collective-permute-start.9
  144.7 2.7 %collective-permute-done.9.refs_1_ = f32[5,16,128]{2,1,0:T(8,128)S(1)} collective-permute-done((f32[5,16,128]{2,1,0:T(8,128)}, f32[5,16,128]{2,1,0:T(8,128)S(1)}, u32[]{:S(2)}, u32[]{:S(2)}) %collective-permute-start.9) | collective-permute-done | bytes 40992 | tf_op jit(solution)/shard_map/ppermute | solution.py:508
  147.4 0.8 copy-done.6
  148.2 1.1 constants.1
  149.3 0.6 copy-done.7
  149.9 11.2 %base.1 = (f32[2,5,48,2048]{3,2,1,0:T(8,128)}, f32[2,5,16,2048]{3,2,1,0:T(8,128)S(1)}, f32[24,2048]{1,0:T(8,128)S(1)}, f32[24,2048]{1,0:T(8,128)S(1)}) custom-call(f32[2,5,64,2048]{3,2,1,0:T(8,128)} %x_ref.3, f32[2,5,64,2048]{3,2,1,0:T(8,128)} %refs_2_.3, s32[2048]{0:T(1024)S(1)} %copy-done.1, f32[10,320]{1,0:T(8,128)S(1)} %get-tuple-element.67.edge_rows_ref, ...), custom_call_target="tpu_custom_call" | custom-call | tf_op jit(solution)/shard_map/base/pallas_call | solution.py:317
  161.1 0.7 copy-done.4
  161.8 1.5 collective-permute-start.10
  163.3 0.5 collective-permute-start.7
  163.8 0.2 collective-permute-start.8
  164.0 0.0 collective-permute-done.6
  164.1 15.1 %collective-permute-done.7 = f32[4,5,8,512]{3,2,1,0:T(8,128)S(1)} collective-permute-done((f32[4,5,8,512]{3,2,1,0:T(8,128)S(1)}, f32[4,5,8,512]{3,2,1,0:T(8,128)S(1)}, u32[]{:S(2)}, u32[]{:S(2)}) %collective-permute-start.7) | collective-permute-done | bytes 327712 | tf_op jit(solution)/shard_map/ppermute | solution.py:680
  179.2 7.3 %collective-permute-done.8 = f32[4,5,8,512]{3,2,1,0:T(8,128)S(1)} collective-permute-done((f32[4,5,8,512]{3,2,1,0:T(8,128)S(1)}, f32[4,5,8,512]{3,2,1,0:T(8,128)S(1)}, u32[]{:S(2)}, u32[]{:S(2)}) %collective-permute-start.8) | collective-permute-done | bytes 327712 | tf_op jit(solution)/shard_map/ppermute | solution.py:680
  186.6 0.8 pad_maximum_fusion.7
  187.3 0.8 pad_maximum_fusion.6
  188.1 0.8 pad_maximum_fusion.5
  188.9 0.0 collective-permute-done.10.refs_3_
  188.9 0.7 copy-done.2
  189.6 2.4 collective-permute-start.11
  191.9 9.8 %collective-permute-start.12 = (f32[4,5,8,512]{3,2,1,0:T(8,128)}, f32[4,5,8,512]{3,2,1,0:T(8,128)S(1)}, u32[]{:S(2)}, u32[]{:S(2)}) collective-permute-start(f32[4,5,8,512]{3,2,1,0:T(8,128)} %pad_maximum_fusion.6), channel_id=1, source_target_pairs={{0,4},{2,6},{4,0},{6,2},{1,5},{3,7},{5,1},{7,3},{8,12},{10,14},{12... | collective-permute-start | bytes 983048 | tf_op jit(solution)/shard_map/ppermute | solution.py:680
  201.8 0.6 collective-permute-start.13
  202.3 30.1 %all-to-all-done.1.in_ref = f32[48,5,8,512]{3,2,1,0:T(8,128)} async-done(((f32[48,5,8,512]{3,2,1,0:T(8,128)}), f32[48,5,8,512]{3,2,1,0:T(8,128)}, u32[]{:S(2)}, u32[]{:S(2)}) %all-to-all-start.1) | async-done | bytes 3932192 | tf_op jit(solution)/shard_map/all_to_all | solution.py:675
  232.4 0.9 copy-done.5
  233.3 4.8 %absorb.1 = (f32[2,5,48,2048]{3,2,1,0:T(8,128)S(1)}, f32[24,2048]{1,0:T(8,128)S(1)}) custom-call(f32[48,5,8,512]{3,2,1,0:T(8,128)} %all-to-all-done.1.in_ref, s32[2048]{0:T(1024)S(1)} %copy-done.1, f32[2,10,120]{2,1,0:T(8,128)S(1)} %get-tuple-element.73.refs_1_, f32[2,5,48,2048]{3,2,1,0:T(8,128)} %get-tuple-element.74.refs_2_, f32[24,2048]{1,0:T(8,128)S(1)} %copy-done.5), custom_call_target="tpu_custom_call" | custom-call | tf_op jit(solution)/shard_map/absorb/pallas_call | solution.py:404
  238.1 0.0 collective-permute-done.11.refs_1_
  238.1 1.3 collective-permute-done.12.refs_2_
  239.4 8.8 %collective-permute-done.13.refs_3_ = f32[4,5,8,512]{3,2,1,0:T(8,128)S(1)} collective-permute-done((f32[4,5,8,512]{3,2,1,0:T(8,128)}, f32[4,5,8,512]{3,2,1,0:T(8,128)S(1)}, u32[]{:S(2)}, u32[]{:S(2)}) %collective-permute-start.13) | collective-permute-done | bytes 327712 | tf_op jit(solution)/shard_map/ppermute | solution.py:680
  248.2 1.6 absorb_apart.1
  249.7 1.5 collective-permute-start.14
  251.3 6.0 %solve.1.solved_ref = f32[2,5,64,2048]{3,2,1,0:T(8,128)S(1)} custom-call(f32[2,5,48,2048]{3,2,1,0:T(8,128)S(1)} %get-tuple-element.76.refs_0_, f32[2,5,16,2048]{3,2,1,0:T(8,128)S(1)} %get-tuple-element.84.refs_1_, f32[2,5,64,2048]{3,2,1,0:T(8,128)} %refs_2_.3, s32[2048]{0:T(1024)S(1)} %copy-done.1, bf16[320,960]{1,0:T(8,128)(2,1)S(1)} %get-tuple-element.85.refs_4_), custom_call_target="tpu_custom_call" | custom-call | tf_op jit(solution)/shard_map/solve/pallas_call | solution.py:436
  257.3 0.0 collective-permute-done.14.refs_1_
  257.3 3.6 %finish.1 = (f32[2,5,64,2048]{3,2,1,0:T(8,128)}, f32[2,2048]{1,0:T(2,128)}) custom-call(f32[2,5,64,2048]{3,2,1,0:T(8,128)S(1)} %solve.1.solved_ref, f32[24,2048]{1,0:T(8,128)S(1)} %get-tuple-element.86.refs_0_, f32[24,2048]{1,0:T(8,128)S(1)} %collective-permute-done.14.refs_1_, f32[24,2048]{1,0:T(8,128)S(1)} %get-tuple-element.87.refs_2_, ...), custom_call_target="tpu_custom_call" | custom-call | tf_op jit(solution)/shard_map/finish/pallas_call | solution.py:491
  (33 shorter events, 0.3 us)
Async XLA Ops:
  4.5 6.5 %copy-start.1 = (s32[2048]{0:T(1024)S(1)}, s32[2048]{0:T(1024)}, u32[]{:S(2)}) copy-start(s32[2048]{0:T(1024)} %refs_3_.3) | copy-start | bytes 24580
  4.5 107.4 %all-to-all-start = ((f32[48,5,8,512]{3,2,1,0:T(8,128)}), f32[48,5,8,512]{3,2,1,0:T(8,128)}, u32[]{:S(2)}, u32[]{:S(2)}) async-start(f32[48,5,8,512]{3,2,1,0:T(8,128)} %prepare.1), calls=%async_computation | async-start | bytes 7864320 | tf_op jit(solution)/shard_map/all_to_all | solution.py:675
  11.0 58.1 %copy-start.9 = (f32[5,5,5]{2,1,0:T(8,128)S(1)}, f32[5,5,5]{2,1,0:T(8,128)}, u32[]{:S(2)}) copy-start(f32[5,5,5]{2,1,0:T(8,128)} %param.17) | copy-start | bytes 1504
  14.3 2.0 collective-permute-start
  14.5 24.1 %collective-permute-start.1 = (f32[4,5,8,512]{3,2,1,0:T(8,128)S(1)}, f32[4,5,8,512]{3,2,1,0:T(8,128)S(1)}, u32[]{:S(2)}, u32[]{:S(2)}) collective-permute-start(f32[4,5,8,512]{3,2,1,0:T(8,128)S(1)} %get-tuple-element.50), channel_id=1, source_target_pairs={{0,16},{8,24},{16,0},{24,8},{1,17},{9,25},{17,1},{25,9},{2,18},{10... | collective-permute-start | bytes 983048 | tf_op jit(solution)/shard_map/ppermute | solution.py:680
  15.1 32.3 %collective-permute-start.2 = (f32[4,5,8,512]{3,2,1,0:T(8,128)S(1)}, f32[4,5,8,512]{3,2,1,0:T(8,128)S(1)}, u32[]{:S(2)}, u32[]{:S(2)}) collective-permute-start(f32[4,5,8,512]{3,2,1,0:T(8,128)S(1)} %get-tuple-element.51), channel_id=1, source_target_pairs={{0,24},{8,16},{16,8},{24,0},{1,25},{9,17},{17,9},{25,1},{2,26},{10... | collective-permute-start | bytes 983048 | tf_op jit(solution)/shard_map/ppermute | solution.py:680
  47.4 36.2 %collective-permute-start.3 = (f32[4,5,8,512]{3,2,1,0:T(8,128)S(1)}, f32[4,5,8,512]{3,2,1,0:T(8,128)S(1)}, u32[]{:S(2)}, u32[]{:S(2)}) collective-permute-start(f32[4,5,8,512]{3,2,1,0:T(8,128)S(1)} %pad_maximum_fusion.1), channel_id=1, source_target_pairs={{0,2},{2,0},{4,6},{6,4},{1,3},{3,1},{5,7},{7,5},{8,10},{10,8},{12,... | collective-permute-start | bytes 983048 | tf_op jit(solution)/shard_map/ppermute | solution.py:680
  66.5 45.4 %collective-permute-start.4 = (f32[4,5,8,512]{3,2,1,0:T(8,128)S(1)}, f32[4,5,8,512]{3,2,1,0:T(8,128)S(1)}, u32[]{:S(2)}, u32[]{:S(2)}) collective-permute-start(f32[4,5,8,512]{3,2,1,0:T(8,128)S(1)} %pad_maximum_fusion.3), channel_id=1, source_target_pairs={{0,6},{2,4},{4,2},{6,0},{1,7},{3,5},{5,3},{7,1},{8,14},{10,12},{12... | collective-permute-start | bytes 983048 | tf_op jit(solution)/shard_map/ppermute | solution.py:680
  111.9 14.1 %collective-permute-start.5 = (f32[4,5,8,512]{3,2,1,0:T(8,128)S(1)}, f32[4,5,8,512]{3,2,1,0:T(8,128)S(1)}, u32[]{:S(2)}, u32[]{:S(2)}) collective-permute-start(f32[4,5,8,512]{3,2,1,0:T(8,128)S(1)} %get-tuple-element.53), channel_id=1, source_target_pairs={{0,4},{2,6},{4,0},{6,2},{1,5},{3,7},{5,1},{7,3},{8,12},{10,14},{12... | collective-permute-start | bytes 983048 | tf_op jit(solution)/shard_map/ppermute | solution.py:680
  126.0 106.4 %all-to-all-start.1 = ((f32[48,5,8,512]{3,2,1,0:T(8,128)}), f32[48,5,8,512]{3,2,1,0:T(8,128)}, u32[]{:S(2)}, u32[]{:S(2)}) async-start(f32[48,5,8,512]{3,2,1,0:T(8,128)} %bitcast.7), calls=%async_computation.1 | async-start | bytes 7864320 | tf_op jit(solution)/shard_map/all_to_all | solution.py:675
  133.1 5.7 %copy-start.13 = (f32[1,5,5]{2,0,1:T(1,128)S(1)}, f32[1,5,5]{2,0,1:T(1,128)}, u32[]{:S(2)}) copy-start(f32[1,5,5]{2,0,1:T(1,128)} %param.19) | copy-start | bytes 304
  133.1 6.3 %copy-start.14 = (f32[1,5,5]{2,0,1:T(1,128)S(1)}, f32[1,5,5]{2,0,1:T(1,128)}, u32[]{:S(2)}) copy-start(f32[1,5,5]{2,0,1:T(1,128)} %param.20) | copy-start | bytes 304
  133.1 6.9 %copy-start.10 = (f32[1,10,10]{2,0,1:T(1,128)S(1)}, f32[1,10,10]{2,0,1:T(1,128)}, u32[]{:S(2)}) copy-start(f32[1,10,10]{2,0,1:T(1,128)} %param.21) | copy-start | bytes 1204
  133.1 7.5 %copy-start.11 = (f32[1,10,10]{2,0,1:T(1,128)S(1)}, f32[1,10,10]{2,0,1:T(1,128)}, u32[]{:S(2)}) copy-start(f32[1,10,10]{2,0,1:T(1,128)} %param.22) | copy-start | bytes 1204
  133.1 8.1 %copy-start.12 = (f32[1,10,10]{2,0,1:T(1,128)S(1)}, f32[1,10,10]{2,0,1:T(1,128)}, u32[]{:S(2)}) copy-start(f32[1,10,10]{2,0,1:T(1,128)} %param.23) | copy-start | bytes 1204
  133.1 14.2 %copy-start = (f32[1,320,320]{2,1,0:T(8,128)S(1)}, f32[1,320,320]{2,1,0:T(8,128)}, u32[]{:S(2)}) copy-start(f32[1,320,320]{2,1,0:T(8,128)} %param.18) | copy-start | bytes 1228804
  138.7 25.4 %collective-permute-start.6 = (f32[4,5,8,512]{3,2,1,0:T(8,128)}, f32[4,5,8,512]{3,2,1,0:T(8,128)S(1)}, u32[]{:S(2)}, u32[]{:S(2)}) collective-permute-start(f32[4,5,8,512]{3,2,1,0:T(8,128)} %get-tuple-element.60), channel_id=1, source_target_pairs={{0,8},{8,0},{16,24},{24,16},{1,9},{9,1},{17,25},{25,17},{2,10},{10... | collective-permute-start | bytes 983048 | tf_op jit(solution)/shard_map/ppermute | solution.py:680
  143.2 4.2 %collective-permute-start.9 = (f32[5,16,128]{2,1,0:T(8,128)}, f32[5,16,128]{2,1,0:T(8,128)S(1)}, u32[]{:S(2)}, u32[]{:S(2)}) collective-permute-start(f32[5,16,128]{2,1,0:T(8,128)} %pack.1.refs_0_), channel_id=1, source_target_pairs={{0,1},{1,0},{2,3},{3,2},{4,5},{5,4},{6,7},{7,6},{8,9},{9,8},{10,11... | collective-permute-start | bytes 122888 | tf_op jit(solution)/shard_map/ppermute | solution.py:508
  147.4 0.8 copy-start.6
  149.3 0.6 copy-start.7
  161.1 0.7 copy-start.4
  161.8 27.1 %collective-permute-start.10 = (f32[24,2048]{1,0:T(8,128)S(1)}, f32[24,2048]{1,0:T(8,128)S(1)}, u32[]{:S(2)}, u32[]{:S(2)}) collective-permute-start(f32[24,2048]{1,0:T(8,128)S(1)} %get-tuple-element.87.refs_2_), channel_id=1, source_target_pairs={{0,1},{1,0},{2,3},{3,2},{4,5},{5,4},{6,7},{7,6},{8,9},{9,8},{10,11... | collective-permute-start | bytes 589832 | tf_op jit(solution)/shard_map/ppermute | solution.py:508
  163.3 15.9 %collective-permute-start.7 = (f32[4,5,8,512]{3,2,1,0:T(8,128)S(1)}, f32[4,5,8,512]{3,2,1,0:T(8,128)S(1)}, u32[]{:S(2)}, u32[]{:S(2)}) collective-permute-start(f32[4,5,8,512]{3,2,1,0:T(8,128)S(1)} %get-tuple-element.61), channel_id=1, source_target_pairs={{0,16},{8,24},{16,0},{24,8},{1,17},{9,25},{17,1},{25,9},{2,18},{10... | collective-permute-start | bytes 983048 | tf_op jit(solution)/shard_map/ppermute | solution.py:680
  163.8 22.7 %collective-permute-start.8 = (f32[4,5,8,512]{3,2,1,0:T(8,128)S(1)}, f32[4,5,8,512]{3,2,1,0:T(8,128)S(1)}, u32[]{:S(2)}, u32[]{:S(2)}) collective-permute-start(f32[4,5,8,512]{3,2,1,0:T(8,128)S(1)} %get-tuple-element.62), channel_id=1, source_target_pairs={{0,24},{8,16},{16,8},{24,0},{1,25},{9,17},{17,9},{25,1},{2,26},{10... | collective-permute-start | bytes 983048 | tf_op jit(solution)/shard_map/ppermute | solution.py:680
  188.9 0.7 copy-start.2
  189.6 48.5 %collective-permute-start.11 = (f32[4,5,8,512]{3,2,1,0:T(8,128)}, f32[4,5,8,512]{3,2,1,0:T(8,128)S(1)}, u32[]{:S(2)}, u32[]{:S(2)}) collective-permute-start(f32[4,5,8,512]{3,2,1,0:T(8,128)} %pad_maximum_fusion.5), channel_id=1, source_target_pairs={{0,2},{2,0},{4,6},{6,4},{1,3},{3,1},{5,7},{7,5},{8,10},{10,8},{12,... | collective-permute-start | bytes 983048 | tf_op jit(solution)/shard_map/ppermute | solution.py:680
  191.9 47.5 %collective-permute-start.12 = (f32[4,5,8,512]{3,2,1,0:T(8,128)}, f32[4,5,8,512]{3,2,1,0:T(8,128)S(1)}, u32[]{:S(2)}, u32[]{:S(2)}) collective-permute-start(f32[4,5,8,512]{3,2,1,0:T(8,128)} %pad_maximum_fusion.6), channel_id=1, source_target_pairs={{0,4},{2,6},{4,0},{6,2},{1,5},{3,7},{5,1},{7,3},{8,12},{10,14},{12... | collective-permute-start | bytes 983048 | tf_op jit(solution)/shard_map/ppermute | solution.py:680
  201.8 46.4 %collective-permute-start.13 = (f32[4,5,8,512]{3,2,1,0:T(8,128)}, f32[4,5,8,512]{3,2,1,0:T(8,128)S(1)}, u32[]{:S(2)}, u32[]{:S(2)}) collective-permute-start(f32[4,5,8,512]{3,2,1,0:T(8,128)} %pad_maximum_fusion.7), channel_id=1, source_target_pairs={{0,6},{2,4},{4,2},{6,0},{1,7},{3,5},{5,3},{7,1},{8,14},{10,12},{12... | collective-permute-start | bytes 983048 | tf_op jit(solution)/shard_map/ppermute | solution.py:680
  232.4 0.9 copy-start.5
  249.7 7.5 %collective-permute-start.14 = (f32[24,2048]{1,0:T(8,128)S(1)}, f32[24,2048]{1,0:T(8,128)S(1)}, u32[]{:S(2)}, u32[]{:S(2)}) collective-permute-start(f32[24,2048]{1,0:T(8,128)S(1)} %get-tuple-element.86.refs_0_), channel_id=1, source_target_pairs={{0,1},{1,0},{2,3},{3,2},{4,5},{5,4},{6,7},{7,6},{8,9},{9,8},{10,11... | collective-permute-start | bytes 589832 | tf_op jit(solution)/shard_map/ppermute | solution.py:508
  251.2 6.0 %copy-start.3 = (f32[24,2048]{1,0:T(8,128)S(1)}, f32[24,2048]{1,0:T(8,128)}, u32[]{:S(2)}) copy-start(f32[24,2048]{1,0:T(8,128)} %copy-done.2) | copy-start | bytes 589828
  251.3 6.0 %copy-start.8 = (bf16[352,96]{1,0:T(8,128)(2,1)S(1)}, bf16[352,96]{1,0:T(8,128)(2,1)}, u32[]{:S(2)}) copy-start(bf16[352,96]{1,0:T(8,128)(2,1)} %copy-done.7) | copy-start | bytes 202756

commit v4 on v3

--- a/solution.py
+++ b/solution.py
@@ -17,7 +17,6 @@
 
 SPLIT = lax.Precision.HIGH
 FULL = lax.Precision.HIGHEST
-GATHERED_ROWS = 24
 
 
 def tables():
@@ -269,71 +268,106 @@
     )(place, coefficients, *blocks, *[in_hbm(table) for table in transforms])
 
 
-def base_body(cuts, x_ref, up_ref, mask_ref, edge_rows_ref, turned_ref, *refs):
-    out_refs, (edge_ref, sum_ref) = refs[: len(cuts)], refs[len(cuts) :]
+def total(value):
+    return jnp.sum(value, axis=0, keepdims=True)
+
+
+def padded(rows, multiple):
+    return rows + -rows % multiple
+
+
+def edge_body(width, x_ref, mask_ref, rows_ref, out_ref):
+    _, variables, heights, lanes = x_ref.shape
+    keep = kept_modes(mask_ref)
+    squares = 0.0
+    out_ref[...] = jnp.zeros(out_ref.shape, jnp.float32)
+    for part in range(2):
+        kept = x_ref[part].reshape(variables * heights, lanes) * keep
+        squares = squares + total(kept * kept)
+        out_ref[part * width : (part + 1) * width] = table_times(rows_ref[...], kept)[:width]
+    out_ref[2 * width : 2 * width + 1] = squares
+
+
+def edge(amplitudes, keep, rows, width):
+    _, variables, heights, modes = amplitudes.shape
+    length = padded(2 * width + 1, 8)
+    return pl.pallas_call(
+        functools.partial(edge_body, width),
+        grid=(modes // NB,),
+        in_specs=[
+            pl.BlockSpec((2, variables, heights, NB), lambda i: (0, 0, 0, i)),
+            pl.BlockSpec((NB,), lambda i: (i,)),
+            whole(rows),
+        ],
+        out_specs=pl.BlockSpec((length, NB), lambda i: (0, i)),
+        out_shape=jax.ShapeDtypeStruct((length, modes), jnp.float32),
+        compiler_params=params(),
+        name="edge",
+    )(in_hbm(amplitudes), keep, rows)
+
+
+def base_body(cuts, walls, width, x_ref, up_ref, mask_ref, turned_ref, ahead_ref, back_ref, *refs):
+    edges, refs = refs[:walls], refs[walls:]
+    out_refs, (sum_ref, square_ref) = refs[: len(cuts)], refs[len(cuts) :]
     _, variables, heights, lanes = x_ref.shape
     extent = variables * heights
-    ends = 2 * variables
+    pushes = walls * width
+    spare = back_ref.shape[1] // 3 - pushes
     keep = kept_modes(mask_ref)
-    squares, moved, sides = 0.0, [], []
+    moved, sides = [], []
+    sum_ref[...] = jnp.zeros(sum_ref.shape, jnp.float32)
     for part in range(2):
         kept = x_ref[part].reshape(extent, lanes) * keep
-        squares = squares + total(kept * kept)
-        moved.append(
-            jnp.dot(turned_ref[...], kept, precision=SPLIT, preferred_element_type=jnp.float32)
-        )
+        taken = [ref[part * width : (part + 1) * width] for ref in edges]
+        if spare:
+            taken.append(jnp.zeros((spare, lanes), jnp.float32))
+        taken = jnp.concatenate(taken, axis=0)
+        moved.append(table_times(turned_ref[...], kept) - table_times(back_ref[...], taken))
         grid = moved[part].reshape(variables, heights, lanes)
         for cut, out_ref in zip(cuts, out_refs):
             out_ref[part] = grid[:, cut]
         sides.append(up_ref[part].reshape(extent, lanes) * keep)
-        sum_ref[part * ends : (part + 1) * ends] = jnp.dot(
-            edge_rows_ref[...], sides[part], precision=SPLIT, preferred_element_type=jnp.float32
-        )
-        for end, point in enumerate((0, heights - 1)):
-            for v in range(variables):
-                row = part * ends + end * variables + v
-                at = v * heights + point
-                edge_ref[row : row + 1] = moved[part][at : at + 1]
-    row = 2 * ends
-    none = jnp.zeros((GATHERED_ROWS - row - 1, lanes), jnp.float32)
-    edge_ref[row : row + 1] = squares
-    edge_ref[row + 1 :] = none
+        added = table_times(ahead_ref[...], sides[part])
+        sum_ref[part * pushes : (part + 1) * pushes] = added[:pushes]
+    row = 2 * pushes
     sum_ref[row : row + 1] = total(moved[0] * sides[0] + moved[1] * sides[1])
     sum_ref[row + 1 : row + 2] = total(moved[0] * sides[1] - moved[1] * sides[0])
-    sum_ref[row + 2 :] = none[1:]
-
-
-def total(value):
-    return jnp.sum(value, axis=0, keepdims=True)
-
-
-def base(amplitudes, upstream, keep, edge_rows, turned, cuts):
+    squares = sum(ref[2 * width : 2 * width + 1] for ref in edges)
+    square_ref[...] = jnp.broadcast_to(squares, square_ref.shape)
+
+
+def base(amplitudes, upstream, keep, turned, ahead, back, edges, width, cuts):
     _, variables, heights, modes = amplitudes.shape
+    walls = len(edges)
     lengths = [cut.stop - cut.start for cut in cuts]
     shapes = [(2, variables, rows, modes) for rows in lengths]
+    sums = padded(2 * walls * width + 2, 8)
     spec = pl.BlockSpec((2, variables, heights, NB), lambda i: (0, 0, 0, i))
-    small = pl.BlockSpec((GATHERED_ROWS, NB), lambda i: (0, i))
-    small_shape = jax.ShapeDtypeStruct((GATHERED_ROWS, modes), jnp.float32)
-    return pl.pallas_call(
-        functools.partial(base_body, cuts),
+
+    def rows_spec(rows):
+        return pl.BlockSpec((rows, NB), lambda i: (0, i))
+
+    return pl.pallas_call(
+        functools.partial(base_body, cuts, walls, width),
         grid=(modes // NB,),
         in_specs=[spec] * 2
-        + [pl.BlockSpec((NB,), lambda i: (i,)), whole(edge_rows), whole(turned)],
+        + [pl.BlockSpec((NB,), lambda i: (i,)), whole(turned), whole(ahead), whole(back)]
+        + [rows_spec(part.shape[0]) for part in edges],
         out_specs=[
             pl.BlockSpec((2, variables, rows, NB), lambda i: (0, 0, 0, i)) for rows in lengths
         ]
-        + [small] * 2,
+        + [rows_spec(sums), rows_spec(8)],
         out_shape=[pltpu.HBM(shapes[0], jnp.float32)]
         + [jax.ShapeDtypeStruct(shape, jnp.float32) for shape in shapes[1:]]
-        + [small_shape] * 2,
+        + [jax.ShapeDtypeStruct((rows, modes), jnp.float32) for rows in (sums, 8)],
         compiler_params=params(24),
         name="base",
-    )(in_hbm(amplitudes), in_hbm(upstream), keep, edge_rows, turned)
-
-
-def absorb_rows(read, mask_ref, edge_ref, adj_ref, before_ref, out_ref, sum_ref):
+    )(in_hbm(amplitudes), in_hbm(upstream), keep, turned, ahead, back, *edges)
+
+
+def absorb_rows(width, read, mask_ref, ahead_ref, adj_ref, before_ref, out_ref, sum_ref, *send_refs):
     _, variables, rows, lanes = out_ref.shape
-    ends = edge_ref.shape[1]
+    pushes = ahead_ref.shape[1]
     keep = kept_modes(mask_ref)
 
     @pl.when(pl.program_id(0) == 0)
@@ -345,24 +379,37 @@
             out_ref[part, v] = read(v, part).reshape(rows, lanes) * keep
     sides = [out_ref[part].reshape(variables * rows, lanes) for part in range(2)]
     for part in range(2):
-        at = slice(part * ends, (part + 1) * ends)
-        sum_ref[at] += jnp.dot(
-            edge_ref[0], sides[part], precision=SPLIT, preferred_element_type=jnp.float32
+        sum_ref[part * pushes : (part + 1) * pushes] += jnp.dot(
+            ahead_ref[0], sides[part], precision=SPLIT, preferred_element_type=jnp.float32
         )
     real, imag = (adj_ref[part].reshape(variables * rows, lanes) for part in range(2))
-    at = 2 * ends
+    at = 2 * pushes
     sum_ref[at : at + 1] += total(real * sides[0] + imag * sides[1])
     sum_ref[at + 1 : at + 2] += total(real * sides[1] - imag * sides[0])
 
-
-def absorb_body(in_ref, *refs):
+    if send_refs:
+
+        @pl.when(pl.program_id(0) == pl.num_programs(0) - 1)
+        def _():
+            for d, send_ref in enumerate(send_refs, 1):
+                for part in range(2):
+                    at = part * pushes + d * width
+                    send_ref[part * width : (part + 1) * width] = sum_ref[at : at + width]
+                at = 2 * pushes
+                send_ref[2 * width : 2 * width + 2] = sum_ref[at : at + 2]
+                rest = send_ref.shape[0] - 2 * width - 2
+                if rest:
+                    send_ref[2 * width + 2 :] = jnp.zeros((rest, lanes), jnp.float32)
+
+
+def absorb_body(width, in_ref, *refs):
     def read(v, part):
         return in_ref[:, v, :, part * NB : (part + 1) * NB]
 
-    absorb_rows(read, *refs)
-
-
-def absorb_apart_body(spans, place_ref, *refs):
+    absorb_rows(width, read, *refs)
+
+
+def absorb_apart_body(width, spans, place_ref, *refs):
     in_refs, refs, rows_ref = refs[:spans], refs[spans:-1], refs[-1]
     for i, in_ref in enumerate(in_refs):
         for j in range(in_ref.shape[0]):
@@ -371,19 +418,19 @@
     def read(v, part):
         return rows_ref[:, v, :, part * NB : (part + 1) * NB]
 
-    absorb_rows(read, *refs)
-
-
-def absorb(place, blocks, keep, edges, adjoint_modes, before):
+    absorb_rows(width, read, *refs)
+
+
+def absorb(place, blocks, keep, ahead, adjoint_modes, before, width, sends):
     blocks = list(blocks)
     apart = place is not None
     _, variables, rows, modes = adjoint_modes.shape
-    steps, ends, width = edges.shape
+    steps, pushes, depth = ahead.shape
     step = rows // steps
     grid_spec = pl.BlockSpec((2, variables, step, modes), lambda r: (0, 0, r, 0))
-    sums = pl.BlockSpec((GATHERED_ROWS, modes), lambda r: (0, 0))
     _, _, freqs, lanes = blocks[0].shape
-    operands = blocks + [keep, edges, adjoint_modes if apart else in_hbm(adjoint_modes), before]
+    sent = jax.ShapeDtypeStruct((padded(2 * width + 2, 8), modes), jnp.float32)
+    operands = blocks + [keep, ahead, adjoint_modes if apart else in_hbm(adjoint_modes), before]
     in_specs = [
         whole(block)
         if apart
@@ -391,107 +438,124 @@
         for block in blocks
     ] + [
         pl.BlockSpec((modes,), lambda r: (0,)),
-        pl.BlockSpec((1, ends, width), lambda r: (r, 0, 0)),
+        pl.BlockSpec((1, pushes, depth), lambda r: (r, 0, 0)),
         grid_spec,
-        sums,
+        whole(before),
     ]
-    body, scratch = absorb_body, []
+    body, scratch = functools.partial(absorb_body, width), []
     if apart:
         operands = [place] + operands
         in_specs = [pl.BlockSpec(memory_space=pltpu.SMEM)] + in_specs
-        body = functools.partial(absorb_apart_body, len(blocks))
+        body = functools.partial(absorb_apart_body, width, len(blocks))
         scratch = [pltpu.VMEM((rows, variables, freqs, lanes), jnp.float32)]
     return pl.pallas_call(
         body,
         grid=(steps,),
         in_specs=in_specs,
-        out_specs=[grid_spec, sums],
+        out_specs=[grid_spec, whole(before)] + [whole(sent)] * sends,
         out_shape=[
             jax.ShapeDtypeStruct((2, variables, rows, modes), jnp.float32),
-            jax.ShapeDtypeStruct((GATHERED_ROWS, modes), jnp.float32),
-        ],
+            jax.ShapeDtypeStruct(before.shape, jnp.float32),
+        ]
+        + [sent] * sends,
         scratch_shapes=scratch,
         compiler_params=params(24),
         name="absorb_apart" if apart else "absorb",
     )(*operands)
 
 
-def solve_body(groups, *refs):
-    side_refs, (up_ref, mask_ref, inverse_ref, out_ref) = refs[:groups], refs[groups:]
+def solve_body(side_ref, up_ref, mask_ref, inverse_ref, out_ref):
     _, variables, heights, lanes = out_ref.shape
     keep = kept_modes(mask_ref)
+    spare = heights - side_ref.shape[2]
     for part in range(2):
-        forced = [ref[part] for ref in side_refs]
-        forced = forced[0] if groups == 1 else jnp.concatenate(forced, axis=1)
-        side = forced + up_ref[part] * keep
-        side = side.reshape(variables * heights, lanes)
-        moved = table_times(inverse_ref[...], side)
-        out_ref[part] = moved.reshape(variables, heights, lanes)
-
-
-def solve(sides, upstream, keep, inverse):
+        forced = side_ref[part]
+        if spare:
+            none = jnp.zeros((variables, spare, lanes), jnp.float32)
+            forced = jnp.concatenate([forced, none], axis=1)
+        side = (forced + up_ref[part] * keep).reshape(variables * heights, lanes)
+        out_ref[part] = table_times(inverse_ref[...], side).reshape(variables, heights, lanes)
+
+
+def solve(side, upstream, keep, inverse):
     _, variables, heights, modes = upstream.shape
     lanes = min(2 * NB, modes)
     spec = pl.BlockSpec((2, variables, heights, lanes), lambda i: (0, 0, 0, i))
     return pl.pallas_call(
-        functools.partial(solve_body, len(sides)),
+        solve_body,
         grid=(modes // lanes,),
         in_specs=[
-            pl.BlockSpec((2, variables, side.shape[2], lanes), lambda i: (0, 0, 0, i))
-            for side in sides
-        ]
-        + [spec, pl.BlockSpec((lanes,), lambda i: (i,)), whole(inverse)],
+            pl.BlockSpec((2, variables, side.shape[2], lanes), lambda i: (0, 0, 0, i)),
+            spec,
+            pl.BlockSpec((lanes,), lambda i: (i,)),
+            whole(inverse),
+        ],
         out_specs=spec,
         out_shape=jax.ShapeDtypeStruct(upstream.shape, jnp.float32),
         compiler_params=params(24),
         name="solve",
-    )(*sides, in_hbm(upstream), keep, inverse)
-
-
-def finish_body(walls, extent, solved_ref, *refs):
-    bounds, refs = refs[:walls], refs[walls:]
-    edges, refs = refs[:walls], refs[walls:]
-    chain_ref, out_ref, shift_ref = refs
+    )(side, in_hbm(upstream), keep, inverse)
+
+
+def solve_more_body(side_ref, before_ref, inverse_ref, out_ref):
     _, variables, heights, lanes = out_ref.shape
-    ends = 2 * variables
-    pushed = []
     for part in range(2):
-        at = slice(part * ends, (part + 1) * ends)
-        everywhere = [ref[at] for ref in bounds]
-        spare = chain_ref.shape[1] // 3 - walls * ends
+        moved = table_times(inverse_ref[...], side_ref[part].reshape(-1, lanes))
+        out_ref[part] = before_ref[part] + moved.reshape(variables, heights, lanes)
+
+
+def solve_more(side, before, inverse):
+    _, variables, rows, modes = side.shape
+    lanes = min(2 * NB, modes)
+    spec = pl.BlockSpec(before.shape[:3] + (lanes,), lambda i: (0, 0, 0, i))
+    return pl.pallas_call(
+        solve_more_body,
+        grid=(modes // lanes,),
+        in_specs=[
+            pl.BlockSpec((2, variables, rows, lanes), lambda i: (0, 0, 0, i)),
+            spec,
+            whole(inverse),
+        ],
+        out_specs=spec,
+        out_shape=jax.ShapeDtypeStruct(before.shape, jnp.float32),
+        compiler_params=params(24),
+        name="solve_more",
+    )(side, before, inverse)
+
+
+def finish_body(walls, width, solved_ref, sum_ref, square_ref, *refs):
+    others, (columns_ref, out_ref, shift_ref) = refs[: walls - 1], refs[walls - 1 :]
+    _, variables, heights, lanes = out_ref.shape
+    spare = columns_ref.shape[1] // 3 - width
+    pushes = walls * width
+    for part in range(2):
+        push = sum_ref[part * pushes : part * pushes + width]
+        for ref in others:
+            push = push + ref[part * width : (part + 1) * width]
         if spare:
-            everywhere.append(jnp.zeros((spare, lanes), jnp.float32))
-        everywhere = jnp.concatenate(everywhere, axis=0)
-        moved = table_times(chain_ref[...], everywhere)
-        pushed.append(moved[extent:])
-        out_ref[part] = solved_ref[part] - moved[:extent].reshape(variables, heights, lanes)
-    real = imag = weight = 0.0
-    for wall in range(walls):
-        at = slice(wall * ends, (wall + 1) * ends)
-        push = [pushed[part][at] for part in range(2)]
-        edge = [edges[wall][part * ends : (part + 1) * ends] for part in range(2)]
-        row = 2 * ends
-        squares = edges[wall][row : row + 1]
-        taken = jnp.sum(edge[0] * push[0] + edge[1] * push[1], axis=0, keepdims=True)
-        real = real + (bounds[wall][row : row + 1] - taken - squares)
-        taken = jnp.sum(edge[0] * push[1] - edge[1] * push[0], axis=0, keepdims=True)
-        imag = imag + (bounds[wall][row + 1 : row + 2] - taken)
-        weight = weight + squares
-    weight = weight + epsilon
-    shift_ref[0:1] = imag / weight
-    shift_ref[1:2] = -real / weight
-
-
-def finish(solved, bounds, edges, chain):
+            push = jnp.concatenate([push, jnp.zeros((spare, lanes), jnp.float32)], axis=0)
+        moved = table_times(columns_ref[...], push)
+        out_ref[part] = solved_ref[part] - moved.reshape(variables, heights, lanes)
+    both = sum_ref[2 * pushes : 2 * pushes + 2]
+    for ref in others:
+        both = both + ref[2 * width : 2 * width + 2]
+    squares = square_ref[:1]
+    weight = squares + epsilon
+    shift_ref[0:1] = both[1:2] / weight
+    shift_ref[1:2] = (squares - both[0:1]) / weight
+
+
+def finish(solved, sums, squares, others, columns, width):
     _, variables, heights, modes = solved.shape
-    walls = len(bounds)
     lanes = min(2 * NB, modes)
-    small = pl.BlockSpec((GATHERED_ROWS, lanes), lambda i: (0, i))
     spec = pl.BlockSpec((2, variables, heights, lanes), lambda i: (0, 0, 0, i))
-    return pl.pallas_call(
-        functools.partial(finish_body, walls, variables * heights),
+    rows = [sums, squares] + others
+    return pl.pallas_call(
+        functools.partial(finish_body, len(others) + 1, width),
         grid=(modes // lanes,),
-        in_specs=[spec] + [small] * (2 * walls) + [whole(chain)],
+        in_specs=[spec]
+        + [pl.BlockSpec((part.shape[0], lanes), lambda i: (0, i)) for part in rows]
+        + [whole(columns)],
         out_specs=[spec, pl.BlockSpec((2, lanes), lambda i: (0, i))],
         out_shape=[
             jax.ShapeDtypeStruct(solved.shape, jnp.float32),
@@ -499,7 +563,7 @@
         ],
         compiler_params=params(),
         name="finish",
-    )(solved, *bounds, *edges, chain)
+    )(solved, *rows, columns)
 
 
 def around(block, axis):
@@ -510,6 +574,14 @@
     ]
 
 
+def hand_back(blocks, axis):
+    count = lax.axis_size(axis)
+    return [
+        lax.ppermute(block, axis, [(i, (i - d) % count) for i in range(count)])
+        for d, block in enumerate(blocks, 1)
+    ]
+
+
 PACKED_ROWS = 16
 
 
@@ -538,34 +610,39 @@
     return jnp.concatenate([high, high, matrix - high], axis=1).astype(jnp.bfloat16)
 
 
+def push_width(walls, variables):
+    return variables if walls == 2 else 2 * variables
+
+
 def constants_body(cuts, variables, walls, place_ref, inverse_ref, *refs):
     packed, refs = refs[:walls], refs[walls:]
-    turned_ref, split_ref, rows_ref = refs[:3]
-    row_refs, (chain_ref, all_ref, step_ref) = refs[3 : 3 + len(cuts)], refs[3 + len(cuts) :]
+    turned_ref, split_ref, last_ref, column_ref, edge_ref, ahead_ref, back_ref = refs[:7]
+    row_refs, (all_ref, step_ref) = refs[7 : 7 + len(cuts)], refs[7 + len(cuts) :]
     extent = inverse_ref.shape[0]
     heights = extent // variables
     ends = 2 * variables
+    width = push_width(walls, variables)
     matrix = inverse_ref[...]
     turned = matrix.T
-    turned_ref[...] = turned
+    turned_ref[...] = split_columns(turned)
     split_ref[...] = split_columns(matrix)
-    for end, point in enumerate((0, heights - 1)):
-        for w in range(variables):
-            at = w * heights + point
-            row = end * variables + w
-            rows_ref[row : row + 1] = matrix[at : at + 1]
-    ends_rows = rows_ref[...]
-    for cut, row_ref in zip(cuts, row_refs):
-        step = row_step(cut.stop - cut.start)
-        for r in range(row_ref.shape[0]):
-            at = cut.start + r * step
-            pieces = [
-                ends_rows[:, v * heights + at : v * heights + at + step] for v in range(variables)
-            ]
-            row_ref[r] = jnp.concatenate(pieces, axis=1)
+    cut = cuts[-1]
+    last = [matrix[:, v * heights : (v + 1) * heights][:, cut] for v in range(variables)]
+    last_ref[...] = split_columns(jnp.concatenate(last, axis=1))
 
     def dot(a, b):
         return jnp.dot(a, b, precision=FULL, preferred_element_type=jnp.float32)
+
+    def ends_of(value):
+        low = [value[v * heights : v * heights + 1] for v in range(variables)]
+        high = [value[(v + 1) * heights - 1 : (v + 1) * heights] for v in range(variables)]
+        return jnp.concatenate(low, axis=0), jnp.concatenate(high, axis=0)
+
+    def extended(value, rows):
+        spare = rows - value.shape[0]
+        if not spare:
+            return value
+        return jnp.concatenate([value, jnp.zeros((spare, value.shape[1]), jnp.float32)], axis=0)
 
     size = walls * PACKED_ROWS
     for d in range(walls):
@@ -588,57 +665,73 @@
     interface[-1] = dot(small(walls - 1, 4), ahead[-1])
     for j in range(walls - 2, -1, -1):
         interface[j] = dot(small(j, 4), ahead[j] - dot(small(j, 3), interface[j + 1]))
+    none = jnp.zeros((variables, size), jnp.float32)
     for j in range(walls):
-        none = jnp.zeros((variables, size), jnp.float32)
         under, over = none, none
         if j > 0:
-            last = jnp.concatenate([interface[j - 1][variables:], none], axis=0)[:PACKED_ROWS]
-            under = dot(small(j, 0), last)[:variables]
+            lower = extended(interface[j - 1][variables:], PACKED_ROWS)
+            under = dot(small(j, 0), lower)[:variables]
         if j < walls - 1:
             over = dot(small(j, 1), interface[j + 1])[:variables]
-        step_ref[(place_ref[0] - j + walls) % walls] = jnp.concatenate(
-            [under, over, jnp.zeros((PACKED_ROWS - ends, size), jnp.float32)], axis=0
-        )
-    pushes = [step_ref[d][:ends] for d in range(walls)]
-    edge = [turned[v * heights : v * heights + 1] for v in range(variables)]
-    edge += [turned[(v + 1) * heights - 1 : (v + 1) * heights] for v in range(variables)]
-    edge.append(jnp.zeros((PACKED_ROWS - ends, extent), jnp.float32))
-    edge = jnp.concatenate(edge, axis=0).T
-    own = dot(edge, step_ref[0])
-    spare = chain_ref.shape[0] - extent - walls * ends
-    full = [own] + pushes
-    if spare:
-        full.append(jnp.zeros((spare, size), jnp.float32))
-    full = jnp.concatenate(full, axis=0)
-    chain_ref[...] = split_columns(full)
+        push = under + over if walls == 2 else jnp.concatenate([under, over], axis=0)
+        step_ref[(place_ref[0] - j + walls) % walls] = extended(push, PACKED_ROWS)
+
+    low, high = ends_of(matrix)
+    bounds = extended(jnp.concatenate([low, high], axis=0), PACKED_ROWS)
+    steps = [step_ref[d][:width, :PACKED_ROWS] for d in range(walls)]
+    steps = [jnp.where(column[:width, :PACKED_ROWS] < ends, step, 0.0) for step in steps]
+    pushes = dot(jnp.concatenate(steps, axis=0), bounds)
+    for cut, row_ref in zip(cuts, row_refs):
+        step = row_step(cut.stop - cut.start)
+        for r in range(row_ref.shape[0]):
+            at = cut.start + r * step
+            pieces = [pushes[:, v * heights + at : v * heights + at + step] for v in range(variables)]
+            row_ref[r] = jnp.concatenate(pieces, axis=1)
+    pushes = extended(pushes, ahead_ref.shape[0])
+    ahead_ref[...] = split_columns(pushes)
+    back_ref[...] = split_columns(pushes.T)
+    low, high = ends_of(turned)
+    edge = jnp.concatenate([low, high], axis=0)
+    if walls == 2:
+        edge = jnp.where(place_ref[0] == 0, high, low)
+    edge = extended(edge, edge_ref.shape[0])
+    edge_ref[...] = split_columns(edge)
+    column_ref[...] = split_columns(edge.T)
 
 
 def constants(place, inverse, packed, cuts, variables):
     walls = len(packed)
     extent = inverse.shape[0]
-    heights = extent // variables
-    ends = 2 * variables
+    width = push_width(walls, variables)
     lengths = [cut.stop - cut.start for cut in cuts]
     size = walls * PACKED_ROWS
-    rows = extent + walls * ends + (-walls * ends) % 16
-    f32 = jnp.float32
+    pushes, edge_rows = padded(walls * width, 16), padded(width, 16)
+
+    def split_shape(rows, columns):
+        return jax.ShapeDtypeStruct((rows, 3 * columns), jnp.bfloat16)
+
     return pl.pallas_call(
         functools.partial(constants_body, cuts, variables, walls),
         in_specs=[pl.BlockSpec(memory_space=pltpu.SMEM)]
         + [pl.BlockSpec(memory_space=pltpu.VMEM)] * (1 + walls),
         out_shape=[
-            jax.ShapeDtypeStruct((extent, extent), f32),
-            jax.ShapeDtypeStruct((extent, 3 * extent), jnp.bfloat16),
-            jax.ShapeDtypeStruct((ends, extent), f32),
+            split_shape(extent, extent),
+            split_shape(extent, extent),
+            split_shape(extent, variables * lengths[-1]),
+            split_shape(extent, edge_rows),
+            split_shape(edge_rows, extent),
+            split_shape(pushes, extent),
+            split_shape(extent, pushes),
         ]
         + [
-            jax.ShapeDtypeStruct((n // row_step(n), ends, variables * row_step(n)), f32)
+            jax.ShapeDtypeStruct(
+                (n // row_step(n), walls * width, variables * row_step(n)), jnp.float32
+            )
             for n in lengths
-        ]
-        + [jax.ShapeDtypeStruct((rows, 3 * size), jnp.bfloat16)],
+        ],
         scratch_shapes=[
-            pltpu.VMEM((walls,) + packed[0].shape, f32),
-            pltpu.VMEM((walls, PACKED_ROWS, size), f32),
+            pltpu.VMEM((walls,) + packed[0].shape, jnp.float32),
+            pltpu.VMEM((walls, PACKED_ROWS, size), jnp.float32),
         ],
         compiler_params=params(),
         name="constants",
@@ -707,24 +800,37 @@
     inverse = slab_inverse[0]
     parts = (lower_coupling, upper_coupling, reduced_lower, reduced_upper, reduced_pivot)
     packed = around(pack(parts), "wall")
-    turned, split, edge_rows, *end_rows, chain = constants(wall, inverse, packed, cuts, variables)
-    *adjoint_modes, edge, sums = base(amplitudes, upstream, keep, edge_rows, turned, cuts)
-    edges = around(edge, "wall")
+    turned, split, last, edge_columns, edge_rows, ahead, back, *rows = constants(
+        wall, inverse, packed, cuts, variables
+    )
+    walls = len(packed)
+    width = push_width(walls, variables)
+    edges = around(edge(amplitudes, keep, edge_rows, width), "wall")
+    *adjoint_modes, sums, squares = base(
+        amplitudes, upstream, keep, turned, ahead, back, edges, width, cuts
+    )
     if apart:
         forced = nonlinear_apart(place, arrived, coefficients, transforms)
         returned = regroup(swap(forced, "freq"))
-        held = (returned, split, end_rows, chain, adjoint_modes, edges, sums)
+        held = (returned, split, last, edge_columns, rows, adjoint_modes, sums, squares)
         held = lax.optimization_barrier(held)
-        returned, split, end_rows, chain, adjoint_modes, edges, sums = held
+        returned, split, last, edge_columns, rows, adjoint_modes, sums, squares = held
         returned = swap(returned, "span")
 
-    sides = [None] * len(cuts)
-    sides[0], sums = absorb(None, [main], keep, end_rows[0], adjoint_modes[0], sums)
+    sends = walls - 1
+    side, sums, *sent = absorb(
+        None, [main], keep, rows[0], adjoint_modes[0], sums, width, 0 if apart else sends
+    )
+    solved = solve(side, upstream, keep, split)
     if apart:
-        sides[1], sums = absorb(place, returned, keep, end_rows[1], adjoint_modes[1], sums)
-    bounds = around(sums, "wall")
-    solved = solve(sides, upstream, keep, split)
-    new_amplitudes, wavenumber_shift = finish(solved, bounds, edges, chain)
+        solved, sums = lax.optimization_barrier((solved, sums))
+        side, sums, *sent = absorb(
+            place, returned, keep, rows[1], adjoint_modes[1], sums, width, sends
+        )
+    others = hand_back(sent, "wall")
+    if apart:
+        solved = solve_more(side, solved, last)
+    new_amplitudes, wavenumber_shift = finish(solved, sums, squares, others, edge_columns, width)
     return (new_amplitudes, wavenumber_shift)
 
 

time: 262 us -> 260 us (level)
  Pallas kernels: 54.2 us -> 60.9 us
  starting transfers between devices: 55.2 us -> 48.9 us
    pallas_call x3 -> x5, Pallas kernels: 20.7 us -> 28.1 us  [the longest x1 10.6 us: base(): pl.pallas_call(functools.partial(base_body, cuts, walls, width), grid=(mo...]
    ppermute x12, starting transfers between devices: 37.2 us -> 30.6 us  [swap(): lax.ppermute(block, axis, [(at, at ^ i) for at in range(count)])]
    unnamed x35 -> x39, local copies, waits for them, and re-layouts: 6.7 us -> 4.53 us
  transfers between devices with their start and end apart: 17 -> 17, of which waited for: 11 -> 11; matrix products, arithmetic and copies ran while one was open for 2% -> 2% of each run, Pallas kernels for 17% -> 20%
where the time goes in v4:
time: 260 us; the launch traced here: 259 us
  waiting for transfers between devices  141 us (54%)
  Pallas kernels  60.9 us (23%)
  starting transfers between devices  48.9 us (19%)
  local copies, waits for them, and re-layouts  4.71 us (2%)
    ppermute x12, waiting for transfers between devices, swap(): lax.ppermute(block, axis, [(at, at ^ i) for at in range(count)])  107 us
    ppermute x12, starting transfers between devices, swap(): lax.ppermute(block, axis, [(at, at ^ i) for at in range(count)])  30.6 us
    all_to_all x2, waiting for transfers between devices, exchange(): return lax.all_to_all(block, axes, split_axis=0, concat_axis=0, tiled=True)  29.2 us
    all_to_all x2, starting transfers between devices, exchange(): return lax.all_to_all(block, axes, split_axis=0, concat_axis=0, tiled=True)  13.6 us
    pallas_call x1, Pallas kernels, nonlinear(): pl.pallas_call(nonlinear_body, grid=(points,), in_specs=[pl.BlockSpec(mem...  12 us
    pallas_call x1, Pallas kernels, base(): pl.pallas_call(functools.partial(base_body, cuts, walls, width), grid=(mo...  10.6 us
    pallas_call x2, Pallas kernels, absorb(): pl.pallas_call(body, grid=(steps,), in_specs=in_specs, out_specs=[grid_sp...  6.37 us
    pallas_call x1, Pallas kernels, edge(): pl.pallas_call(functools.partial(edge_body, width), grid=(modes // NB,),...  6.02 us
  transfers between devices with their start and end apart: 17, of which 11 were waited for; matrix products, arithmetic and copies ran while one was open for 2% of the time, Pallas kernels for 20%

profile of v4, /device:TPU:10, one launch (start us, length us, event | category | flops | bytes accessed | tf_op | source)
XLA Modules:
  0.0 258.5 jit_solution(5750808471476767525)
XLA Ops:
  0.6 3.9 %prepare.1 = f32[48,5,8,512]{3,2,1,0:T(8,128)} custom-call(f32[2,5,64,2048]{3,2,1,0:T(8,128)} %x_ref.4, s32[2048]{0:T(1024)} %refs_4_.3), custom_call_target="tpu_custom_call" | custom-call | tf_op jit(solution)/shard_map/prepare/pallas_call | solution.py:82
  4.5 6.4 %all-to-all-start = ((f32[48,5,8,512]{3,2,1,0:T(8,128)}), f32[48,5,8,512]{3,2,1,0:T(8,128)}, u32[]{:S(2)}, u32[]{:S(2)}) async-start(f32[48,5,8,512]{3,2,1,0:T(8,128)} %prepare.1), calls=%async_computation | async-start | bytes 7864320 | tf_op jit(solution)/shard_map/all_to_all | solution.py:768
  10.9 0.1 pad_add_fusion.place_ref
  11.0 3.3 %prepare_apart.1 = (f32[4,5,8,512]{3,2,1,0:T(8,128)S(1)}, f32[4,5,8,512]{3,2,1,0:T(8,128)S(1)}, f32[4,5,8,512]{3,2,1,0:T(8,128)S(1)}, f32[4,5,8,512]{3,2,1,0:T(8,128)S(1)}) custom-call(s32[2]{0:T(128)S(1)} %pad_add_fusion.place_ref, f32[2,5,64,2048]{3,2,1,0:T(8,128)} %x_ref.4, s32[2048]{0:T(1024)S(1)} %copy-done.1), custom_call_target="tpu_custom_call" | custom-call | tf_op jit(solution)/shard_map/prepare_apart/pallas_call | solution.py:118
  14.3 0.2 collective-permute-start
  14.5 0.6 collective-permute-start.1
  15.1 1.1 collective-permute-start.2
  16.2 0.0 collective-permute-done
  16.3 22.3 %collective-permute-done.1 = f32[4,5,8,512]{3,2,1,0:T(8,128)S(1)} collective-permute-done((f32[4,5,8,512]{3,2,1,0:T(8,128)S(1)}, f32[4,5,8,512]{3,2,1,0:T(8,128)S(1)}, u32[]{:S(2)}, u32[]{:S(2)}) %collective-permute-start.1) | collective-permute-done | bytes 327712 | tf_op jit(solution)/shard_map/ppermute | solution.py:773
  38.6 8.7 %collective-permute-done.2 = f32[4,5,8,512]{3,2,1,0:T(8,128)S(1)} collective-permute-done((f32[4,5,8,512]{3,2,1,0:T(8,128)S(1)}, f32[4,5,8,512]{3,2,1,0:T(8,128)S(1)}, u32[]{:S(2)}, u32[]{:S(2)}) %collective-permute-start.2) | collective-permute-done | bytes 327712 | tf_op jit(solution)/shard_map/ppermute | solution.py:773
  47.4 19.1 %collective-permute-start.3 = (f32[4,5,8,512]{3,2,1,0:T(8,128)S(1)}, f32[4,5,8,512]{3,2,1,0:T(8,128)S(1)}, u32[]{:S(2)}, u32[]{:S(2)}) collective-permute-start(f32[4,5,8,512]{3,2,1,0:T(8,128)S(1)} %pad_maximum_fusion.1), channel_id=1, source_target_pairs={{0,2},{2,0},{4,6},{6,4},{1,3},{3,1},{5,7},{7,5},{8,10},{10,8},{12,... | collective-permute-start | bytes 983048 | tf_op jit(solution)/shard_map/ppermute | solution.py:773
  66.5 2.5 collective-permute-start.4
  69.1 0.0 copy-done.11
  69.1 0.1 pad_maximum_fusion
  69.1 14.5 %collective-permute-done.3.refs_1_ = f32[4,5,8,512]{3,2,1,0:T(8,128)S(1)} collective-permute-done((f32[4,5,8,512]{3,2,1,0:T(8,128)S(1)}, f32[4,5,8,512]{3,2,1,0:T(8,128)S(1)}, u32[]{:S(2)}, u32[]{:S(2)}) %collective-permute-start.3) | collective-permute-done | bytes 327712 | tf_op jit(solution)/shard_map/ppermute | solution.py:773
  83.6 28.3 %collective-permute-done.4.refs_3_ = f32[4,5,8,512]{3,2,1,0:T(8,128)S(1)} collective-permute-done((f32[4,5,8,512]{3,2,1,0:T(8,128)S(1)}, f32[4,5,8,512]{3,2,1,0:T(8,128)S(1)}, u32[]{:S(2)}, u32[]{:S(2)}) %collective-permute-start.4) | collective-permute-done | bytes 327712 | tf_op jit(solution)/shard_map/ppermute | solution.py:773
  111.9 0.0 all-to-all-done
  111.9 0.0 collective-permute-start.5
  111.9 12.0 %nonlinear.1 = f32[16,3,5,8,512]{4,3,2,1,0:T(8,128)} custom-call(f32[25,5]{1,0:T(8,128)S(1)} %reshape.20.q_ref, f32[16,3,5,8,512]{4,3,2,1,0:T(8,128)} %bitcast.2.in_ref, bf16[256,768]{1,0:T(8,128)(2,1)} %constant.19.clone.refs_0_.refs_4_, bf16[1536,256]{1,0:T(8,128)(2,1)} %constant.20.clone.refs_1_.refs_5_, bf16[768,512]{1,0:T(8,128)(2,1)} %constant.21.clone.refs_2_.refs_6_, ...), custom_call_target="tpu_custom_call" | custom-call | flops 4529848320 | bytes 7864320 | tf_op jit(solution)/shard_map/nonlinear/pallas_call | solution.py:214
  123.9 2.1 collective-permute-done.5.refs_2_
  126.0 0.0 copy-start
  126.0 7.2 %all-to-all-start.1 = ((f32[48,5,8,512]{3,2,1,0:T(8,128)}), f32[48,5,8,512]{3,2,1,0:T(8,128)}, u32[]{:S(2)}, u32[]{:S(2)}) async-start(f32[48,5,8,512]{3,2,1,0:T(8,128)} %bitcast.7), calls=%async_computation.1 | async-start | bytes 7864320 | tf_op jit(solution)/shard_map/all_to_all | solution.py:768
  133.3 0.6 copy.19.refs_0_
  133.8 0.0 copy-done.16
  133.8 0.6 copy.20.refs_1_
  134.4 0.6 copy.21.refs_2_
  135.0 0.6 copy.22.refs_3_
  135.6 0.0 copy-done.14
  135.6 0.6 copy.23.refs_4_
  136.2 1.4 pack.1.refs_0_
  137.6 1.5 collective-permute-start.9
  139.1 2.7 %collective-permute-done.9.refs_1_ = f32[5,16,128]{2,1,0:T(8,128)S(1)} collective-permute-done((f32[5,16,128]{2,1,0:T(8,128)}, f32[5,16,128]{2,1,0:T(8,128)S(1)}, u32[]{:S(2)}, u32[]{:S(2)}) %collective-permute-start.9) | collective-permute-done | bytes 40992 | tf_op jit(solution)/shard_map/ppermute | solution.py:572
  141.8 0.8 copy-done.2
  142.6 1.2 constants.1
  143.9 0.0 copy-start.7
  143.9 6.0 %edge.1.refs_0_ = f32[16,2048]{1,0:T(8,128)S(1)} custom-call(f32[2,5,64,2048]{3,2,1,0:T(8,128)} %x_ref.4, s32[2048]{0:T(1024)S(1)} %copy-done.1, bf16[16,960]{1,0:T(8,128)(2,1)S(1)} %get-tuple-element.76.rows_ref), custom_call_target="tpu_custom_call" | custom-call | tf_op jit(solution)/shard_map/edge/pallas_call | solution.py:294
  149.9 1.6 collective-permute-start.10
  151.5 4.7 %nonlinear_apart.1 = (f32[4,5,8,512]{3,2,1,0:T(8,128)S(1)}, f32[4,5,8,512]{3,2,1,0:T(8,128)S(1)}, f32[4,5,8,512]{3,2,1,0:T(8,128)S(1)}, f32[4,5,8,512]{3,2,1,0:T(8,128)S(1)}) custom-call(s32[2]{0:T(128)S(1)} %pad_add_fusion.place_ref, f32[25,5]{1,0:T(8,128)S(1)} %reshape.20.q_ref, f32[4,5,8,512]{3,2,1,0:T(8,128)S(1)} %get-tuple-element.58.refs_0_, ...), custom_call_target="tpu_custom_call" | custom-call | flops 1509949440 | bytes 2621440 | tf_op jit(solution)/shard_map/nonlinear_apart/pallas_call | solution.py:255
  156.2 0.1 collective-permute-start.6
  156.3 0.0 collective-permute-done.10.refs_1_
  156.3 10.6 %base.1 = (f32[2,5,48,2048]{3,2,1,0:T(8,128)}, f32[2,5,16,2048]{3,2,1,0:T(8,128)S(1)}, f32[24,2048]{1,0:T(8,128)S(1)}, f32[8,2048]{1,0:T(8,128)S(1)}) custom-call(f32[2,5,64,2048]{3,2,1,0:T(8,128)} %x_ref.4, f32[2,5,64,2048]{3,2,1,0:T(8,128)} %up_ref.3, s32[2048]{0:T(1024)S(1)} %copy-done.1, bf16[320,960]{1,0:T(8,128)(2,1)S(1)} %get-tuple-element.73.turned_ref, ...), custom_call_target="tpu_custom_call" | custom-call | tf_op jit(solution)/shard_map/base/pallas_call | solution.py:350
  166.8 0.5 collective-permute-start.7
  167.4 1.4 collective-permute-start.8
  168.8 0.0 collective-permute-done.6
  168.8 13.8 %collective-permute-done.7 = f32[4,5,8,512]{3,2,1,0:T(8,128)S(1)} collective-permute-done((f32[4,5,8,512]{3,2,1,0:T(8,128)S(1)}, f32[4,5,8,512]{3,2,1,0:T(8,128)S(1)}, u32[]{:S(2)}, u32[]{:S(2)}) %collective-permute-start.7) | collective-permute-done | bytes 327712 | tf_op jit(solution)/shard_map/ppermute | solution.py:773
  182.7 13.2 %collective-permute-done.8 = f32[4,5,8,512]{3,2,1,0:T(8,128)S(1)} collective-permute-done((f32[4,5,8,512]{3,2,1,0:T(8,128)S(1)}, f32[4,5,8,512]{3,2,1,0:T(8,128)S(1)}, u32[]{:S(2)}, u32[]{:S(2)}) %collective-permute-start.8) | collective-permute-done | bytes 327712 | tf_op jit(solution)/shard_map/ppermute | solution.py:773
  195.9 0.8 pad_maximum_fusion.7
  196.6 0.8 pad_maximum_fusion.6
  197.4 0.8 pad_maximum_fusion.5
  198.2 0.1 collective-permute-start.11
  198.3 4.5 %collective-permute-start.12 = (f32[4,5,8,512]{3,2,1,0:T(8,128)}, f32[4,5,8,512]{3,2,1,0:T(8,128)S(1)}, u32[]{:S(2)}, u32[]{:S(2)}) collective-permute-start(f32[4,5,8,512]{3,2,1,0:T(8,128)} %pad_maximum_fusion.6), channel_id=1, source_target_pairs={{0,4},{2,6},{4,0},{6,2},{1,5},{3,7},{5,1},{7,3},{8,12},{10,14},{12... | collective-permute-start | bytes 983048 | tf_op jit(solution)/shard_map/ppermute | solution.py:773
  202.8 0.5 collective-permute-start.13
  203.3 29.2 %all-to-all-done.1.in_ref = f32[48,5,8,512]{3,2,1,0:T(8,128)} async-done(((f32[48,5,8,512]{3,2,1,0:T(8,128)}), f32[48,5,8,512]{3,2,1,0:T(8,128)}, u32[]{:S(2)}, u32[]{:S(2)}) %all-to-all-start.1) | async-done | bytes 3932192 | tf_op jit(solution)/shard_map/all_to_all | solution.py:768
  232.5 0.7 copy-done.8
  233.2 4.8 %absorb.1 = (f32[2,5,48,2048]{3,2,1,0:T(8,128)S(1)}, f32[24,2048]{1,0:T(8,128)S(1)}) custom-call(f32[48,5,8,512]{3,2,1,0:T(8,128)} %all-to-all-done.1.in_ref, s32[2048]{0:T(1024)S(1)} %copy-done.1, f32[2,10,120]{2,1,0:T(8,128)S(1)} %copy-done.8, f32[2,5,48,2048]{3,2,1,0:T(8,128)} %get-tuple-element.89.refs_2_, f32[24,2048]{1,0:T(8,128)S(1)} %get-tuple-element.90.refs_3_), custom_call_target="tpu_custom_call" | custom-call | tf_op jit(solution)/shard_map/absorb/pallas_call | solution.py:451
  238.0 5.8 %solve.1.before_ref = f32[2,5,64,2048]{3,2,1,0:T(8,128)S(1)} custom-call(f32[2,5,48,2048]{3,2,1,0:T(8,128)S(1)} %get-tuple-element.91.side_ref, f32[2,5,64,2048]{3,2,1,0:T(8,128)} %up_ref.3, s32[2048]{0:T(1024)S(1)} %copy-done.1, bf16[320,960]{1,0:T(8,128)(2,1)S(1)} %get-tuple-element.92.inverse_ref), custom_call_target="tpu_custom_call" | custom-call | tf_op jit(solution)/shard_map/solve/pallas_call | solution.py:484
  243.9 0.0 collective-permute-done.11.refs_1_
  243.9 0.0 collective-permute-done.12.refs_2_
  243.9 4.4 %collective-permute-done.13.refs_3_ = f32[4,5,8,512]{3,2,1,0:T(8,128)S(1)} collective-permute-done((f32[4,5,8,512]{3,2,1,0:T(8,128)}, f32[4,5,8,512]{3,2,1,0:T(8,128)S(1)}, u32[]{:S(2)}, u32[]{:S(2)}) %collective-permute-start.13) | collective-permute-done | bytes 327712 | tf_op jit(solution)/shard_map/ppermute | solution.py:773
  248.3 1.6 absorb_apart.1
  249.9 1.6 collective-permute-start.14
  251.5 2.2 solve_more.1.solved_ref
  253.7 1.3 collective-permute-done.14.refs_0_
  255.0 3.5 %finish.1 = (f32[2,5,64,2048]{3,2,1,0:T(8,128)}, f32[2,2048]{1,0:T(2,128)}) custom-call(f32[2,5,64,2048]{3,2,1,0:T(8,128)S(1)} %solve_more.1.solved_ref, f32[24,2048]{1,0:T(8,128)S(1)} %get-tuple-element.98.sum_ref, f32[8,2048]{1,0:T(8,128)S(1)} %get-tuple-element.99.square_ref, f32[16,2048]{1,0:T(8,128)S(1)} %collective-permute-done.14.refs_0_, ...), custom_call_target="tpu_custom_call" | custom-call | tf_op jit(solution)/shard_map/finish/pallas_call | solution.py:553
  (39 shorter events, 0.3 us)
Async XLA Ops:
  4.5 6.5 %copy-start.1 = (s32[2048]{0:T(1024)S(1)}, s32[2048]{0:T(1024)}, u32[]{:S(2)}) copy-start(s32[2048]{0:T(1024)} %refs_4_.3) | copy-start | bytes 24580
  4.5 107.4 %all-to-all-start = ((f32[48,5,8,512]{3,2,1,0:T(8,128)}), f32[48,5,8,512]{3,2,1,0:T(8,128)}, u32[]{:S(2)}, u32[]{:S(2)}) async-start(f32[48,5,8,512]{3,2,1,0:T(8,128)} %prepare.1), calls=%async_computation | async-start | bytes 7864320 | tf_op jit(solution)/shard_map/all_to_all | solution.py:768
  11.0 140.5 %copy-start.9 = (s32[2]{0:T(128)}, s32[2]{0:T(128)S(1)}, u32[]{:S(2)}) copy-start(s32[2]{0:T(128)S(1)} %pad_add_fusion.place_ref) | copy-start | bytes 28
  11.0 58.1 %copy-start.11 = (f32[5,5,5]{2,1,0:T(8,128)S(1)}, f32[5,5,5]{2,1,0:T(8,128)}, u32[]{:S(2)}) copy-start(f32[5,5,5]{2,1,0:T(8,128)} %param.17) | copy-start | bytes 1504
  14.3 2.0 collective-permute-start
  14.5 24.1 %collective-permute-start.1 = (f32[4,5,8,512]{3,2,1,0:T(8,128)S(1)}, f32[4,5,8,512]{3,2,1,0:T(8,128)S(1)}, u32[]{:S(2)}, u32[]{:S(2)}) collective-permute-start(f32[4,5,8,512]{3,2,1,0:T(8,128)S(1)} %get-tuple-element.56), channel_id=1, source_target_pairs={{0,16},{8,24},{16,0},{24,8},{1,17},{9,25},{17,1},{25,9},{2,18},{10... | collective-permute-start | bytes 983048 | tf_op jit(solution)/shard_map/ppermute | solution.py:773
  15.1 32.2 %collective-permute-start.2 = (f32[4,5,8,512]{3,2,1,0:T(8,128)S(1)}, f32[4,5,8,512]{3,2,1,0:T(8,128)S(1)}, u32[]{:S(2)}, u32[]{:S(2)}) collective-permute-start(f32[4,5,8,512]{3,2,1,0:T(8,128)S(1)} %get-tuple-element.57), channel_id=1, source_target_pairs={{0,24},{8,16},{16,8},{24,0},{1,25},{9,17},{17,9},{25,1},{2,26},{10... | collective-permute-start | bytes 983048 | tf_op jit(solution)/shard_map/ppermute | solution.py:773
  47.4 36.2 %collective-permute-start.3 = (f32[4,5,8,512]{3,2,1,0:T(8,128)S(1)}, f32[4,5,8,512]{3,2,1,0:T(8,128)S(1)}, u32[]{:S(2)}, u32[]{:S(2)}) collective-permute-start(f32[4,5,8,512]{3,2,1,0:T(8,128)S(1)} %pad_maximum_fusion.1), channel_id=1, source_target_pairs={{0,2},{2,0},{4,6},{6,4},{1,3},{3,1},{5,7},{7,5},{8,10},{10,8},{12,... | collective-permute-start | bytes 983048 | tf_op jit(solution)/shard_map/ppermute | solution.py:773
  66.5 45.4 %collective-permute-start.4 = (f32[4,5,8,512]{3,2,1,0:T(8,128)S(1)}, f32[4,5,8,512]{3,2,1,0:T(8,128)S(1)}, u32[]{:S(2)}, u32[]{:S(2)}) collective-permute-start(f32[4,5,8,512]{3,2,1,0:T(8,128)S(1)} %pad_maximum_fusion.3), channel_id=1, source_target_pairs={{0,6},{2,4},{4,2},{6,0},{1,7},{3,5},{5,3},{7,1},{8,14},{10,12},{12... | collective-permute-start | bytes 983048 | tf_op jit(solution)/shard_map/ppermute | solution.py:773
  111.9 14.1 %collective-permute-start.5 = (f32[4,5,8,512]{3,2,1,0:T(8,128)S(1)}, f32[4,5,8,512]{3,2,1,0:T(8,128)S(1)}, u32[]{:S(2)}, u32[]{:S(2)}) collective-permute-start(f32[4,5,8,512]{3,2,1,0:T(8,128)S(1)} %get-tuple-element.61), channel_id=1, source_target_pairs={{0,4},{2,6},{4,0},{6,2},{1,5},{3,7},{5,1},{7,3},{8,12},{10,14},{12... | collective-permute-start | bytes 983048 | tf_op jit(solution)/shard_map/ppermute | solution.py:773
  126.0 7.2 %copy-start.15 = (f32[1,5,5]{2,0,1:T(1,128)S(1)}, f32[1,5,5]{2,0,1:T(1,128)}, u32[]{:S(2)}) copy-start(f32[1,5,5]{2,0,1:T(1,128)} %param.19) | copy-start | bytes 304
  126.0 7.8 %copy-start.16 = (f32[1,5,5]{2,0,1:T(1,128)S(1)}, f32[1,5,5]{2,0,1:T(1,128)}, u32[]{:S(2)}) copy-start(f32[1,5,5]{2,0,1:T(1,128)} %param.20) | copy-start | bytes 304
  126.0 8.4 %copy-start.12 = (f32[1,10,10]{2,0,1:T(1,128)S(1)}, f32[1,10,10]{2,0,1:T(1,128)}, u32[]{:S(2)}) copy-start(f32[1,10,10]{2,0,1:T(1,128)} %param.21) | copy-start | bytes 1204
  126.0 9.0 %copy-start.13 = (f32[1,10,10]{2,0,1:T(1,128)S(1)}, f32[1,10,10]{2,0,1:T(1,128)}, u32[]{:S(2)}) copy-start(f32[1,10,10]{2,0,1:T(1,128)} %param.22) | copy-start | bytes 1204
  126.0 9.6 %copy-start.14 = (f32[1,10,10]{2,0,1:T(1,128)S(1)}, f32[1,10,10]{2,0,1:T(1,128)}, u32[]{:S(2)}) copy-start(f32[1,10,10]{2,0,1:T(1,128)} %param.23) | copy-start | bytes 1204
  126.0 15.8 %copy-start = (f32[1,320,320]{2,1,0:T(8,128)S(1)}, f32[1,320,320]{2,1,0:T(8,128)}, u32[]{:S(2)}) copy-start(f32[1,320,320]{2,1,0:T(8,128)} %param.18) | copy-start | bytes 1228804
  126.0 106.5 %all-to-all-start.1 = ((f32[48,5,8,512]{3,2,1,0:T(8,128)}), f32[48,5,8,512]{3,2,1,0:T(8,128)}, u32[]{:S(2)}, u32[]{:S(2)}) async-start(f32[48,5,8,512]{3,2,1,0:T(8,128)} %bitcast.7), calls=%async_computation.1 | async-start | bytes 7864320 | tf_op jit(solution)/shard_map/all_to_all | solution.py:768
  137.6 4.2 %collective-permute-start.9 = (f32[5,16,128]{2,1,0:T(8,128)}, f32[5,16,128]{2,1,0:T(8,128)S(1)}, u32[]{:S(2)}, u32[]{:S(2)}) collective-permute-start(f32[5,16,128]{2,1,0:T(8,128)} %pack.1.refs_0_), channel_id=1, source_target_pairs={{0,1},{1,0},{2,3},{3,2},{4,5},{5,4},{6,7},{7,6},{8,9},{9,8},{10,11... | collective-permute-start | bytes 122888 | tf_op jit(solution)/shard_map/ppermute | solution.py:572
  141.8 0.8 copy-start.2
  143.8 6.1 %copy-start.3 = (bf16[320,240]{1,0:T(8,128)(2,1)}, bf16[320,240]{1,0:T(8,128)(2,1)S(1)}, u32[]{:S(2)}) copy-start(bf16[320,240]{1,0:T(8,128)(2,1)S(1)} %get-tuple-element.97.inverse_ref) | copy-start | bytes 460804
  143.8 6.0 %copy-start.5 = (bf16[320,48]{1,0:T(8,128)(2,1)}, bf16[320,48]{1,0:T(8,128)(2,1)S(1)}, u32[]{:S(2)}) copy-start(bf16[320,48]{1,0:T(8,128)(2,1)S(1)} %get-tuple-element.101.refs_1_) | copy-start | bytes 92164
  143.9 6.0 %copy-start.7 = (f32[2,10,120]{2,1,0:T(8,128)}, f32[2,10,120]{2,1,0:T(8,128)S(1)}, u32[]{:S(2)}) copy-start(f32[2,10,120]{2,1,0:T(8,128)S(1)} %get-tuple-element.88.refs_1_) | copy-start | bytes 28804
  149.9 6.4 %collective-permute-start.10 = (f32[16,2048]{1,0:T(8,128)S(1)}, f32[16,2048]{1,0:T(8,128)S(1)}, u32[]{:S(2)}, u32[]{:S(2)}) collective-permute-start(f32[16,2048]{1,0:T(8,128)S(1)} %edge.1.refs_0_), channel_id=1, source_target_pairs={{0,1},{1,0},{2,3},{3,2},{4,5},{5,4},{6,7},{7,6},{8,9},{9,8},{10,11... | collective-permute-start | bytes 393224 | tf_op jit(solution)/shard_map/ppermute | solution.py:572
  156.2 12.6 %collective-permute-start.6 = (f32[4,5,8,512]{3,2,1,0:T(8,128)S(1)}, f32[4,5,8,512]{3,2,1,0:T(8,128)S(1)}, u32[]{:S(2)}, u32[]{:S(2)}) collective-permute-start(f32[4,5,8,512]{3,2,1,0:T(8,128)S(1)} %get-tuple-element.65), channel_id=1, source_target_pairs={{0,8},{8,0},{16,24},{24,16},{1,9},{9,1},{17,25},{25,17},{2,10},{10... | collective-permute-start | bytes 983048 | tf_op jit(solution)/shard_map/ppermute | solution.py:773
  166.8 15.8 %collective-permute-start.7 = (f32[4,5,8,512]{3,2,1,0:T(8,128)S(1)}, f32[4,5,8,512]{3,2,1,0:T(8,128)S(1)}, u32[]{:S(2)}, u32[]{:S(2)}) collective-permute-start(f32[4,5,8,512]{3,2,1,0:T(8,128)S(1)} %get-tuple-element.66), channel_id=1, source_target_pairs={{0,16},{8,24},{16,0},{24,8},{1,17},{9,25},{17,1},{25,9},{2,18},{10... | collective-permute-start | bytes 983048 | tf_op jit(solution)/shard_map/ppermute | solution.py:773
  167.4 28.4 %collective-permute-start.8 = (f32[4,5,8,512]{3,2,1,0:T(8,128)S(1)}, f32[4,5,8,512]{3,2,1,0:T(8,128)S(1)}, u32[]{:S(2)}, u32[]{:S(2)}) collective-permute-start(f32[4,5,8,512]{3,2,1,0:T(8,128)S(1)} %get-tuple-element.67), channel_id=1, source_target_pairs={{0,24},{8,16},{16,8},{24,0},{1,25},{9,17},{17,9},{25,1},{2,26},{10... | collective-permute-start | bytes 983048 | tf_op jit(solution)/shard_map/ppermute | solution.py:773
  198.2 45.7 %collective-permute-start.11 = (f32[4,5,8,512]{3,2,1,0:T(8,128)}, f32[4,5,8,512]{3,2,1,0:T(8,128)S(1)}, u32[]{:S(2)}, u32[]{:S(2)}) collective-permute-start(f32[4,5,8,512]{3,2,1,0:T(8,128)} %pad_maximum_fusion.5), channel_id=1, source_target_pairs={{0,2},{2,0},{4,6},{6,4},{1,3},{3,1},{5,7},{7,5},{8,10},{10,8},{12,... | collective-permute-start | bytes 983048 | tf_op jit(solution)/shard_map/ppermute | solution.py:773
  198.3 45.6 %collective-permute-start.12 = (f32[4,5,8,512]{3,2,1,0:T(8,128)}, f32[4,5,8,512]{3,2,1,0:T(8,128)S(1)}, u32[]{:S(2)}, u32[]{:S(2)}) collective-permute-start(f32[4,5,8,512]{3,2,1,0:T(8,128)} %pad_maximum_fusion.6), channel_id=1, source_target_pairs={{0,4},{2,6},{4,0},{6,2},{1,5},{3,7},{5,1},{7,3},{8,12},{10,14},{12... | collective-permute-start | bytes 983048 | tf_op jit(solution)/shard_map/ppermute | solution.py:773
  202.8 45.5 %collective-permute-start.13 = (f32[4,5,8,512]{3,2,1,0:T(8,128)}, f32[4,5,8,512]{3,2,1,0:T(8,128)S(1)}, u32[]{:S(2)}, u32[]{:S(2)}) collective-permute-start(f32[4,5,8,512]{3,2,1,0:T(8,128)} %pad_maximum_fusion.7), channel_id=1, source_target_pairs={{0,6},{2,4},{4,2},{6,0},{1,7},{3,5},{5,3},{7,1},{8,14},{10,12},{12... | collective-permute-start | bytes 983048 | tf_op jit(solution)/shard_map/ppermute | solution.py:773
  232.5 0.7 copy-start.8
  238.0 10.3 %copy-start.10 = (s32[2]{0:T(128)S(1)}, s32[2]{0:T(128)}, u32[]{:S(2)}) copy-start(s32[2]{0:T(128)} %copy-done.9) | copy-start | bytes 28
  238.0 13.5 %copy-start.4 = (bf16[320,240]{1,0:T(8,128)(2,1)S(1)}, bf16[320,240]{1,0:T(8,128)(2,1)}, u32[]{:S(2)}) copy-start(bf16[320,240]{1,0:T(8,128)(2,1)} %copy-done.3) | copy-start | bytes 460804
  249.9 5.1 %collective-permute-start.14 = (f32[16,2048]{1,0:T(8,128)S(1)}, f32[16,2048]{1,0:T(8,128)S(1)}, u32[]{:S(2)}, u32[]{:S(2)}) collective-permute-start(f32[16,2048]{1,0:T(8,128)S(1)} %get-tuple-element.100), channel_id=1, source_target_pairs={{0,1},{1,0},{2,3},{3,2},{4,5},{5,4},{6,7},{7,6},{8,9},{9,8},{10,11... | collective-permute-start | bytes 393224 | tf_op jit(solution)/shard_map/ppermute | solution.py:580
  251.5 3.5 %copy-start.6 = (bf16[320,48]{1,0:T(8,128)(2,1)S(1)}, bf16[320,48]{1,0:T(8,128)(2,1)}, u32[]{:S(2)}) copy-start(bf16[320,48]{1,0:T(8,128)(2,1)} %copy-done.5) | copy-start | bytes 92164

commit v5 on v4

--- a/solution.py
+++ b/solution.py
@@ -392,14 +392,35 @@
         @pl.when(pl.program_id(0) == pl.num_programs(0) - 1)
         def _():
             for d, send_ref in enumerate(send_refs, 1):
+                pieces = []
                 for part in range(2):
                     at = part * pushes + d * width
-                    send_ref[part * width : (part + 1) * width] = sum_ref[at : at + width]
-                at = 2 * pushes
-                send_ref[2 * width : 2 * width + 2] = sum_ref[at : at + 2]
-                rest = send_ref.shape[0] - 2 * width - 2
-                if rest:
-                    send_ref[2 * width + 2 :] = jnp.zeros((rest, lanes), jnp.float32)
+                    pieces.append(sum_ref[at : at + width])
+                pieces.append(sum_ref[2 * pushes : 2 * pushes + 2])
+                pack_rows(send_ref, jnp.concatenate(pieces, axis=0))
+
+
+def folded(rows, modes):
+    return rows == 12 and modes % 256 == 0 and modes <= 8 * NB
+
+
+def travelling(rows, modes):
+    if folded(rows, modes):
+        return jax.ShapeDtypeStruct((rows - 4, modes + modes // 2), jnp.float32)
+    return jax.ShapeDtypeStruct((padded(rows, 8), modes), jnp.float32)
+
+
+def pack_rows(out_ref, value):
+    rows, modes = value.shape
+    if folded(rows, modes):
+        half = modes // 2
+        out_ref[:, :modes] = value[: rows - 4]
+        out_ref[:4, modes:] = value[rows - 4 :, :half]
+        out_ref[4:8, modes:] = value[rows - 4 :, half:]
+        return
+    out_ref[:rows] = value
+    if out_ref.shape[0] > rows:
+        out_ref[rows:] = jnp.zeros((out_ref.shape[0] - rows, modes), jnp.float32)
 
 
 def absorb_body(width, in_ref, *refs):
@@ -429,7 +450,7 @@
     step = rows // steps
     grid_spec = pl.BlockSpec((2, variables, step, modes), lambda r: (0, 0, r, 0))
     _, _, freqs, lanes = blocks[0].shape
-    sent = jax.ShapeDtypeStruct((padded(2 * width + 2, 8), modes), jnp.float32)
+    sent = travelling(2 * width + 2, modes)
     operands = blocks + [keep, ahead, adjoint_modes if apart else in_hbm(adjoint_modes), before]
     in_specs = [
         whole(block)
@@ -479,7 +500,7 @@
 
 def solve(side, upstream, keep, inverse):
     _, variables, heights, modes = upstream.shape
-    lanes = min(2 * NB, modes)
+    lanes = min(4 * NB, modes)
     spec = pl.BlockSpec((2, variables, heights, lanes), lambda i: (0, 0, 0, i))
     return pl.pallas_call(
         solve_body,
@@ -492,7 +513,7 @@
         ],
         out_specs=spec,
         out_shape=jax.ShapeDtypeStruct(upstream.shape, jnp.float32),
-        compiler_params=params(24),
+        compiler_params=params(32),
         name="solve",
     )(side, in_hbm(upstream), keep, inverse)
 
@@ -506,7 +527,7 @@
 
 def solve_more(side, before, inverse):
     _, variables, rows, modes = side.shape
-    lanes = min(2 * NB, modes)
+    lanes = min(4 * NB, modes)
     spec = pl.BlockSpec(before.shape[:3] + (lanes,), lambda i: (0, 0, 0, i))
     return pl.pallas_call(
         solve_more_body,
@@ -518,27 +539,35 @@
         ],
         out_specs=spec,
         out_shape=jax.ShapeDtypeStruct(before.shape, jnp.float32),
-        compiler_params=params(24),
+        compiler_params=params(32),
         name="solve_more",
     )(side, before, inverse)
 
 
-def finish_body(walls, width, solved_ref, sum_ref, square_ref, *refs):
-    others, (columns_ref, out_ref, shift_ref) = refs[: walls - 1], refs[walls - 1 :]
+def finish_body(walls, width, fold, solved_ref, sum_ref, square_ref, *refs):
+    each = 2 if fold else 1
+    other_refs, (columns_ref, out_ref, shift_ref) = refs[: each * (walls - 1)], refs[-3:]
     _, variables, heights, lanes = out_ref.shape
     spare = columns_ref.shape[1] // 3 - width
     pushes = walls * width
+    others = [ref[...] for ref in other_refs]
+    if fold:
+        first = pl.program_id(0) == 0
+        others = [
+            jnp.concatenate([rows, jnp.where(first, rest[:4], rest[4:8])], axis=0)
+            for rows, rest in zip(others[::2], others[1::2])
+        ]
     for part in range(2):
         push = sum_ref[part * pushes : part * pushes + width]
-        for ref in others:
-            push = push + ref[part * width : (part + 1) * width]
+        for other in others:
+            push = push + other[part * width : (part + 1) * width]
         if spare:
             push = jnp.concatenate([push, jnp.zeros((spare, lanes), jnp.float32)], axis=0)
         moved = table_times(columns_ref[...], push)
         out_ref[part] = solved_ref[part] - moved.reshape(variables, heights, lanes)
     both = sum_ref[2 * pushes : 2 * pushes + 2]
-    for ref in others:
-        both = both + ref[2 * width : 2 * width + 2]
+    for other in others:
+        both = both + other[2 * width : 2 * width + 2]
     squares = square_ref[:1]
     weight = squares + epsilon
     shift_ref[0:1] = both[1:2] / weight
@@ -547,23 +576,33 @@
 
 def finish(solved, sums, squares, others, columns, width):
     _, variables, heights, modes = solved.shape
-    lanes = min(2 * NB, modes)
+    fold = folded(2 * width + 2, modes)
+    lanes = modes // 2 if fold else min(4 * NB, modes)
+
+    def rows_spec(rows):
+        return pl.BlockSpec((rows, lanes), lambda i: (0, i))
+
     spec = pl.BlockSpec((2, variables, heights, lanes), lambda i: (0, 0, 0, i))
-    rows = [sums, squares] + others
-    return pl.pallas_call(
-        functools.partial(finish_body, len(others) + 1, width),
+    operands, in_specs = [solved, sums, squares], [spec]
+    in_specs += [rows_spec(part.shape[0]) for part in (sums, squares)]
+    for part in others:
+        operands.append(part)
+        in_specs.append(rows_spec(part.shape[0]))
+        if fold:
+            operands.append(part)
+            in_specs.append(pl.BlockSpec((8, lanes), lambda i: (0, 2)))
+    return pl.pallas_call(
+        functools.partial(finish_body, len(others) + 1, width, fold),
         grid=(modes // lanes,),
-        in_specs=[spec]
-        + [pl.BlockSpec((part.shape[0], lanes), lambda i: (0, i)) for part in rows]
-        + [whole(columns)],
+        in_specs=in_specs + [whole(columns)],
         out_specs=[spec, pl.BlockSpec((2, lanes), lambda i: (0, i))],
         out_shape=[
             jax.ShapeDtypeStruct(solved.shape, jnp.float32),
             jax.ShapeDtypeStruct((2, modes), jnp.float32),
         ],
-        compiler_params=params(),
+        compiler_params=params(32),
         name="finish",
-    )(solved, *rows, columns)
+    )(*operands, columns)
 
 
 def around(block, axis):
@@ -787,16 +826,6 @@
         arrived = swap(regroup(swap(sent, "freq")), "span", set(range(spans)) - far)
     main = exchange(main)
 
-    if apart:
-        main, arrived = lax.optimization_barrier((main, arrived))
-        arrived = swap(arrived, "span", far)
-    size = edge_at // devices
-    shape = main.shape
-    main = nonlinear(main.reshape((devices, size) + shape[1:]), coefficients, transforms)
-    main = main.reshape(shape)
-    if apart:
-        main, arrived[spans // 2] = lax.optimization_barrier((main, arrived[spans // 2]))
-    main = exchange(main)
     inverse = slab_inverse[0]
     parts = (lower_coupling, upper_coupling, reduced_lower, reduced_upper, reduced_pivot)
     packed = around(pack(parts), "wall")
@@ -810,11 +839,20 @@
         amplitudes, upstream, keep, turned, ahead, back, edges, width, cuts
     )
     if apart:
+        held = (arrived[1], arrived[spans // 2], adjoint_modes, sums, squares)
+        held = lax.optimization_barrier(held)
+        arrived[1], arrived[spans // 2], adjoint_modes, sums, squares = held
+        arrived = swap(arrived, "span", far)
+    size = edge_at // devices
+    shape = main.shape
+    main = nonlinear(main.reshape((devices, size) + shape[1:]), coefficients, transforms)
+    main = main.reshape(shape)
+    if apart:
+        main, arrived = lax.optimization_barrier((main, arrived))
+    main = exchange(main)
+    if apart:
         forced = nonlinear_apart(place, arrived, coefficients, transforms)
         returned = regroup(swap(forced, "freq"))
-        held = (returned, split, last, edge_columns, rows, adjoint_modes, sums, squares)
-        held = lax.optimization_barrier(held)
-        returned, split, last, edge_columns, rows, adjoint_modes, sums, squares = held
         returned = swap(returned, "span")
 
     sends = walls - 1

time: 260 us -> 257 us (0.988)
  waiting for transfers between devices: 141 us -> 118 us
  starting transfers between devices: 48.9 us -> 64.3 us
  local copies, waits for them, and re-layouts: 4.71 us -> 8.38 us
    ppermute x12, waiting for transfers between devices: 107 us -> 48.3 us  [swap(): lax.ppermute(block, axis, [(at, at ^ i) for at in range(count)])]
    all_to_all x2, waiting for transfers between devices: 29.2 us -> 64.4 us  [exchange(): return lax.all_to_all(block, axes, split_axis=0, concat_axis=0, tiled=True)]
    ppermute x12, starting transfers between devices: 30.6 us -> 45.6 us  [swap(): lax.ppermute(block, axis, [(at, at ^ i) for at in range(count)])]
    slice x8, local copies, waits for them, and re-layouts: 0.18 us -> 3.83 us  [regroup(): block[j]]
  transfers between devices with their start and end apart: 17 -> 17, of which waited for: 11 -> 10; matrix products, arithmetic and copies ran while one was open for 2% -> 4% of each run, Pallas kernels for 20% -> 20%
where the time goes in v5:
time: 257 us; the launch traced here: 256 us
  waiting for transfers between devices  118 us (46%)
  starting transfers between devices  64.3 us (25%)
  Pallas kernels  60.8 us (24%)
  local copies, waits for them, and re-layouts  8.38 us (3%)
  other arithmetic  4.02 us (2%)
    all_to_all x2, waiting for transfers between devices, exchange(): return lax.all_to_all(block, axes, split_axis=0, concat_axis=0, tiled=True)  64.4 us
    ppermute x12, waiting for transfers between devices, swap(): lax.ppermute(block, axis, [(at, at ^ i) for at in range(count)])  48.3 us
    ppermute x12, starting transfers between devices, swap(): lax.ppermute(block, axis, [(at, at ^ i) for at in range(count)])  45.6 us
    all_to_all x2, starting transfers between devices, exchange(): return lax.all_to_all(block, axes, split_axis=0, concat_axis=0, tiled=True)  14 us
    pallas_call x1, Pallas kernels, nonlinear(): pl.pallas_call(nonlinear_body, grid=(points,), in_specs=[pl.BlockSpec(mem...  12 us
    pallas_call x1, Pallas kernels, base(): pl.pallas_call(functools.partial(base_body, cuts, walls, width), grid=(mo...  10.6 us
    pallas_call x2, Pallas kernels, absorb(): pl.pallas_call(body, grid=(steps,), in_specs=in_specs, out_specs=[grid_sp...  6.26 us
    pallas_call x1, Pallas kernels, edge(): pl.pallas_call(functools.partial(edge_body, width), grid=(modes // NB,),...  6.01 us
  transfers between devices with their start and end apart: 17, of which 10 were waited for; matrix products, arithmetic and copies ran while one was open for 4% of the time, Pallas kernels for 20%

profile of v5, /device:TPU:10, one launch (start us, length us, event | category | flops | bytes accessed | tf_op | source)
XLA Modules:
  0.0 256.4 jit_solution(9725874367512126696)
XLA Ops:
  0.6 3.9 %prepare.1 = f32[48,5,8,512]{3,2,1,0:T(8,128)} custom-call(f32[2,5,64,2048]{3,2,1,0:T(8,128)} %x_ref.4, s32[2048]{0:T(1024)} %refs_4_.3), custom_call_target="tpu_custom_call" | custom-call | tf_op jit(solution)/shard_map/prepare/pallas_call | solution.py:82
  4.6 6.4 %all-to-all-start = ((f32[48,5,8,512]{3,2,1,0:T(8,128)}), f32[48,5,8,512]{3,2,1,0:T(8,128)}, u32[]{:S(2)}, u32[]{:S(2)}) async-start(f32[48,5,8,512]{3,2,1,0:T(8,128)} %prepare.1), calls=%async_computation | async-start | bytes 7864320 | tf_op jit(solution)/shard_map/all_to_all | solution.py:807
  10.9 0.0 copy-start.17
  10.9 0.0 copy-start.13
  11.0 0.0 copy-start.14
  11.0 0.0 copy-start.15
  11.0 0.0 copy-start
  11.0 0.1 pad_add_fusion.place_ref
  11.1 4.1 %prepare_apart.1 = (f32[4,5,8,512]{3,2,1,0:T(8,128)S(1)}, f32[4,5,8,512]{3,2,1,0:T(8,128)}, f32[4,5,8,512]{3,2,1,0:T(8,128)}, f32[4,5,8,512]{3,2,1,0:T(8,128)}) custom-call(s32[2]{0:T(128)S(1)} %pad_add_fusion.place_ref, f32[2,5,64,2048]{3,2,1,0:T(8,128)} %x_ref.4, s32[2048]{0:T(1024)S(1)} %copy-done.1), custom_call_target="tpu_custom_call" | custom-call | tf_op jit(solution)/shard_map/prepare_apart/pallas_call | solution.py:118
  15.2 0.2 collective-permute-start
  15.4 0.6 copy.18.refs_0_
  16.0 0.6 copy.19.refs_1_
  16.6 0.6 copy.20.refs_2_
  17.2 0.6 copy.21.refs_3_
  17.8 0.6 copy.22.refs_4_
  18.4 1.4 pack.1.refs_0_
  19.7 1.5 collective-permute-start.4
  21.3 0.6 collective-permute-start.1
  21.8 0.8 collective-permute-start.2
  22.7 1.3 collective-permute-done.4.refs_1_
  24.0 0.8 copy-done.2
  24.7 1.2 constants.1
  26.0 0.0 copy-start.7
  26.0 6.0 %edge.1.refs_0_ = f32[16,2048]{1,0:T(8,128)S(1)} custom-call(f32[2,5,64,2048]{3,2,1,0:T(8,128)} %x_ref.4, s32[2048]{0:T(1024)S(1)} %copy-done.1, bf16[16,960]{1,0:T(8,128)(2,1)S(1)} %get-tuple-element.52.rows_ref), custom_call_target="tpu_custom_call" | custom-call | tf_op jit(solution)/shard_map/edge/pallas_call | solution.py:294
  32.0 1.5 collective-permute-start.5
  33.5 0.7 fusion.4
  34.2 2.8 %collective-permute-done.5.refs_1_ = f32[16,2048]{1,0:T(8,128)S(1)} collective-permute-done((f32[16,2048]{1,0:T(8,128)S(1)}, f32[16,2048]{1,0:T(8,128)S(1)}, u32[]{:S(2)}, u32[]{:S(2)}) %collective-permute-start.5) | collective-permute-done | bytes 131104 | tf_op jit(solution)/shard_map/ppermute | solution.py:611
  37.0 10.6 %base.1 = (f32[2,5,48,2048]{3,2,1,0:T(8,128)}, f32[2,5,16,2048]{3,2,1,0:T(8,128)S(1)}, f32[24,2048]{1,0:T(8,128)S(1)}, f32[8,2048]{1,0:T(8,128)S(1)}) custom-call(f32[2,5,64,2048]{3,2,1,0:T(8,128)} %x_ref.4, f32[2,5,64,2048]{3,2,1,0:T(8,128)} %up_ref.3, s32[2048]{0:T(1024)S(1)} %copy-done.1, bf16[320,960]{1,0:T(8,128)(2,1)S(1)} %get-tuple-element.49.turned_ref, ...), custom_call_target="tpu_custom_call" | custom-call | tf_op jit(solution)/shard_map/base/pallas_call | solution.py:350
  47.7 0.0 collective-permute-done
  47.7 1.0 fusion.5
  48.7 1.0 fusion.6
  49.7 1.0 fusion.7
  50.8 16.8 %collective-permute-start.3 = (f32[4,5,8,512]{3,2,1,0:T(8,128)S(1)}, f32[4,5,8,512]{3,2,1,0:T(8,128)S(1)}, u32[]{:S(2)}, u32[]{:S(2)}) collective-permute-start(f32[4,5,8,512]{3,2,1,0:T(8,128)S(1)} %pad_maximum_fusion.1), channel_id=1, source_target_pairs={{0,2},{2,0},{4,6},{6,4},{1,3},{3,1},{5,7},{7,5},{8,10},{10,8},{12,... | collective-permute-start | bytes 983048 | tf_op jit(solution)/shard_map/ppermute | solution.py:812
  67.6 0.8 pad_maximum_fusion.3
  68.4 2.5 collective-permute-start.7
  70.9 0.8 pad_maximum_fusion.2
  71.7 11.9 %collective-permute-done.3.refs_1_ = f32[4,5,8,512]{3,2,1,0:T(8,128)S(1)} collective-permute-done((f32[4,5,8,512]{3,2,1,0:T(8,128)S(1)}, f32[4,5,8,512]{3,2,1,0:T(8,128)S(1)}, u32[]{:S(2)}, u32[]{:S(2)}) %collective-permute-start.3) | collective-permute-done | bytes 327712 | tf_op jit(solution)/shard_map/ppermute | solution.py:812
  83.6 1.4 collective-permute-start.6
  85.0 25.2 %all-to-all-done = f32[48,5,8,512]{3,2,1,0:T(8,128)} async-done(((f32[48,5,8,512]{3,2,1,0:T(8,128)}), f32[48,5,8,512]{3,2,1,0:T(8,128)}, u32[]{:S(2)}, u32[]{:S(2)}) %all-to-all-start) | async-done | bytes 3932192 | tf_op jit(solution)/shard_map/all_to_all | solution.py:807
  110.2 12.0 %nonlinear.1 = f32[16,3,5,8,512]{4,3,2,1,0:T(8,128)} custom-call(f32[25,5]{1,0:T(8,128)S(1)} %reshape.20.q_ref, f32[16,3,5,8,512]{4,3,2,1,0:T(8,128)} %bitcast.2.in_ref, bf16[256,768]{1,0:T(8,128)(2,1)} %constant.19.clone.refs_0_.refs_4_, bf16[1536,256]{1,0:T(8,128)(2,1)} %constant.20.clone.refs_1_.refs_5_, bf16[768,512]{1,0:T(8,128)(2,1)} %constant.21.clone.refs_2_.refs_6_, ...), custom_call_target="tpu_custom_call" | custom-call | flops 4529848320 | bytes 7864320 | tf_op jit(solution)/shard_map/nonlinear/pallas_call | solution.py:214
  122.2 2.0 collective-permute-done.6.refs_2_
  124.2 7.7 %all-to-all-start.1 = ((f32[48,5,8,512]{3,2,1,0:T(8,128)}), f32[48,5,8,512]{3,2,1,0:T(8,128)}, u32[]{:S(2)}, u32[]{:S(2)}) async-start(f32[48,5,8,512]{3,2,1,0:T(8,128)} %bitcast.7), calls=%async_computation.1 | async-start | bytes 7864320 | tf_op jit(solution)/shard_map/all_to_all | solution.py:807
  131.9 4.8 %nonlinear_apart.1 = (f32[4,5,8,512]{3,2,1,0:T(8,128)S(1)}, f32[4,5,8,512]{3,2,1,0:T(8,128)S(1)}, f32[4,5,8,512]{3,2,1,0:T(8,128)S(1)}, f32[4,5,8,512]{3,2,1,0:T(8,128)S(1)}) custom-call(s32[2]{0:T(128)S(1)} %pad_add_fusion.place_ref, f32[25,5]{1,0:T(8,128)S(1)} %reshape.20.q_ref, f32[4,5,8,512]{3,2,1,0:T(8,128)S(1)} %pad_maximum_fusion.refs_0_, ...), custom_call_target="tpu_custom_call" | custom-call | flops 1509949440 | bytes 2621440 | tf_op jit(solution)/shard_map/nonlinear_apart/pallas_call | solution.py:255
  136.7 0.2 collective-permute-start.8
  136.9 0.5 collective-permute-start.9
  137.5 1.3 collective-permute-start.10
  138.7 20.8 %collective-permute-done.9 = f32[4,5,8,512]{3,2,1,0:T(8,128)S(1)} collective-permute-done((f32[4,5,8,512]{3,2,1,0:T(8,128)S(1)}, f32[4,5,8,512]{3,2,1,0:T(8,128)S(1)}, u32[]{:S(2)}, u32[]{:S(2)}) %collective-permute-start.9) | collective-permute-done | bytes 327712 | tf_op jit(solution)/shard_map/ppermute | solution.py:812
  159.6 8.6 %collective-permute-done.10 = f32[4,5,8,512]{3,2,1,0:T(8,128)S(1)} collective-permute-done((f32[4,5,8,512]{3,2,1,0:T(8,128)S(1)}, f32[4,5,8,512]{3,2,1,0:T(8,128)S(1)}, u32[]{:S(2)}, u32[]{:S(2)}) %collective-permute-start.10) | collective-permute-done | bytes 327712 | tf_op jit(solution)/shard_map/ppermute | solution.py:812
  168.3 0.8 pad_maximum_fusion.5
  169.0 18.9 %collective-permute-start.11 = (f32[4,5,8,512]{3,2,1,0:T(8,128)}, f32[4,5,8,512]{3,2,1,0:T(8,128)S(1)}, u32[]{:S(2)}, u32[]{:S(2)}) collective-permute-start(f32[4,5,8,512]{3,2,1,0:T(8,128)} %pad_maximum_fusion.5), channel_id=1, source_target_pairs={{0,2},{2,0},{4,6},{6,4},{1,3},{3,1},{5,7},{7,5},{8,10},{10,8},{12,... | collective-permute-start | bytes 983048 | tf_op jit(solution)/shard_map/ppermute | solution.py:812
  187.9 0.8 pad_maximum_fusion.6
  188.7 1.9 collective-permute-start.12
  190.5 0.8 pad_maximum_fusion.7
  191.3 0.6 collective-permute-start.13
  191.9 39.3 %all-to-all-done.1.in_ref = f32[48,5,8,512]{3,2,1,0:T(8,128)} async-done(((f32[48,5,8,512]{3,2,1,0:T(8,128)}), f32[48,5,8,512]{3,2,1,0:T(8,128)}, u32[]{:S(2)}, u32[]{:S(2)}) %all-to-all-start.1) | async-done | bytes 3932192 | tf_op jit(solution)/shard_map/all_to_all | solution.py:807
  231.2 0.7 copy-done.8
  231.9 4.8 %absorb.1 = (f32[2,5,48,2048]{3,2,1,0:T(8,128)S(1)}, f32[24,2048]{1,0:T(8,128)S(1)}) custom-call(f32[48,5,8,512]{3,2,1,0:T(8,128)} %all-to-all-done.1.in_ref, s32[2048]{0:T(1024)S(1)} %copy-done.1, f32[2,10,120]{2,1,0:T(8,128)S(1)} %copy-done.8, f32[2,5,48,2048]{3,2,1,0:T(8,128)} %get-tuple-element.71.refs_2_, f32[24,2048]{1,0:T(8,128)S(1)} %get-tuple-element.72.refs_3_), custom_call_target="tpu_custom_call" | custom-call | tf_op jit(solution)/shard_map/absorb/pallas_call | solution.py:472
  236.7 5.4 %solve.1.before_ref = f32[2,5,64,2048]{3,2,1,0:T(8,128)S(1)} custom-call(f32[2,5,48,2048]{3,2,1,0:T(8,128)S(1)} %get-tuple-element.73.side_ref, f32[2,5,64,2048]{3,2,1,0:T(8,128)} %up_ref.3, s32[2048]{0:T(1024)S(1)} %copy-done.1, bf16[320,960]{1,0:T(8,128)(2,1)S(1)} %get-tuple-element.74.inverse_ref), custom_call_target="tpu_custom_call" | custom-call | tf_op jit(solution)/shard_map/solve/pallas_call | solution.py:505
  242.1 4.9 %collective-permute-done.13.refs_3_ = f32[4,5,8,512]{3,2,1,0:T(8,128)S(1)} collective-permute-done((f32[4,5,8,512]{3,2,1,0:T(8,128)}, f32[4,5,8,512]{3,2,1,0:T(8,128)S(1)}, u32[]{:S(2)}, u32[]{:S(2)}) %collective-permute-start.13) | collective-permute-done | bytes 327712 | tf_op jit(solution)/shard_map/ppermute | solution.py:812
  247.0 1.5 absorb_apart.1
  248.5 1.6 collective-permute-start.14
  250.1 1.8 solve_more.1.solved_ref
  251.9 1.3 collective-permute-done.14.refs_0_.refs_1_
  253.1 3.2 %finish.1 = (f32[2,5,64,2048]{3,2,1,0:T(8,128)}, f32[2,2048]{1,0:T(2,128)}) custom-call(f32[2,5,64,2048]{3,2,1,0:T(8,128)S(1)} %solve_more.1.solved_ref, f32[24,2048]{1,0:T(8,128)S(1)} %get-tuple-element.80.sum_ref, f32[8,2048]{1,0:T(8,128)S(1)} %get-tuple-element.81.square_ref, f32[8,3072]{1,0:T(8,128)S(1)} %collective-permute-done.14.refs_0_.refs_1_, ...), custom_call_target="tpu_custom_call" | custom-call | tf_op jit(solution)/shard_map/finish/pallas_call | solution.py:594
  (42 shorter events, 0.2 us)
Async XLA Ops:
  4.6 6.5 %copy-start.1 = (s32[2048]{0:T(1024)S(1)}, s32[2048]{0:T(1024)}, u32[]{:S(2)}) copy-start(s32[2048]{0:T(1024)} %refs_4_.3) | copy-start | bytes 24580
  4.6 105.7 %all-to-all-start = ((f32[48,5,8,512]{3,2,1,0:T(8,128)}), f32[48,5,8,512]{3,2,1,0:T(8,128)}, u32[]{:S(2)}, u32[]{:S(2)}) async-start(f32[48,5,8,512]{3,2,1,0:T(8,128)} %prepare.1), calls=%async_computation | async-start | bytes 7864320 | tf_op jit(solution)/shard_map/all_to_all | solution.py:807
  10.9 4.5 %copy-start.16 = (f32[1,5,5]{2,0,1:T(1,128)S(1)}, f32[1,5,5]{2,0,1:T(1,128)}, u32[]{:S(2)}) copy-start(f32[1,5,5]{2,0,1:T(1,128)} %param.19) | copy-start | bytes 304
  10.9 5.0 %copy-start.17 = (f32[1,5,5]{2,0,1:T(1,128)S(1)}, f32[1,5,5]{2,0,1:T(1,128)}, u32[]{:S(2)}) copy-start(f32[1,5,5]{2,0,1:T(1,128)} %param.20) | copy-start | bytes 304
  10.9 5.6 %copy-start.13 = (f32[1,10,10]{2,0,1:T(1,128)S(1)}, f32[1,10,10]{2,0,1:T(1,128)}, u32[]{:S(2)}) copy-start(f32[1,10,10]{2,0,1:T(1,128)} %param.21) | copy-start | bytes 1204
  11.0 6.2 %copy-start.14 = (f32[1,10,10]{2,0,1:T(1,128)S(1)}, f32[1,10,10]{2,0,1:T(1,128)}, u32[]{:S(2)}) copy-start(f32[1,10,10]{2,0,1:T(1,128)} %param.22) | copy-start | bytes 1204
  11.0 6.8 %copy-start.15 = (f32[1,10,10]{2,0,1:T(1,128)S(1)}, f32[1,10,10]{2,0,1:T(1,128)}, u32[]{:S(2)}) copy-start(f32[1,10,10]{2,0,1:T(1,128)} %param.23) | copy-start | bytes 1204
  11.0 13.0 %copy-start = (f32[1,320,320]{2,1,0:T(8,128)S(1)}, f32[1,320,320]{2,1,0:T(8,128)}, u32[]{:S(2)}) copy-start(f32[1,320,320]{2,1,0:T(8,128)} %param.18) | copy-start | bytes 1228804
  11.1 120.8 %copy-start.9 = (s32[2]{0:T(128)}, s32[2]{0:T(128)S(1)}, u32[]{:S(2)}) copy-start(s32[2]{0:T(128)S(1)} %pad_add_fusion.place_ref) | copy-start | bytes 28
  15.2 18.9 %copy-start.12 = (f32[5,5,5]{2,1,0:T(8,128)S(1)}, f32[5,5,5]{2,1,0:T(8,128)}, u32[]{:S(2)}) copy-start(f32[5,5,5]{2,1,0:T(8,128)} %param.17) | copy-start | bytes 1504
  15.2 32.4 %collective-permute-start = (f32[4,5,8,512]{3,2,1,0:T(8,128)}, f32[4,5,8,512]{3,2,1,0:T(8,128)}, u32[]{:S(2)}, u32[]{:S(2)}) collective-permute-start(f32[4,5,8,512]{3,2,1,0:T(8,128)} %get-tuple-element.46), channel_id=1, source_target_pairs={{0,8},{8,0},{16,24},{24,16},{1,9},{9,1},{17,25},{25,17},{2,10},{10... | collective-permute-start | bytes 983048 | tf_op jit(solution)/shard_map/ppermute | solution.py:812
  19.7 4.2 %collective-permute-start.4 = (f32[5,16,128]{2,1,0:T(8,128)}, f32[5,16,128]{2,1,0:T(8,128)S(1)}, u32[]{:S(2)}, u32[]{:S(2)}) collective-permute-start(f32[5,16,128]{2,1,0:T(8,128)} %pack.1.refs_0_), channel_id=1, source_target_pairs={{0,1},{1,0},{2,3},{3,2},{4,5},{5,4},{6,7},{7,6},{8,9},{9,8},{10,11... | collective-permute-start | bytes 122888 | tf_op jit(solution)/shard_map/ppermute | solution.py:611
  21.3 27.4 %collective-permute-start.1 = (f32[4,5,8,512]{3,2,1,0:T(8,128)}, f32[4,5,8,512]{3,2,1,0:T(8,128)}, u32[]{:S(2)}, u32[]{:S(2)}) collective-permute-start(f32[4,5,8,512]{3,2,1,0:T(8,128)} %get-tuple-element.47), channel_id=1, source_target_pairs={{0,16},{8,24},{16,0},{24,8},{1,17},{9,25},{17,1},{25,9},{2,18},{10... | collective-permute-start | bytes 983048 | tf_op jit(solution)/shard_map/ppermute | solution.py:812
  21.8 27.9 %collective-permute-start.2 = (f32[4,5,8,512]{3,2,1,0:T(8,128)}, f32[4,5,8,512]{3,2,1,0:T(8,128)}, u32[]{:S(2)}, u32[]{:S(2)}) collective-permute-start(f32[4,5,8,512]{3,2,1,0:T(8,128)} %get-tuple-element.48), channel_id=1, source_target_pairs={{0,24},{8,16},{16,8},{24,0},{1,25},{9,17},{17,9},{25,1},{2,26},{10... | collective-permute-start | bytes 983048 | tf_op jit(solution)/shard_map/ppermute | solution.py:812
  24.0 0.8 copy-start.2
  26.0 11.1 %copy-start.3 = (bf16[320,240]{1,0:T(8,128)(2,1)}, bf16[320,240]{1,0:T(8,128)(2,1)S(1)}, u32[]{:S(2)}) copy-start(bf16[320,240]{1,0:T(8,128)(2,1)S(1)} %get-tuple-element.79.inverse_ref) | copy-start | bytes 460804
  26.0 11.1 %copy-start.5 = (bf16[320,48]{1,0:T(8,128)(2,1)}, bf16[320,48]{1,0:T(8,128)(2,1)S(1)}, u32[]{:S(2)}) copy-start(bf16[320,48]{1,0:T(8,128)(2,1)S(1)} %get-tuple-element.83.refs_2_) | copy-start | bytes 92164
  26.0 11.0 %copy-start.7 = (f32[2,10,120]{2,1,0:T(8,128)}, f32[2,10,120]{2,1,0:T(8,128)S(1)}, u32[]{:S(2)}) copy-start(f32[2,10,120]{2,1,0:T(8,128)S(1)} %get-tuple-element.70.refs_1_) | copy-start | bytes 28804
  32.0 5.0 %collective-permute-start.5 = (f32[16,2048]{1,0:T(8,128)S(1)}, f32[16,2048]{1,0:T(8,128)S(1)}, u32[]{:S(2)}, u32[]{:S(2)}) collective-permute-start(f32[16,2048]{1,0:T(8,128)S(1)} %edge.1.refs_0_), channel_id=1, source_target_pairs={{0,1},{1,0},{2,3},{3,2},{4,5},{5,4},{6,7},{7,6},{8,9},{9,8},{10,11... | collective-permute-start | bytes 393224 | tf_op jit(solution)/shard_map/ppermute | solution.py:611
  37.0 13.8 %copy-start.11 = (f32[1,5,8,512]{3,2,1,0:T(8,128)S(1)}, f32[1,5,8,512]{3,2,1,0:T(8,128)}, u32[]{:S(2)}) copy-start(f32[1,5,8,512]{3,2,1,0:T(8,128)} %get-tuple-element.102) | copy-start | bytes 245764
  50.8 32.8 %collective-permute-start.3 = (f32[4,5,8,512]{3,2,1,0:T(8,128)S(1)}, f32[4,5,8,512]{3,2,1,0:T(8,128)S(1)}, u32[]{:S(2)}, u32[]{:S(2)}) collective-permute-start(f32[4,5,8,512]{3,2,1,0:T(8,128)S(1)} %pad_maximum_fusion.1), channel_id=1, source_target_pairs={{0,2},{2,0},{4,6},{6,4},{1,3},{3,1},{5,7},{7,5},{8,10},{10,8},{12,... | collective-permute-start | bytes 983048 | tf_op jit(solution)/shard_map/ppermute | solution.py:812
  68.4 53.8 %collective-permute-start.7 = (f32[4,5,8,512]{3,2,1,0:T(8,128)}, f32[4,5,8,512]{3,2,1,0:T(8,128)S(1)}, u32[]{:S(2)}, u32[]{:S(2)}) collective-permute-start(f32[4,5,8,512]{3,2,1,0:T(8,128)} %pad_maximum_fusion.3), channel_id=1, source_target_pairs={{0,6},{2,4},{4,2},{6,0},{1,7},{3,5},{5,3},{7,1},{8,14},{10,12},{12... | collective-permute-start | bytes 983048 | tf_op jit(solution)/shard_map/ppermute | solution.py:812
  83.6 40.6 %collective-permute-start.6 = (f32[4,5,8,512]{3,2,1,0:T(8,128)}, f32[4,5,8,512]{3,2,1,0:T(8,128)}, u32[]{:S(2)}, u32[]{:S(2)}) collective-permute-start(f32[4,5,8,512]{3,2,1,0:T(8,128)} %pad_maximum_fusion.2), channel_id=1, source_target_pairs={{0,4},{2,6},{4,0},{6,2},{1,5},{3,7},{5,1},{7,3},{8,12},{10,14},{12... | collective-permute-start | bytes 983048 | tf_op jit(solution)/shard_map/ppermute | solution.py:812
  124.2 106.9 %all-to-all-start.1 = ((f32[48,5,8,512]{3,2,1,0:T(8,128)}), f32[48,5,8,512]{3,2,1,0:T(8,128)}, u32[]{:S(2)}, u32[]{:S(2)}) async-start(f32[48,5,8,512]{3,2,1,0:T(8,128)} %bitcast.7), calls=%async_computation.1 | async-start | bytes 7864320 | tf_op jit(solution)/shard_map/all_to_all | solution.py:807
  136.7 2.0 collective-permute-start.8
  136.9 22.7 %collective-permute-start.9 = (f32[4,5,8,512]{3,2,1,0:T(8,128)S(1)}, f32[4,5,8,512]{3,2,1,0:T(8,128)S(1)}, u32[]{:S(2)}, u32[]{:S(2)}) collective-permute-start(f32[4,5,8,512]{3,2,1,0:T(8,128)S(1)} %get-tuple-element.65), channel_id=1, source_target_pairs={{0,16},{8,24},{16,0},{24,8},{1,17},{9,25},{17,1},{25,9},{2,18},{10... | collective-permute-start | bytes 983048 | tf_op jit(solution)/shard_map/ppermute | solution.py:812
  137.5 30.8 %collective-permute-start.10 = (f32[4,5,8,512]{3,2,1,0:T(8,128)S(1)}, f32[4,5,8,512]{3,2,1,0:T(8,128)S(1)}, u32[]{:S(2)}, u32[]{:S(2)}) collective-permute-start(f32[4,5,8,512]{3,2,1,0:T(8,128)S(1)} %get-tuple-element.66), channel_id=1, source_target_pairs={{0,24},{8,16},{16,8},{24,0},{1,25},{9,17},{17,9},{25,1},{2,26},{10... | collective-permute-start | bytes 983048 | tf_op jit(solution)/shard_map/ppermute | solution.py:812
  169.0 73.0 %collective-permute-start.11 = (f32[4,5,8,512]{3,2,1,0:T(8,128)}, f32[4,5,8,512]{3,2,1,0:T(8,128)S(1)}, u32[]{:S(2)}, u32[]{:S(2)}) collective-permute-start(f32[4,5,8,512]{3,2,1,0:T(8,128)} %pad_maximum_fusion.5), channel_id=1, source_target_pairs={{0,2},{2,0},{4,6},{6,4},{1,3},{3,1},{5,7},{7,5},{8,10},{10,8},{12,... | collective-permute-start | bytes 983048 | tf_op jit(solution)/shard_map/ppermute | solution.py:812
  188.7 53.4 %collective-permute-start.12 = (f32[4,5,8,512]{3,2,1,0:T(8,128)}, f32[4,5,8,512]{3,2,1,0:T(8,128)S(1)}, u32[]{:S(2)}, u32[]{:S(2)}) collective-permute-start(f32[4,5,8,512]{3,2,1,0:T(8,128)} %pad_maximum_fusion.6), channel_id=1, source_target_pairs={{0,4},{2,6},{4,0},{6,2},{1,5},{3,7},{5,1},{7,3},{8,12},{10,14},{12... | collective-permute-start | bytes 983048 | tf_op jit(solution)/shard_map/ppermute | solution.py:812
  191.3 55.6 %collective-permute-start.13 = (f32[4,5,8,512]{3,2,1,0:T(8,128)}, f32[4,5,8,512]{3,2,1,0:T(8,128)S(1)}, u32[]{:S(2)}, u32[]{:S(2)}) collective-permute-start(f32[4,5,8,512]{3,2,1,0:T(8,128)} %pad_maximum_fusion.7), channel_id=1, source_target_pairs={{0,6},{2,4},{4,2},{6,0},{1,7},{3,5},{5,3},{7,1},{8,14},{10,12},{12... | collective-permute-start | bytes 983048 | tf_op jit(solution)/shard_map/ppermute | solution.py:812
  231.2 0.7 copy-start.8
  236.7 10.3 %copy-start.10 = (s32[2]{0:T(128)S(1)}, s32[2]{0:T(128)}, u32[]{:S(2)}) copy-start(s32[2]{0:T(128)} %copy-done.9) | copy-start | bytes 28
  236.7 13.4 %copy-start.4 = (bf16[320,240]{1,0:T(8,128)(2,1)S(1)}, bf16[320,240]{1,0:T(8,128)(2,1)}, u32[]{:S(2)}) copy-start(bf16[320,240]{1,0:T(8,128)(2,1)} %copy-done.3) | copy-start | bytes 460804
  248.5 4.7 %collective-permute-start.14 = (f32[8,3072]{1,0:T(8,128)S(1)}, f32[8,3072]{1,0:T(8,128)S(1)}, u32[]{:S(2)}, u32[]{:S(2)}) collective-permute-start(f32[8,3072]{1,0:T(8,128)S(1)} %get-tuple-element.82), channel_id=1, source_target_pairs={{0,1},{1,0},{2,3},{3,2},{4,5},{5,4},{6,7},{7,6},{8,9},{9,8},{10,11... | collective-permute-start | bytes 294920 | tf_op jit(solution)/shard_map/ppermute | solution.py:619
  250.1 3.1 %copy-start.6 = (bf16[320,48]{1,0:T(8,128)(2,1)S(1)}, bf16[320,48]{1,0:T(8,128)(2,1)}, u32[]{:S(2)}) copy-start(bf16[320,48]{1,0:T(8,128)(2,1)} %copy-done.5) | copy-start | bytes 92164

commit v6 on v5

--- a/solution.py
+++ b/solution.py
@@ -806,24 +806,21 @@
     def exchange(block):
         return lax.all_to_all(block, axes, split_axis=0, concat_axis=0, tiled=True)
 
-    def swap(blocks, axis, only=None):
+    def swap(blocks, axis):
         count = len(blocks)
-        return [
-            lax.ppermute(block, axis, [(at, at ^ i) for at in range(count)])
-            if i and (only is None or i in only)
-            else block
-            for i, block in enumerate(blocks)
+        return [blocks[0]] + [
+            lax.ppermute(blocks[i], axis, [(at, at ^ i) for at in range(count)])
+            for i in range(1, count)
         ]
 
     def regroup(blocks):
         return [jnp.stack([block[j] for block in blocks]) for j in range(blocks[0].shape[0])]
 
-    far = {spans // 2}
     main = prepare(amplitudes, keep, cuts[0])
     if apart:
         main, amplitudes = lax.optimization_barrier((main, amplitudes))
         sent = prepare_apart(place, amplitudes, keep, cuts[1], groups, spans)
-        arrived = swap(regroup(swap(sent, "freq")), "span", set(range(spans)) - far)
+        arrived = swap(regroup(swap(sent, "freq")), "span")
     main = exchange(main)
 
     inverse = slab_inverse[0]
@@ -838,11 +835,6 @@
     *adjoint_modes, sums, squares = base(
         amplitudes, upstream, keep, turned, ahead, back, edges, width, cuts
     )
-    if apart:
-        held = (arrived[1], arrived[spans // 2], adjoint_modes, sums, squares)
-        held = lax.optimization_barrier(held)
-        arrived[1], arrived[spans // 2], adjoint_modes, sums, squares = held
-        arrived = swap(arrived, "span", far)
     size = edge_at // devices
     shape = main.shape
     main = nonlinear(main.reshape((devices, size) + shape[1:]), coefficients, transforms)

time: 257 us -> 256 us (level)
  waiting for transfers between devices: 118 us -> 121 us
    ppermute x12, waiting for transfers between devices: 48.3 us -> 66.7 us  [swap(): lax.ppermute(blocks[i], axis, [(at, at ^ i) for at in range(count)])]
    all_to_all x2, waiting for transfers between devices: 64.4 us -> 46.9 us  [exchange(): return lax.all_to_all(block, axes, split_axis=0, concat_axis=0, tiled=True)]
    all_to_all x2, starting transfers between devices: 14 us -> 11 us  [exchange(): return lax.all_to_all(block, axes, split_axis=0, concat_axis=0, tiled=True)]
  transfers between devices with their start and end apart: 17 -> 17, of which waited for: 10 -> 11; matrix products, arithmetic and copies ran while one was open for 4% -> 3% of each run, Pallas kernels for 20% -> 20%
where the time goes in v6:
time: 256 us; the launch traced here: 255 us
  waiting for transfers between devices  121 us (47%)
  starting transfers between devices  62.9 us (25%)
  Pallas kernels  59.8 us (23%)
  local copies, waits for them, and re-layouts  7.27 us (3%)
    ppermute x12, waiting for transfers between devices, swap(): lax.ppermute(blocks[i], axis, [(at, at ^ i) for at in range(count)])  66.7 us
    ppermute x12, starting transfers between devices, swap(): lax.ppermute(blocks[i], axis, [(at, at ^ i) for at in range(count)])  47.3 us
    all_to_all x2, waiting for transfers between devices, exchange(): return lax.all_to_all(block, axes, split_axis=0, concat_axis=0, tiled=True)  46.9 us
    pallas_call x1, Pallas kernels, nonlinear(): pl.pallas_call(nonlinear_body, grid=(points,), in_specs=[pl.BlockSpec(mem...  11.9 us
    all_to_all x2, starting transfers between devices, exchange(): return lax.all_to_all(block, axes, split_axis=0, concat_axis=0, tiled=True)  11 us
    pallas_call x1, Pallas kernels, base(): pl.pallas_call(functools.partial(base_body, cuts, walls, width), grid=(mo...  10.7 us
    ppermute x2, waiting for transfers between devices, around(): lax.ppermute(block, axis, [(i, (i + d) % count) for i in range(count)])  6.34 us
    pallas_call x2, Pallas kernels, absorb(): pl.pallas_call(body, grid=(steps,), in_specs=in_specs, out_specs=[grid_sp...  6.28 us
  transfers between devices with their start and end apart: 17, of which 11 were waited for; matrix products, arithmetic and copies ran while one was open for 3% of the time, Pallas kernels for 20%

profile of v6, /device:TPU:10, one launch (start us, length us, event | category | flops | bytes accessed | tf_op | source)
XLA Modules:
  0.0 254.7 jit_solution(15608541035001581158)
XLA Ops:
  0.6 3.9 %prepare.1 = f32[48,5,8,512]{3,2,1,0:T(8,128)} custom-call(f32[2,5,64,2048]{3,2,1,0:T(8,128)} %x_ref.4, s32[2048]{0:T(1024)} %refs_4_.3), custom_call_target="tpu_custom_call" | custom-call | tf_op jit(solution)/shard_map/prepare/pallas_call | solution.py:82
  4.5 6.4 %all-to-all-start = ((f32[48,5,8,512]{3,2,1,0:T(8,128)}), f32[48,5,8,512]{3,2,1,0:T(8,128)}, u32[]{:S(2)}, u32[]{:S(2)}) async-start(f32[48,5,8,512]{3,2,1,0:T(8,128)} %prepare.1), calls=%async_computation | async-start | bytes 7864320 | tf_op jit(solution)/shard_map/all_to_all | solution.py:807
  10.9 0.1 pad_add_fusion.place_ref
  11.0 3.3 %prepare_apart.1 = (f32[4,5,8,512]{3,2,1,0:T(8,128)S(1)}, f32[4,5,8,512]{3,2,1,0:T(8,128)S(1)}, f32[4,5,8,512]{3,2,1,0:T(8,128)S(1)}, f32[4,5,8,512]{3,2,1,0:T(8,128)S(1)}) custom-call(s32[2]{0:T(128)S(1)} %pad_add_fusion.place_ref, f32[2,5,64,2048]{3,2,1,0:T(8,128)} %x_ref.4, s32[2048]{0:T(1024)S(1)} %copy-done.1), custom_call_target="tpu_custom_call" | custom-call | tf_op jit(solution)/shard_map/prepare_apart/pallas_call | solution.py:118
  14.3 0.2 collective-permute-start
  14.5 0.6 collective-permute-start.1
  15.1 1.1 collective-permute-start.2
  16.2 0.0 collective-permute-done
  16.3 22.3 %collective-permute-done.1 = f32[4,5,8,512]{3,2,1,0:T(8,128)S(1)} collective-permute-done((f32[4,5,8,512]{3,2,1,0:T(8,128)S(1)}, f32[4,5,8,512]{3,2,1,0:T(8,128)S(1)}, u32[]{:S(2)}, u32[]{:S(2)}) %collective-permute-start.1) | collective-permute-done | bytes 327712 | tf_op jit(solution)/shard_map/ppermute | solution.py:812
  38.6 8.7 %collective-permute-done.2 = f32[4,5,8,512]{3,2,1,0:T(8,128)S(1)} collective-permute-done((f32[4,5,8,512]{3,2,1,0:T(8,128)S(1)}, f32[4,5,8,512]{3,2,1,0:T(8,128)S(1)}, u32[]{:S(2)}, u32[]{:S(2)}) %collective-permute-start.2) | collective-permute-done | bytes 327712 | tf_op jit(solution)/shard_map/ppermute | solution.py:812
  47.4 19.1 %collective-permute-start.3 = (f32[4,5,8,512]{3,2,1,0:T(8,128)S(1)}, f32[4,5,8,512]{3,2,1,0:T(8,128)S(1)}, u32[]{:S(2)}, u32[]{:S(2)}) collective-permute-start(f32[4,5,8,512]{3,2,1,0:T(8,128)S(1)} %pad_maximum_fusion.1), channel_id=1, source_target_pairs={{0,2},{2,0},{4,6},{6,4},{1,3},{3,1},{5,7},{7,5},{8,10},{10,8},{12,... | collective-permute-start | bytes 983048 | tf_op jit(solution)/shard_map/ppermute | solution.py:812
  66.5 2.0 collective-permute-start.4
  68.5 0.6 collective-permute-start.5
  69.2 41.0 %all-to-all-done = f32[48,5,8,512]{3,2,1,0:T(8,128)} async-done(((f32[48,5,8,512]{3,2,1,0:T(8,128)}), f32[48,5,8,512]{3,2,1,0:T(8,128)}, u32[]{:S(2)}, u32[]{:S(2)}) %all-to-all-start) | async-done | bytes 3932192 | tf_op jit(solution)/shard_map/all_to_all | solution.py:807
  110.2 11.9 %nonlinear.1 = f32[16,3,5,8,512]{4,3,2,1,0:T(8,128)} custom-call(f32[25,5]{1,0:T(8,128)S(1)} %reshape.20.q_ref, f32[16,3,5,8,512]{4,3,2,1,0:T(8,128)} %bitcast.2.in_ref, bf16[256,768]{1,0:T(8,128)(2,1)} %constant.19.clone.refs_0_.refs_4_, bf16[1536,256]{1,0:T(8,128)(2,1)} %constant.20.clone.refs_1_.refs_5_, bf16[768,512]{1,0:T(8,128)(2,1)} %constant.21.clone.refs_2_.refs_6_, ...), custom_call_target="tpu_custom_call" | custom-call | flops 4529848320 | bytes 7864320 | tf_op jit(solution)/shard_map/nonlinear/pallas_call | solution.py:214
  122.1 3.8 %collective-permute-done.5.refs_3_ = f32[4,5,8,512]{3,2,1,0:T(8,128)S(1)} collective-permute-done((f32[4,5,8,512]{3,2,1,0:T(8,128)S(1)}, f32[4,5,8,512]{3,2,1,0:T(8,128)S(1)}, u32[]{:S(2)}, u32[]{:S(2)}) %collective-permute-start.5) | collective-permute-done | bytes 327712 | tf_op jit(solution)/shard_map/ppermute | solution.py:812
  126.0 4.6 %all-to-all-start.1 = ((f32[48,5,8,512]{3,2,1,0:T(8,128)}), f32[48,5,8,512]{3,2,1,0:T(8,128)}, u32[]{:S(2)}, u32[]{:S(2)}) async-start(f32[48,5,8,512]{3,2,1,0:T(8,128)} %bitcast.7), calls=%async_computation.1 | async-start | bytes 7864320 | tf_op jit(solution)/shard_map/all_to_all | solution.py:807
  130.6 0.0 copy-start.19
  130.6 0.0 copy-start.20
  130.6 0.0 copy-start.16
  130.6 0.0 copy-start.17
  130.6 0.0 copy-start.18
  130.7 0.0 copy-start
  130.7 4.8 %nonlinear_apart.1 = (f32[4,5,8,512]{3,2,1,0:T(8,128)S(1)}, f32[4,5,8,512]{3,2,1,0:T(8,128)S(1)}, f32[4,5,8,512]{3,2,1,0:T(8,128)S(1)}, f32[4,5,8,512]{3,2,1,0:T(8,128)S(1)}) custom-call(s32[2]{0:T(128)S(1)} %pad_add_fusion.place_ref, f32[25,5]{1,0:T(8,128)S(1)} %reshape.20.q_ref, f32[4,5,8,512]{3,2,1,0:T(8,128)S(1)} %pad_maximum_fusion.refs_0_, ...), custom_call_target="tpu_custom_call" | custom-call | flops 1509949440 | bytes 2621440 | tf_op jit(solution)/shard_map/nonlinear_apart/pallas_call | solution.py:255
  135.4 0.1 collective-permute-start.6
  135.5 0.6 collective-permute-start.7
  136.2 0.7 fusion
  136.8 1.2 collective-permute-start.8
  138.0 0.7 fusion.1
  138.7 19.8 %collective-permute-done.7 = f32[4,5,8,512]{3,2,1,0:T(8,128)S(1)} collective-permute-done((f32[4,5,8,512]{3,2,1,0:T(8,128)S(1)}, f32[4,5,8,512]{3,2,1,0:T(8,128)S(1)}, u32[]{:S(2)}, u32[]{:S(2)}) %collective-permute-start.7) | collective-permute-done | bytes 327712 | tf_op jit(solution)/shard_map/ppermute | solution.py:812
  158.5 0.6 fusion.2
  159.1 7.3 %collective-permute-done.8 = f32[4,5,8,512]{3,2,1,0:T(8,128)S(1)} collective-permute-done((f32[4,5,8,512]{3,2,1,0:T(8,128)S(1)}, f32[4,5,8,512]{3,2,1,0:T(8,128)S(1)}, u32[]{:S(2)}, u32[]{:S(2)}) %collective-permute-start.8) | collective-permute-done | bytes 327712 | tf_op jit(solution)/shard_map/ppermute | solution.py:812
  166.4 0.7 fusion.3
  167.0 0.8 pad_maximum_fusion.5
  167.8 19.2 %collective-permute-start.9 = (f32[4,5,8,512]{3,2,1,0:T(8,128)}, f32[4,5,8,512]{3,2,1,0:T(8,128)S(1)}, u32[]{:S(2)}, u32[]{:S(2)}) collective-permute-start(f32[4,5,8,512]{3,2,1,0:T(8,128)} %pad_maximum_fusion.5), channel_id=1, source_target_pairs={{0,2},{2,0},{4,6},{6,4},{1,3},{3,1},{5,7},{7,5},{8,10},{10,8},{12,... | collective-permute-start | bytes 983048 | tf_op jit(solution)/shard_map/ppermute | solution.py:812
  187.0 0.8 pad_maximum_fusion.6
  187.8 1.9 collective-permute-start.10
  189.7 0.8 pad_maximum_fusion.7
  190.5 0.6 collective-permute-start.11
  191.0 0.6 copy.19.refs_0_
  191.6 0.6 copy.20.refs_1_
  192.2 0.6 copy.21.refs_2_
  192.8 0.6 copy.22.refs_3_
  193.4 0.6 copy.23.refs_4_
  194.0 1.4 pack.1.refs_0_
  195.4 1.5 collective-permute-start.12
  196.9 2.7 %collective-permute-done.12.refs_1_ = f32[5,16,128]{2,1,0:T(8,128)S(1)} collective-permute-done((f32[5,16,128]{2,1,0:T(8,128)}, f32[5,16,128]{2,1,0:T(8,128)S(1)}, u32[]{:S(2)}, u32[]{:S(2)}) %collective-permute-start.12) | collective-permute-done | bytes 40992 | tf_op jit(solution)/shard_map/ppermute | solution.py:611
  199.6 0.8 copy-done.2
  200.4 1.2 constants.1
  201.6 0.0 copy-start.7
  201.6 6.0 %edge.1.refs_0_ = f32[16,2048]{1,0:T(8,128)S(1)} custom-call(f32[2,5,64,2048]{3,2,1,0:T(8,128)} %x_ref.4, s32[2048]{0:T(1024)S(1)} %copy-done.1, bf16[16,960]{1,0:T(8,128)(2,1)S(1)} %get-tuple-element.55.rows_ref), custom_call_target="tpu_custom_call" | custom-call | tf_op jit(solution)/shard_map/edge/pallas_call | solution.py:294
  207.7 1.5 collective-permute-start.13
  209.2 3.6 %collective-permute-done.13.refs_1_ = f32[16,2048]{1,0:T(8,128)S(1)} collective-permute-done((f32[16,2048]{1,0:T(8,128)S(1)}, f32[16,2048]{1,0:T(8,128)S(1)}, u32[]{:S(2)}, u32[]{:S(2)}) %collective-permute-start.13) | collective-permute-done | bytes 131104 | tf_op jit(solution)/shard_map/ppermute | solution.py:611
  212.9 10.7 %base.1 = (f32[2,5,48,2048]{3,2,1,0:T(8,128)}, f32[2,5,16,2048]{3,2,1,0:T(8,128)S(1)}, f32[24,2048]{1,0:T(8,128)S(1)}, f32[8,2048]{1,0:T(8,128)S(1)}) custom-call(f32[2,5,64,2048]{3,2,1,0:T(8,128)} %x_ref.4, f32[2,5,64,2048]{3,2,1,0:T(8,128)} %up_ref.3, s32[2048]{0:T(1024)S(1)} %copy-done.1, bf16[320,960]{1,0:T(8,128)(2,1)S(1)} %get-tuple-element.52.turned_ref, ...), custom_call_target="tpu_custom_call" | custom-call | tf_op jit(solution)/shard_map/base/pallas_call | solution.py:350
  223.6 5.9 %all-to-all-done.1.in_ref = f32[48,5,8,512]{3,2,1,0:T(8,128)} async-done(((f32[48,5,8,512]{3,2,1,0:T(8,128)}), f32[48,5,8,512]{3,2,1,0:T(8,128)}, u32[]{:S(2)}, u32[]{:S(2)}) %all-to-all-start.1) | async-done | bytes 3932192 | tf_op jit(solution)/shard_map/all_to_all | solution.py:807
  229.5 0.7 copy-done.8
  230.3 4.8 %absorb.1 = (f32[2,5,48,2048]{3,2,1,0:T(8,128)S(1)}, f32[24,2048]{1,0:T(8,128)S(1)}) custom-call(f32[48,5,8,512]{3,2,1,0:T(8,128)} %all-to-all-done.1.in_ref, s32[2048]{0:T(1024)S(1)} %copy-done.1, f32[2,10,120]{2,1,0:T(8,128)S(1)} %copy-done.8, f32[2,5,48,2048]{3,2,1,0:T(8,128)} %get-tuple-element.59.refs_2_, f32[24,2048]{1,0:T(8,128)S(1)} %get-tuple-element.60.refs_3_), custom_call_target="tpu_custom_call" | custom-call | tf_op jit(solution)/shard_map/absorb/pallas_call | solution.py:472
  235.1 5.4 %solve.1.before_ref = f32[2,5,64,2048]{3,2,1,0:T(8,128)S(1)} custom-call(f32[2,5,48,2048]{3,2,1,0:T(8,128)S(1)} %get-tuple-element.61.side_ref, f32[2,5,64,2048]{3,2,1,0:T(8,128)} %up_ref.3, s32[2048]{0:T(1024)S(1)} %copy-done.1, bf16[320,960]{1,0:T(8,128)(2,1)S(1)} %get-tuple-element.62.inverse_ref), custom_call_target="tpu_custom_call" | custom-call | tf_op jit(solution)/shard_map/solve/pallas_call | solution.py:505
  240.5 4.8 %collective-permute-done.11.refs_3_ = f32[4,5,8,512]{3,2,1,0:T(8,128)S(1)} collective-permute-done((f32[4,5,8,512]{3,2,1,0:T(8,128)}, f32[4,5,8,512]{3,2,1,0:T(8,128)S(1)}, u32[]{:S(2)}, u32[]{:S(2)}) %collective-permute-start.11) | collective-permute-done | bytes 327712 | tf_op jit(solution)/shard_map/ppermute | solution.py:812
  245.3 1.5 absorb_apart.1
  246.8 1.6 collective-permute-start.14
  248.4 1.8 solve_more.1.solved_ref
  250.2 1.3 collective-permute-done.14.refs_0_.refs_1_
  251.5 3.2 %finish.1 = (f32[2,5,64,2048]{3,2,1,0:T(8,128)}, f32[2,2048]{1,0:T(2,128)}) custom-call(f32[2,5,64,2048]{3,2,1,0:T(8,128)S(1)} %solve_more.1.solved_ref, f32[24,2048]{1,0:T(8,128)S(1)} %get-tuple-element.68.sum_ref, f32[8,2048]{1,0:T(8,128)S(1)} %get-tuple-element.69.square_ref, f32[8,3072]{1,0:T(8,128)S(1)} %collective-permute-done.14.refs_0_.refs_1_, ...), custom_call_target="tpu_custom_call" | custom-call | tf_op jit(solution)/shard_map/finish/pallas_call | solution.py:594
  (48 shorter events, 0.3 us)
Async XLA Ops:
  4.5 6.5 %copy-start.1 = (s32[2048]{0:T(1024)S(1)}, s32[2048]{0:T(1024)}, u32[]{:S(2)}) copy-start(s32[2048]{0:T(1024)} %refs_4_.3) | copy-start | bytes 24580
  4.5 105.7 %all-to-all-start = ((f32[48,5,8,512]{3,2,1,0:T(8,128)}), f32[48,5,8,512]{3,2,1,0:T(8,128)}, u32[]{:S(2)}, u32[]{:S(2)}) async-start(f32[48,5,8,512]{3,2,1,0:T(8,128)} %prepare.1), calls=%async_computation | async-start | bytes 7864320 | tf_op jit(solution)/shard_map/all_to_all | solution.py:807
  10.9 5.3 %copy-start.15 = (f32[5,5,5]{2,1,0:T(8,128)S(1)}, f32[5,5,5]{2,1,0:T(8,128)}, u32[]{:S(2)}) copy-start(f32[5,5,5]{2,1,0:T(8,128)} %param.17) | copy-start | bytes 1504
  11.0 119.6 %copy-start.9 = (s32[2]{0:T(128)}, s32[2]{0:T(128)S(1)}, u32[]{:S(2)}) copy-start(s32[2]{0:T(128)S(1)} %pad_add_fusion.place_ref) | copy-start | bytes 28
  14.3 2.0 collective-permute-start
  14.5 24.1 %collective-permute-start.1 = (f32[4,5,8,512]{3,2,1,0:T(8,128)S(1)}, f32[4,5,8,512]{3,2,1,0:T(8,128)S(1)}, u32[]{:S(2)}, u32[]{:S(2)}) collective-permute-start(f32[4,5,8,512]{3,2,1,0:T(8,128)S(1)} %get-tuple-element.41), channel_id=1, source_target_pairs={{0,16},{8,24},{16,0},{24,8},{1,17},{9,25},{17,1},{25,9},{2,18},{10... | collective-permute-start | bytes 983048 | tf_op jit(solution)/shard_map/ppermute | solution.py:812
  15.1 32.2 %collective-permute-start.2 = (f32[4,5,8,512]{3,2,1,0:T(8,128)S(1)}, f32[4,5,8,512]{3,2,1,0:T(8,128)S(1)}, u32[]{:S(2)}, u32[]{:S(2)}) collective-permute-start(f32[4,5,8,512]{3,2,1,0:T(8,128)S(1)} %get-tuple-element.42), channel_id=1, source_target_pairs={{0,24},{8,16},{16,8},{24,0},{1,25},{9,17},{17,9},{25,1},{2,26},{10... | collective-permute-start | bytes 983048 | tf_op jit(solution)/shard_map/ppermute | solution.py:812
  47.4 74.8 %collective-permute-start.3 = (f32[4,5,8,512]{3,2,1,0:T(8,128)S(1)}, f32[4,5,8,512]{3,2,1,0:T(8,128)S(1)}, u32[]{:S(2)}, u32[]{:S(2)}) collective-permute-start(f32[4,5,8,512]{3,2,1,0:T(8,128)S(1)} %pad_maximum_fusion.1), channel_id=1, source_target_pairs={{0,2},{2,0},{4,6},{6,4},{1,3},{3,1},{5,7},{7,5},{8,10},{10,8},{12,... | collective-permute-start | bytes 983048 | tf_op jit(solution)/shard_map/ppermute | solution.py:812
  66.5 55.6 %collective-permute-start.4 = (f32[4,5,8,512]{3,2,1,0:T(8,128)S(1)}, f32[4,5,8,512]{3,2,1,0:T(8,128)S(1)}, u32[]{:S(2)}, u32[]{:S(2)}) collective-permute-start(f32[4,5,8,512]{3,2,1,0:T(8,128)S(1)} %pad_maximum_fusion.2), channel_id=1, source_target_pairs={{0,4},{2,6},{4,0},{6,2},{1,5},{3,7},{5,1},{7,3},{8,12},{10,14},{12... | collective-permute-start | bytes 983048 | tf_op jit(solution)/shard_map/ppermute | solution.py:812
  68.5 57.4 %collective-permute-start.5 = (f32[4,5,8,512]{3,2,1,0:T(8,128)S(1)}, f32[4,5,8,512]{3,2,1,0:T(8,128)S(1)}, u32[]{:S(2)}, u32[]{:S(2)}) collective-permute-start(f32[4,5,8,512]{3,2,1,0:T(8,128)S(1)} %pad_maximum_fusion.3), channel_id=1, source_target_pairs={{0,6},{2,4},{4,2},{6,0},{1,7},{3,5},{5,3},{7,1},{8,14},{10,12},{12... | collective-permute-start | bytes 983048 | tf_op jit(solution)/shard_map/ppermute | solution.py:812
  126.0 103.6 %all-to-all-start.1 = ((f32[48,5,8,512]{3,2,1,0:T(8,128)}), f32[48,5,8,512]{3,2,1,0:T(8,128)}, u32[]{:S(2)}, u32[]{:S(2)}) async-start(f32[48,5,8,512]{3,2,1,0:T(8,128)} %bitcast.7), calls=%async_computation.1 | async-start | bytes 7864320 | tf_op jit(solution)/shard_map/all_to_all | solution.py:807
  130.6 60.4 %copy-start.19 = (f32[1,5,5]{2,0,1:T(1,128)S(1)}, f32[1,5,5]{2,0,1:T(1,128)}, u32[]{:S(2)}) copy-start(f32[1,5,5]{2,0,1:T(1,128)} %param.19) | copy-start | bytes 304
  130.6 61.0 %copy-start.20 = (f32[1,5,5]{2,0,1:T(1,128)S(1)}, f32[1,5,5]{2,0,1:T(1,128)}, u32[]{:S(2)}) copy-start(f32[1,5,5]{2,0,1:T(1,128)} %param.20) | copy-start | bytes 304
  130.6 61.6 %copy-start.16 = (f32[1,10,10]{2,0,1:T(1,128)S(1)}, f32[1,10,10]{2,0,1:T(1,128)}, u32[]{:S(2)}) copy-start(f32[1,10,10]{2,0,1:T(1,128)} %param.21) | copy-start | bytes 1204
  130.6 62.2 %copy-start.17 = (f32[1,10,10]{2,0,1:T(1,128)S(1)}, f32[1,10,10]{2,0,1:T(1,128)}, u32[]{:S(2)}) copy-start(f32[1,10,10]{2,0,1:T(1,128)} %param.22) | copy-start | bytes 1204
  130.6 62.8 %copy-start.18 = (f32[1,10,10]{2,0,1:T(1,128)S(1)}, f32[1,10,10]{2,0,1:T(1,128)}, u32[]{:S(2)}) copy-start(f32[1,10,10]{2,0,1:T(1,128)} %param.23) | copy-start | bytes 1204
  130.7 68.9 %copy-start = (f32[1,320,320]{2,1,0:T(8,128)S(1)}, f32[1,320,320]{2,1,0:T(8,128)}, u32[]{:S(2)}) copy-start(f32[1,320,320]{2,1,0:T(8,128)} %param.18) | copy-start | bytes 1228804
  135.4 2.6 %collective-permute-start.6 = (f32[4,5,8,512]{3,2,1,0:T(8,128)S(1)}, f32[4,5,8,512]{3,2,1,0:T(8,128)S(1)}, u32[]{:S(2)}, u32[]{:S(2)}) collective-permute-start(f32[4,5,8,512]{3,2,1,0:T(8,128)S(1)} %get-tuple-element.48), channel_id=1, source_target_pairs={{0,8},{8,0},{16,24},{24,16},{1,9},{9,1},{17,25},{25,17},{2,10},{10... | collective-permute-start | bytes 983048 | tf_op jit(solution)/shard_map/ppermute | solution.py:812
  135.5 23.0 %collective-permute-start.7 = (f32[4,5,8,512]{3,2,1,0:T(8,128)S(1)}, f32[4,5,8,512]{3,2,1,0:T(8,128)S(1)}, u32[]{:S(2)}, u32[]{:S(2)}) collective-permute-start(f32[4,5,8,512]{3,2,1,0:T(8,128)S(1)} %get-tuple-element.49), channel_id=1, source_target_pairs={{0,16},{8,24},{16,0},{24,8},{1,17},{9,25},{17,1},{25,9},{2,18},{10... | collective-permute-start | bytes 983048 | tf_op jit(solution)/shard_map/ppermute | solution.py:812
  136.8 29.5 %collective-permute-start.8 = (f32[4,5,8,512]{3,2,1,0:T(8,128)S(1)}, f32[4,5,8,512]{3,2,1,0:T(8,128)S(1)}, u32[]{:S(2)}, u32[]{:S(2)}) collective-permute-start(f32[4,5,8,512]{3,2,1,0:T(8,128)S(1)} %get-tuple-element.50), channel_id=1, source_target_pairs={{0,24},{8,16},{16,8},{24,0},{1,25},{9,17},{17,9},{25,1},{2,26},{10... | collective-permute-start | bytes 983048 | tf_op jit(solution)/shard_map/ppermute | solution.py:812
  167.8 72.7 %collective-permute-start.9 = (f32[4,5,8,512]{3,2,1,0:T(8,128)}, f32[4,5,8,512]{3,2,1,0:T(8,128)S(1)}, u32[]{:S(2)}, u32[]{:S(2)}) collective-permute-start(f32[4,5,8,512]{3,2,1,0:T(8,128)} %pad_maximum_fusion.5), channel_id=1, source_target_pairs={{0,2},{2,0},{4,6},{6,4},{1,3},{3,1},{5,7},{7,5},{8,10},{10,8},{12,... | collective-permute-start | bytes 983048 | tf_op jit(solution)/shard_map/ppermute | solution.py:812
  187.8 52.7 %collective-permute-start.10 = (f32[4,5,8,512]{3,2,1,0:T(8,128)}, f32[4,5,8,512]{3,2,1,0:T(8,128)S(1)}, u32[]{:S(2)}, u32[]{:S(2)}) collective-permute-start(f32[4,5,8,512]{3,2,1,0:T(8,128)} %pad_maximum_fusion.6), channel_id=1, source_target_pairs={{0,4},{2,6},{4,0},{6,2},{1,5},{3,7},{5,1},{7,3},{8,12},{10,14},{12... | collective-permute-start | bytes 983048 | tf_op jit(solution)/shard_map/ppermute | solution.py:812
  190.5 54.8 %collective-permute-start.11 = (f32[4,5,8,512]{3,2,1,0:T(8,128)}, f32[4,5,8,512]{3,2,1,0:T(8,128)S(1)}, u32[]{:S(2)}, u32[]{:S(2)}) collective-permute-start(f32[4,5,8,512]{3,2,1,0:T(8,128)} %pad_maximum_fusion.7), channel_id=1, source_target_pairs={{0,6},{2,4},{4,2},{6,0},{1,7},{3,5},{5,3},{7,1},{8,14},{10,12},{12... | collective-permute-start | bytes 983048 | tf_op jit(solution)/shard_map/ppermute | solution.py:812
  195.4 4.2 %collective-permute-start.12 = (f32[5,16,128]{2,1,0:T(8,128)}, f32[5,16,128]{2,1,0:T(8,128)S(1)}, u32[]{:S(2)}, u32[]{:S(2)}) collective-permute-start(f32[5,16,128]{2,1,0:T(8,128)} %pack.1.refs_0_), channel_id=1, source_target_pairs={{0,1},{1,0},{2,3},{3,2},{4,5},{5,4},{6,7},{7,6},{8,9},{9,8},{10,11... | collective-permute-start | bytes 122888 | tf_op jit(solution)/shard_map/ppermute | solution.py:611
  199.6 0.8 copy-start.2
  201.6 11.2 %copy-start.3 = (bf16[320,240]{1,0:T(8,128)(2,1)}, bf16[320,240]{1,0:T(8,128)(2,1)S(1)}, u32[]{:S(2)}) copy-start(bf16[320,240]{1,0:T(8,128)(2,1)S(1)} %get-tuple-element.67.inverse_ref) | copy-start | bytes 460804
  201.6 11.2 %copy-start.5 = (bf16[320,48]{1,0:T(8,128)(2,1)}, bf16[320,48]{1,0:T(8,128)(2,1)S(1)}, u32[]{:S(2)}) copy-start(bf16[320,48]{1,0:T(8,128)(2,1)S(1)} %get-tuple-element.71.refs_2_) | copy-start | bytes 92164
  201.6 11.2 %copy-start.7 = (f32[2,10,120]{2,1,0:T(8,128)}, f32[2,10,120]{2,1,0:T(8,128)S(1)}, u32[]{:S(2)}) copy-start(f32[2,10,120]{2,1,0:T(8,128)S(1)} %get-tuple-element.58.refs_1_) | copy-start | bytes 28804
  207.7 5.2 %collective-permute-start.13 = (f32[16,2048]{1,0:T(8,128)S(1)}, f32[16,2048]{1,0:T(8,128)S(1)}, u32[]{:S(2)}, u32[]{:S(2)}) collective-permute-start(f32[16,2048]{1,0:T(8,128)S(1)} %edge.1.refs_0_), channel_id=1, source_target_pairs={{0,1},{1,0},{2,3},{3,2},{4,5},{5,4},{6,7},{7,6},{8,9},{9,8},{10,11... | collective-permute-start | bytes 393224 | tf_op jit(solution)/shard_map/ppermute | solution.py:611
  212.8 10.7 %copy-start.11 = (f32[1,5,8,512]{3,2,1,0:T(8,128)S(1)}, f32[1,5,8,512]{3,2,1,0:T(8,128)}, u32[]{:S(2)}) copy-start(f32[1,5,8,512]{3,2,1,0:T(8,128)} %get-tuple-element.75) | copy-start | bytes 245764
  212.8 10.7 %copy-start.12 = (f32[1,5,8,512]{3,2,1,0:T(8,128)S(1)}, f32[1,5,8,512]{3,2,1,0:T(8,128)}, u32[]{:S(2)}) copy-start(f32[1,5,8,512]{3,2,1,0:T(8,128)} %get-tuple-element.79) | copy-start | bytes 245764
  212.9 10.7 %copy-start.13 = (f32[1,5,8,512]{3,2,1,0:T(8,128)S(1)}, f32[1,5,8,512]{3,2,1,0:T(8,128)}, u32[]{:S(2)}) copy-start(f32[1,5,8,512]{3,2,1,0:T(8,128)} %get-tuple-element.83) | copy-start | bytes 245764
  212.9 10.7 %copy-start.14 = (f32[1,5,8,512]{3,2,1,0:T(8,128)S(1)}, f32[1,5,8,512]{3,2,1,0:T(8,128)}, u32[]{:S(2)}) copy-start(f32[1,5,8,512]{3,2,1,0:T(8,128)} %get-tuple-element.87) | copy-start | bytes 245764
  229.5 0.7 copy-start.8
  235.0 10.3 %copy-start.10 = (s32[2]{0:T(128)S(1)}, s32[2]{0:T(128)}, u32[]{:S(2)}) copy-start(s32[2]{0:T(128)} %copy-done.9) | copy-start | bytes 28
  235.1 13.3 %copy-start.4 = (bf16[320,240]{1,0:T(8,128)(2,1)S(1)}, bf16[320,240]{1,0:T(8,128)(2,1)}, u32[]{:S(2)}) copy-start(bf16[320,240]{1,0:T(8,128)(2,1)} %copy-done.3) | copy-start | bytes 460804
  246.8 4.7 %collective-permute-start.14 = (f32[8,3072]{1,0:T(8,128)S(1)}, f32[8,3072]{1,0:T(8,128)S(1)}, u32[]{:S(2)}, u32[]{:S(2)}) collective-permute-start(f32[8,3072]{1,0:T(8,128)S(1)} %get-tuple-element.70), channel_id=1, source_target_pairs={{0,1},{1,0},{2,3},{3,2},{4,5},{5,4},{6,7},{7,6},{8,9},{9,8},{10,11... | collective-permute-start | bytes 294920 | tf_op jit(solution)/shard_map/ppermute | solution.py:619
  248.4 3.1 %copy-start.6 = (bf16[320,48]{1,0:T(8,128)(2,1)S(1)}, bf16[320,48]{1,0:T(8,128)(2,1)}, u32[]{:S(2)}) copy-start(bf16[320,48]{1,0:T(8,128)(2,1)} %copy-done.5) | copy-start | bytes 92164

commit v7 on v6

--- a/solution.py
+++ b/solution.py
@@ -263,7 +263,7 @@
         scratch_shapes=[pltpu.VMEM((groups * spans, variables, freqs, lanes), jnp.float32)]
         + work_shapes(variables),
         compiler_params=params(24),
-        cost_estimate=nonlinear_cost(1, variables),
+        cost_estimate=pl.CostEstimate(flops=2 * 10**11, bytes_accessed=0, transcendentals=0),
         name="nonlinear_apart",
     )(place, coefficients, *blocks, *[in_hbm(table) for table in transforms])
 
@@ -820,7 +820,9 @@
     if apart:
         main, amplitudes = lax.optimization_barrier((main, amplitudes))
         sent = prepare_apart(place, amplitudes, keep, cuts[1], groups, spans)
-        arrived = swap(regroup(swap(sent, "freq")), "span")
+        arrived = regroup(swap(sent, "freq"))
+        moved = swap(arrived, "span")
+        moved[1], held = lax.optimization_barrier((moved[1], amplitudes))
     main = exchange(main)
 
     inverse = slab_inverse[0]
@@ -831,7 +833,8 @@
     )
     walls = len(packed)
     width = push_width(walls, variables)
-    edges = around(edge(amplitudes, keep, edge_rows, width), "wall")
+    edges = edge(held if apart else amplitudes, keep, edge_rows, width)
+    edges = around(edges, "wall")
     *adjoint_modes, sums, squares = base(
         amplitudes, upstream, keep, turned, ahead, back, edges, width, cuts
     )
@@ -839,10 +842,12 @@
     shape = main.shape
     main = nonlinear(main.reshape((devices, size) + shape[1:]), coefficients, transforms)
     main = main.reshape(shape)
-    if apart:
-        main, arrived = lax.optimization_barrier((main, arrived))
     main = exchange(main)
     if apart:
+        half = spans // 2
+        sums, arrived[half] = lax.optimization_barrier((sums, arrived[half]))
+        moved[half] = swap(arrived, "span")[half]
+        arrived = moved
         forced = nonlinear_apart(place, arrived, coefficients, transforms)
         returned = regroup(swap(forced, "freq"))
         returned = swap(returned, "span")

time: 256 us -> 251 us (0.980)
  waiting for transfers between devices: 121 us -> 113 us
  starting transfers between devices: 62.9 us -> 66.8 us
    all_to_all x2, waiting for transfers between devices: 46.9 us -> 38.3 us  [exchange(): return lax.all_to_all(block, axes, split_axis=0, concat_axis=0, tiled=True)]
  transfers between devices with their start and end apart: 17 -> 17, of which waited for: 11 -> 10; matrix products, arithmetic and copies ran while one was open for 3% -> 3% of each run, Pallas kernels for 20% -> 21%
where the time goes in v7:
time: 251 us; the launch traced here: 250 us
  waiting for transfers between devices  113 us (45%)
  starting transfers between devices  66.8 us (27%)
  Pallas kernels  60.1 us (24%)
  local copies, waits for them, and re-layouts  4.73 us (2%)
  other arithmetic  4.01 us (2%)
    ppermute x12, waiting for transfers between devices, swap(): lax.ppermute(blocks[i], axis, [(at, at ^ i) for at in range(count)])  68.4 us
    ppermute x12, starting transfers between devices, swap(): lax.ppermute(blocks[i], axis, [(at, at ^ i) for at in range(count)])  49.1 us
    all_to_all x2, waiting for transfers between devices, exchange(): return lax.all_to_all(block, axes, split_axis=0, concat_axis=0, tiled=True)  38.3 us
    all_to_all x2, starting transfers between devices, exchange(): return lax.all_to_all(block, axes, split_axis=0, concat_axis=0, tiled=True)  13.2 us
    pallas_call x1, Pallas kernels, nonlinear(): pl.pallas_call(nonlinear_body, grid=(points,), in_specs=[pl.BlockSpec(mem...  12 us
    pallas_call x1, Pallas kernels, base(): pl.pallas_call(functools.partial(base_body, cuts, walls, width), grid=(mo...  10.5 us
    pallas_call x2, Pallas kernels, absorb(): pl.pallas_call(body, grid=(steps,), in_specs=in_specs, out_specs=[grid_sp...  6.36 us
    pallas_call x1, Pallas kernels, edge(): pl.pallas_call(functools.partial(edge_body, width), grid=(modes // NB,),...  5.94 us
  transfers between devices with their start and end apart: 17, of which 10 were waited for; matrix products, arithmetic and copies ran while one was open for 3% of the time, Pallas kernels for 21%

profile of v7, /device:TPU:10, one launch (start us, length us, event | category | flops | bytes accessed | tf_op | source)
XLA Modules:
  0.0 249.8 jit_solution(3842591714629712068)
XLA Ops:
  0.6 3.9 %prepare.1 = f32[48,5,8,512]{3,2,1,0:T(8,128)} custom-call(f32[2,5,64,2048]{3,2,1,0:T(8,128)} %x_ref.4, s32[2048]{0:T(1024)} %refs_4_.3), custom_call_target="tpu_custom_call" | custom-call | tf_op jit(solution)/shard_map/prepare/pallas_call | solution.py:82
  4.5 6.4 %all-to-all-start = ((f32[48,5,8,512]{3,2,1,0:T(8,128)}), f32[48,5,8,512]{3,2,1,0:T(8,128)}, u32[]{:S(2)}, u32[]{:S(2)}) async-start(f32[48,5,8,512]{3,2,1,0:T(8,128)} %prepare.1), calls=%async_computation | async-start | bytes 7864320 | tf_op jit(solution)/shard_map/all_to_all | solution.py:807
  10.9 0.1 pad_add_fusion.place_ref
  11.0 0.0 copy-start.12
  11.0 0.0 copy-start.13
  11.0 0.0 copy-start.14
  11.0 0.0 copy-start.11
  11.1 0.0 copy-start
  11.1 3.4 %prepare_apart.1 = (f32[4,5,8,512]{3,2,1,0:T(8,128)S(1)}, f32[4,5,8,512]{3,2,1,0:T(8,128)S(1)}, f32[4,5,8,512]{3,2,1,0:T(8,128)S(1)}, f32[4,5,8,512]{3,2,1,0:T(8,128)S(1)}) custom-call(s32[2]{0:T(128)S(1)} %pad_add_fusion.place_ref, f32[2,5,64,2048]{3,2,1,0:T(8,128)} %x_ref.4, s32[2048]{0:T(1024)S(1)} %copy-done.1), custom_call_target="tpu_custom_call" | custom-call | tf_op jit(solution)/shard_map/prepare_apart/pallas_call | solution.py:118
  14.5 0.4 collective-permute-start.2
  14.8 1.5 collective-permute-start.1
  16.3 0.1 collective-permute-start
  16.4 21.2 %collective-permute-done.2 = f32[4,5,8,512]{3,2,1,0:T(8,128)S(1)} collective-permute-done((f32[4,5,8,512]{3,2,1,0:T(8,128)S(1)}, f32[4,5,8,512]{3,2,1,0:T(8,128)S(1)}, u32[]{:S(2)}, u32[]{:S(2)}) %collective-permute-start.2) | collective-permute-done | bytes 327712 | tf_op jit(solution)/shard_map/ppermute | solution.py:812
  37.7 10.1 %collective-permute-done.1 = f32[4,5,8,512]{3,2,1,0:T(8,128)S(1)} collective-permute-done((f32[4,5,8,512]{3,2,1,0:T(8,128)S(1)}, f32[4,5,8,512]{3,2,1,0:T(8,128)S(1)}, u32[]{:S(2)}, u32[]{:S(2)}) %collective-permute-start.1) | collective-permute-done | bytes 327712 | tf_op jit(solution)/shard_map/ppermute | solution.py:812
  47.8 0.0 collective-permute-done
  47.9 18.9 %collective-permute-start.3 = (f32[4,5,8,512]{3,2,1,0:T(8,128)S(1)}, f32[4,5,8,512]{3,2,1,0:T(8,128)S(1)}, u32[]{:S(2)}, u32[]{:S(2)}) collective-permute-start(f32[4,5,8,512]{3,2,1,0:T(8,128)S(1)} %pad_maximum_fusion.1), channel_id=1, source_target_pairs={{0,2},{2,0},{4,6},{6,4},{1,3},{3,1},{5,7},{7,5},{8,10},{10,8},{12,... | collective-permute-start | bytes 983048 | tf_op jit(solution)/shard_map/ppermute | solution.py:812
  66.8 0.6 copy.17.refs_0_
  67.4 0.6 copy.18.refs_1_
  67.9 0.6 copy.19.refs_2_
  68.5 0.6 copy.20.refs_3_
  69.1 0.6 copy.21.refs_4_
  69.7 1.4 pack.1.refs_0_
  71.1 1.5 collective-permute-start.4
  72.6 2.7 %collective-permute-done.4.refs_1_ = f32[5,16,128]{2,1,0:T(8,128)S(1)} collective-permute-done((f32[5,16,128]{2,1,0:T(8,128)}, f32[5,16,128]{2,1,0:T(8,128)S(1)}, u32[]{:S(2)}, u32[]{:S(2)}) %collective-permute-start.4) | collective-permute-done | bytes 40992 | tf_op jit(solution)/shard_map/ppermute | solution.py:611
  75.3 0.8 copy-done.2
  76.1 1.2 constants.1
  77.4 0.0 copy-start.7
  77.4 0.8 pad_maximum_fusion.3
  78.2 3.1 %collective-permute-start.7 = (f32[4,5,8,512]{3,2,1,0:T(8,128)}, f32[4,5,8,512]{3,2,1,0:T(8,128)S(1)}, u32[]{:S(2)}, u32[]{:S(2)}) collective-permute-start(f32[4,5,8,512]{3,2,1,0:T(8,128)} %pad_maximum_fusion.3), channel_id=1, source_target_pairs={{0,6},{2,4},{4,2},{6,0},{1,7},{3,5},{5,3},{7,1},{8,14},{10,12},{12... | collective-permute-start | bytes 983048 | tf_op jit(solution)/shard_map/ppermute | solution.py:812
  81.3 2.3 collective-permute-done.3.refs_1_
  83.6 5.9 %edge.1.refs_0_ = f32[16,2048]{1,0:T(8,128)S(1)} custom-call(f32[2,5,64,2048]{3,2,1,0:T(8,128)} %x_ref.4, s32[2048]{0:T(1024)S(1)} %copy-done.1, bf16[16,960]{1,0:T(8,128)(2,1)S(1)} %get-tuple-element.46.rows_ref), custom_call_target="tpu_custom_call" | custom-call | tf_op jit(solution)/shard_map/edge/pallas_call | solution.py:294
  89.5 1.5 collective-permute-start.5
  91.1 0.8 pad_maximum_fusion.2
  91.8 2.7 %collective-permute-done.5.refs_1_ = f32[16,2048]{1,0:T(8,128)S(1)} collective-permute-done((f32[16,2048]{1,0:T(8,128)S(1)}, f32[16,2048]{1,0:T(8,128)S(1)}, u32[]{:S(2)}, u32[]{:S(2)}) %collective-permute-start.5) | collective-permute-done | bytes 131104 | tf_op jit(solution)/shard_map/ppermute | solution.py:611
  94.5 10.5 %base.1 = (f32[2,5,48,2048]{3,2,1,0:T(8,128)}, f32[2,5,16,2048]{3,2,1,0:T(8,128)S(1)}, f32[24,2048]{1,0:T(8,128)S(1)}, f32[8,2048]{1,0:T(8,128)S(1)}) custom-call(f32[2,5,64,2048]{3,2,1,0:T(8,128)} %x_ref.4, f32[2,5,64,2048]{3,2,1,0:T(8,128)} %up_ref.3, s32[2048]{0:T(1024)S(1)} %copy-done.1, bf16[320,960]{1,0:T(8,128)(2,1)S(1)} %get-tuple-element.42.turned_ref, ...), custom_call_target="tpu_custom_call" | custom-call | tf_op jit(solution)/shard_map/base/pallas_call | solution.py:350
  105.1 1.4 collective-permute-start.6
  106.5 0.0 all-to-all-done
  106.5 12.0 %nonlinear.1 = f32[16,3,5,8,512]{4,3,2,1,0:T(8,128)} custom-call(f32[25,5]{1,0:T(8,128)S(1)} %reshape.20.q_ref, f32[16,3,5,8,512]{4,3,2,1,0:T(8,128)} %bitcast.4.in_ref, bf16[256,768]{1,0:T(8,128)(2,1)} %constant.19.clone.refs_4_.refs_0_, bf16[1536,256]{1,0:T(8,128)(2,1)} %constant.20.clone.refs_5_.refs_1_, bf16[768,512]{1,0:T(8,128)(2,1)} %constant.21.clone.refs_6_.refs_2_, ...), custom_call_target="tpu_custom_call" | custom-call | flops 4529848320 | bytes 7864320 | tf_op jit(solution)/shard_map/nonlinear/pallas_call | solution.py:214
  118.5 6.8 %all-to-all-start.1 = ((f32[48,5,8,512]{3,2,1,0:T(8,128)}), f32[48,5,8,512]{3,2,1,0:T(8,128)}, u32[]{:S(2)}, u32[]{:S(2)}) async-start(f32[48,5,8,512]{3,2,1,0:T(8,128)} %bitcast.7), calls=%async_computation.1 | async-start | bytes 7864320 | tf_op jit(solution)/shard_map/all_to_all | solution.py:807
  125.3 0.0 collective-permute-done.7.refs_3_
  125.3 0.0 collective-permute-done.6.refs_2_
  125.3 4.8 %nonlinear_apart.1 = (f32[4,5,8,512]{3,2,1,0:T(8,128)S(1)}, f32[4,5,8,512]{3,2,1,0:T(8,128)S(1)}, f32[4,5,8,512]{3,2,1,0:T(8,128)S(1)}, f32[4,5,8,512]{3,2,1,0:T(8,128)S(1)}) custom-call(s32[2]{0:T(128)S(1)} %pad_add_fusion.place_ref, f32[25,5]{1,0:T(8,128)S(1)} %reshape.20.q_ref, f32[4,5,8,512]{3,2,1,0:T(8,128)S(1)} %pad_maximum_fusion.refs_0_, ...), custom_call_target="tpu_custom_call" | custom-call | flops 199999995904 | tf_op jit(solution)/shard_map/nonlinear_apart/pallas_call | solution.py:255
  130.1 0.3 collective-permute-start.10
  130.5 1.5 collective-permute-start.9
  132.0 0.1 collective-permute-start.8
  132.1 19.9 %collective-permute-done.10 = f32[4,5,8,512]{3,2,1,0:T(8,128)S(1)} collective-permute-done((f32[4,5,8,512]{3,2,1,0:T(8,128)S(1)}, f32[4,5,8,512]{3,2,1,0:T(8,128)S(1)}, u32[]{:S(2)}, u32[]{:S(2)}) %collective-permute-start.10) | collective-permute-done | bytes 327712 | tf_op jit(solution)/shard_map/ppermute | solution.py:812
  152.0 10.1 %collective-permute-done.9 = f32[4,5,8,512]{3,2,1,0:T(8,128)S(1)} collective-permute-done((f32[4,5,8,512]{3,2,1,0:T(8,128)S(1)}, f32[4,5,8,512]{3,2,1,0:T(8,128)S(1)}, u32[]{:S(2)}, u32[]{:S(2)}) %collective-permute-start.9) | collective-permute-done | bytes 327712 | tf_op jit(solution)/shard_map/ppermute | solution.py:812
  162.1 0.0 collective-permute-done.8
  162.2 0.8 pad_maximum_fusion.5
  162.9 18.8 %collective-permute-start.11 = (f32[4,5,8,512]{3,2,1,0:T(8,128)}, f32[4,5,8,512]{3,2,1,0:T(8,128)S(1)}, u32[]{:S(2)}, u32[]{:S(2)}) collective-permute-start(f32[4,5,8,512]{3,2,1,0:T(8,128)} %pad_maximum_fusion.5), channel_id=1, source_target_pairs={{0,2},{2,0},{4,6},{6,4},{1,3},{3,1},{5,7},{7,5},{8,10},{10,8},{12,... | collective-permute-start | bytes 983048 | tf_op jit(solution)/shard_map/ppermute | solution.py:812
  181.7 0.8 pad_maximum_fusion.6
  182.5 2.4 collective-permute-start.12
  184.9 0.8 pad_maximum_fusion.7
  185.7 0.6 collective-permute-start.13
  186.3 38.3 %all-to-all-done.1.in_ref = f32[48,5,8,512]{3,2,1,0:T(8,128)} async-done(((f32[48,5,8,512]{3,2,1,0:T(8,128)}), f32[48,5,8,512]{3,2,1,0:T(8,128)}, u32[]{:S(2)}, u32[]{:S(2)}) %all-to-all-start.1) | async-done | bytes 3932192 | tf_op jit(solution)/shard_map/all_to_all | solution.py:807
  224.6 0.7 copy-done.8
  225.3 4.8 %absorb.1 = (f32[2,5,48,2048]{3,2,1,0:T(8,128)S(1)}, f32[24,2048]{1,0:T(8,128)S(1)}) custom-call(f32[48,5,8,512]{3,2,1,0:T(8,128)} %all-to-all-done.1.in_ref, s32[2048]{0:T(1024)S(1)} %copy-done.1, f32[2,10,120]{2,1,0:T(8,128)S(1)} %copy-done.8, f32[2,5,48,2048]{3,2,1,0:T(8,128)} %get-tuple-element.57.refs_2_, f32[24,2048]{1,0:T(8,128)S(1)} %get-tuple-element.58.refs_3_), custom_call_target="tpu_custom_call" | custom-call | tf_op jit(solution)/shard_map/absorb/pallas_call | solution.py:472
  230.1 5.5 %solve.1.before_ref = f32[2,5,64,2048]{3,2,1,0:T(8,128)S(1)} custom-call(f32[2,5,48,2048]{3,2,1,0:T(8,128)S(1)} %get-tuple-element.59.side_ref, f32[2,5,64,2048]{3,2,1,0:T(8,128)} %up_ref.3, s32[2048]{0:T(1024)S(1)} %copy-done.1, bf16[320,960]{1,0:T(8,128)(2,1)S(1)} %get-tuple-element.60.inverse_ref), custom_call_target="tpu_custom_call" | custom-call | tf_op jit(solution)/shard_map/solve/pallas_call | solution.py:505
  235.6 4.8 %collective-permute-done.13.refs_3_ = f32[4,5,8,512]{3,2,1,0:T(8,128)S(1)} collective-permute-done((f32[4,5,8,512]{3,2,1,0:T(8,128)}, f32[4,5,8,512]{3,2,1,0:T(8,128)S(1)}, u32[]{:S(2)}, u32[]{:S(2)}) %collective-permute-start.13) | collective-permute-done | bytes 327712 | tf_op jit(solution)/shard_map/ppermute | solution.py:812
  240.4 1.6 absorb_apart.1
  241.9 1.6 collective-permute-start.14
  243.5 1.9 solve_more.1.solved_ref
  245.4 1.2 collective-permute-done.14.refs_0_.refs_1_
  246.6 3.2 %finish.1 = (f32[2,5,64,2048]{3,2,1,0:T(8,128)}, f32[2,2048]{1,0:T(2,128)}) custom-call(f32[2,5,64,2048]{3,2,1,0:T(8,128)S(1)} %solve_more.1.solved_ref, f32[24,2048]{1,0:T(8,128)S(1)} %get-tuple-element.66.sum_ref, f32[8,2048]{1,0:T(8,128)S(1)} %get-tuple-element.67.square_ref, f32[8,3072]{1,0:T(8,128)S(1)} %collective-permute-done.14.refs_0_.refs_1_, ...), custom_call_target="tpu_custom_call" | custom-call | tf_op jit(solution)/shard_map/finish/pallas_call | solution.py:594
  (40 shorter events, 0.3 us)
Async XLA Ops:
  4.5 6.5 %copy-start.1 = (s32[2048]{0:T(1024)S(1)}, s32[2048]{0:T(1024)}, u32[]{:S(2)}) copy-start(s32[2048]{0:T(1024)} %refs_4_.3) | copy-start | bytes 24580
  4.5 101.9 %all-to-all-start = ((f32[48,5,8,512]{3,2,1,0:T(8,128)}), f32[48,5,8,512]{3,2,1,0:T(8,128)}, u32[]{:S(2)}, u32[]{:S(2)}) async-start(f32[48,5,8,512]{3,2,1,0:T(8,128)} %prepare.1), calls=%async_computation | async-start | bytes 7864320 | tf_op jit(solution)/shard_map/all_to_all | solution.py:807
  11.0 114.3 %copy-start.9 = (s32[2]{0:T(128)}, s32[2]{0:T(128)S(1)}, u32[]{:S(2)}) copy-start(s32[2]{0:T(128)S(1)} %pad_add_fusion.place_ref) | copy-start | bytes 28
  11.0 55.8 %copy-start.15 = (f32[1,5,5]{2,0,1:T(1,128)S(1)}, f32[1,5,5]{2,0,1:T(1,128)}, u32[]{:S(2)}) copy-start(f32[1,5,5]{2,0,1:T(1,128)} %param.19) | copy-start | bytes 304
  11.0 56.3 %copy-start.16 = (f32[1,5,5]{2,0,1:T(1,128)S(1)}, f32[1,5,5]{2,0,1:T(1,128)}, u32[]{:S(2)}) copy-start(f32[1,5,5]{2,0,1:T(1,128)} %param.20) | copy-start | bytes 304
  11.0 56.9 %copy-start.12 = (f32[1,10,10]{2,0,1:T(1,128)S(1)}, f32[1,10,10]{2,0,1:T(1,128)}, u32[]{:S(2)}) copy-start(f32[1,10,10]{2,0,1:T(1,128)} %param.21) | copy-start | bytes 1204
  11.0 57.5 %copy-start.13 = (f32[1,10,10]{2,0,1:T(1,128)S(1)}, f32[1,10,10]{2,0,1:T(1,128)}, u32[]{:S(2)}) copy-start(f32[1,10,10]{2,0,1:T(1,128)} %param.22) | copy-start | bytes 1204
  11.0 58.1 %copy-start.14 = (f32[1,10,10]{2,0,1:T(1,128)S(1)}, f32[1,10,10]{2,0,1:T(1,128)}, u32[]{:S(2)}) copy-start(f32[1,10,10]{2,0,1:T(1,128)} %param.23) | copy-start | bytes 1204
  11.0 61.6 %copy-start.11 = (f32[5,5,5]{2,1,0:T(8,128)S(1)}, f32[5,5,5]{2,1,0:T(8,128)}, u32[]{:S(2)}) copy-start(f32[5,5,5]{2,1,0:T(8,128)} %param.17) | copy-start | bytes 1504
  11.1 64.3 %copy-start = (f32[1,320,320]{2,1,0:T(8,128)S(1)}, f32[1,320,320]{2,1,0:T(8,128)}, u32[]{:S(2)}) copy-start(f32[1,320,320]{2,1,0:T(8,128)} %param.18) | copy-start | bytes 1228804
  14.5 23.2 %collective-permute-start.2 = (f32[4,5,8,512]{3,2,1,0:T(8,128)S(1)}, f32[4,5,8,512]{3,2,1,0:T(8,128)S(1)}, u32[]{:S(2)}, u32[]{:S(2)}) collective-permute-start(f32[4,5,8,512]{3,2,1,0:T(8,128)S(1)} %get-tuple-element.40), channel_id=1, source_target_pairs={{0,24},{8,16},{16,8},{24,0},{1,25},{9,17},{17,9},{25,1},{2,26},{10... | collective-permute-start | bytes 983048 | tf_op jit(solution)/shard_map/ppermute | solution.py:812
  14.8 33.0 %collective-permute-start.1 = (f32[4,5,8,512]{3,2,1,0:T(8,128)S(1)}, f32[4,5,8,512]{3,2,1,0:T(8,128)S(1)}, u32[]{:S(2)}, u32[]{:S(2)}) collective-permute-start(f32[4,5,8,512]{3,2,1,0:T(8,128)S(1)} %get-tuple-element.39), channel_id=1, source_target_pairs={{0,16},{8,24},{16,0},{24,8},{1,17},{9,25},{17,1},{25,9},{2,18},{10... | collective-permute-start | bytes 983048 | tf_op jit(solution)/shard_map/ppermute | solution.py:812
  16.3 31.5 %collective-permute-start = (f32[4,5,8,512]{3,2,1,0:T(8,128)S(1)}, f32[4,5,8,512]{3,2,1,0:T(8,128)S(1)}, u32[]{:S(2)}, u32[]{:S(2)}) collective-permute-start(f32[4,5,8,512]{3,2,1,0:T(8,128)S(1)} %get-tuple-element.38), channel_id=1, source_target_pairs={{0,8},{8,0},{16,24},{24,16},{1,9},{9,1},{17,25},{25,17},{2,10},{10... | collective-permute-start | bytes 983048 | tf_op jit(solution)/shard_map/ppermute | solution.py:812
  47.9 35.7 %collective-permute-start.3 = (f32[4,5,8,512]{3,2,1,0:T(8,128)S(1)}, f32[4,5,8,512]{3,2,1,0:T(8,128)S(1)}, u32[]{:S(2)}, u32[]{:S(2)}) collective-permute-start(f32[4,5,8,512]{3,2,1,0:T(8,128)S(1)} %pad_maximum_fusion.1), channel_id=1, source_target_pairs={{0,2},{2,0},{4,6},{6,4},{1,3},{3,1},{5,7},{7,5},{8,10},{10,8},{12,... | collective-permute-start | bytes 983048 | tf_op jit(solution)/shard_map/ppermute | solution.py:812
  71.1 4.2 %collective-permute-start.4 = (f32[5,16,128]{2,1,0:T(8,128)}, f32[5,16,128]{2,1,0:T(8,128)S(1)}, u32[]{:S(2)}, u32[]{:S(2)}) collective-permute-start(f32[5,16,128]{2,1,0:T(8,128)} %pack.1.refs_0_), channel_id=1, source_target_pairs={{0,1},{1,0},{2,3},{3,2},{4,5},{5,4},{6,7},{7,6},{8,9},{9,8},{10,11... | collective-permute-start | bytes 122888 | tf_op jit(solution)/shard_map/ppermute | solution.py:611
  75.3 0.8 copy-start.2
  77.3 6.3 %copy-start.3 = (bf16[320,240]{1,0:T(8,128)(2,1)}, bf16[320,240]{1,0:T(8,128)(2,1)S(1)}, u32[]{:S(2)}) copy-start(bf16[320,240]{1,0:T(8,128)(2,1)S(1)} %get-tuple-element.65.inverse_ref) | copy-start | bytes 460804
  77.3 6.3 %copy-start.5 = (bf16[320,48]{1,0:T(8,128)(2,1)}, bf16[320,48]{1,0:T(8,128)(2,1)S(1)}, u32[]{:S(2)}) copy-start(bf16[320,48]{1,0:T(8,128)(2,1)S(1)} %get-tuple-element.69.refs_2_) | copy-start | bytes 92164
  77.4 17.2 %copy-start.7 = (f32[2,10,120]{2,1,0:T(8,128)}, f32[2,10,120]{2,1,0:T(8,128)S(1)}, u32[]{:S(2)}) copy-start(f32[2,10,120]{2,1,0:T(8,128)S(1)} %get-tuple-element.56.refs_1_) | copy-start | bytes 28804
  78.2 47.1 %collective-permute-start.7 = (f32[4,5,8,512]{3,2,1,0:T(8,128)}, f32[4,5,8,512]{3,2,1,0:T(8,128)S(1)}, u32[]{:S(2)}, u32[]{:S(2)}) collective-permute-start(f32[4,5,8,512]{3,2,1,0:T(8,128)} %pad_maximum_fusion.3), channel_id=1, source_target_pairs={{0,6},{2,4},{4,2},{6,0},{1,7},{3,5},{5,3},{7,1},{8,14},{10,12},{12... | collective-permute-start | bytes 983048 | tf_op jit(solution)/shard_map/ppermute | solution.py:812
  89.5 5.0 %collective-permute-start.5 = (f32[16,2048]{1,0:T(8,128)S(1)}, f32[16,2048]{1,0:T(8,128)S(1)}, u32[]{:S(2)}, u32[]{:S(2)}) collective-permute-start(f32[16,2048]{1,0:T(8,128)S(1)} %edge.1.refs_0_), channel_id=1, source_target_pairs={{0,1},{1,0},{2,3},{3,2},{4,5},{5,4},{6,7},{7,6},{8,9},{9,8},{10,11... | collective-permute-start | bytes 393224 | tf_op jit(solution)/shard_map/ppermute | solution.py:611
  105.1 20.2 %collective-permute-start.6 = (f32[4,5,8,512]{3,2,1,0:T(8,128)}, f32[4,5,8,512]{3,2,1,0:T(8,128)}, u32[]{:S(2)}, u32[]{:S(2)}) collective-permute-start(f32[4,5,8,512]{3,2,1,0:T(8,128)} %pad_maximum_fusion.2), channel_id=1, source_target_pairs={{0,4},{2,6},{4,0},{6,2},{1,5},{3,7},{5,1},{7,3},{8,12},{10,14},{12... | collective-permute-start | bytes 983048 | tf_op jit(solution)/shard_map/ppermute | solution.py:812
  118.5 106.1 %all-to-all-start.1 = ((f32[48,5,8,512]{3,2,1,0:T(8,128)}), f32[48,5,8,512]{3,2,1,0:T(8,128)}, u32[]{:S(2)}, u32[]{:S(2)}) async-start(f32[48,5,8,512]{3,2,1,0:T(8,128)} %bitcast.7), calls=%async_computation.1 | async-start | bytes 7864320 | tf_op jit(solution)/shard_map/all_to_all | solution.py:807
  130.1 21.9 %collective-permute-start.10 = (f32[4,5,8,512]{3,2,1,0:T(8,128)S(1)}, f32[4,5,8,512]{3,2,1,0:T(8,128)S(1)}, u32[]{:S(2)}, u32[]{:S(2)}) collective-permute-start(f32[4,5,8,512]{3,2,1,0:T(8,128)S(1)} %get-tuple-element.52), channel_id=1, source_target_pairs={{0,24},{8,16},{16,8},{24,0},{1,25},{9,17},{17,9},{25,1},{2,26},{10... | collective-permute-start | bytes 983048 | tf_op jit(solution)/shard_map/ppermute | solution.py:812
  130.5 31.6 %collective-permute-start.9 = (f32[4,5,8,512]{3,2,1,0:T(8,128)S(1)}, f32[4,5,8,512]{3,2,1,0:T(8,128)S(1)}, u32[]{:S(2)}, u32[]{:S(2)}) collective-permute-start(f32[4,5,8,512]{3,2,1,0:T(8,128)S(1)} %get-tuple-element.51), channel_id=1, source_target_pairs={{0,16},{8,24},{16,0},{24,8},{1,17},{9,25},{17,1},{25,9},{2,18},{10... | collective-permute-start | bytes 983048 | tf_op jit(solution)/shard_map/ppermute | solution.py:812
  132.0 30.2 %collective-permute-start.8 = (f32[4,5,8,512]{3,2,1,0:T(8,128)S(1)}, f32[4,5,8,512]{3,2,1,0:T(8,128)S(1)}, u32[]{:S(2)}, u32[]{:S(2)}) collective-permute-start(f32[4,5,8,512]{3,2,1,0:T(8,128)S(1)} %get-tuple-element.50), channel_id=1, source_target_pairs={{0,8},{8,0},{16,24},{24,16},{1,9},{9,1},{17,25},{25,17},{2,10},{10... | collective-permute-start | bytes 983048 | tf_op jit(solution)/shard_map/ppermute | solution.py:812
  162.9 72.6 %collective-permute-start.11 = (f32[4,5,8,512]{3,2,1,0:T(8,128)}, f32[4,5,8,512]{3,2,1,0:T(8,128)S(1)}, u32[]{:S(2)}, u32[]{:S(2)}) collective-permute-start(f32[4,5,8,512]{3,2,1,0:T(8,128)} %pad_maximum_fusion.5), channel_id=1, source_target_pairs={{0,2},{2,0},{4,6},{6,4},{1,3},{3,1},{5,7},{7,5},{8,10},{10,8},{12,... | collective-permute-start | bytes 983048 | tf_op jit(solution)/shard_map/ppermute | solution.py:812
  182.5 53.0 %collective-permute-start.12 = (f32[4,5,8,512]{3,2,1,0:T(8,128)}, f32[4,5,8,512]{3,2,1,0:T(8,128)S(1)}, u32[]{:S(2)}, u32[]{:S(2)}) collective-permute-start(f32[4,5,8,512]{3,2,1,0:T(8,128)} %pad_maximum_fusion.6), channel_id=1, source_target_pairs={{0,4},{2,6},{4,0},{6,2},{1,5},{3,7},{5,1},{7,3},{8,12},{10,14},{12... | collective-permute-start | bytes 983048 | tf_op jit(solution)/shard_map/ppermute | solution.py:812
  185.7 54.7 %collective-permute-start.13 = (f32[4,5,8,512]{3,2,1,0:T(8,128)}, f32[4,5,8,512]{3,2,1,0:T(8,128)S(1)}, u32[]{:S(2)}, u32[]{:S(2)}) collective-permute-start(f32[4,5,8,512]{3,2,1,0:T(8,128)} %pad_maximum_fusion.7), channel_id=1, source_target_pairs={{0,6},{2,4},{4,2},{6,0},{1,7},{3,5},{5,3},{7,1},{8,14},{10,12},{12... | collective-permute-start | bytes 983048 | tf_op jit(solution)/shard_map/ppermute | solution.py:812
  224.6 0.7 copy-start.8
  230.1 10.3 %copy-start.10 = (s32[2]{0:T(128)S(1)}, s32[2]{0:T(128)}, u32[]{:S(2)}) copy-start(s32[2]{0:T(128)} %copy-done.9) | copy-start | bytes 28
  230.1 13.4 %copy-start.4 = (bf16[320,240]{1,0:T(8,128)(2,1)S(1)}, bf16[320,240]{1,0:T(8,128)(2,1)}, u32[]{:S(2)}) copy-start(bf16[320,240]{1,0:T(8,128)(2,1)} %copy-done.3) | copy-start | bytes 460804
  241.9 4.7 %collective-permute-start.14 = (f32[8,3072]{1,0:T(8,128)S(1)}, f32[8,3072]{1,0:T(8,128)S(1)}, u32[]{:S(2)}, u32[]{:S(2)}) collective-permute-start(f32[8,3072]{1,0:T(8,128)S(1)} %get-tuple-element.68), channel_id=1, source_target_pairs={{0,1},{1,0},{2,3},{3,2},{4,5},{5,4},{6,7},{7,6},{8,9},{9,8},{10,11... | collective-permute-start | bytes 294920 | tf_op jit(solution)/shard_map/ppermute | solution.py:619
  243.5 3.1 %copy-start.6 = (bf16[320,48]{1,0:T(8,128)(2,1)S(1)}, bf16[320,48]{1,0:T(8,128)(2,1)}, u32[]{:S(2)}) copy-start(bf16[320,48]{1,0:T(8,128)(2,1)} %copy-done.5) | copy-start | bytes 92164

commit v8 on v7

--- a/solution.py
+++ b/solution.py
@@ -844,9 +844,9 @@
     main = main.reshape(shape)
     main = exchange(main)
     if apart:
-        half = spans // 2
-        sums, arrived[half] = lax.optimization_barrier((sums, arrived[half]))
-        moved[half] = swap(arrived, "span")[half]
+        last_one = spans - 1
+        sums, arrived[last_one] = lax.optimization_barrier((sums, arrived[last_one]))
+        moved[last_one] = swap(arrived, "span")[last_one]
         arrived = moved
         forced = nonlinear_apart(place, arrived, coefficients, transforms)
         returned = regroup(swap(forced, "freq"))

time: 251 us -> 250 us (level)
  transfers between devices with their start and end apart: 17 -> 17, of which waited for: 10 -> 11; matrix products, arithmetic and copies ran while one was open for 3% -> 3% of each run, Pallas kernels for 21% -> 21%
where the time goes in v8:
time: 250 us; the launch traced here: 249 us
  waiting for transfers between devices  114 us (46%)
  starting transfers between devices  65.3 us (26%)
  Pallas kernels  60.1 us (24%)
  local copies, waits for them, and re-layouts  4.73 us (2%)
  other arithmetic  4.03 us (2%)
    ppermute x12, waiting for transfers between devices, swap(): lax.ppermute(blocks[i], axis, [(at, at ^ i) for at in range(count)])  69 us
    ppermute x12, starting transfers between devices, swap(): lax.ppermute(blocks[i], axis, [(at, at ^ i) for at in range(count)])  49.5 us
    all_to_all x2, waiting for transfers between devices, exchange(): return lax.all_to_all(block, axes, split_axis=0, concat_axis=0, tiled=True)  38.3 us
    pallas_call x1, Pallas kernels, nonlinear(): pl.pallas_call(nonlinear_body, grid=(points,), in_specs=[pl.BlockSpec(mem...  12 us
    all_to_all x2, starting transfers between devices, exchange(): return lax.all_to_all(block, axes, split_axis=0, concat_axis=0, tiled=True)  11.1 us
    pallas_call x1, Pallas kernels, base(): pl.pallas_call(functools.partial(base_body, cuts, walls, width), grid=(mo...  10.5 us
    pallas_call x2, Pallas kernels, absorb(): pl.pallas_call(body, grid=(steps,), in_specs=in_specs, out_specs=[grid_sp...  6.36 us
    pallas_call x1, Pallas kernels, edge(): pl.pallas_call(functools.partial(edge_body, width), grid=(modes // NB,),...  5.94 us
  transfers between devices with their start and end apart: 17, of which 11 were waited for; matrix products, arithmetic and copies ran while one was open for 3% of the time, Pallas kernels for 21%

profile of v8, /device:TPU:10, one launch (start us, length us, event | category | flops | bytes accessed | tf_op | source)
XLA Modules:
  0.0 248.8 jit_solution(13158527216284162875)
XLA Ops:
  0.6 3.9 %prepare.1 = f32[48,5,8,512]{3,2,1,0:T(8,128)} custom-call(f32[2,5,64,2048]{3,2,1,0:T(8,128)} %x_ref.4, s32[2048]{0:T(1024)} %refs_4_.3), custom_call_target="tpu_custom_call" | custom-call | tf_op jit(solution)/shard_map/prepare/pallas_call | solution.py:82
  4.5 6.4 %all-to-all-start = ((f32[48,5,8,512]{3,2,1,0:T(8,128)}), f32[48,5,8,512]{3,2,1,0:T(8,128)}, u32[]{:S(2)}, u32[]{:S(2)}) async-start(f32[48,5,8,512]{3,2,1,0:T(8,128)} %prepare.1), calls=%async_computation | async-start | bytes 7864320 | tf_op jit(solution)/shard_map/all_to_all | solution.py:807
  10.9 0.1 pad_add_fusion.place_ref
  11.0 0.0 copy-start.12
  11.0 0.0 copy-start.13
  11.0 0.0 copy-start.14
  11.0 0.0 copy-start.11
  11.1 0.0 copy-start
  11.1 3.4 %prepare_apart.1 = (f32[4,5,8,512]{3,2,1,0:T(8,128)S(1)}, f32[4,5,8,512]{3,2,1,0:T(8,128)S(1)}, f32[4,5,8,512]{3,2,1,0:T(8,128)S(1)}, f32[4,5,8,512]{3,2,1,0:T(8,128)S(1)}) custom-call(s32[2]{0:T(128)S(1)} %pad_add_fusion.place_ref, f32[2,5,64,2048]{3,2,1,0:T(8,128)} %x_ref.4, s32[2048]{0:T(1024)S(1)} %copy-done.1), custom_call_target="tpu_custom_call" | custom-call | tf_op jit(solution)/shard_map/prepare_apart/pallas_call | solution.py:118
  14.5 0.4 collective-permute-start.2
  14.8 1.5 collective-permute-start.1
  16.3 0.1 collective-permute-start
  16.4 21.2 %collective-permute-done.2 = f32[4,5,8,512]{3,2,1,0:T(8,128)S(1)} collective-permute-done((f32[4,5,8,512]{3,2,1,0:T(8,128)S(1)}, f32[4,5,8,512]{3,2,1,0:T(8,128)S(1)}, u32[]{:S(2)}, u32[]{:S(2)}) %collective-permute-start.2) | collective-permute-done | bytes 327712 | tf_op jit(solution)/shard_map/ppermute | solution.py:812
  37.7 10.1 %collective-permute-done.1 = f32[4,5,8,512]{3,2,1,0:T(8,128)S(1)} collective-permute-done((f32[4,5,8,512]{3,2,1,0:T(8,128)S(1)}, f32[4,5,8,512]{3,2,1,0:T(8,128)S(1)}, u32[]{:S(2)}, u32[]{:S(2)}) %collective-permute-start.1) | collective-permute-done | bytes 327712 | tf_op jit(solution)/shard_map/ppermute | solution.py:812
  47.8 0.0 collective-permute-done
  47.9 18.9 %collective-permute-start.3 = (f32[4,5,8,512]{3,2,1,0:T(8,128)S(1)}, f32[4,5,8,512]{3,2,1,0:T(8,128)S(1)}, u32[]{:S(2)}, u32[]{:S(2)}) collective-permute-start(f32[4,5,8,512]{3,2,1,0:T(8,128)S(1)} %pad_maximum_fusion.1), channel_id=1, source_target_pairs={{0,2},{2,0},{4,6},{6,4},{1,3},{3,1},{5,7},{7,5},{8,10},{10,8},{12,... | collective-permute-start | bytes 983048 | tf_op jit(solution)/shard_map/ppermute | solution.py:812
  66.8 0.6 copy.17.refs_0_
  67.4 0.6 copy.18.refs_1_
  67.9 0.6 copy.19.refs_2_
  68.5 0.6 copy.20.refs_3_
  69.1 0.6 copy.21.refs_4_
  69.7 1.4 pack.1.refs_0_
  71.1 1.5 collective-permute-start.5
  72.6 2.7 %collective-permute-done.5.refs_1_ = f32[5,16,128]{2,1,0:T(8,128)S(1)} collective-permute-done((f32[5,16,128]{2,1,0:T(8,128)}, f32[5,16,128]{2,1,0:T(8,128)S(1)}, u32[]{:S(2)}, u32[]{:S(2)}) %collective-permute-start.5) | collective-permute-done | bytes 40992 | tf_op jit(solution)/shard_map/ppermute | solution.py:611
  75.3 0.8 copy-done.2
  76.1 1.2 constants.1
  77.4 0.0 copy-start.7
  77.4 0.8 pad_maximum_fusion.2
  78.2 2.6 %collective-permute-start.4 = (f32[4,5,8,512]{3,2,1,0:T(8,128)}, f32[4,5,8,512]{3,2,1,0:T(8,128)S(1)}, u32[]{:S(2)}, u32[]{:S(2)}) collective-permute-start(f32[4,5,8,512]{3,2,1,0:T(8,128)} %pad_maximum_fusion.2), channel_id=1, source_target_pairs={{0,4},{2,6},{4,0},{6,2},{1,5},{3,7},{5,1},{7,3},{8,12},{10,14},{12... | collective-permute-start | bytes 983048 | tf_op jit(solution)/shard_map/ppermute | solution.py:812
  80.7 2.9 %collective-permute-done.3.refs_1_ = f32[4,5,8,512]{3,2,1,0:T(8,128)S(1)} collective-permute-done((f32[4,5,8,512]{3,2,1,0:T(8,128)S(1)}, f32[4,5,8,512]{3,2,1,0:T(8,128)S(1)}, u32[]{:S(2)}, u32[]{:S(2)}) %collective-permute-start.3) | collective-permute-done | bytes 327712 | tf_op jit(solution)/shard_map/ppermute | solution.py:812
  83.6 5.9 %edge.1.refs_0_ = f32[16,2048]{1,0:T(8,128)S(1)} custom-call(f32[2,5,64,2048]{3,2,1,0:T(8,128)} %x_ref.4, s32[2048]{0:T(1024)S(1)} %copy-done.1, bf16[16,960]{1,0:T(8,128)(2,1)S(1)} %get-tuple-element.46.rows_ref), custom_call_target="tpu_custom_call" | custom-call | tf_op jit(solution)/shard_map/edge/pallas_call | solution.py:294
  89.5 1.5 collective-permute-start.6
  91.1 0.8 pad_maximum_fusion.3
  91.9 2.6 %collective-permute-done.6.refs_1_ = f32[16,2048]{1,0:T(8,128)S(1)} collective-permute-done((f32[16,2048]{1,0:T(8,128)S(1)}, f32[16,2048]{1,0:T(8,128)S(1)}, u32[]{:S(2)}, u32[]{:S(2)}) %collective-permute-start.6) | collective-permute-done | bytes 131104 | tf_op jit(solution)/shard_map/ppermute | solution.py:611
  94.5 10.5 %base.1 = (f32[2,5,48,2048]{3,2,1,0:T(8,128)}, f32[2,5,16,2048]{3,2,1,0:T(8,128)S(1)}, f32[24,2048]{1,0:T(8,128)S(1)}, f32[8,2048]{1,0:T(8,128)S(1)}) custom-call(f32[2,5,64,2048]{3,2,1,0:T(8,128)} %x_ref.4, f32[2,5,64,2048]{3,2,1,0:T(8,128)} %up_ref.3, s32[2048]{0:T(1024)S(1)} %copy-done.1, bf16[320,960]{1,0:T(8,128)(2,1)S(1)} %get-tuple-element.42.turned_ref, ...), custom_call_target="tpu_custom_call" | custom-call | tf_op jit(solution)/shard_map/base/pallas_call | solution.py:350
  105.1 2.5 collective-permute-start.7
  107.5 0.0 all-to-all-done
  107.5 12.0 %nonlinear.1 = f32[16,3,5,8,512]{4,3,2,1,0:T(8,128)} custom-call(f32[25,5]{1,0:T(8,128)S(1)} %reshape.20.q_ref, f32[16,3,5,8,512]{4,3,2,1,0:T(8,128)} %bitcast.4.in_ref, bf16[256,768]{1,0:T(8,128)(2,1)} %constant.19.clone.refs_4_.refs_0_, bf16[1536,256]{1,0:T(8,128)(2,1)} %constant.20.clone.refs_5_.refs_1_, bf16[768,512]{1,0:T(8,128)(2,1)} %constant.21.clone.refs_6_.refs_2_, ...), custom_call_target="tpu_custom_call" | custom-call | flops 4529848320 | bytes 7864320 | tf_op jit(solution)/shard_map/nonlinear/pallas_call | solution.py:214
  119.5 4.7 %all-to-all-start.1 = ((f32[48,5,8,512]{3,2,1,0:T(8,128)}), f32[48,5,8,512]{3,2,1,0:T(8,128)}, u32[]{:S(2)}, u32[]{:S(2)}) async-start(f32[48,5,8,512]{3,2,1,0:T(8,128)} %bitcast.7), calls=%async_computation.1 | async-start | bytes 7864320 | tf_op jit(solution)/shard_map/all_to_all | solution.py:807
  124.2 0.0 collective-permute-done.4.refs_2_
  124.3 1.8 collective-permute-done.7.refs_3_
  126.1 4.8 %nonlinear_apart.1 = (f32[4,5,8,512]{3,2,1,0:T(8,128)S(1)}, f32[4,5,8,512]{3,2,1,0:T(8,128)S(1)}, f32[4,5,8,512]{3,2,1,0:T(8,128)S(1)}, f32[4,5,8,512]{3,2,1,0:T(8,128)S(1)}) custom-call(s32[2]{0:T(128)S(1)} %pad_add_fusion.place_ref, f32[25,5]{1,0:T(8,128)S(1)} %reshape.20.q_ref, f32[4,5,8,512]{3,2,1,0:T(8,128)S(1)} %pad_maximum_fusion.refs_0_, ...), custom_call_target="tpu_custom_call" | custom-call | flops 199999995904 | tf_op jit(solution)/shard_map/nonlinear_apart/pallas_call | solution.py:255
  130.9 0.1 collective-permute-start.10
  131.0 1.3 collective-permute-start.9
  132.2 0.6 collective-permute-start.8
  132.9 18.1 %collective-permute-done.10 = f32[4,5,8,512]{3,2,1,0:T(8,128)S(1)} collective-permute-done((f32[4,5,8,512]{3,2,1,0:T(8,128)S(1)}, f32[4,5,8,512]{3,2,1,0:T(8,128)S(1)}, u32[]{:S(2)}, u32[]{:S(2)}) %collective-permute-start.10) | collective-permute-done | bytes 327712 | tf_op jit(solution)/shard_map/ppermute | solution.py:812
  151.0 10.1 %collective-permute-done.9 = f32[4,5,8,512]{3,2,1,0:T(8,128)S(1)} collective-permute-done((f32[4,5,8,512]{3,2,1,0:T(8,128)S(1)}, f32[4,5,8,512]{3,2,1,0:T(8,128)S(1)}, u32[]{:S(2)}, u32[]{:S(2)}) %collective-permute-start.9) | collective-permute-done | bytes 327712 | tf_op jit(solution)/shard_map/ppermute | solution.py:812
  161.1 0.0 collective-permute-done.8
  161.1 0.8 pad_maximum_fusion.5
  161.9 18.8 %collective-permute-start.11 = (f32[4,5,8,512]{3,2,1,0:T(8,128)}, f32[4,5,8,512]{3,2,1,0:T(8,128)S(1)}, u32[]{:S(2)}, u32[]{:S(2)}) collective-permute-start(f32[4,5,8,512]{3,2,1,0:T(8,128)} %pad_maximum_fusion.5), channel_id=1, source_target_pairs={{0,2},{2,0},{4,6},{6,4},{1,3},{3,1},{5,7},{7,5},{8,10},{10,8},{12,... | collective-permute-start | bytes 983048 | tf_op jit(solution)/shard_map/ppermute | solution.py:812
  180.7 0.8 pad_maximum_fusion.6
  181.5 2.4 collective-permute-start.12
  183.9 0.8 pad_maximum_fusion.7
  184.7 0.6 collective-permute-start.13
  185.3 38.3 %all-to-all-done.1.in_ref = f32[48,5,8,512]{3,2,1,0:T(8,128)} async-done(((f32[48,5,8,512]{3,2,1,0:T(8,128)}), f32[48,5,8,512]{3,2,1,0:T(8,128)}, u32[]{:S(2)}, u32[]{:S(2)}) %all-to-all-start.1) | async-done | bytes 3932192 | tf_op jit(solution)/shard_map/all_to_all | solution.py:807
  223.5 0.7 copy-done.8
  224.3 4.8 %absorb.1 = (f32[2,5,48,2048]{3,2,1,0:T(8,128)S(1)}, f32[24,2048]{1,0:T(8,128)S(1)}) custom-call(f32[48,5,8,512]{3,2,1,0:T(8,128)} %all-to-all-done.1.in_ref, s32[2048]{0:T(1024)S(1)} %copy-done.1, f32[2,10,120]{2,1,0:T(8,128)S(1)} %copy-done.8, f32[2,5,48,2048]{3,2,1,0:T(8,128)} %get-tuple-element.57.refs_2_, f32[24,2048]{1,0:T(8,128)S(1)} %get-tuple-element.58.refs_3_), custom_call_target="tpu_custom_call" | custom-call | tf_op jit(solution)/shard_map/absorb/pallas_call | solution.py:472
  229.1 5.5 %solve.1.before_ref = f32[2,5,64,2048]{3,2,1,0:T(8,128)S(1)} custom-call(f32[2,5,48,2048]{3,2,1,0:T(8,128)S(1)} %get-tuple-element.59.side_ref, f32[2,5,64,2048]{3,2,1,0:T(8,128)} %up_ref.3, s32[2048]{0:T(1024)S(1)} %copy-done.1, bf16[320,960]{1,0:T(8,128)(2,1)S(1)} %get-tuple-element.60.inverse_ref), custom_call_target="tpu_custom_call" | custom-call | tf_op jit(solution)/shard_map/solve/pallas_call | solution.py:505
  234.5 4.8 %collective-permute-done.13.refs_3_ = f32[4,5,8,512]{3,2,1,0:T(8,128)S(1)} collective-permute-done((f32[4,5,8,512]{3,2,1,0:T(8,128)}, f32[4,5,8,512]{3,2,1,0:T(8,128)S(1)}, u32[]{:S(2)}, u32[]{:S(2)}) %collective-permute-start.13) | collective-permute-done | bytes 327712 | tf_op jit(solution)/shard_map/ppermute | solution.py:812
  239.3 1.6 absorb_apart.1
  240.9 1.6 collective-permute-start.14
  242.5 1.9 solve_more.1.solved_ref
  244.4 1.2 collective-permute-done.14.refs_0_.refs_1_
  245.6 3.2 %finish.1 = (f32[2,5,64,2048]{3,2,1,0:T(8,128)}, f32[2,2048]{1,0:T(2,128)}) custom-call(f32[2,5,64,2048]{3,2,1,0:T(8,128)S(1)} %solve_more.1.solved_ref, f32[24,2048]{1,0:T(8,128)S(1)} %get-tuple-element.66.sum_ref, f32[8,2048]{1,0:T(8,128)S(1)} %get-tuple-element.67.square_ref, f32[8,3072]{1,0:T(8,128)S(1)} %collective-permute-done.14.refs_0_.refs_1_, ...), custom_call_target="tpu_custom_call" | custom-call | tf_op jit(solution)/shard_map/finish/pallas_call | solution.py:594
  (40 shorter events, 0.3 us)
Async XLA Ops:
  4.5 6.5 %copy-start.1 = (s32[2048]{0:T(1024)S(1)}, s32[2048]{0:T(1024)}, u32[]{:S(2)}) copy-start(s32[2048]{0:T(1024)} %refs_4_.3) | copy-start | bytes 24580
  4.5 103.0 %all-to-all-start = ((f32[48,5,8,512]{3,2,1,0:T(8,128)}), f32[48,5,8,512]{3,2,1,0:T(8,128)}, u32[]{:S(2)}, u32[]{:S(2)}) async-start(f32[48,5,8,512]{3,2,1,0:T(8,128)} %prepare.1), calls=%async_computation | async-start | bytes 7864320 | tf_op jit(solution)/shard_map/all_to_all | solution.py:807
  11.0 115.1 %copy-start.9 = (s32[2]{0:T(128)}, s32[2]{0:T(128)S(1)}, u32[]{:S(2)}) copy-start(s32[2]{0:T(128)S(1)} %pad_add_fusion.place_ref) | copy-start | bytes 28
  11.0 55.8 %copy-start.15 = (f32[1,5,5]{2,0,1:T(1,128)S(1)}, f32[1,5,5]{2,0,1:T(1,128)}, u32[]{:S(2)}) copy-start(f32[1,5,5]{2,0,1:T(1,128)} %param.19) | copy-start | bytes 304
  11.0 56.3 %copy-start.16 = (f32[1,5,5]{2,0,1:T(1,128)S(1)}, f32[1,5,5]{2,0,1:T(1,128)}, u32[]{:S(2)}) copy-start(f32[1,5,5]{2,0,1:T(1,128)} %param.20) | copy-start | bytes 304
  11.0 56.9 %copy-start.12 = (f32[1,10,10]{2,0,1:T(1,128)S(1)}, f32[1,10,10]{2,0,1:T(1,128)}, u32[]{:S(2)}) copy-start(f32[1,10,10]{2,0,1:T(1,128)} %param.21) | copy-start | bytes 1204
  11.0 57.5 %copy-start.13 = (f32[1,10,10]{2,0,1:T(1,128)S(1)}, f32[1,10,10]{2,0,1:T(1,128)}, u32[]{:S(2)}) copy-start(f32[1,10,10]{2,0,1:T(1,128)} %param.22) | copy-start | bytes 1204
  11.0 58.1 %copy-start.14 = (f32[1,10,10]{2,0,1:T(1,128)S(1)}, f32[1,10,10]{2,0,1:T(1,128)}, u32[]{:S(2)}) copy-start(f32[1,10,10]{2,0,1:T(1,128)} %param.23) | copy-start | bytes 1204
  11.0 61.6 %copy-start.11 = (f32[5,5,5]{2,1,0:T(8,128)S(1)}, f32[5,5,5]{2,1,0:T(8,128)}, u32[]{:S(2)}) copy-start(f32[5,5,5]{2,1,0:T(8,128)} %param.17) | copy-start | bytes 1504
  11.1 64.3 %copy-start = (f32[1,320,320]{2,1,0:T(8,128)S(1)}, f32[1,320,320]{2,1,0:T(8,128)}, u32[]{:S(2)}) copy-start(f32[1,320,320]{2,1,0:T(8,128)} %param.18) | copy-start | bytes 1228804
  14.5 23.2 %collective-permute-start.2 = (f32[4,5,8,512]{3,2,1,0:T(8,128)S(1)}, f32[4,5,8,512]{3,2,1,0:T(8,128)S(1)}, u32[]{:S(2)}, u32[]{:S(2)}) collective-permute-start(f32[4,5,8,512]{3,2,1,0:T(8,128)S(1)} %get-tuple-element.40), channel_id=1, source_target_pairs={{0,24},{8,16},{16,8},{24,0},{1,25},{9,17},{17,9},{25,1},{2,26},{10... | collective-permute-start | bytes 983048 | tf_op jit(solution)/shard_map/ppermute | solution.py:812
  14.8 33.0 %collective-permute-start.1 = (f32[4,5,8,512]{3,2,1,0:T(8,128)S(1)}, f32[4,5,8,512]{3,2,1,0:T(8,128)S(1)}, u32[]{:S(2)}, u32[]{:S(2)}) collective-permute-start(f32[4,5,8,512]{3,2,1,0:T(8,128)S(1)} %get-tuple-element.39), channel_id=1, source_target_pairs={{0,16},{8,24},{16,0},{24,8},{1,17},{9,25},{17,1},{25,9},{2,18},{10... | collective-permute-start | bytes 983048 | tf_op jit(solution)/shard_map/ppermute | solution.py:812
  16.3 31.5 %collective-permute-start = (f32[4,5,8,512]{3,2,1,0:T(8,128)S(1)}, f32[4,5,8,512]{3,2,1,0:T(8,128)S(1)}, u32[]{:S(2)}, u32[]{:S(2)}) collective-permute-start(f32[4,5,8,512]{3,2,1,0:T(8,128)S(1)} %get-tuple-element.38), channel_id=1, source_target_pairs={{0,8},{8,0},{16,24},{24,16},{1,9},{9,1},{17,25},{25,17},{2,10},{10... | collective-permute-start | bytes 983048 | tf_op jit(solution)/shard_map/ppermute | solution.py:812
  47.9 35.7 %collective-permute-start.3 = (f32[4,5,8,512]{3,2,1,0:T(8,128)S(1)}, f32[4,5,8,512]{3,2,1,0:T(8,128)S(1)}, u32[]{:S(2)}, u32[]{:S(2)}) collective-permute-start(f32[4,5,8,512]{3,2,1,0:T(8,128)S(1)} %pad_maximum_fusion.1), channel_id=1, source_target_pairs={{0,2},{2,0},{4,6},{6,4},{1,3},{3,1},{5,7},{7,5},{8,10},{10,8},{12,... | collective-permute-start | bytes 983048 | tf_op jit(solution)/shard_map/ppermute | solution.py:812
  71.1 4.2 %collective-permute-start.5 = (f32[5,16,128]{2,1,0:T(8,128)}, f32[5,16,128]{2,1,0:T(8,128)S(1)}, u32[]{:S(2)}, u32[]{:S(2)}) collective-permute-start(f32[5,16,128]{2,1,0:T(8,128)} %pack.1.refs_0_), channel_id=1, source_target_pairs={{0,1},{1,0},{2,3},{3,2},{4,5},{5,4},{6,7},{7,6},{8,9},{9,8},{10,11... | collective-permute-start | bytes 122888 | tf_op jit(solution)/shard_map/ppermute | solution.py:611
  75.3 0.8 copy-start.2
  77.3 6.3 %copy-start.3 = (bf16[320,240]{1,0:T(8,128)(2,1)}, bf16[320,240]{1,0:T(8,128)(2,1)S(1)}, u32[]{:S(2)}) copy-start(bf16[320,240]{1,0:T(8,128)(2,1)S(1)} %get-tuple-element.65.inverse_ref) | copy-start | bytes 460804
  77.3 6.3 %copy-start.5 = (bf16[320,48]{1,0:T(8,128)(2,1)}, bf16[320,48]{1,0:T(8,128)(2,1)S(1)}, u32[]{:S(2)}) copy-start(bf16[320,48]{1,0:T(8,128)(2,1)S(1)} %get-tuple-element.69.refs_2_) | copy-start | bytes 92164
  77.4 17.2 %copy-start.7 = (f32[2,10,120]{2,1,0:T(8,128)}, f32[2,10,120]{2,1,0:T(8,128)S(1)}, u32[]{:S(2)}) copy-start(f32[2,10,120]{2,1,0:T(8,128)S(1)} %get-tuple-element.56.refs_1_) | copy-start | bytes 28804
  78.2 46.1 %collective-permute-start.4 = (f32[4,5,8,512]{3,2,1,0:T(8,128)}, f32[4,5,8,512]{3,2,1,0:T(8,128)S(1)}, u32[]{:S(2)}, u32[]{:S(2)}) collective-permute-start(f32[4,5,8,512]{3,2,1,0:T(8,128)} %pad_maximum_fusion.2), channel_id=1, source_target_pairs={{0,4},{2,6},{4,0},{6,2},{1,5},{3,7},{5,1},{7,3},{8,12},{10,14},{12... | collective-permute-start | bytes 983048 | tf_op jit(solution)/shard_map/ppermute | solution.py:812
  89.5 5.0 %collective-permute-start.6 = (f32[16,2048]{1,0:T(8,128)S(1)}, f32[16,2048]{1,0:T(8,128)S(1)}, u32[]{:S(2)}, u32[]{:S(2)}) collective-permute-start(f32[16,2048]{1,0:T(8,128)S(1)} %edge.1.refs_0_), channel_id=1, source_target_pairs={{0,1},{1,0},{2,3},{3,2},{4,5},{5,4},{6,7},{7,6},{8,9},{9,8},{10,11... | collective-permute-start | bytes 393224 | tf_op jit(solution)/shard_map/ppermute | solution.py:611
  105.1 21.0 %collective-permute-start.7 = (f32[4,5,8,512]{3,2,1,0:T(8,128)}, f32[4,5,8,512]{3,2,1,0:T(8,128)}, u32[]{:S(2)}, u32[]{:S(2)}) collective-permute-start(f32[4,5,8,512]{3,2,1,0:T(8,128)} %pad_maximum_fusion.3), channel_id=1, source_target_pairs={{0,6},{2,4},{4,2},{6,0},{1,7},{3,5},{5,3},{7,1},{8,14},{10,12},{12... | collective-permute-start | bytes 983048 | tf_op jit(solution)/shard_map/ppermute | solution.py:812
  119.5 104.0 %all-to-all-start.1 = ((f32[48,5,8,512]{3,2,1,0:T(8,128)}), f32[48,5,8,512]{3,2,1,0:T(8,128)}, u32[]{:S(2)}, u32[]{:S(2)}) async-start(f32[48,5,8,512]{3,2,1,0:T(8,128)} %bitcast.7), calls=%async_computation.1 | async-start | bytes 7864320 | tf_op jit(solution)/shard_map/all_to_all | solution.py:807
  130.9 20.0 %collective-permute-start.10 = (f32[4,5,8,512]{3,2,1,0:T(8,128)S(1)}, f32[4,5,8,512]{3,2,1,0:T(8,128)S(1)}, u32[]{:S(2)}, u32[]{:S(2)}) collective-permute-start(f32[4,5,8,512]{3,2,1,0:T(8,128)S(1)} %get-tuple-element.52), channel_id=1, source_target_pairs={{0,24},{8,16},{16,8},{24,0},{1,25},{9,17},{17,9},{25,1},{2,26},{10... | collective-permute-start | bytes 983048 | tf_op jit(solution)/shard_map/ppermute | solution.py:812
  131.0 30.1 %collective-permute-start.9 = (f32[4,5,8,512]{3,2,1,0:T(8,128)S(1)}, f32[4,5,8,512]{3,2,1,0:T(8,128)S(1)}, u32[]{:S(2)}, u32[]{:S(2)}) collective-permute-start(f32[4,5,8,512]{3,2,1,0:T(8,128)S(1)} %get-tuple-element.51), channel_id=1, source_target_pairs={{0,16},{8,24},{16,0},{24,8},{1,17},{9,25},{17,1},{25,9},{2,18},{10... | collective-permute-start | bytes 983048 | tf_op jit(solution)/shard_map/ppermute | solution.py:812
  132.2 28.9 %collective-permute-start.8 = (f32[4,5,8,512]{3,2,1,0:T(8,128)S(1)}, f32[4,5,8,512]{3,2,1,0:T(8,128)S(1)}, u32[]{:S(2)}, u32[]{:S(2)}) collective-permute-start(f32[4,5,8,512]{3,2,1,0:T(8,128)S(1)} %get-tuple-element.50), channel_id=1, source_target_pairs={{0,8},{8,0},{16,24},{24,16},{1,9},{9,1},{17,25},{25,17},{2,10},{10... | collective-permute-start | bytes 983048 | tf_op jit(solution)/shard_map/ppermute | solution.py:812
  161.9 72.6 %collective-permute-start.11 = (f32[4,5,8,512]{3,2,1,0:T(8,128)}, f32[4,5,8,512]{3,2,1,0:T(8,128)S(1)}, u32[]{:S(2)}, u32[]{:S(2)}) collective-permute-start(f32[4,5,8,512]{3,2,1,0:T(8,128)} %pad_maximum_fusion.5), channel_id=1, source_target_pairs={{0,2},{2,0},{4,6},{6,4},{1,3},{3,1},{5,7},{7,5},{8,10},{10,8},{12,... | collective-permute-start | bytes 983048 | tf_op jit(solution)/shard_map/ppermute | solution.py:812
  181.5 53.0 %collective-permute-start.12 = (f32[4,5,8,512]{3,2,1,0:T(8,128)}, f32[4,5,8,512]{3,2,1,0:T(8,128)S(1)}, u32[]{:S(2)}, u32[]{:S(2)}) collective-permute-start(f32[4,5,8,512]{3,2,1,0:T(8,128)} %pad_maximum_fusion.6), channel_id=1, source_target_pairs={{0,4},{2,6},{4,0},{6,2},{1,5},{3,7},{5,1},{7,3},{8,12},{10,14},{12... | collective-permute-start | bytes 983048 | tf_op jit(solution)/shard_map/ppermute | solution.py:812
  184.7 54.7 %collective-permute-start.13 = (f32[4,5,8,512]{3,2,1,0:T(8,128)}, f32[4,5,8,512]{3,2,1,0:T(8,128)S(1)}, u32[]{:S(2)}, u32[]{:S(2)}) collective-permute-start(f32[4,5,8,512]{3,2,1,0:T(8,128)} %pad_maximum_fusion.7), channel_id=1, source_target_pairs={{0,6},{2,4},{4,2},{6,0},{1,7},{3,5},{5,3},{7,1},{8,14},{10,12},{12... | collective-permute-start | bytes 983048 | tf_op jit(solution)/shard_map/ppermute | solution.py:812
  223.5 0.7 copy-start.8
  229.0 10.3 %copy-start.10 = (s32[2]{0:T(128)S(1)}, s32[2]{0:T(128)}, u32[]{:S(2)}) copy-start(s32[2]{0:T(128)} %copy-done.9) | copy-start | bytes 28
  229.1 13.4 %copy-start.4 = (bf16[320,240]{1,0:T(8,128)(2,1)S(1)}, bf16[320,240]{1,0:T(8,128)(2,1)}, u32[]{:S(2)}) copy-start(bf16[320,240]{1,0:T(8,128)(2,1)} %copy-done.3) | copy-start | bytes 460804
  240.9 4.7 %collective-permute-start.14 = (f32[8,3072]{1,0:T(8,128)S(1)}, f32[8,3072]{1,0:T(8,128)S(1)}, u32[]{:S(2)}, u32[]{:S(2)}) collective-permute-start(f32[8,3072]{1,0:T(8,128)S(1)} %get-tuple-element.68), channel_id=1, source_target_pairs={{0,1},{1,0},{2,3},{3,2},{4,5},{5,4},{6,7},{7,6},{8,9},{9,8},{10,11... | collective-permute-start | bytes 294920 | tf_op jit(solution)/shard_map/ppermute | solution.py:619
  242.5 3.1 %copy-start.6 = (bf16[320,48]{1,0:T(8,128)(2,1)S(1)}, bf16[320,48]{1,0:T(8,128)(2,1)}, u32[]{:S(2)}) copy-start(bf16[320,48]{1,0:T(8,128)(2,1)} %copy-done.5) | copy-start | bytes 92164
